TPU v7x, 32 devices: a whole 2x2x4 slice. The times are simulated.
32 devices in a mesh: gx: 4 (over y, core), yz: 8 (over z, x).
Axes of the slice: x: 2, y: 2, z: 4, core: 2. Of those that a mesh axis runs over, the one named last changes fastest.
Arguments:
- forcing: float32 [4, 8, 128, 512], P('gx', 'yz'), may hold values from -60 to 60
- viscosity: float32 [4, 8, 128, 512], P('gx', 'yz'), may hold values from 0.02 to 0.5
- mass_rate: float32 [4, 8, 128, 512], P('gx', 'yz'), may hold values from 10 to 80
- slot_element: int32 [4, 8, 128], P('gx', 'yz'), may hold values from 0 to 127, as said below
Outputs:
- solution: float32 [4, 8, 128, 512], P('gx', 'yz')
- residual: float32 [4, 8, 128, 512], P('gx', 'yz')
Inputs may be any that keep to these rules, and one draw needn't show every extreme that they name: `slot_element`: in each device block the 128 entries are every number 0 to 127 once.
All inputs are finite; a program needn't handle non-finite values.
Results may differ from a plain program's by a relative error of at most 0.0045.
Values sent between devices are 32-bit elements; how exact they have to be, the bound alone decides.
No kernel may reach another device: no remote copies, remote signals or barrier semaphores. Data moves between devices by JAX's collectives and lax.ppermute only.
A program may use at most 64 MiB of HBM per device.

v0:
```python
import jax
import jax.numpy as jnp
import numpy as np
from jax import lax
from jax.sharding import PartitionSpec as P

EX = 2
EY = 1
EZ = 64
ITERS = 3


axis_weights = (1.0, 1.0, 4.0)
highest = lax.Precision.HIGHEST


def passed_along(block, axis, distance):
    devices = range(lax.axis_size(axis))
    route = [((i - distance) % len(devices), i) for i in devices]
    return lax.ppermute(block, axis, route)


def legendre_rows(nodes, degree):
    rows = [nodes * 0.0 + 1.0, nodes]
    for order in range(2, degree + 1):
        rows.append(((2 * order - 1) * nodes * rows[-1] - (order - 1) * rows[-2]) / order)
    return np.stack(rows, 1)


def spectral_tables():
    degree = 7
    nodes = np.cos(np.pi * np.arange(degree + 1) / degree)
    for sweep in range(60):
        legendre = legendre_rows(nodes, degree)
        nodes = nodes - (nodes * legendre[:, degree] - legendre[:, degree - 1]) / (
            (degree + 1) * legendre[:, degree]
        )
    nodes = nodes[::-1].copy()
    top_values = legendre_rows(nodes, degree)[:, degree]
    weights = 2.0 / (degree * (degree + 1) * top_values**2)
    identity = np.eye(degree + 1)
    spacing = nodes[:, None] - nodes[None, :] + identity
    derivative = top_values[:, None] / top_values[None, :] / spacing * (1.0 - identity)
    corner_fix = np.zeros(degree + 1)
    corner_fix[0] = -degree * (degree + 1) / 4.0
    corner_fix[degree] = degree * (degree + 1) / 4.0
    derivative = derivative + identity * corner_fix[None, :]
    kron_table = np.concatenate(
        (np.kron(derivative, identity).T, np.kron(identity, derivative).T), 1
    )
    weights3 = (weights[:, None, None] * weights[None, :, None] * weights[None, None, :]).reshape(
        -1
    )
    return (derivative, kron_table, weights3)


def inverse_multiplicity(depth):
    point = np.arange(512)
    ends_a = (point // 64 % 7 == 0) * 1.0
    ends_b = (point // 8 % 8 % 7 == 0) * 1.0
    within = point % 8
    layer = np.arange(depth)[:, None]
    vertical = 1.0 + ((within == 0) & (layer > 0)) + ((within == 7) & (layer < depth - 1))
    return 1.0 / ((1.0 + ends_a) * (1.0 + ends_b) * vertical)


def contract(values, coef_x, coef_yz, coef_mass, derivative, kron_table):
    elements = values.shape[0]
    slab_view = values.reshape(elements, 8, 64)
    grad_x = jnp.einsum("ab,ebk->eak", derivative, slab_view, precision=highest)
    grad_yz = jnp.dot(values.reshape(elements * 8, 64), kron_table, precision=highest)
    back_x = jnp.einsum("ba,ebk->eak", derivative, grad_x * coef_x, precision=highest).reshape(
        elements, 512
    )
    back_yz = jnp.dot(grad_yz * coef_yz, kron_table.T, precision=highest).reshape(elements, 512)
    return back_x + back_yz + coef_mass * values


def join_faces(low_face, high_face, high_before, low_after, position):
    extent = low_face.shape[position]
    shifted_low = jnp.concatenate(
        (
            lax.slice_in_dim(low_face, 1, extent, axis=position),
            jnp.expand_dims(low_after, position),
        ),
        position,
    )
    summed = high_face + shifted_low
    first_sum = high_before + lax.index_in_dim(low_face, 0, position, keepdims=False)
    new_low = jnp.concatenate(
        (
            jnp.expand_dims(first_sum, position),
            lax.slice_in_dim(summed, 0, extent - 1, axis=position),
        ),
        position,
    )
    return (new_low, summed)


def join_walls(low_face, high_face, position):
    extent = low_face.shape[position]
    summed = lax.slice_in_dim(high_face, 0, extent - 1, axis=position) + lax.slice_in_dim(
        low_face, 1, extent, axis=position
    )
    new_high = jnp.concatenate(
        (summed, lax.slice_in_dim(high_face, extent - 1, extent, axis=position)), position
    )
    new_low = jnp.concatenate((lax.slice_in_dim(low_face, 0, 1, axis=position), summed), position)
    return (new_low, new_high)


def sides_in_turn(values):
    outer_shape = values.shape
    low_face = values[..., :64]
    high_face = values[..., 448:]
    last_x = outer_shape[1] - 1
    high_before = passed_along(high_face[:, last_x], "gx", 1)
    low_after = passed_along(low_face[:, 0], "gx", -1)
    new_low, new_high = join_faces(low_face, high_face, high_before, low_after, 1)
    values = jnp.concatenate((new_low, values[..., 64:448], new_high), -1)
    planes = values.reshape(outer_shape[:4] + (8, 64))
    low_face = planes[..., 0:8]
    high_face = planes[..., 56:64]
    last_y = outer_shape[2] - 1
    high_before = passed_along(high_face[:, :, last_y], "yz", 1)
    low_after = passed_along(low_face[:, :, 0], "yz", -1)
    new_low, new_high = join_faces(low_face, high_face, high_before, low_after, 2)
    return jnp.concatenate((new_low, planes[..., 8:56], new_high), -1).reshape(outer_shape)


def assemble(values):
    outer_shape = values.shape
    values = sides_in_turn(values)
    column_view = values.reshape(outer_shape[:4] + (64, 8))
    new_low, new_high = join_walls(column_view[..., 0], column_view[..., 7], 3)
    return jnp.concatenate(
        (new_low[..., None], column_view[..., 1:7], new_high[..., None]), -1
    ).reshape(outer_shape)


def residual_norm(residual, precond, inv_mult):
    return lax.psum(jnp.sum(residual * precond * inv_mult), ("gx", "yz"))


def body(forcing, viscosity, mass_rate, slot_element):
    elements = slot_element.shape[2]
    order_slots = slot_element[0, 0]
    inverse = (
        jnp.zeros((elements,), jnp.int32).at[order_slots].set(jnp.arange(elements, dtype=jnp.int32))
    )
    derivative_np, kron_np, weights_np = spectral_tables()
    derivative = jnp.asarray(derivative_np, jnp.float32)
    kron_table = jnp.asarray(kron_np, jnp.float32)
    weights3 = jnp.asarray(weights_np, jnp.float32)
    inv_mult = jnp.asarray(inverse_multiplicity(EZ), jnp.float32)
    grid_shape = (1, EX, EY, EZ, 512)

    def to_grid(values):
        return jnp.take(values[0, 0], inverse, axis=0)

    def to_slots(values):
        return jnp.take(values.reshape(elements, 512), order_slots, axis=0).reshape(
            1, 1, elements, 512
        )

    spread = to_grid(viscosity) * weights3
    coef_x = (axis_weights[0] * spread).reshape(elements, 8, 64)
    coef_yz = jnp.concatenate(
        (
            (axis_weights[1] * spread).reshape(elements * 8, 64),
            (axis_weights[2] * spread).reshape(elements * 8, 64),
        ),
        1,
    )
    coef_mass = to_grid(mass_rate) * weights3
    part_x = jnp.einsum("ba,ebk->eak", derivative * derivative, coef_x, precision=highest).reshape(
        elements, 512
    )
    part_yz = jnp.dot(coef_yz, (kron_table * kron_table).T, precision=highest).reshape(
        elements, 512
    )
    diagonal_local = part_x + part_yz + coef_mass
    stacked = jnp.stack((to_grid(forcing), diagonal_local), 0).reshape((2, EX, EY, EZ, 512))
    assembled = assemble(stacked)
    right_side = assembled[0]
    jacobi = 1.0 / assembled[1]
    solution = jnp.zeros(right_side.shape, jnp.float32)
    residual = right_side
    precond = jacobi * residual
    direction = precond
    norm_now = residual_norm(residual, precond, inv_mult)
    for step in range(ITERS):
        local_terms = contract(
            direction.reshape(elements, 512), coef_x, coef_yz, coef_mass, derivative, kron_table
        )
        mapped = assemble(local_terms.reshape(grid_shape))[0]
        step_len = norm_now / lax.psum(jnp.sum(direction * mapped * inv_mult), ("gx", "yz"))
        solution = solution + step_len * direction
        residual = residual - step_len * mapped
        if step + 1 < ITERS:
            precond = jacobi * residual
            norm_next = residual_norm(residual, precond, inv_mult)
            direction = precond + norm_next / norm_now * direction
            norm_now = norm_next
    return (to_slots(solution), to_slots(residual))


def solution(mesh):
    placed = (
        P("gx", "yz", None, None),
        P("gx", "yz", None, None),
        P("gx", "yz", None, None),
        P("gx", "yz", None),
    )
    return jax.shard_map(
        body,
        mesh=mesh,
        in_specs=placed,
        out_specs=(P("gx", "yz", None, None), P("gx", "yz", None, None)),
        check_vma=False,
    )
```

profile of v0, /device:TPU:0, one launch (start us, length us, event | category | flops | bytes accessed | tf_op | source)
XLA Modules:
  0.0 422.2 jit_solution(11806960799100842596)
XLA Ops:
  9.5 3.9 collective-permute-done
  17.9 5.4 %collective-permute-start.3 = (f32[2,2,64,8,8]{2,4,3,1,0:T(8,128)S(1)}, f32[2,2,64,8,8]{2,4,3,1,0:T(8,128)S(1)}, u32[]{:S(2)}, u32[]{:S(2)}) collective-permute-start(f32[2,2,64,8,8]{2,4,3,1,0:T(8,128)S(1)} %slice_bitcast_fusion), channel_id=1, source_target_pairs={{1,0},{2,1},{3,2},{4,3},{5,4},{6,5},{7,6},{0,7},{9,8},{10,9},{11,1... | collective-permute-start | bytes 196616 | tf_op jit(solution)/shard_map/ppermute | solution.py:20
  23.3 3.2 collective-permute-done.3
  29.2 7.8 %collective-permute-done.2 = f32[2,2,64,8,8]{2,4,3,1,0:T(8,128)S(1)} collective-permute-done((f32[2,2,64,8,8]{2,4,3,1,0:T(8,128)S(1)}, f32[2,2,64,8,8]{2,4,3,1,0:T(8,128)S(1)}, u32[]{:S(2)}, u32[]{:S(2)}) %collective-permute-start.2) | collective-permute-done | bytes 65568 | tf_op jit(solution)/shard_map/ppermute | solution.py:20
  40.8 4.4 %copy.56 = f32[1,2,1,64,64,8]{5,4,3,1,2,0:T(8,128)} copy(f32[1,2,1,64,64,8]{3,5,4,1,0,2:T(8,128)S(1)} %get-tuple-element.25) | data formatting | bytes 524288 | tf_op jit(solution)/shard_map/div | solution.py:186
  46.6 5.4 %copy.57 = f32[1,2,1,64,64,8]{5,4,3,1,2,0:T(8,128)} copy(f32[1,2,1,64,64,8]{3,5,4,1,0,2:T(8,128)} %get-tuple-element.24) | data formatting | bytes 524288 | tf_op jit(solution)/shard_map/slice | solution.py:185
  51.9 2.2 copy.53
  56.2 2.0 squeeze.112
  58.3 2.1 squeeze.114
  60.3 3.2 div.60
  63.6 3.9 squeeze.113
  83.1 2.0 collective-permute-done.4
  86.0 2.0 copy.68
  90.4 2.7 collective-permute-done.7
  95.0 5.9 %collective-permute-done.6 = f32[1,2,64,8,8]{2,4,3,1,0:T(8,128)S(1)} collective-permute-done((f32[1,2,64,8,8]{2,4,3,1,0:T(8,128)S(1)}, f32[1,2,64,8,8]{2,4,3,1,0:T(8,128)S(1)}, u32[]{:S(2)}, u32[]{:S(2)}) %collective-permute-start.6) | collective-permute-done | bytes 32800 | tf_op jit(solution)/shard_map/ppermute | solution.py:20
  104.2 37.3 %all-reduce = (f32[]{:T(128)}, f32[]{:T(128)}) all-reduce(f32[]{:T(128)} %get-tuple-element.4, f32[]{:T(128)} %get-tuple-element.3), channel_id=1, replica_groups=mesh['gx'=4,'yz'=8] {'gx','yz'}, use_global_device_ids=true, to_apply=%region_2.4 | all-reduce | flops 2 | bytes 16 | tf_op jit(solution)/shard_map/psum | solution.py:142
  142.8 2.1 multiply_reduce_fusion.3
  144.9 4.4 %copy.77 = f32[1,2,1,64,64,8]{5,4,3,1,2,0:T(8,128)} copy(f32[1,2,1,64,64,8]{3,5,4,1,0,2:T(8,128)S(1)} %get-tuple-element.16) | data formatting | bytes 524288 | tf_op jit(solution)/shard_map/mul | solution.py:199
  150.5 2.0 mul.429
  152.5 2.1 mul.439
  154.6 3.9 mul.434
  158.5 2.1 sub.60
  160.6 42.4 %psum.44 = f32[]{:T(128)} all-reduce(f32[]{:T(128)} %get-tuple-element.15), channel_id=1, replica_groups=mesh['gx'=4,'yz'=8] {'gx','yz'}, use_global_device_ids=true, to_apply=%region_6.8 | all-reduce | flops 1 | bytes 8 | tf_op jit(solution)/shard_map/psum | solution.py:142
  209.4 2.0 multiply_add_fusion.10
  217.7 2.2 multiply_add_fusion.8
  222.2 2.2 collective-permute-done.8
  225.2 1.9 copy.88
  228.1 2.3 collective-permute-start.11
  230.4 2.0 collective-permute-done.11
  233.2 2.3 collective-permute-start.10
  236.5 4.0 collective-permute-done.10
  243.5 37.4 %psum.45 = f32[]{:T(128)} all-reduce(f32[]{:T(128)} %multiply_reduce_fusion.2), channel_id=1, replica_groups=mesh['gx'=4,'yz'=8] {'gx','yz'}, use_global_device_ids=true, to_apply=%region_8.10 | all-reduce | flops 1 | bytes 8 | tf_op jit(solution)/shard_map/psum | solution.py:197
  282.2 3.0 multiply_reduce_fusion.1
  285.2 5.3 %copy.97 = f32[1,2,1,64,64,8]{5,4,3,1,2,0:T(8,128)} copy(f32[1,2,1,64,64,8]{3,5,4,1,0,2:T(8,128)} %get-tuple-element.10) | data formatting | bytes 524288 | tf_op jit(solution)/shard_map/mul | solution.py:199
  290.5 2.3 copy.94
  292.7 2.0 mul.455
  294.8 2.1 mul.465
  296.8 3.9 mul.460
  300.8 42.4 %psum.46 = f32[]{:T(128)} all-reduce(f32[]{:T(128)} %get-tuple-element.9), channel_id=1, replica_groups=mesh['gx'=4,'yz'=8] {'gx','yz'}, use_global_device_ids=true, to_apply=%region_10.12 | all-reduce | flops 1 | bytes 8 | tf_op jit(solution)/shard_map/psum | solution.py:142
  344.5 2.0 convolution_multiply_fusion
  353.1 2.1 multiply_add_fusion.5
  357.4 2.2 collective-permute-done.12
  361.6 2.2 collective-permute-start.15
  363.9 2.0 collective-permute-done.15
  366.7 2.2 collective-permute-start.14
  370.0 4.0 collective-permute-done.14
  375.4 2.1 multiply_reduce_fusion
  377.5 37.3 %psum.47 = f32[]{:T(128)} all-reduce(f32[]{:T(128)} %multiply_reduce_fusion), channel_id=1, replica_groups=mesh['gx'=4,'yz'=8] {'gx','yz'}, use_global_device_ids=true, to_apply=%region_12.14 | all-reduce | flops 1 | bytes 8 | tf_op jit(solution)/shard_map/psum | solution.py:197
  (213 shorter events, 87.9 us)
Async XLA Ops:
  0.6 1.8 copy-start
  0.6 4.4 %copy-start.26 = (f32[512]{0:T(512)S(1)}, f32[512]{0:T(512)}, u32[]{:S(2)}) copy-start(f32[512]{0:T(512)} %constant.30.clone) | copy-start | bytes 6148
  0.7 4.9 %copy-start.28 = (f32[64,64]{1,0:T(8,128)S(1)}, f32[64,64]{1,0:T(8,128)}, u32[]{:S(2)}) copy-start(f32[64,64]{1,0:T(8,128)} %constant.39) | copy-start | bytes 49156
  2.4 3.9 copy-start.27
  3.2 4.2 copy-start.29
  5.0 3.1 copy-start.1
  5.4 69.5 %copy-start.4 = (f32[128,512]{0,1:T(8,128)}, f32[128,512]{0,1:T(8,128)S(1)}, u32[]{:S(2)}) copy-start(f32[128,512]{0,1:T(8,128)S(1)} %copy.38) | copy-start | bytes 786436
  8.9 20.3 %copy-start.7 = (f32[128,512]{1,0:T(8,128)}, f32[128,512]{1,0:T(8,128)S(1)}, u32[]{:S(2)}) copy-start(f32[128,512]{1,0:T(8,128)S(1)} %gather_fusion.2) | copy-start | bytes 786436
  9.1 4.4 %collective-permute-start = (f32[2,1,64,64]{3,2,0,1:T(8,128)S(1)}, f32[2,1,64,64]{3,2,0,1:T(8,128)S(1)}, u32[]{:S(2)}, u32[]{:S(2)}) collective-permute-start(f32[2,1,64,64]{3,2,0,1:T(8,128)S(1)} %get-tuple-element.43), channel_id=1, source_target_pairs={{24,0},{0,8},{8,16},{16,24},{25,1},{1,9},{9,17},{17,25},{26,2},{2,... | collective-permute-start | bytes 98312 | tf_op jit(solution)/shard_map/ppermute | solution.py:20
  13.5 2.0 collective-permute-start.1
  17.9 8.6 %collective-permute-start.3 = (f32[2,2,64,8,8]{2,4,3,1,0:T(8,128)S(1)}, f32[2,2,64,8,8]{2,4,3,1,0:T(8,128)S(1)}, u32[]{:S(2)}, u32[]{:S(2)}) collective-permute-start(f32[2,2,64,8,8]{2,4,3,1,0:T(8,128)S(1)} %slice_bitcast_fusion), channel_id=1, source_target_pairs={{1,0},{2,1},{3,2},{4,3},{5,4},{6,5},{7,6},{0,7},{9,8},{10,9},{11,1... | collective-permute-start | bytes 196616 | tf_op jit(solution)/shard_map/ppermute | solution.py:20
  27.4 9.6 %collective-permute-start.2 = (f32[2,2,64,8,8]{2,4,3,1,0:T(8,128)S(1)}, f32[2,2,64,8,8]{2,4,3,1,0:T(8,128)S(1)}, u32[]{:S(2)}, u32[]{:S(2)}) collective-permute-start(f32[2,2,64,8,8]{2,4,3,1,0:T(8,128)S(1)} %get-tuple-element.28), channel_id=1, source_target_pairs={{7,0},{0,1},{1,2},{2,3},{3,4},{4,5},{5,6},{6,7},{15,8},{8,9},{9,10... | collective-permute-start | bytes 196616 | tf_op jit(solution)/shard_map/ppermute | solution.py:20
  40.0 0.8 copy-start.13
  63.6 5.9 %copy-start.21 = (f32[64,128]{1,0:T(8,128)S(1)}, f32[64,128]{1,0:T(8,128)}, u32[]{:S(2)}) copy-start(f32[64,128]{1,0:T(8,128)} %constant.14.clone) | copy-start | bytes 98308
  67.5 6.8 %copy-start.25 = (f32[8,8,1]{0,1,2:T(8,128)S(1)}, f32[8,8,1]{0,1,2:T(8,128)}, u32[]{:S(2)}) copy-start(f32[8,8,1]{0,1,2:T(8,128)} %constant.42) | copy-start | bytes 772
  68.6 0.8 copy-start.3
  69.4 10.0 %copy-start.8 = (f32[128,512]{1,0:T(8,128)S(1)}, f32[128,512]{1,0:T(8,128)}, u32[]{:S(2)}) copy-start(f32[128,512]{1,0:T(8,128)} %copy-done.7) | copy-start | bytes 786436
  74.4 0.7 copy-start.19
  77.6 24.4 %copy-start.5 = (f32[128,512]{1,0:T(8,128)}, f32[128,512]{1,0:T(8,128)S(1)}, u32[]{:S(2)}) copy-start(f32[128,512]{1,0:T(8,128)S(1)} %copy.62) | copy-start | bytes 786436
  81.3 21.0 %copy-start.10 = (f32[64,64,8]{0,2,1:T(8,128)S(1)}, f32[64,64,8]{0,2,1:T(8,128)}, u32[]{:S(2)}) copy-start(f32[64,64,8]{0,2,1:T(8,128)} %constant.38) | copy-start | bytes 393220
  81.4 1.6 collective-permute-start.5
  81.4 3.7 collective-permute-start.4
  88.8 4.3 %collective-permute-start.7 = (f32[1,2,64,8,8]{2,4,3,1,0:T(8,128)S(1)}, f32[1,2,64,8,8]{2,4,3,1,0:T(8,128)S(1)}, u32[]{:S(2)}, u32[]{:S(2)}) collective-permute-start(f32[1,2,64,8,8]{2,4,3,1,0:T(8,128)S(1)} %slice_bitcast_fusion.4), channel_id=1, source_target_pairs={{1,0},{2,1},{3,2},{4,3},{5,4},{6,5},{7,6},{0,7},{9,8},{10,9},{11,1... | collective-permute-start | bytes 98312 | tf_op jit(solution)/shard_map/ppermute | solution.py:20
  93.9 7.0 %collective-permute-start.6 = (f32[1,2,64,8,8]{2,4,3,1,0:T(8,128)S(1)}, f32[1,2,64,8,8]{2,4,3,1,0:T(8,128)S(1)}, u32[]{:S(2)}, u32[]{:S(2)}) collective-permute-start(f32[1,2,64,8,8]{2,4,3,1,0:T(8,128)S(1)} %get-tuple-element.40), channel_id=1, source_target_pairs={{7,0},{0,1},{1,2},{2,3},{3,4},{4,5},{5,6},{6,7},{15,8},{8,9},{9,10... | collective-permute-start | bytes 98312 | tf_op jit(solution)/shard_map/ppermute | solution.py:20
  101.9 2.3 copy-start.15
  102.3 1.9 copy-start.23
  220.0 2.1 collective-permute-start.9
  220.5 3.9 collective-permute-start.8
  227.2 15.3 %copy-start.11 = (f32[64,64,8]{0,2,1:T(8,128)S(1)}, f32[64,64,8]{0,2,1:T(8,128)}, u32[]{:S(2)}) copy-start(f32[64,64,8]{0,2,1:T(8,128)} %constant.38) | copy-start | bytes 393220
  227.2 15.3 %copy-start.17 = (f32[1,2,1,64,64,8]{3,5,4,1,0,2:T(8,128)S(1)}, f32[1,2,1,64,64,8]{3,5,4,1,0,2:T(8,128)}, u32[]{:S(2)}) copy-start(f32[1,2,1,64,64,8]{3,5,4,1,0,2:T(8,128)} %get-tuple-element.17) | copy-start | bytes 786436
  228.1 4.3 %collective-permute-start.11 = (f32[1,2,64,8,8]{2,4,3,1,0:T(8,128)S(1)}, f32[1,2,64,8,8]{2,4,3,1,0:T(8,128)S(1)}, u32[]{:S(2)}, u32[]{:S(2)}) collective-permute-start(f32[1,2,64,8,8]{2,4,3,1,0:T(8,128)S(1)} %slice_bitcast_fusion.3), channel_id=1, source_target_pairs={{1,0},{2,1},{3,2},{4,3},{5,4},{6,5},{7,6},{0,7},{9,8},{10,9},{11,1... | collective-permute-start | bytes 98312 | tf_op jit(solution)/shard_map/ppermute | solution.py:20
  233.2 7.3 %collective-permute-start.10 = (f32[1,2,64,8,8]{2,4,3,1,0:T(8,128)S(1)}, f32[1,2,64,8,8]{2,4,3,1,0:T(8,128)S(1)}, u32[]{:S(2)}, u32[]{:S(2)}) collective-permute-start(f32[1,2,64,8,8]{2,4,3,1,0:T(8,128)S(1)} %get-tuple-element.36), channel_id=1, source_target_pairs={{7,0},{0,1},{1,2},{2,3},{3,4},{4,5},{5,6},{6,7},{15,8},{8,9},{9,10... | collective-permute-start | bytes 98312 | tf_op jit(solution)/shard_map/ppermute | solution.py:20
  241.4 0.8 copy-start.16
  241.8 0.6 copy-start.24
  346.5 5.7 %copy-start.22 = (f32[128,512]{0,1:T(8,128)S(1)}, f32[128,512]{0,1:T(8,128)}, u32[]{:S(2)}) copy-start(f32[128,512]{0,1:T(8,128)} %mul.465) | copy-start | bytes 786436
  346.5 6.5 %copy-start.6 = (f32[128,512]{1,0:T(8,128)S(1)}, f32[128,512]{1,0:T(8,128)}, u32[]{:S(2)}) copy-start(f32[128,512]{1,0:T(8,128)} %copy-done.5) | copy-start | bytes 786436
  346.5 6.5 %copy-start.9 = (f32[128,512]{1,0:T(8,128)S(1)}, f32[128,512]{1,0:T(8,128)}, u32[]{:S(2)}) copy-start(f32[128,512]{1,0:T(8,128)} %copy-done.7) | copy-start | bytes 786436
  346.5 6.5 %copy-start.18 = (f32[128,512]{1,0:T(8,128)S(1)}, f32[128,512]{1,0:T(8,128)}, u32[]{:S(2)}) copy-start(f32[128,512]{1,0:T(8,128)} %get-tuple-element.19) | copy-start | bytes 786436
  349.2 14.6 %copy-start.30 = (s32[1,1,128]{2,1,0:T(1,128)S(1)}, s32[1,1,128]{2,1,0:T(1,128)}, u32[]{:S(2)}) copy-start(s32[1,1,128]{2,1,0:T(1,128)} %param.13) | copy-start | bytes 1540
  353.0 22.3 %copy-start.2 = (f32[1,2,1,64,64,8]{3,5,4,1,0,2:T(8,128)S(1)}, f32[1,2,1,64,64,8]{3,5,4,1,0,2:T(8,128)}, u32[]{:S(2)}) copy-start(f32[1,2,1,64,64,8]{3,5,4,1,0,2:T(8,128)} %get-tuple-element.10) | copy-start | bytes 786436
  353.0 22.3 %copy-start.12 = (f32[64,64,8]{0,2,1:T(8,128)S(1)}, f32[64,64,8]{0,2,1:T(8,128)}, u32[]{:S(2)}) copy-start(f32[64,64,8]{0,2,1:T(8,128)} %constant.38) | copy-start | bytes 393220
  355.2 2.1 collective-permute-start.13
  355.7 3.9 collective-permute-start.12
  361.6 4.3 %collective-permute-start.15 = (f32[1,2,64,8,8]{2,4,3,1,0:T(8,128)S(1)}, f32[1,2,64,8,8]{2,4,3,1,0:T(8,128)S(1)}, u32[]{:S(2)}, u32[]{:S(2)}) collective-permute-start(f32[1,2,64,8,8]{2,4,3,1,0:T(8,128)S(1)} %slice_bitcast_fusion.2), channel_id=1, source_target_pairs={{1,0},{2,1},{3,2},{4,3},{5,4},{6,5},{7,6},{0,7},{9,8},{10,9},{11,1... | collective-permute-start | bytes 98312 | tf_op jit(solution)/shard_map/ppermute | solution.py:20
  366.7 7.2 %collective-permute-start.14 = (f32[1,2,64,8,8]{2,4,3,1,0:T(8,128)S(1)}, f32[1,2,64,8,8]{2,4,3,1,0:T(8,128)S(1)}, u32[]{:S(2)}, u32[]{:S(2)}) collective-permute-start(f32[1,2,64,8,8]{2,4,3,1,0:T(8,128)S(1)} %get-tuple-element.32), channel_id=1, source_target_pairs={{7,0},{0,1},{1,2},{2,3},{3,4},{4,5},{5,6},{6,7},{15,8},{8,9},{9,10... | collective-permute-start | bytes 98312 | tf_op jit(solution)/shard_map/ppermute | solution.py:20
  375.0 2.5 copy-start.14
  375.0 43.2 %copy-start.20 = (f32[128,512]{1,0:T(8,128)S(1)}, f32[128,512]{1,0:T(8,128)}, u32[]{:S(2)}) copy-start(f32[128,512]{1,0:T(8,128)} %get-tuple-element.12) | copy-start | bytes 786436
where the time goes:
time: 429 us; the launch traced here: 422 us
  blocking collectives  197 us (46%)
  local copies, waits for them, and re-layouts  96.1 us (22%)
  waiting for transfers between devices  47.7 us (11%)
  other arithmetic  41.8 us (10%)
  starting transfers between devices  18.7 us (4%)
  matrix products  12.6 us (3%)
  between operations  8.56 us (2%)
    psum x3, blocking collectives, residual_norm(): return lax.psum(jnp.sum(residual * precond * inv_mult), ('gx', 'yz'))  122 us
    psum x2, blocking collectives, body(): lax.psum(jnp.sum(direction * mapped * inv_mult), ('gx', 'yz'))  74.7 us
    ppermute x16, waiting for transfers between devices, passed_along(): return lax.ppermute(block, axis, route)  47.7 us
    mul x15, local copies, waits for them, and re-layouts, body(): residual = residual - step_len * mapped  32.6 us
    ppermute x16, starting transfers between devices, passed_along(): return lax.ppermute(block, axis, route)  18.7 us
    div x6, local copies, waits for them, and re-layouts, body(): jacobi = 1.0 / assembled[1]  12.2 us
    squeeze x4, local copies, waits for them, and re-layouts, body(): right_side = assembled[0]  9.92 us
  transfers between devices with their start and end apart: 16, of which 16 were waited for; matrix products, arithmetic and copies ran while one was open for 1% of the time, Pallas kernels for 0%

commit v1 on v0

v1 whole, which is shorter than its diff:
```python
import functools

import jax
import jax.numpy as jnp
import numpy as np
from jax import lax
from jax.experimental import pallas as pl
from jax.experimental.pallas import tpu as pltpu
from jax.sharding import PartitionSpec as P

EZ = 64
LANES = 128
HALF = 64
POINTS = 512
SPLIT = 2
VERTICAL = 4.0
VMEM_BYTES = 24 * 1024 * 1024


def legendre_rows(nodes, degree):
    rows = [nodes * 0.0 + 1.0, nodes]
    for order in range(2, degree + 1):
        rows.append(((2 * order - 1) * nodes * rows[-1] - (order - 1) * rows[-2]) / order)
    return np.stack(rows, 1)


def spectral_tables():
    degree = 7
    nodes = np.cos(np.pi * np.arange(degree + 1) / degree)
    for sweep in range(60):
        legendre = legendre_rows(nodes, degree)
        nodes = nodes - (nodes * legendre[:, degree] - legendre[:, degree - 1]) / (
            (degree + 1) * legendre[:, degree]
        )
    nodes = nodes[::-1].copy()
    top_values = legendre_rows(nodes, degree)[:, degree]
    weights = 2.0 / (degree * (degree + 1) * top_values**2)
    identity = np.eye(degree + 1)
    spacing = nodes[:, None] - nodes[None, :] + identity
    derivative = top_values[:, None] / top_values[None, :] / spacing * (1.0 - identity)
    corner_fix = np.zeros(degree + 1)
    corner_fix[0] = -degree * (degree + 1) / 4.0
    corner_fix[degree] = degree * (degree + 1) / 4.0
    derivative = derivative + identity * corner_fix[None, :]
    weights3 = (weights[:, None, None] * weights[None, :, None] * weights[None, None, :]).reshape(
        -1
    )
    return (derivative, weights3)


DERIVATIVE, WEIGHTS3 = spectral_tables()


def row(a, b):
    return pl.ds(64 * a + 8 * b, 8)


def across(a, c):
    return pl.ds(64 * a + c, 8, stride=8)


def along(matrix, lines, sign):
    evens = [lines[j] + lines[7 - j] for j in range(4)]
    odds = [lines[j] - lines[7 - j] for j in range(4)]
    out = [None] * 8
    for i in range(4):
        even = odd = None
        for j in range(4):
            even_term = evens[j] * float((matrix[i, j] + matrix[i, 7 - j]) / 2)
            odd_term = odds[j] * float((matrix[i, j] - matrix[i, 7 - j]) / 2)
            even = even_term if even is None else even + even_term
            odd = odd_term if odd is None else odd + odd_term
        out[i] = even + odd
        out[7 - i] = even - odd if sign > 0 else odd - even
    return out


def lane_index():
    return lax.broadcasted_iota(jnp.int32, (8, LANES), 1)


def sublane_index():
    return lax.broadcasted_iota(jnp.int32, (8, LANES), 0)


def join_vertical(low, high):
    layer = lane_index() % EZ
    new_low = low + jnp.where(layer > 0, pltpu.roll(high, 1, 1), 0.0)
    new_high = high + jnp.where(layer < EZ - 1, pltpu.roll(low, LANES - 1, 1), 0.0)
    return new_low, new_high


def pack_faces(grid, face_x, face_y, field):
    first = lane_index() < HALF
    for b in range(8):
        face_x[pl.ds(64 * field + 8 * b, 8), :] = jnp.where(
            first, grid[row(0, b), :], grid[row(7, b), :]
        )
    for a in range(8):
        face_y[pl.ds(128 * field + 8 * a, 8), :] = grid[row(a, 0), :]
        face_y[pl.ds(128 * field + 64 + 8 * a, 8), :] = grid[row(a, 7), :]


def ghost_x(from_even, from_odd, field, b):
    rows = pl.ds(64 * field + 8 * b, 8)
    odd = lax.axis_index("gx") % 2
    first = (lane_index() < HALF).astype(jnp.int32)
    return jnp.where(first != odd, from_even[rows, :], from_odd[rows, :])


def joined_x(a, low, high, ghost):
    first = lane_index() < HALF
    if a == 0:
        return low + pltpu.roll(jnp.where(first, high, ghost), HALF, 1)
    return high + pltpu.roll(jnp.where(first, ghost, low), HALF, 1)


def assembled(a, b, grid, received, field):
    even_x, odd_x, even_y, odd_y = received
    value = grid[row(a, b), :]
    if a in (0, 7):
        value = joined_x(
            a, grid[row(0, b), :], grid[row(7, b), :], ghost_x(even_x, odd_x, field, b)
        )
    if b in (0, 7):
        rows = pl.ds(64 * field + 8 * a, 8)
        odd = lax.axis_index("yz") % 2 == 1
        pick = odd if b == 0 else jnp.logical_not(odd)
        value = value + jnp.where(pick, even_y[rows, :], odd_y[rows, :])
    return value


def edges_kernel(fields, face_y, even_x, odd_x, to_even, to_odd):
    odd = lax.axis_index("yz") % 2 == 1
    for field in range(fields):
        faces = []
        for side in range(2):
            part = [face_y[pl.ds(128 * field + 64 * side + 8 * a, 8), :] for a in range(8)]
            ghost = ghost_x(even_x, odd_x, field, 7 * side)
            low, high = part[0], part[7]
            part[0] = joined_x(0, low, high, ghost)
            part[7] = joined_x(7, low, high, ghost)
            faces.append(part)
        for a in range(8):
            rows = pl.ds(64 * field + 8 * a, 8)
            to_even[rows, :] = jnp.where(odd, faces[0][a], faces[1][a])
            to_odd[rows, :] = jnp.where(odd, faces[1][a], faces[0][a])


def selection(slots):
    elements = lax.broadcasted_iota(jnp.int32, (LANES, LANES), 0)
    return jnp.where(elements == slots[...], 1.0, 0.0)


def parts_of(values):
    parts = []
    for _ in range(SPLIT):
        parts.append(values.astype(jnp.bfloat16))
        values = values - parts[-1].astype(jnp.float32)
    return parts


def to_grid(chosen, values):
    parts = jnp.concatenate(parts_of(values[0, 0]), 0)
    picked = jnp.dot(
        jnp.concatenate([chosen.astype(jnp.bfloat16)] * SPLIT, 1),
        parts,
        preferred_element_type=jnp.float32,
    )
    return picked.T


def setup_kernel(
    forcing, viscosity, mass_rate, slots, weights, right, diagonal, spread, mass, face_x, face_y
):
    chosen = selection(slots)
    right[...] = to_grid(chosen, forcing)
    spread[...] = to_grid(chosen, viscosity) * weights[...]
    mass[...] = to_grid(chosen, mass_rate) * weights[...]
    squares = (DERIVATIVE * DERIVATIVE).T
    for b in range(8):
        lines = along(squares, [spread[row(a, b), :] for a in range(8)], 1)
        for a in range(8):
            diagonal[row(a, b), :] = lines[a] + mass[row(a, b), :]
    for a in range(8):
        lines = along(squares, [spread[row(a, b), :] for b in range(8)], 1)
        for b in range(8):
            diagonal[row(a, b), :] += lines[b]
    for a in range(8):
        lines = along(VERTICAL * squares, [spread[across(a, c), :] for c in range(8)], 1)
        lines = [lines[c] + diagonal[across(a, c), :] for c in range(8)]
        lines[0], lines[7] = join_vertical(lines[0], lines[7])
        for c in range(8):
            diagonal[across(a, c), :] = lines[c]
        low, high = join_vertical(right[across(a, 0), :], right[across(a, 7), :])
        right[across(a, 0), :] = low
        right[across(a, 7), :] = high
    pack_faces(right, face_x, face_y, 0)
    pack_faces(diagonal, face_x, face_y, 1)


def operate(values, spread, mass, image, face_x, face_y):
    forward, backward = DERIVATIVE, DERIVATIVE.T
    for b in range(8):
        lines = [values[row(a, b), :] for a in range(8)]
        slopes = along(forward, lines, -1)
        back = along(backward, [slopes[a] * spread[row(a, b), :] for a in range(8)], -1)
        for a in range(8):
            image[row(a, b), :] = back[a] + mass[row(a, b), :] * lines[a]
    for a in range(8):
        slopes = along(forward, [values[row(a, b), :] for b in range(8)], -1)
        back = along(backward, [slopes[b] * spread[row(a, b), :] for b in range(8)], -1)
        for b in range(8):
            image[row(a, b), :] += back[b]
    energy = jnp.zeros((8, LANES), jnp.float32)
    for a in range(8):
        lines = [values[across(a, c), :] for c in range(8)]
        slopes = along(forward, lines, -1)
        back = along(
            VERTICAL * backward, [slopes[c] * spread[across(a, c), :] for c in range(8)], -1
        )
        back = [back[c] + image[across(a, c), :] for c in range(8)]
        for c in range(8):
            energy = energy + back[c] * lines[c]
        back[0], back[7] = join_vertical(back[0], back[7])
        for c in range(8):
            image[across(a, c), :] = back[c]
    pack_faces(image, face_x, face_y, 0)
    return energy


def weighted(sums):
    layer, point = lane_index() % EZ, sublane_index()
    below = jnp.logical_and(point == 0, layer > 0)
    above = jnp.logical_and(point == 7, layer < EZ - 1)
    shared = jnp.where(jnp.logical_or(below, above), 0.5, 1.0)
    return (sums[0] + 0.5 * sums[1] + 0.25 * sums[2]) * shared


def ends(a, b):
    return int(a in (0, 7)) + int(b in (0, 7))


def first_kernel(
    right, diagonal, even_x, odd_x, even_y, odd_y, spread, mass,
    whole_diagonal, values, image, face_x, face_y, moments,
):
    received = (even_x, odd_x, even_y, odd_y)
    sums = [jnp.zeros((8, LANES), jnp.float32)] * 3
    for a in range(8):
        for b in range(8):
            source = assembled(a, b, right, received, 0)
            scale = assembled(a, b, diagonal, received, 1)
            value = source / scale
            whole_diagonal[row(a, b), :] = scale
            values[row(a, b), :] = value
            sums[ends(a, b)] = sums[ends(a, b)] + source * value
    moments[...] = weighted(sums)
    operate(values, spread, mass, image, face_x, face_y)


def next_values(before_image, received, diagonal, before, values):
    cross = [jnp.zeros((8, LANES), jnp.float32)] * 3
    square = [jnp.zeros((8, LANES), jnp.float32)] * 3
    for a in range(8):
        for b in range(8):
            scale = diagonal[row(a, b), :]
            old = before[row(a, b), :]
            value = assembled(a, b, before_image, received, 0) / scale - old
            values[row(a, b), :] = value
            scaled = scale * value
            kind = ends(a, b)
            cross[kind] = cross[kind] + scaled * old
            square[kind] = square[kind] + scaled * value
    return weighted(cross), weighted(square)


def second_kernel(
    before_image, even_x, odd_x, even_y, odd_y, diagonal, before, spread, mass,
    values, image, face_x, face_y, moments,
):
    received = (even_x, odd_x, even_y, odd_y)
    cross, square = next_values(before_image, received, diagonal, before, values)
    moments[pl.ds(0, 8), :] = cross
    moments[pl.ds(8, 8), :] = square
    operate(values, spread, mass, image, face_x, face_y)


def third_kernel(
    before_image, even_x, odd_x, even_y, odd_y, diagonal, before, spread, mass, moments0, moments1,
    values, image, face_x, face_y, sums,
):
    received = (even_x, odd_x, even_y, odd_y)
    cross, square = next_values(before_image, received, diagonal, before, values)
    energy = operate(values, spread, mass, image, face_x, face_y)
    parts = [
        moments0[...], moments1[pl.ds(0, 8), :], moments1[pl.ds(8, 8), :], cross, square, energy
    ]
    lane = lax.broadcasted_iota(jnp.int32, (1, LANES), 1)
    line = jnp.zeros((1, LANES), jnp.float32)
    for k, part in enumerate(parts):
        total = jnp.sum(jnp.sum(part, 0, keepdims=True), 1, keepdims=True)
        line = jnp.where(lane == k, total, line)
    sums[...] = jnp.broadcast_to(line[None], sums.shape)


def recurrence(moments):
    moments = moments[:5] + [moments[5] - moments[4]]
    zero = jnp.zeros_like(moments[0])
    one = zero + 1.0

    def form(left, right, shift):
        total = zero
        for i in range(3):
            for j in range(3):
                if left[i] is not None and right[j] is not None:
                    entry = moments[i + j]
                    if shift:
                        entry = entry + moments[i + j + 1]
                    total = total + left[i] * right[j] * entry
        return total

    def ratio(top, bottom):
        fine = jnp.logical_and(bottom > 0.0, top > 0.0)
        return jnp.where(fine, top / jnp.where(fine, bottom, 1.0), 0.0)

    def add(left, scale, right):
        out = []
        for x, y in zip(left, right):
            if y is None:
                out.append(x)
            else:
                out.append(scale * y if x is None else x + scale * y)
        return out

    direction = [one, None, None, None]
    precond = [one, None, None, None]
    result = [None, None, None, None]
    norm = moments[0]
    for step in range(3):
        curve = form(direction, direction, True)
        length = ratio(norm, curve)
        result = add(result, length, direction)
        moved = add(direction, 1.0, [None] + direction[:3])
        if step == 0:
            precond = [jnp.where(curve > 0.0, moments[1] / curve, 1.0), -length, None, None]
        else:
            precond = add(precond, -length, moved)
        if step < 2:
            norm_next = form(precond, precond, False)
            direction = add(precond, ratio(norm_next, norm), direction)
            norm = norm_next
    return result[:3], precond


def last_kernel(
    before_image, even_x, odd_x, even_y, odd_y, diagonal, values0, values1, values2, sums, slots,
    solution, residual, solution_grid, residual_grid,
):
    received = (even_x, odd_x, even_y, odd_y)
    line = jnp.sum(sums[...], 0)
    lane = lax.broadcasted_iota(jnp.int32, (1, LANES), 1)
    moments = [
        jnp.sum(jnp.where(lane == k, line, 0.0), 1, keepdims=True) for k in range(6)
    ]
    result, precond = recurrence(moments)
    spread_out = lambda scalar: jnp.broadcast_to(scalar, (8, LANES))
    result = [spread_out(entry) for entry in result]
    precond = [spread_out(entry) for entry in precond]
    for a in range(8):
        for b in range(8):
            rows = row(a, b)
            basis = [values0[rows, :], values1[rows, :], values2[rows, :]]
            scale = diagonal[rows, :]
            image = assembled(a, b, before_image, received, 0) - scale * basis[2]
            near = result[0] * basis[0] + result[1] * basis[1] + result[2] * basis[2]
            far = precond[0] * basis[0] + precond[1] * basis[1] + precond[2] * basis[2]
            solution_grid[rows, :] = near
            residual_grid[rows, :] = scale * far + precond[3] * image
    chosen = selection(slots).T.astype(jnp.bfloat16)
    for grid, out in ((solution_grid, solution), (residual_grid, residual)):
        total = None
        for part in parts_of(grid[...]):
            term = lax.dot_general(
                chosen, part, (((1,), (1,)), ((), ())), preferred_element_type=jnp.float32
            )
            total = term if total is None else total + term
        out[0, 0] = total


def call(kernel, name, shapes, scratch, *operands):
    return pl.pallas_call(
        kernel,
        out_shape=[jax.ShapeDtypeStruct(shape, jnp.float32) for shape in shapes],
        in_specs=[pl.BlockSpec(memory_space=pltpu.VMEM)] * len(operands),
        out_specs=[pl.BlockSpec(memory_space=pltpu.VMEM)] * len(shapes),
        scratch_shapes=[pltpu.VMEM(shape, jnp.float32) for shape in scratch],
        compiler_params=pltpu.CompilerParams(vmem_limit_bytes=VMEM_BYTES),
        name=name,
    )(*operands)


def swapped(block, axis):
    extent = lax.axis_size(axis)
    even = [(i, i ^ 1) for i in range(extent)]
    odd = [(i, (((i + 1) ^ 1) - 1) % extent) for i in range(extent)]
    return lax.ppermute(block[0], axis, even), lax.ppermute(block[1], axis, odd)


def exchange(fields, face_x, face_y):
    received_x = swapped((face_x, face_x), "gx")
    shape = (64 * fields, LANES)
    sent_y = call(
        functools.partial(edges_kernel, fields), "edges", [shape, shape], [], face_y, *received_x
    )
    return (*received_x, *swapped(sent_y, "yz"))


def body(forcing, viscosity, mass_rate, slot_element):
    devices = lax.axis_size("gx") * lax.axis_size("yz")
    slots = slot_element[0]
    weights = jnp.broadcast_to(jnp.asarray(WEIGHTS3, jnp.float32)[:, None], (POINTS, LANES))
    grid = (POINTS, LANES)
    face_x, face_y, moment = (64, LANES), (128, LANES), (8, LANES)
    right, diagonal, spread, mass, out_x, out_y = call(
        setup_kernel, "setup", [grid] * 4 + [(128, LANES), (256, LANES)], [],
        forcing, viscosity, mass_rate, slots, weights,
    )
    received = exchange(2, out_x, out_y)
    diagonal, values0, image, out_x, out_y, moments0 = call(
        first_kernel, "first", [grid] * 3 + [face_x, face_y, moment], [],
        right, diagonal, *received, spread, mass,
    )
    received = exchange(1, out_x, out_y)
    values1, image, out_x, out_y, moments1 = call(
        second_kernel, "second", [grid] * 2 + [face_x, face_y, (16, LANES)], [],
        image, *received, diagonal, values0, spread, mass,
    )
    received = exchange(1, out_x, out_y)
    values2, image, out_x, out_y, sums = call(
        third_kernel, "third", [grid] * 2 + [face_x, face_y, (devices, 1, LANES)], [],
        image, *received, diagonal, values1, spread, mass, moments0, moments1,
    )
    sums = lax.all_to_all(sums, ("gx", "yz"), 0, 0)
    received = exchange(1, out_x, out_y)
    return call(
        last_kernel, "last", [forcing.shape] * 2, [grid] * 2,
        image, *received, diagonal, values0, values1, values2, sums, slots,
    )


def solution(mesh):
    placed = (
        P("gx", "yz", None, None),
        P("gx", "yz", None, None),
        P("gx", "yz", None, None),
        P("gx", "yz", None),
    )
    return jax.shard_map(
        body,
        mesh=mesh,
        in_specs=placed,
        out_specs=(P("gx", "yz", None, None), P("gx", "yz", None, None)),
        check_vma=False,
    )
```

time: 429 us -> 60.5 us (0.14); the launches traced: 422 us -> 60.3 us
  blocking collectives: 197 us -> 9.76 us
  local copies, waits for them, and re-layouts: 96.1 us -> 2.84 us
  other arithmetic: 41.8 us -> 0 us
  waiting for transfers between devices: 47.7 us -> 17.3 us
  matrix products: 12.6 us -> 0 us
  between operations: 8.56 us -> 0.71 us
  starting transfers between devices: 18.7 us -> 24.8 us
  Pallas kernels: 0 us -> 4.89 us
    psum x5 -> x0, blocking collectives: 197 us -> none  [the longest x3 122 us: residual_norm(): return lax.psum(jnp.sum(residual * precond * inv_mult), ('gx', 'yz'))]
    mul x16 -> x0, local copies, waits for them, and re-layouts: 32.8 us -> none  [the longest x15 32.6 us: body(): residual = residual - step_len * mapped]
    ppermute x16, waiting for transfers between devices: 47.7 us -> 17.3 us  [the longest x8 16.9 us: swapped(): lax.ppermute(block[1], axis, odd)]
    squeeze x11 -> x0, local copies, waits for them, and re-layouts: 13.7 us -> none  [the longest x4 9.92 us: body(): right_side = assembled[0]]
    slice x25 -> x0, local copies, waits for them, and re-layouts: 13.2 us -> none  [the longest x2 7.61 us: body(): right_side = assembled[0]]
    dot_general x15 -> x0, matrix products: 12.6 us -> none  [the longest x3 4.32 us: contract(): jnp.dot(values.reshape(elements * 8, 64), kron_table, precision=highest)]
    div x6 -> x0, local copies, waits for them, and re-layouts: 12.2 us -> none  [body(): jacobi = 1.0 / assembled[1]]
    add x14 -> x0, other arithmetic: 10.2 us -> none  [the longest x3 6.14 us: contract(): return back_x + back_yz + coef_mass * values]
  transfers between devices with their start and end apart: 16 -> 16, of which waited for: 16 -> 9; matrix products, arithmetic and copies ran while one was open for 1% -> 0% of each run, Pallas kernels for 0% -> 0%
where the time goes in v1:
time: 60.5 us; the launch traced here: 60.3 us
  starting transfers between devices  24.8 us (41%)
  waiting for transfers between devices  17.3 us (29%)
  blocking collectives  9.76 us (16%)
  Pallas kernels  4.89 us (8%)
  local copies, waits for them, and re-layouts  2.84 us (5%)
  between operations  0.71 us (1%)
    ppermute x8, starting transfers between devices, swapped(): lax.ppermute(block[1], axis, odd)  17.1 us
    ppermute x8, waiting for transfers between devices, swapped(): lax.ppermute(block[1], axis, odd)  16.9 us
    all_to_all x1, blocking collectives, body(): sums = lax.all_to_all(sums, ('gx', 'yz'), 0, 0)  9.76 us
    ppermute x8, starting transfers between devices, swapped(): lax.ppermute(block[0], axis, even)  7.68 us
    pallas_call x9, Pallas kernels, call(): pl.pallas_call(kernel, out_shape=[jax.ShapeDtypeStruct(shape, jnp.float32...  4.89 us
    unnamed x8, local copies, waits for them, and re-layouts  2 us
  transfers between devices with their start and end apart: 16, of which 9 were waited for; matrix products, arithmetic and copies ran while one was open for 0% of the time, Pallas kernels for 0%

profile of v1, /device:TPU:0, one launch (start us, length us, event | category | flops | bytes accessed | tf_op | source)
XLA Modules:
  0.0 60.3 jit_solution(8980360099254495453)
XLA Ops:
  0.6 0.0 copy-start
  0.6 0.0 copy-start.3
  0.6 0.8 %broadcast_in_dim.2.weights = f32[512,128]{1,0:T(8,128)S(1)} broadcast(f32[512]{0:T(512)} %constant.2.clone), dimensions={0} | broadcast | bytes 264192 | tf_op jit(solution)/shard_map/broadcast_in_dim | solution.py:422
  1.5 0.1 copy-done
  1.6 0.9 %copy-done.1 = f32[1,1,128,512]{3,2,1,0:T(8,128)S(1)} copy-done((f32[1,1,128,512]{3,2,1,0:T(8,128)S(1)}, f32[1,1,128,512]{3,2,1,0:T(8,128)}, u32[]{:S(2)}) %copy-start.1) | copy-done | bytes 262168
  2.6 0.9 %copy-done.2 = f32[1,1,128,512]{3,2,1,0:T(8,128)S(1)} copy-done((f32[1,1,128,512]{3,2,1,0:T(8,128)S(1)}, f32[1,1,128,512]{3,2,1,0:T(8,128)}, u32[]{:S(2)}) %copy-start.2) | copy-done | bytes 262168
  3.5 0.8 %setup.1 = (f32[512,128]{1,0:T(8,128)S(1)}, f32[512,128]{1,0:T(8,128)S(1)}, f32[512,128]{1,0:T(8,128)S(1)}, f32[512,128]{1,0:T(8,128)S(1)}, f32[128,128]{1,0:T(8,128)S(1)}, /*index=5*/f32[256,128]{1,0:T(8,128)S(1)}) custom-call(f32[1,1,128,512]{3,2,1,0:T(8,128)S(1)} %copy-done, f32[1,1,128,512]{3,2,1,0:T(8,128)S(1)} %copy-done.1, ...), custom_call_target="tpu_custom_call" | custom-call | tf_op jit(solution)/shard_map/setup/pallas_call | solution.py:392
  4.3 2.5 %collective-permute-start.1 = (f32[128,128]{1,0:T(8,128)S(1)}, f32[128,128]{1,0:T(8,128)S(1)}, u32[]{:S(2)}, u32[]{:S(2)}) collective-permute-start(f32[128,128]{1,0:T(8,128)S(1)} %get-tuple-element.34), channel_id=1, source_target_pairs={{0,24},{8,16},{16,8},{24,0},{1,25},{9,17},{17,9},{25,1},{2,26},{10... | collective-permute-start | bytes 196616 | tf_op jit(solution)/shard_map/ppermute | solution.py:407
  6.7 0.7 %collective-permute-start = (f32[128,128]{1,0:T(8,128)S(1)}, f32[128,128]{1,0:T(8,128)S(1)}, u32[]{:S(2)}, u32[]{:S(2)}) collective-permute-start(f32[128,128]{1,0:T(8,128)S(1)} %get-tuple-element.34), channel_id=1, source_target_pairs={{0,8},{8,0},{16,24},{24,16},{1,9},{9,1},{17,25},{25,17},{2,10},{10... | collective-permute-start | bytes 196616 | tf_op jit(solution)/shard_map/ppermute | solution.py:407
  7.4 1.8 %collective-permute-done.1.odd_x = f32[128,128]{1,0:T(8,128)S(1)} collective-permute-done((f32[128,128]{1,0:T(8,128)S(1)}, f32[128,128]{1,0:T(8,128)S(1)}, u32[]{:S(2)}, u32[]{:S(2)}) %collective-permute-start.1) | collective-permute-done | bytes 65568 | tf_op jit(solution)/shard_map/ppermute | solution.py:407
  9.2 0.0 collective-permute-done.even_x
  9.2 0.1 edges.4
  9.3 2.4 %collective-permute-start.2 = (f32[128,128]{1,0:T(8,128)S(1)}, f32[128,128]{1,0:T(8,128)S(1)}, u32[]{:S(2)}, u32[]{:S(2)}) collective-permute-start(f32[128,128]{1,0:T(8,128)S(1)} %get-tuple-element.36), channel_id=1, source_target_pairs={{0,1},{1,0},{2,3},{3,2},{4,5},{5,4},{6,7},{7,6},{8,9},{9,8},{10,11... | collective-permute-start | bytes 196616 | tf_op jit(solution)/shard_map/ppermute | solution.py:407
  11.7 3.6 %collective-permute-start.3 = (f32[128,128]{1,0:T(8,128)S(1)}, f32[128,128]{1,0:T(8,128)S(1)}, u32[]{:S(2)}, u32[]{:S(2)}) collective-permute-start(f32[128,128]{1,0:T(8,128)S(1)} %get-tuple-element.37), channel_id=1, source_target_pairs={{0,7},{1,2},{2,1},{3,4},{4,3},{5,6},{6,5},{7,0},{8,15},{9,10},{10,... | collective-permute-start | bytes 196616 | tf_op jit(solution)/shard_map/ppermute | solution.py:407
  15.3 0.0 collective-permute-done.2.even_y
  15.3 3.4 %collective-permute-done.3.odd_y = f32[128,128]{1,0:T(8,128)S(1)} collective-permute-done((f32[128,128]{1,0:T(8,128)S(1)}, f32[128,128]{1,0:T(8,128)S(1)}, u32[]{:S(2)}, u32[]{:S(2)}) %collective-permute-start.3) | collective-permute-done | bytes 65568 | tf_op jit(solution)/shard_map/ppermute | solution.py:407
  18.6 0.8 %first.1 = (f32[512,128]{1,0:T(8,128)S(1)}, f32[512,128]{1,0:T(8,128)S(1)}, f32[512,128]{1,0:T(8,128)S(1)}, f32[64,128]{1,0:T(8,128)S(1)}, f32[128,128]{1,0:T(8,128)S(1)}, /*index=5*/f32[8,128]{1,0:T(8,128)S(1)}) custom-call(f32[512,128]{1,0:T(8,128)S(1)} %get-tuple-element.32.right, f32[512,128]{1,0:T(8,128)S(1)} %get-tuple-element.33.diagonal, ...), custom_call_target="tpu_custom_call" | custom-call | tf_op jit(solution)/shard_map/first/pallas_call | solution.py:392
  19.4 0.1 collective-permute-start.5
  19.5 1.7 %collective-permute-start.4 = (f32[64,128]{1,0:T(8,128)S(1)}, f32[64,128]{1,0:T(8,128)S(1)}, u32[]{:S(2)}, u32[]{:S(2)}) collective-permute-start(f32[64,128]{1,0:T(8,128)S(1)} %get-tuple-element.41), channel_id=1, source_target_pairs={{0,8},{8,0},{16,24},{24,16},{1,9},{9,1},{17,25},{25,17},{2,10},{10... | collective-permute-start | bytes 98312 | tf_op jit(solution)/shard_map/ppermute | solution.py:407
  21.2 1.8 %collective-permute-done.5.odd_x = f32[64,128]{1,0:T(8,128)S(1)} collective-permute-done((f32[64,128]{1,0:T(8,128)S(1)}, f32[64,128]{1,0:T(8,128)S(1)}, u32[]{:S(2)}, u32[]{:S(2)}) %collective-permute-start.5) | collective-permute-done | bytes 32800 | tf_op jit(solution)/shard_map/ppermute | solution.py:407
  23.0 0.0 collective-permute-done.4.even_x
  23.0 0.1 edges.5
  23.1 0.0 collective-permute-start.6
  23.1 3.7 %collective-permute-start.7 = (f32[64,128]{1,0:T(8,128)S(1)}, f32[64,128]{1,0:T(8,128)S(1)}, u32[]{:S(2)}, u32[]{:S(2)}) collective-permute-start(f32[64,128]{1,0:T(8,128)S(1)} %get-tuple-element.44), channel_id=1, source_target_pairs={{0,7},{1,2},{2,1},{3,4},{4,3},{5,6},{6,5},{7,0},{8,15},{9,10},{10,... | collective-permute-start | bytes 98312 | tf_op jit(solution)/shard_map/ppermute | solution.py:407
  26.8 0.2 collective-permute-done.6.even_y
  27.0 2.8 %collective-permute-done.7.odd_y = f32[64,128]{1,0:T(8,128)S(1)} collective-permute-done((f32[64,128]{1,0:T(8,128)S(1)}, f32[64,128]{1,0:T(8,128)S(1)}, u32[]{:S(2)}, u32[]{:S(2)}) %collective-permute-start.7) | collective-permute-done | bytes 32800 | tf_op jit(solution)/shard_map/ppermute | solution.py:407
  29.8 0.8 %second.1 = (f32[512,128]{1,0:T(8,128)S(1)}, f32[512,128]{1,0:T(8,128)S(1)}, f32[64,128]{1,0:T(8,128)S(1)}, f32[128,128]{1,0:T(8,128)S(1)}, f32[16,128]{1,0:T(8,128)S(1)}) custom-call(f32[512,128]{1,0:T(8,128)S(1)} %get-tuple-element.40.before_image, f32[64,128]{1,0:T(8,128)S(1)} %collective-permute-done.4.even_x, ...), custom_call_target="tpu_custom_call" | custom-call | tf_op jit(solution)/shard_map/second/pallas_call | solution.py:392
  30.6 0.1 collective-permute-start.9
  30.7 1.5 %collective-permute-start.8 = (f32[64,128]{1,0:T(8,128)S(1)}, f32[64,128]{1,0:T(8,128)S(1)}, u32[]{:S(2)}, u32[]{:S(2)}) collective-permute-start(f32[64,128]{1,0:T(8,128)S(1)} %get-tuple-element.48), channel_id=1, source_target_pairs={{0,8},{8,0},{16,24},{24,16},{1,9},{9,1},{17,25},{25,17},{2,10},{10... | collective-permute-start | bytes 98312 | tf_op jit(solution)/shard_map/ppermute | solution.py:407
  32.2 2.1 %collective-permute-done.9.odd_x = f32[64,128]{1,0:T(8,128)S(1)} collective-permute-done((f32[64,128]{1,0:T(8,128)S(1)}, f32[64,128]{1,0:T(8,128)S(1)}, u32[]{:S(2)}, u32[]{:S(2)}) %collective-permute-start.9) | collective-permute-done | bytes 32800 | tf_op jit(solution)/shard_map/ppermute | solution.py:407
  34.3 0.0 collective-permute-done.8.even_x
  34.3 0.1 edges.6
  34.4 0.2 collective-permute-start.10
  34.6 3.6 %collective-permute-start.11 = (f32[64,128]{1,0:T(8,128)S(1)}, f32[64,128]{1,0:T(8,128)S(1)}, u32[]{:S(2)}, u32[]{:S(2)}) collective-permute-start(f32[64,128]{1,0:T(8,128)S(1)} %get-tuple-element.51), channel_id=1, source_target_pairs={{0,7},{1,2},{2,1},{3,4},{4,3},{5,6},{6,5},{7,0},{8,15},{9,10},{10,... | collective-permute-start | bytes 98312 | tf_op jit(solution)/shard_map/ppermute | solution.py:407
  38.1 0.2 collective-permute-done.10.even_y
  38.3 2.8 %collective-permute-done.11.odd_y = f32[64,128]{1,0:T(8,128)S(1)} collective-permute-done((f32[64,128]{1,0:T(8,128)S(1)}, f32[64,128]{1,0:T(8,128)S(1)}, u32[]{:S(2)}, u32[]{:S(2)}) %collective-permute-start.11) | collective-permute-done | bytes 32800 | tf_op jit(solution)/shard_map/ppermute | solution.py:407
  41.2 0.9 %third.1 = (f32[512,128]{1,0:T(8,128)S(1)}, f32[512,128]{1,0:T(8,128)S(1)}, f32[64,128]{1,0:T(8,128)S(1)}, f32[128,128]{1,0:T(8,128)S(1)}, f32[32,1,128]{2,1,0:T(1,128)S(1)}) custom-call(f32[512,128]{1,0:T(8,128)S(1)} %get-tuple-element.47.before_image, f32[64,128]{1,0:T(8,128)S(1)} %collective-permute-done.8.even_x, ...), custom_call_target="tpu_custom_call" | custom-call | tf_op jit(solution)/shard_map/third/pallas_call | solution.py:392
  42.1 0.1 collective-permute-start.13
  42.1 1.2 %collective-permute-start.12 = (f32[64,128]{1,0:T(8,128)S(1)}, f32[64,128]{1,0:T(8,128)S(1)}, u32[]{:S(2)}, u32[]{:S(2)}) collective-permute-start(f32[64,128]{1,0:T(8,128)S(1)} %get-tuple-element.56), channel_id=1, source_target_pairs={{0,8},{8,0},{16,24},{24,16},{1,9},{9,1},{17,25},{25,17},{2,10},{10... | collective-permute-start | bytes 98312 | tf_op jit(solution)/shard_map/ppermute | solution.py:407
  43.3 2.1 %collective-permute-done.13.odd_x = f32[64,128]{1,0:T(8,128)S(1)} collective-permute-done((f32[64,128]{1,0:T(8,128)S(1)}, f32[64,128]{1,0:T(8,128)S(1)}, u32[]{:S(2)}, u32[]{:S(2)}) %collective-permute-start.13) | collective-permute-done | bytes 32800 | tf_op jit(solution)/shard_map/ppermute | solution.py:407
  45.5 0.0 collective-permute-done.12.even_x
  45.5 0.1 edges.7
  45.6 0.1 collective-permute-start.14
  45.6 3.6 %collective-permute-start.15 = (f32[64,128]{1,0:T(8,128)S(1)}, f32[64,128]{1,0:T(8,128)S(1)}, u32[]{:S(2)}, u32[]{:S(2)}) collective-permute-start(f32[64,128]{1,0:T(8,128)S(1)} %get-tuple-element.59), channel_id=1, source_target_pairs={{0,7},{1,2},{2,1},{3,4},{4,3},{5,6},{6,5},{7,0},{8,15},{9,10},{10,... | collective-permute-start | bytes 98312 | tf_op jit(solution)/shard_map/ppermute | solution.py:407
  49.2 9.8 %all_to_all.5.sums = f32[32,1,128]{2,1,0:T(1,128)S(1)} all-to-all(f32[32,1,128]{2,1,0:T(1,128)S(1)} %get-tuple-element.61), channel_id=1, replica_groups=mesh['gx'=4,'yz'=8] {'gx','yz'}, dimensions={0} | all-to-all | bytes 32768 | tf_op jit(solution)/shard_map/all_to_all | solution.py:444
  59.0 0.0 collective-permute-done.14.even_y
  59.0 0.0 collective-permute-done.15.odd_y
  59.0 1.3 %last.1 = (f32[1,1,128,512]{3,2,1,0:T(8,128)}, f32[1,1,128,512]{3,2,1,0:T(8,128)}) custom-call(f32[512,128]{1,0:T(8,128)S(1)} %get-tuple-element.55.before_image, f32[64,128]{1,0:T(8,128)S(1)} %collective-permute-done.12.even_x, f32[64,128]{1,0:T(8,128)S(1)} %collective-permute-done.13.odd_x, f32[64,128]{1,0:T(8,128)S(1)} %collective-permute-done.14.even_y, ...), custom_call_target="tpu_custom_call" | custom-call | tf_op jit(solution)/shard_map/last/pallas_call | solution.py:392
  (3 shorter events, 0.0 us)
Async XLA Ops:
  0.6 1.0 %copy-start = (f32[1,1,128,512]{3,2,1,0:T(8,128)S(1)}, f32[1,1,128,512]{3,2,1,0:T(8,128)}, u32[]{:S(2)}) copy-start(f32[1,1,128,512]{3,2,1,0:T(8,128)} %forcing.1) | copy-start | bytes 786436
  0.6 1.0 %copy-start.3 = (s32[1,1,128]{2,1,0:T(1,128)S(1)}, s32[1,1,128]{2,1,0:T(1,128)}, u32[]{:S(2)}) copy-start(s32[1,1,128]{2,1,0:T(1,128)} %param.8) | copy-start | bytes 1540
  1.6 1.0 %copy-start.1 = (f32[1,1,128,512]{3,2,1,0:T(8,128)S(1)}, f32[1,1,128,512]{3,2,1,0:T(8,128)}, u32[]{:S(2)}) copy-start(f32[1,1,128,512]{3,2,1,0:T(8,128)} %viscosity.1) | copy-start | bytes 786436
  2.5 0.9 %copy-start.2 = (f32[1,1,128,512]{3,2,1,0:T(8,128)S(1)}, f32[1,1,128,512]{3,2,1,0:T(8,128)}, u32[]{:S(2)}) copy-start(f32[1,1,128,512]{3,2,1,0:T(8,128)} %mass_rate.1) | copy-start | bytes 786436
  4.3 5.0 %collective-permute-start.1 = (f32[128,128]{1,0:T(8,128)S(1)}, f32[128,128]{1,0:T(8,128)S(1)}, u32[]{:S(2)}, u32[]{:S(2)}) collective-permute-start(f32[128,128]{1,0:T(8,128)S(1)} %get-tuple-element.34), channel_id=1, source_target_pairs={{0,24},{8,16},{16,8},{24,0},{1,25},{9,17},{17,9},{25,1},{2,26},{10... | collective-permute-start | bytes 196616 | tf_op jit(solution)/shard_map/ppermute | solution.py:407
  6.7 2.5 %collective-permute-start = (f32[128,128]{1,0:T(8,128)S(1)}, f32[128,128]{1,0:T(8,128)S(1)}, u32[]{:S(2)}, u32[]{:S(2)}) collective-permute-start(f32[128,128]{1,0:T(8,128)S(1)} %get-tuple-element.34), channel_id=1, source_target_pairs={{0,8},{8,0},{16,24},{24,16},{1,9},{9,1},{17,25},{25,17},{2,10},{10... | collective-permute-start | bytes 196616 | tf_op jit(solution)/shard_map/ppermute | solution.py:407
  9.3 6.0 %collective-permute-start.2 = (f32[128,128]{1,0:T(8,128)S(1)}, f32[128,128]{1,0:T(8,128)S(1)}, u32[]{:S(2)}, u32[]{:S(2)}) collective-permute-start(f32[128,128]{1,0:T(8,128)S(1)} %get-tuple-element.36), channel_id=1, source_target_pairs={{0,1},{1,0},{2,3},{3,2},{4,5},{5,4},{6,7},{7,6},{8,9},{9,8},{10,11... | collective-permute-start | bytes 196616 | tf_op jit(solution)/shard_map/ppermute | solution.py:407
  11.7 7.0 %collective-permute-start.3 = (f32[128,128]{1,0:T(8,128)S(1)}, f32[128,128]{1,0:T(8,128)S(1)}, u32[]{:S(2)}, u32[]{:S(2)}) collective-permute-start(f32[128,128]{1,0:T(8,128)S(1)} %get-tuple-element.37), channel_id=1, source_target_pairs={{0,7},{1,2},{2,1},{3,4},{4,3},{5,6},{6,5},{7,0},{8,15},{9,10},{10,... | collective-permute-start | bytes 196616 | tf_op jit(solution)/shard_map/ppermute | solution.py:407
  19.4 3.6 %collective-permute-start.5 = (f32[64,128]{1,0:T(8,128)S(1)}, f32[64,128]{1,0:T(8,128)S(1)}, u32[]{:S(2)}, u32[]{:S(2)}) collective-permute-start(f32[64,128]{1,0:T(8,128)S(1)} %get-tuple-element.41), channel_id=1, source_target_pairs={{0,24},{8,16},{16,8},{24,0},{1,25},{9,17},{17,9},{25,1},{2,26},{10... | collective-permute-start | bytes 98312 | tf_op jit(solution)/shard_map/ppermute | solution.py:407
  19.5 3.5 %collective-permute-start.4 = (f32[64,128]{1,0:T(8,128)S(1)}, f32[64,128]{1,0:T(8,128)S(1)}, u32[]{:S(2)}, u32[]{:S(2)}) collective-permute-start(f32[64,128]{1,0:T(8,128)S(1)} %get-tuple-element.41), channel_id=1, source_target_pairs={{0,8},{8,0},{16,24},{24,16},{1,9},{9,1},{17,25},{25,17},{2,10},{10... | collective-permute-start | bytes 98312 | tf_op jit(solution)/shard_map/ppermute | solution.py:407
  23.1 3.9 %collective-permute-start.6 = (f32[64,128]{1,0:T(8,128)S(1)}, f32[64,128]{1,0:T(8,128)S(1)}, u32[]{:S(2)}, u32[]{:S(2)}) collective-permute-start(f32[64,128]{1,0:T(8,128)S(1)} %get-tuple-element.43), channel_id=1, source_target_pairs={{0,1},{1,0},{2,3},{3,2},{4,5},{5,4},{6,7},{7,6},{8,9},{9,8},{10,11... | collective-permute-start | bytes 98312 | tf_op jit(solution)/shard_map/ppermute | solution.py:407
  23.1 6.7 %collective-permute-start.7 = (f32[64,128]{1,0:T(8,128)S(1)}, f32[64,128]{1,0:T(8,128)S(1)}, u32[]{:S(2)}, u32[]{:S(2)}) collective-permute-start(f32[64,128]{1,0:T(8,128)S(1)} %get-tuple-element.44), channel_id=1, source_target_pairs={{0,7},{1,2},{2,1},{3,4},{4,3},{5,6},{6,5},{7,0},{8,15},{9,10},{10,... | collective-permute-start | bytes 98312 | tf_op jit(solution)/shard_map/ppermute | solution.py:407
  30.6 3.7 %collective-permute-start.9 = (f32[64,128]{1,0:T(8,128)S(1)}, f32[64,128]{1,0:T(8,128)S(1)}, u32[]{:S(2)}, u32[]{:S(2)}) collective-permute-start(f32[64,128]{1,0:T(8,128)S(1)} %get-tuple-element.48), channel_id=1, source_target_pairs={{0,24},{8,16},{16,8},{24,0},{1,25},{9,17},{17,9},{25,1},{2,26},{10... | collective-permute-start | bytes 98312 | tf_op jit(solution)/shard_map/ppermute | solution.py:407
  30.7 3.6 %collective-permute-start.8 = (f32[64,128]{1,0:T(8,128)S(1)}, f32[64,128]{1,0:T(8,128)S(1)}, u32[]{:S(2)}, u32[]{:S(2)}) collective-permute-start(f32[64,128]{1,0:T(8,128)S(1)} %get-tuple-element.48), channel_id=1, source_target_pairs={{0,8},{8,0},{16,24},{24,16},{1,9},{9,1},{17,25},{25,17},{2,10},{10... | collective-permute-start | bytes 98312 | tf_op jit(solution)/shard_map/ppermute | solution.py:407
  34.4 3.9 %collective-permute-start.10 = (f32[64,128]{1,0:T(8,128)S(1)}, f32[64,128]{1,0:T(8,128)S(1)}, u32[]{:S(2)}, u32[]{:S(2)}) collective-permute-start(f32[64,128]{1,0:T(8,128)S(1)} %get-tuple-element.50), channel_id=1, source_target_pairs={{0,1},{1,0},{2,3},{3,2},{4,5},{5,4},{6,7},{7,6},{8,9},{9,8},{10,11... | collective-permute-start | bytes 98312 | tf_op jit(solution)/shard_map/ppermute | solution.py:407
  34.6 6.6 %collective-permute-start.11 = (f32[64,128]{1,0:T(8,128)S(1)}, f32[64,128]{1,0:T(8,128)S(1)}, u32[]{:S(2)}, u32[]{:S(2)}) collective-permute-start(f32[64,128]{1,0:T(8,128)S(1)} %get-tuple-element.51), channel_id=1, source_target_pairs={{0,7},{1,2},{2,1},{3,4},{4,3},{5,6},{6,5},{7,0},{8,15},{9,10},{10,... | collective-permute-start | bytes 98312 | tf_op jit(solution)/shard_map/ppermute | solution.py:407
  42.1 3.4 %collective-permute-start.13 = (f32[64,128]{1,0:T(8,128)S(1)}, f32[64,128]{1,0:T(8,128)S(1)}, u32[]{:S(2)}, u32[]{:S(2)}) collective-permute-start(f32[64,128]{1,0:T(8,128)S(1)} %get-tuple-element.56), channel_id=1, source_target_pairs={{0,24},{8,16},{16,8},{24,0},{1,25},{9,17},{17,9},{25,1},{2,26},{10... | collective-permute-start | bytes 98312 | tf_op jit(solution)/shard_map/ppermute | solution.py:407
  42.1 3.3 %collective-permute-start.12 = (f32[64,128]{1,0:T(8,128)S(1)}, f32[64,128]{1,0:T(8,128)S(1)}, u32[]{:S(2)}, u32[]{:S(2)}) collective-permute-start(f32[64,128]{1,0:T(8,128)S(1)} %get-tuple-element.56), channel_id=1, source_target_pairs={{0,8},{8,0},{16,24},{24,16},{1,9},{9,1},{17,25},{25,17},{2,10},{10... | collective-permute-start | bytes 98312 | tf_op jit(solution)/shard_map/ppermute | solution.py:407
  45.6 13.4 %collective-permute-start.14 = (f32[64,128]{1,0:T(8,128)S(1)}, f32[64,128]{1,0:T(8,128)S(1)}, u32[]{:S(2)}, u32[]{:S(2)}) collective-permute-start(f32[64,128]{1,0:T(8,128)S(1)} %get-tuple-element.58), channel_id=1, source_target_pairs={{0,1},{1,0},{2,3},{3,2},{4,5},{5,4},{6,7},{7,6},{8,9},{9,8},{10,11... | collective-permute-start | bytes 98312 | tf_op jit(solution)/shard_map/ppermute | solution.py:407
  45.6 13.3 %collective-permute-start.15 = (f32[64,128]{1,0:T(8,128)S(1)}, f32[64,128]{1,0:T(8,128)S(1)}, u32[]{:S(2)}, u32[]{:S(2)}) collective-permute-start(f32[64,128]{1,0:T(8,128)S(1)} %get-tuple-element.59), channel_id=1, source_target_pairs={{0,7},{1,2},{2,1},{3,4},{4,3},{5,6},{6,5},{7,0},{8,15},{9,10},{10,... | collective-permute-start | bytes 98312 | tf_op jit(solution)/shard_map/ppermute | solution.py:407

commit v2 on v1

--- a/solution.py
+++ b/solution.py
@@ -42,13 +42,10 @@
     corner_fix[0] = -degree * (degree + 1) / 4.0
     corner_fix[degree] = degree * (degree + 1) / 4.0
     derivative = derivative + identity * corner_fix[None, :]
-    weights3 = (weights[:, None, None] * weights[None, :, None] * weights[None, None, :]).reshape(
-        -1
-    )
-    return (derivative, weights3)
-
-
-DERIVATIVE, WEIGHTS3 = spectral_tables()
+    return (derivative, weights)
+
+
+DERIVATIVE, WEIGHTS = spectral_tables()
 
 
 def row(a, b):
@@ -161,7 +158,7 @@
 
 
 def to_grid(chosen, values):
-    parts = jnp.concatenate(parts_of(values[0, 0]), 0)
+    parts = jnp.concatenate(parts_of(values), 0)
     picked = jnp.dot(
         jnp.concatenate([chosen.astype(jnp.bfloat16)] * SPLIT, 1),
         parts,
@@ -171,12 +168,31 @@
 
 
 def setup_kernel(
-    forcing, viscosity, mass_rate, slots, weights, right, diagonal, spread, mass, face_x, face_y
+    forcing, viscosity, mass_rate, slots, right, diagonal, spread, mass, face_x, face_y,
+    held, arrived,
 ):
+    copies = [
+        pltpu.make_async_copy(source.at[0, 0], held.at[k], arrived.at[k])
+        for k, source in enumerate((viscosity, mass_rate, forcing))
+    ]
+    for copy in copies:
+        copy.start()
     chosen = selection(slots)
-    right[...] = to_grid(chosen, forcing)
-    spread[...] = to_grid(chosen, viscosity) * weights[...]
-    mass[...] = to_grid(chosen, mass_rate) * weights[...]
+    point = sublane_index()
+    last_weight = jnp.zeros((8, LANES), jnp.float32)
+    for c in range(8):
+        last_weight = jnp.where(point == c, float(WEIGHTS[c]), last_weight)
+    copies[0].wait()
+    spread[...] = to_grid(chosen, held[0])
+    copies[1].wait()
+    mass[...] = to_grid(chosen, held[1])
+    for a in range(8):
+        for b in range(8):
+            weight = last_weight * float(WEIGHTS[a] * WEIGHTS[b])
+            spread[row(a, b), :] *= weight
+            mass[row(a, b), :] *= weight
+    copies[2].wait()
+    right[...] = to_grid(chosen, held[2])
     squares = (DERIVATIVE * DERIVATIVE).T
     for b in range(8):
         lines = along(squares, [spread[row(a, b), :] for a in range(8)], 1)
@@ -388,13 +404,14 @@
         out[0, 0] = total
 
 
-def call(kernel, name, shapes, scratch, *operands):
+def call(kernel, name, shapes, scratch, *operands, outside=0):
+    places = [pltpu.HBM] * outside + [pltpu.VMEM] * (len(operands) - outside)
     return pl.pallas_call(
         kernel,
         out_shape=[jax.ShapeDtypeStruct(shape, jnp.float32) for shape in shapes],
-        in_specs=[pl.BlockSpec(memory_space=pltpu.VMEM)] * len(operands),
+        in_specs=[pl.BlockSpec(memory_space=place) for place in places],
         out_specs=[pl.BlockSpec(memory_space=pltpu.VMEM)] * len(shapes),
-        scratch_shapes=[pltpu.VMEM(shape, jnp.float32) for shape in scratch],
+        scratch_shapes=scratch,
         compiler_params=pltpu.CompilerParams(vmem_limit_bytes=VMEM_BYTES),
         name=name,
     )(*operands)
@@ -419,12 +436,12 @@
 def body(forcing, viscosity, mass_rate, slot_element):
     devices = lax.axis_size("gx") * lax.axis_size("yz")
     slots = slot_element[0]
-    weights = jnp.broadcast_to(jnp.asarray(WEIGHTS3, jnp.float32)[:, None], (POINTS, LANES))
     grid = (POINTS, LANES)
     face_x, face_y, moment = (64, LANES), (128, LANES), (8, LANES)
     right, diagonal, spread, mass, out_x, out_y = call(
-        setup_kernel, "setup", [grid] * 4 + [(128, LANES), (256, LANES)], [],
-        forcing, viscosity, mass_rate, slots, weights,
+        setup_kernel, "setup", [grid] * 4 + [(128, LANES), (256, LANES)],
+        [pltpu.VMEM((3, LANES, POINTS), jnp.float32), pltpu.SemaphoreType.DMA((3,))],
+        forcing, viscosity, mass_rate, slots, outside=3,
     )
     received = exchange(2, out_x, out_y)
     diagonal, values0, image, out_x, out_y, moments0 = call(
@@ -444,7 +461,7 @@
     sums = lax.all_to_all(sums, ("gx", "yz"), 0, 0)
     received = exchange(1, out_x, out_y)
     return call(
-        last_kernel, "last", [forcing.shape] * 2, [grid] * 2,
+        last_kernel, "last", [forcing.shape] * 2, [pltpu.VMEM(grid, jnp.float32)] * 2,
         image, *received, diagonal, values0, values1, values2, sums, slots,
     )
 

time: 60.5 us -> 61.6 us (1.018)
  local copies, waits for them, and re-layouts: 2.84 us -> 3.5 us
    unnamed x8, local copies, waits for them, and re-layouts: 2 us -> 3.5 us
    broadcast_in_dim x1 -> x0, local copies, waits for them, and re-layouts: 0.85 us -> none  [body(): jnp.broadcast_to(jnp.asarray(WEIGHTS3, jnp.float32)[:, None], (POINTS, LA...]
where the time goes in v2:
time: 61.6 us; the launch traced here: 61.4 us
  starting transfers between devices  24.7 us (40%)
  waiting for transfers between devices  17.4 us (28%)
  blocking collectives  9.76 us (16%)
  Pallas kernels  5.35 us (9%)
  local copies, waits for them, and re-layouts  3.5 us (6%)
  between operations  0.7 us (1%)
    ppermute x8, starting transfers between devices, swapped(): lax.ppermute(block[1], axis, odd)  17 us
    ppermute x8, waiting for transfers between devices, swapped(): lax.ppermute(block[1], axis, odd)  16.9 us
    all_to_all x1, blocking collectives, body(): sums = lax.all_to_all(sums, ('gx', 'yz'), 0, 0)  9.76 us
    ppermute x8, starting transfers between devices, swapped(): lax.ppermute(block[0], axis, even)  7.66 us
    pallas_call x9, Pallas kernels, call(): pl.pallas_call(kernel, out_shape=[jax.ShapeDtypeStruct(shape, jnp.float32...  5.35 us
    unnamed x8, local copies, waits for them, and re-layouts  3.5 us
  transfers between devices with their start and end apart: 16, of which 9 were waited for; matrix products, arithmetic and copies ran while one was open for 0% of the time, Pallas kernels for 0%

profile of v2, /device:TPU:0, one launch (start us, length us, event | category | flops | bytes accessed | tf_op | source)
XLA Modules:
  0.0 61.4 jit_solution(17759576381340052316)
XLA Ops:
  0.6 0.0 copy-start.3
  0.6 0.6 %copy-done.3 = s32[1,1,128]{2,1,0:T(1,128)S(1)} copy-done((s32[1,1,128]{2,1,0:T(1,128)S(1)}, s32[1,1,128]{2,1,0:T(1,128)}, u32[]{:S(2)}) %copy-start.3) | copy-done | bytes 536
  1.3 0.0 copy-start
  1.3 0.9 %copy-done = f32[1,1,128,512]{3,2,1,0:T(8,128)S(1)} copy-done((f32[1,1,128,512]{3,2,1,0:T(8,128)S(1)}, f32[1,1,128,512]{3,2,1,0:T(8,128)}, u32[]{:S(2)}) %copy-start) | copy-done | bytes 262168
  2.2 0.9 %copy-done.1 = f32[1,1,128,512]{3,2,1,0:T(8,128)S(1)} copy-done((f32[1,1,128,512]{3,2,1,0:T(8,128)S(1)}, f32[1,1,128,512]{3,2,1,0:T(8,128)}, u32[]{:S(2)}) %copy-start.1) | copy-done | bytes 262168
  3.2 0.9 %copy-done.2 = f32[1,1,128,512]{3,2,1,0:T(8,128)S(1)} copy-done((f32[1,1,128,512]{3,2,1,0:T(8,128)S(1)}, f32[1,1,128,512]{3,2,1,0:T(8,128)}, u32[]{:S(2)}) %copy-start.2) | copy-done | bytes 262168
  4.1 1.2 %setup.1 = (f32[512,128]{1,0:T(8,128)S(1)}, f32[512,128]{1,0:T(8,128)S(1)}, f32[512,128]{1,0:T(8,128)S(1)}, f32[512,128]{1,0:T(8,128)S(1)}, f32[128,128]{1,0:T(8,128)S(1)}, /*index=5*/f32[256,128]{1,0:T(8,128)S(1)}) custom-call(f32[1,1,128,512]{3,2,1,0:T(8,128)S(1)} %copy-done, f32[1,1,128,512]{3,2,1,0:T(8,128)S(1)} %copy-done.1, ...), custom_call_target="tpu_custom_call" | custom-call | tf_op jit(solution)/shard_map/setup/pallas_call | solution.py:409
  5.4 2.5 %collective-permute-start.1 = (f32[128,128]{1,0:T(8,128)S(1)}, f32[128,128]{1,0:T(8,128)S(1)}, u32[]{:S(2)}, u32[]{:S(2)}) collective-permute-start(f32[128,128]{1,0:T(8,128)S(1)} %get-tuple-element.34), channel_id=1, source_target_pairs={{0,24},{8,16},{16,8},{24,0},{1,25},{9,17},{17,9},{25,1},{2,26},{10... | collective-permute-start | bytes 196616 | tf_op jit(solution)/shard_map/ppermute | solution.py:424
  7.8 0.7 %collective-permute-start = (f32[128,128]{1,0:T(8,128)S(1)}, f32[128,128]{1,0:T(8,128)S(1)}, u32[]{:S(2)}, u32[]{:S(2)}) collective-permute-start(f32[128,128]{1,0:T(8,128)S(1)} %get-tuple-element.34), channel_id=1, source_target_pairs={{0,8},{8,0},{16,24},{24,16},{1,9},{9,1},{17,25},{25,17},{2,10},{10... | collective-permute-start | bytes 196616 | tf_op jit(solution)/shard_map/ppermute | solution.py:424
  8.5 1.8 %collective-permute-done.1.odd_x = f32[128,128]{1,0:T(8,128)S(1)} collective-permute-done((f32[128,128]{1,0:T(8,128)S(1)}, f32[128,128]{1,0:T(8,128)S(1)}, u32[]{:S(2)}, u32[]{:S(2)}) %collective-permute-start.1) | collective-permute-done | bytes 65568 | tf_op jit(solution)/shard_map/ppermute | solution.py:424
  10.3 0.0 collective-permute-done.even_x
  10.3 0.1 edges.4
  10.4 2.4 %collective-permute-start.2 = (f32[128,128]{1,0:T(8,128)S(1)}, f32[128,128]{1,0:T(8,128)S(1)}, u32[]{:S(2)}, u32[]{:S(2)}) collective-permute-start(f32[128,128]{1,0:T(8,128)S(1)} %get-tuple-element.36), channel_id=1, source_target_pairs={{0,1},{1,0},{2,3},{3,2},{4,5},{5,4},{6,7},{7,6},{8,9},{9,8},{10,11... | collective-permute-start | bytes 196616 | tf_op jit(solution)/shard_map/ppermute | solution.py:424
  12.8 3.6 %collective-permute-start.3 = (f32[128,128]{1,0:T(8,128)S(1)}, f32[128,128]{1,0:T(8,128)S(1)}, u32[]{:S(2)}, u32[]{:S(2)}) collective-permute-start(f32[128,128]{1,0:T(8,128)S(1)} %get-tuple-element.37), channel_id=1, source_target_pairs={{0,7},{1,2},{2,1},{3,4},{4,3},{5,6},{6,5},{7,0},{8,15},{9,10},{10,... | collective-permute-start | bytes 196616 | tf_op jit(solution)/shard_map/ppermute | solution.py:424
  16.4 0.0 collective-permute-done.2.even_y
  16.4 3.4 %collective-permute-done.3.odd_y = f32[128,128]{1,0:T(8,128)S(1)} collective-permute-done((f32[128,128]{1,0:T(8,128)S(1)}, f32[128,128]{1,0:T(8,128)S(1)}, u32[]{:S(2)}, u32[]{:S(2)}) %collective-permute-start.3) | collective-permute-done | bytes 65568 | tf_op jit(solution)/shard_map/ppermute | solution.py:424
  19.8 0.8 %first.1 = (f32[512,128]{1,0:T(8,128)S(1)}, f32[512,128]{1,0:T(8,128)S(1)}, f32[512,128]{1,0:T(8,128)S(1)}, f32[64,128]{1,0:T(8,128)S(1)}, f32[128,128]{1,0:T(8,128)S(1)}, /*index=5*/f32[8,128]{1,0:T(8,128)S(1)}) custom-call(f32[512,128]{1,0:T(8,128)S(1)} %get-tuple-element.32.right, f32[512,128]{1,0:T(8,128)S(1)} %get-tuple-element.33.diagonal, ...), custom_call_target="tpu_custom_call" | custom-call | tf_op jit(solution)/shard_map/first/pallas_call | solution.py:409
  20.6 0.1 collective-permute-start.5
  20.6 1.7 %collective-permute-start.4 = (f32[64,128]{1,0:T(8,128)S(1)}, f32[64,128]{1,0:T(8,128)S(1)}, u32[]{:S(2)}, u32[]{:S(2)}) collective-permute-start(f32[64,128]{1,0:T(8,128)S(1)} %get-tuple-element.41), channel_id=1, source_target_pairs={{0,8},{8,0},{16,24},{24,16},{1,9},{9,1},{17,25},{25,17},{2,10},{10... | collective-permute-start | bytes 98312 | tf_op jit(solution)/shard_map/ppermute | solution.py:424
  22.3 1.9 %collective-permute-done.5.odd_x = f32[64,128]{1,0:T(8,128)S(1)} collective-permute-done((f32[64,128]{1,0:T(8,128)S(1)}, f32[64,128]{1,0:T(8,128)S(1)}, u32[]{:S(2)}, u32[]{:S(2)}) %collective-permute-start.5) | collective-permute-done | bytes 32800 | tf_op jit(solution)/shard_map/ppermute | solution.py:424
  24.2 0.0 collective-permute-done.4.even_x
  24.2 0.1 edges.5
  24.3 0.0 collective-permute-start.6
  24.3 3.6 %collective-permute-start.7 = (f32[64,128]{1,0:T(8,128)S(1)}, f32[64,128]{1,0:T(8,128)S(1)}, u32[]{:S(2)}, u32[]{:S(2)}) collective-permute-start(f32[64,128]{1,0:T(8,128)S(1)} %get-tuple-element.44), channel_id=1, source_target_pairs={{0,7},{1,2},{2,1},{3,4},{4,3},{5,6},{6,5},{7,0},{8,15},{9,10},{10,... | collective-permute-start | bytes 98312 | tf_op jit(solution)/shard_map/ppermute | solution.py:424
  27.9 0.3 collective-permute-done.6.even_y
  28.2 2.8 %collective-permute-done.7.odd_y = f32[64,128]{1,0:T(8,128)S(1)} collective-permute-done((f32[64,128]{1,0:T(8,128)S(1)}, f32[64,128]{1,0:T(8,128)S(1)}, u32[]{:S(2)}, u32[]{:S(2)}) %collective-permute-start.7) | collective-permute-done | bytes 32800 | tf_op jit(solution)/shard_map/ppermute | solution.py:424
  31.0 0.8 %second.1 = (f32[512,128]{1,0:T(8,128)S(1)}, f32[512,128]{1,0:T(8,128)S(1)}, f32[64,128]{1,0:T(8,128)S(1)}, f32[128,128]{1,0:T(8,128)S(1)}, f32[16,128]{1,0:T(8,128)S(1)}) custom-call(f32[512,128]{1,0:T(8,128)S(1)} %get-tuple-element.40.before_image, f32[64,128]{1,0:T(8,128)S(1)} %collective-permute-done.4.even_x, ...), custom_call_target="tpu_custom_call" | custom-call | tf_op jit(solution)/shard_map/second/pallas_call | solution.py:409
  31.7 0.1 collective-permute-start.9
  31.8 1.5 %collective-permute-start.8 = (f32[64,128]{1,0:T(8,128)S(1)}, f32[64,128]{1,0:T(8,128)S(1)}, u32[]{:S(2)}, u32[]{:S(2)}) collective-permute-start(f32[64,128]{1,0:T(8,128)S(1)} %get-tuple-element.48), channel_id=1, source_target_pairs={{0,8},{8,0},{16,24},{24,16},{1,9},{9,1},{17,25},{25,17},{2,10},{10... | collective-permute-start | bytes 98312 | tf_op jit(solution)/shard_map/ppermute | solution.py:424
  33.3 2.1 %collective-permute-done.9.odd_x = f32[64,128]{1,0:T(8,128)S(1)} collective-permute-done((f32[64,128]{1,0:T(8,128)S(1)}, f32[64,128]{1,0:T(8,128)S(1)}, u32[]{:S(2)}, u32[]{:S(2)}) %collective-permute-start.9) | collective-permute-done | bytes 32800 | tf_op jit(solution)/shard_map/ppermute | solution.py:424
  35.4 0.0 collective-permute-done.8.even_x
  35.4 0.1 edges.6
  35.5 0.2 collective-permute-start.10
  35.7 3.6 %collective-permute-start.11 = (f32[64,128]{1,0:T(8,128)S(1)}, f32[64,128]{1,0:T(8,128)S(1)}, u32[]{:S(2)}, u32[]{:S(2)}) collective-permute-start(f32[64,128]{1,0:T(8,128)S(1)} %get-tuple-element.51), channel_id=1, source_target_pairs={{0,7},{1,2},{2,1},{3,4},{4,3},{5,6},{6,5},{7,0},{8,15},{9,10},{10,... | collective-permute-start | bytes 98312 | tf_op jit(solution)/shard_map/ppermute | solution.py:424
  39.2 0.2 collective-permute-done.10.even_y
  39.4 2.8 %collective-permute-done.11.odd_y = f32[64,128]{1,0:T(8,128)S(1)} collective-permute-done((f32[64,128]{1,0:T(8,128)S(1)}, f32[64,128]{1,0:T(8,128)S(1)}, u32[]{:S(2)}, u32[]{:S(2)}) %collective-permute-start.11) | collective-permute-done | bytes 32800 | tf_op jit(solution)/shard_map/ppermute | solution.py:424
  42.3 0.9 %third.1 = (f32[512,128]{1,0:T(8,128)S(1)}, f32[512,128]{1,0:T(8,128)S(1)}, f32[64,128]{1,0:T(8,128)S(1)}, f32[128,128]{1,0:T(8,128)S(1)}, f32[32,1,128]{2,1,0:T(1,128)S(1)}) custom-call(f32[512,128]{1,0:T(8,128)S(1)} %get-tuple-element.47.before_image, f32[64,128]{1,0:T(8,128)S(1)} %collective-permute-done.8.even_x, ...), custom_call_target="tpu_custom_call" | custom-call | tf_op jit(solution)/shard_map/third/pallas_call | solution.py:409
  43.2 0.1 collective-permute-start.13
  43.2 1.2 %collective-permute-start.12 = (f32[64,128]{1,0:T(8,128)S(1)}, f32[64,128]{1,0:T(8,128)S(1)}, u32[]{:S(2)}, u32[]{:S(2)}) collective-permute-start(f32[64,128]{1,0:T(8,128)S(1)} %get-tuple-element.56), channel_id=1, source_target_pairs={{0,8},{8,0},{16,24},{24,16},{1,9},{9,1},{17,25},{25,17},{2,10},{10... | collective-permute-start | bytes 98312 | tf_op jit(solution)/shard_map/ppermute | solution.py:424
  44.4 2.1 %collective-permute-done.13.odd_x = f32[64,128]{1,0:T(8,128)S(1)} collective-permute-done((f32[64,128]{1,0:T(8,128)S(1)}, f32[64,128]{1,0:T(8,128)S(1)}, u32[]{:S(2)}, u32[]{:S(2)}) %collective-permute-start.13) | collective-permute-done | bytes 32800 | tf_op jit(solution)/shard_map/ppermute | solution.py:424
  46.6 0.0 collective-permute-done.12.even_x
  46.6 0.1 edges.7
  46.7 0.1 collective-permute-start.14
  46.7 3.6 %collective-permute-start.15 = (f32[64,128]{1,0:T(8,128)S(1)}, f32[64,128]{1,0:T(8,128)S(1)}, u32[]{:S(2)}, u32[]{:S(2)}) collective-permute-start(f32[64,128]{1,0:T(8,128)S(1)} %get-tuple-element.59), channel_id=1, source_target_pairs={{0,7},{1,2},{2,1},{3,4},{4,3},{5,6},{6,5},{7,0},{8,15},{9,10},{10,... | collective-permute-start | bytes 98312 | tf_op jit(solution)/shard_map/ppermute | solution.py:424
  50.3 9.8 %all_to_all.5.sums = f32[32,1,128]{2,1,0:T(1,128)S(1)} all-to-all(f32[32,1,128]{2,1,0:T(1,128)S(1)} %get-tuple-element.61), channel_id=1, replica_groups=mesh['gx'=4,'yz'=8] {'gx','yz'}, dimensions={0} | all-to-all | bytes 32768 | tf_op jit(solution)/shard_map/all_to_all | solution.py:461
  60.1 0.0 collective-permute-done.14.even_y
  60.1 0.0 collective-permute-done.15.odd_y
  60.1 1.3 %last.1 = (f32[1,1,128,512]{3,2,1,0:T(8,128)}, f32[1,1,128,512]{3,2,1,0:T(8,128)}) custom-call(f32[512,128]{1,0:T(8,128)S(1)} %get-tuple-element.55.before_image, f32[64,128]{1,0:T(8,128)S(1)} %collective-permute-done.12.even_x, f32[64,128]{1,0:T(8,128)S(1)} %collective-permute-done.13.odd_x, f32[64,128]{1,0:T(8,128)S(1)} %collective-permute-done.14.even_y, ...), custom_call_target="tpu_custom_call" | custom-call | tf_op jit(solution)/shard_map/last/pallas_call | solution.py:409
  (2 shorter events, 0.0 us)
Async XLA Ops:
  0.6 0.7 %copy-start.3 = (s32[1,1,128]{2,1,0:T(1,128)S(1)}, s32[1,1,128]{2,1,0:T(1,128)}, u32[]{:S(2)}) copy-start(s32[1,1,128]{2,1,0:T(1,128)} %param.7) | copy-start | bytes 1540
  1.3 0.9 %copy-start = (f32[1,1,128,512]{3,2,1,0:T(8,128)S(1)}, f32[1,1,128,512]{3,2,1,0:T(8,128)}, u32[]{:S(2)}) copy-start(f32[1,1,128,512]{3,2,1,0:T(8,128)} %forcing.1) | copy-start | bytes 786436
  2.2 0.9 %copy-start.1 = (f32[1,1,128,512]{3,2,1,0:T(8,128)S(1)}, f32[1,1,128,512]{3,2,1,0:T(8,128)}, u32[]{:S(2)}) copy-start(f32[1,1,128,512]{3,2,1,0:T(8,128)} %viscosity.1) | copy-start | bytes 786436
  3.2 0.9 %copy-start.2 = (f32[1,1,128,512]{3,2,1,0:T(8,128)S(1)}, f32[1,1,128,512]{3,2,1,0:T(8,128)}, u32[]{:S(2)}) copy-start(f32[1,1,128,512]{3,2,1,0:T(8,128)} %mass_rate.1) | copy-start | bytes 786436
  5.4 5.0 %collective-permute-start.1 = (f32[128,128]{1,0:T(8,128)S(1)}, f32[128,128]{1,0:T(8,128)S(1)}, u32[]{:S(2)}, u32[]{:S(2)}) collective-permute-start(f32[128,128]{1,0:T(8,128)S(1)} %get-tuple-element.34), channel_id=1, source_target_pairs={{0,24},{8,16},{16,8},{24,0},{1,25},{9,17},{17,9},{25,1},{2,26},{10... | collective-permute-start | bytes 196616 | tf_op jit(solution)/shard_map/ppermute | solution.py:424
  7.8 2.5 %collective-permute-start = (f32[128,128]{1,0:T(8,128)S(1)}, f32[128,128]{1,0:T(8,128)S(1)}, u32[]{:S(2)}, u32[]{:S(2)}) collective-permute-start(f32[128,128]{1,0:T(8,128)S(1)} %get-tuple-element.34), channel_id=1, source_target_pairs={{0,8},{8,0},{16,24},{24,16},{1,9},{9,1},{17,25},{25,17},{2,10},{10... | collective-permute-start | bytes 196616 | tf_op jit(solution)/shard_map/ppermute | solution.py:424
  10.4 6.0 %collective-permute-start.2 = (f32[128,128]{1,0:T(8,128)S(1)}, f32[128,128]{1,0:T(8,128)S(1)}, u32[]{:S(2)}, u32[]{:S(2)}) collective-permute-start(f32[128,128]{1,0:T(8,128)S(1)} %get-tuple-element.36), channel_id=1, source_target_pairs={{0,1},{1,0},{2,3},{3,2},{4,5},{5,4},{6,7},{7,6},{8,9},{9,8},{10,11... | collective-permute-start | bytes 196616 | tf_op jit(solution)/shard_map/ppermute | solution.py:424
  12.8 7.0 %collective-permute-start.3 = (f32[128,128]{1,0:T(8,128)S(1)}, f32[128,128]{1,0:T(8,128)S(1)}, u32[]{:S(2)}, u32[]{:S(2)}) collective-permute-start(f32[128,128]{1,0:T(8,128)S(1)} %get-tuple-element.37), channel_id=1, source_target_pairs={{0,7},{1,2},{2,1},{3,4},{4,3},{5,6},{6,5},{7,0},{8,15},{9,10},{10,... | collective-permute-start | bytes 196616 | tf_op jit(solution)/shard_map/ppermute | solution.py:424
  20.6 3.6 %collective-permute-start.5 = (f32[64,128]{1,0:T(8,128)S(1)}, f32[64,128]{1,0:T(8,128)S(1)}, u32[]{:S(2)}, u32[]{:S(2)}) collective-permute-start(f32[64,128]{1,0:T(8,128)S(1)} %get-tuple-element.41), channel_id=1, source_target_pairs={{0,24},{8,16},{16,8},{24,0},{1,25},{9,17},{17,9},{25,1},{2,26},{10... | collective-permute-start | bytes 98312 | tf_op jit(solution)/shard_map/ppermute | solution.py:424
  20.6 3.5 %collective-permute-start.4 = (f32[64,128]{1,0:T(8,128)S(1)}, f32[64,128]{1,0:T(8,128)S(1)}, u32[]{:S(2)}, u32[]{:S(2)}) collective-permute-start(f32[64,128]{1,0:T(8,128)S(1)} %get-tuple-element.41), channel_id=1, source_target_pairs={{0,8},{8,0},{16,24},{24,16},{1,9},{9,1},{17,25},{25,17},{2,10},{10... | collective-permute-start | bytes 98312 | tf_op jit(solution)/shard_map/ppermute | solution.py:424
  24.3 3.9 %collective-permute-start.6 = (f32[64,128]{1,0:T(8,128)S(1)}, f32[64,128]{1,0:T(8,128)S(1)}, u32[]{:S(2)}, u32[]{:S(2)}) collective-permute-start(f32[64,128]{1,0:T(8,128)S(1)} %get-tuple-element.43), channel_id=1, source_target_pairs={{0,1},{1,0},{2,3},{3,2},{4,5},{5,4},{6,7},{7,6},{8,9},{9,8},{10,11... | collective-permute-start | bytes 98312 | tf_op jit(solution)/shard_map/ppermute | solution.py:424
  24.3 6.7 %collective-permute-start.7 = (f32[64,128]{1,0:T(8,128)S(1)}, f32[64,128]{1,0:T(8,128)S(1)}, u32[]{:S(2)}, u32[]{:S(2)}) collective-permute-start(f32[64,128]{1,0:T(8,128)S(1)} %get-tuple-element.44), channel_id=1, source_target_pairs={{0,7},{1,2},{2,1},{3,4},{4,3},{5,6},{6,5},{7,0},{8,15},{9,10},{10,... | collective-permute-start | bytes 98312 | tf_op jit(solution)/shard_map/ppermute | solution.py:424
  31.7 3.7 %collective-permute-start.9 = (f32[64,128]{1,0:T(8,128)S(1)}, f32[64,128]{1,0:T(8,128)S(1)}, u32[]{:S(2)}, u32[]{:S(2)}) collective-permute-start(f32[64,128]{1,0:T(8,128)S(1)} %get-tuple-element.48), channel_id=1, source_target_pairs={{0,24},{8,16},{16,8},{24,0},{1,25},{9,17},{17,9},{25,1},{2,26},{10... | collective-permute-start | bytes 98312 | tf_op jit(solution)/shard_map/ppermute | solution.py:424
  31.8 3.6 %collective-permute-start.8 = (f32[64,128]{1,0:T(8,128)S(1)}, f32[64,128]{1,0:T(8,128)S(1)}, u32[]{:S(2)}, u32[]{:S(2)}) collective-permute-start(f32[64,128]{1,0:T(8,128)S(1)} %get-tuple-element.48), channel_id=1, source_target_pairs={{0,8},{8,0},{16,24},{24,16},{1,9},{9,1},{17,25},{25,17},{2,10},{10... | collective-permute-start | bytes 98312 | tf_op jit(solution)/shard_map/ppermute | solution.py:424
  35.5 3.9 %collective-permute-start.10 = (f32[64,128]{1,0:T(8,128)S(1)}, f32[64,128]{1,0:T(8,128)S(1)}, u32[]{:S(2)}, u32[]{:S(2)}) collective-permute-start(f32[64,128]{1,0:T(8,128)S(1)} %get-tuple-element.50), channel_id=1, source_target_pairs={{0,1},{1,0},{2,3},{3,2},{4,5},{5,4},{6,7},{7,6},{8,9},{9,8},{10,11... | collective-permute-start | bytes 98312 | tf_op jit(solution)/shard_map/ppermute | solution.py:424
  35.7 6.6 %collective-permute-start.11 = (f32[64,128]{1,0:T(8,128)S(1)}, f32[64,128]{1,0:T(8,128)S(1)}, u32[]{:S(2)}, u32[]{:S(2)}) collective-permute-start(f32[64,128]{1,0:T(8,128)S(1)} %get-tuple-element.51), channel_id=1, source_target_pairs={{0,7},{1,2},{2,1},{3,4},{4,3},{5,6},{6,5},{7,0},{8,15},{9,10},{10,... | collective-permute-start | bytes 98312 | tf_op jit(solution)/shard_map/ppermute | solution.py:424
  43.2 3.4 %collective-permute-start.13 = (f32[64,128]{1,0:T(8,128)S(1)}, f32[64,128]{1,0:T(8,128)S(1)}, u32[]{:S(2)}, u32[]{:S(2)}) collective-permute-start(f32[64,128]{1,0:T(8,128)S(1)} %get-tuple-element.56), channel_id=1, source_target_pairs={{0,24},{8,16},{16,8},{24,0},{1,25},{9,17},{17,9},{25,1},{2,26},{10... | collective-permute-start | bytes 98312 | tf_op jit(solution)/shard_map/ppermute | solution.py:424
  43.2 3.3 %collective-permute-start.12 = (f32[64,128]{1,0:T(8,128)S(1)}, f32[64,128]{1,0:T(8,128)S(1)}, u32[]{:S(2)}, u32[]{:S(2)}) collective-permute-start(f32[64,128]{1,0:T(8,128)S(1)} %get-tuple-element.56), channel_id=1, source_target_pairs={{0,8},{8,0},{16,24},{24,16},{1,9},{9,1},{17,25},{25,17},{2,10},{10... | collective-permute-start | bytes 98312 | tf_op jit(solution)/shard_map/ppermute | solution.py:424
  46.7 13.4 %collective-permute-start.14 = (f32[64,128]{1,0:T(8,128)S(1)}, f32[64,128]{1,0:T(8,128)S(1)}, u32[]{:S(2)}, u32[]{:S(2)}) collective-permute-start(f32[64,128]{1,0:T(8,128)S(1)} %get-tuple-element.58), channel_id=1, source_target_pairs={{0,1},{1,0},{2,3},{3,2},{4,5},{5,4},{6,7},{7,6},{8,9},{9,8},{10,11... | collective-permute-start | bytes 98312 | tf_op jit(solution)/shard_map/ppermute | solution.py:424
  46.7 13.3 %collective-permute-start.15 = (f32[64,128]{1,0:T(8,128)S(1)}, f32[64,128]{1,0:T(8,128)S(1)}, u32[]{:S(2)}, u32[]{:S(2)}) collective-permute-start(f32[64,128]{1,0:T(8,128)S(1)} %get-tuple-element.59), channel_id=1, source_target_pairs={{0,7},{1,2},{2,1},{3,4},{4,3},{5,6},{6,5},{7,0},{8,15},{9,10},{10,... | collective-permute-start | bytes 98312 | tf_op jit(solution)/shard_map/ppermute | solution.py:424

commit v3 on v2

--- a/solution.py
+++ b/solution.py
@@ -168,20 +168,22 @@
 
 
 def setup_kernel(
-    forcing, viscosity, mass_rate, slots, right, diagonal, spread, mass, face_x, face_y,
-    held, arrived,
+    slots, forcing, viscosity, mass_rate, right, diagonal, spread, mass, face_x, face_y,
+    order, held, arrived,
 ):
+    ordered = pltpu.make_async_copy(slots, order, arrived.at[3])
     copies = [
         pltpu.make_async_copy(source.at[0, 0], held.at[k], arrived.at[k])
         for k, source in enumerate((viscosity, mass_rate, forcing))
     ]
-    for copy in copies:
+    for copy in [ordered] + copies:
         copy.start()
-    chosen = selection(slots)
     point = sublane_index()
     last_weight = jnp.zeros((8, LANES), jnp.float32)
     for c in range(8):
         last_weight = jnp.where(point == c, float(WEIGHTS[c]), last_weight)
+    ordered.wait()
+    chosen = selection(order)
     copies[0].wait()
     spread[...] = to_grid(chosen, held[0])
     copies[1].wait()
@@ -406,6 +408,10 @@
 
 def call(kernel, name, shapes, scratch, *operands, outside=0):
     places = [pltpu.HBM] * outside + [pltpu.VMEM] * (len(operands) - outside)
+    operands = [
+        pltpu.with_memory_space_constraint(operand, place) if place == pltpu.HBM else operand
+        for operand, place in zip(operands, places)
+    ]
     return pl.pallas_call(
         kernel,
         out_shape=[jax.ShapeDtypeStruct(shape, jnp.float32) for shape in shapes],
@@ -440,8 +446,12 @@
     face_x, face_y, moment = (64, LANES), (128, LANES), (8, LANES)
     right, diagonal, spread, mass, out_x, out_y = call(
         setup_kernel, "setup", [grid] * 4 + [(128, LANES), (256, LANES)],
-        [pltpu.VMEM((3, LANES, POINTS), jnp.float32), pltpu.SemaphoreType.DMA((3,))],
-        forcing, viscosity, mass_rate, slots, outside=3,
+        [
+            pltpu.VMEM((1, LANES), jnp.int32),
+            pltpu.VMEM((3, LANES, POINTS), jnp.float32),
+            pltpu.SemaphoreType.DMA((4,)),
+        ],
+        slots, forcing, viscosity, mass_rate, outside=4,
     )
     received = exchange(2, out_x, out_y)
     diagonal, values0, image, out_x, out_y, moments0 = call(

time: 61.6 us -> 59.6 us (0.968)
  local copies, waits for them, and re-layouts: 3.5 us -> 0.65 us
  Pallas kernels: 5.35 us -> 6.26 us
    unnamed x8 -> x2, local copies, waits for them, and re-layouts: 3.5 us -> 0.65 us
    pallas_call x9, Pallas kernels: 5.35 us -> 6.26 us  [call(): pl.pallas_call(kernel, out_shape=[jax.ShapeDtypeStruct(shape, jnp.float32...]
where the time goes in v3:
time: 59.6 us; the launch traced here: 59.5 us
  starting transfers between devices  24.7 us (41%)
  waiting for transfers between devices  17.4 us (29%)
  blocking collectives  9.76 us (16%)
  Pallas kernels  6.26 us (11%)
  between operations  0.7 us (1%)
  local copies, waits for them, and re-layouts  0.65 us (1%)
    ppermute x8, starting transfers between devices, swapped(): lax.ppermute(block[1], axis, odd)  17 us
    ppermute x8, waiting for transfers between devices, swapped(): lax.ppermute(block[1], axis, odd)  16.9 us
    all_to_all x1, blocking collectives, body(): sums = lax.all_to_all(sums, ('gx', 'yz'), 0, 0)  9.76 us
    ppermute x8, starting transfers between devices, swapped(): lax.ppermute(block[0], axis, even)  7.66 us
    pallas_call x9, Pallas kernels, call(): pl.pallas_call(kernel, out_shape=[jax.ShapeDtypeStruct(shape, jnp.float32...  6.26 us
  transfers between devices with their start and end apart: 16, of which 9 were waited for; matrix products, arithmetic and copies ran while one was open for 0% of the time, Pallas kernels for 0%

profile of v3, /device:TPU:0, one launch (start us, length us, event | category | flops | bytes accessed | tf_op | source)
XLA Modules:
  0.0 59.5 jit_solution(5340412393420337894)
XLA Ops:
  0.6 2.1 %setup.1 = (f32[512,128]{1,0:T(8,128)S(1)}, f32[512,128]{1,0:T(8,128)S(1)}, f32[512,128]{1,0:T(8,128)S(1)}, f32[512,128]{1,0:T(8,128)S(1)}, f32[128,128]{1,0:T(8,128)S(1)}, /*index=5*/f32[256,128]{1,0:T(8,128)S(1)}) custom-call(s32[1,128]{1,0:T(1,128)} %bitcast.1, f32[1,1,128,512]{3,2,1,0:T(8,128)} %forcing.1, f32[1,1,128,512]{3,2,1,0:T(8,128)} %viscosity.1, ...), custom_call_target="tpu_custom_call" | custom-call | tf_op jit(solution)/shard_map/setup/pallas_call | solution.py:415
  2.8 2.5 %collective-permute-start.1 = (f32[128,128]{1,0:T(8,128)S(1)}, f32[128,128]{1,0:T(8,128)S(1)}, u32[]{:S(2)}, u32[]{:S(2)}) collective-permute-start(f32[128,128]{1,0:T(8,128)S(1)} %get-tuple-element.34), channel_id=1, source_target_pairs={{0,24},{8,16},{16,8},{24,0},{1,25},{9,17},{17,9},{25,1},{2,26},{10... | collective-permute-start | bytes 196616 | tf_op jit(solution)/shard_map/ppermute | solution.py:430
  5.3 0.7 %collective-permute-start = (f32[128,128]{1,0:T(8,128)S(1)}, f32[128,128]{1,0:T(8,128)S(1)}, u32[]{:S(2)}, u32[]{:S(2)}) collective-permute-start(f32[128,128]{1,0:T(8,128)S(1)} %get-tuple-element.34), channel_id=1, source_target_pairs={{0,8},{8,0},{16,24},{24,16},{1,9},{9,1},{17,25},{25,17},{2,10},{10... | collective-permute-start | bytes 196616 | tf_op jit(solution)/shard_map/ppermute | solution.py:430
  5.9 1.8 %collective-permute-done.1.odd_x = f32[128,128]{1,0:T(8,128)S(1)} collective-permute-done((f32[128,128]{1,0:T(8,128)S(1)}, f32[128,128]{1,0:T(8,128)S(1)}, u32[]{:S(2)}, u32[]{:S(2)}) %collective-permute-start.1) | collective-permute-done | bytes 65568 | tf_op jit(solution)/shard_map/ppermute | solution.py:430
  7.7 0.0 collective-permute-done.even_x
  7.7 0.1 edges.4
  7.8 2.4 %collective-permute-start.2 = (f32[128,128]{1,0:T(8,128)S(1)}, f32[128,128]{1,0:T(8,128)S(1)}, u32[]{:S(2)}, u32[]{:S(2)}) collective-permute-start(f32[128,128]{1,0:T(8,128)S(1)} %get-tuple-element.36), channel_id=1, source_target_pairs={{0,1},{1,0},{2,3},{3,2},{4,5},{5,4},{6,7},{7,6},{8,9},{9,8},{10,11... | collective-permute-start | bytes 196616 | tf_op jit(solution)/shard_map/ppermute | solution.py:430
  10.2 3.6 %collective-permute-start.3 = (f32[128,128]{1,0:T(8,128)S(1)}, f32[128,128]{1,0:T(8,128)S(1)}, u32[]{:S(2)}, u32[]{:S(2)}) collective-permute-start(f32[128,128]{1,0:T(8,128)S(1)} %get-tuple-element.37), channel_id=1, source_target_pairs={{0,7},{1,2},{2,1},{3,4},{4,3},{5,6},{6,5},{7,0},{8,15},{9,10},{10,... | collective-permute-start | bytes 196616 | tf_op jit(solution)/shard_map/ppermute | solution.py:430
  13.8 0.0 collective-permute-done.2.even_y
  13.8 3.4 %collective-permute-done.3.odd_y = f32[128,128]{1,0:T(8,128)S(1)} collective-permute-done((f32[128,128]{1,0:T(8,128)S(1)}, f32[128,128]{1,0:T(8,128)S(1)}, u32[]{:S(2)}, u32[]{:S(2)}) %collective-permute-start.3) | collective-permute-done | bytes 65568 | tf_op jit(solution)/shard_map/ppermute | solution.py:430
  17.2 0.8 %first.1 = (f32[512,128]{1,0:T(8,128)S(1)}, f32[512,128]{1,0:T(8,128)S(1)}, f32[512,128]{1,0:T(8,128)S(1)}, f32[64,128]{1,0:T(8,128)S(1)}, f32[128,128]{1,0:T(8,128)S(1)}, /*index=5*/f32[8,128]{1,0:T(8,128)S(1)}) custom-call(f32[512,128]{1,0:T(8,128)S(1)} %get-tuple-element.32.right, f32[512,128]{1,0:T(8,128)S(1)} %get-tuple-element.33.diagonal, ...), custom_call_target="tpu_custom_call" | custom-call | tf_op jit(solution)/shard_map/first/pallas_call | solution.py:415
  18.0 0.1 collective-permute-start.5
  18.0 1.7 %collective-permute-start.4 = (f32[64,128]{1,0:T(8,128)S(1)}, f32[64,128]{1,0:T(8,128)S(1)}, u32[]{:S(2)}, u32[]{:S(2)}) collective-permute-start(f32[64,128]{1,0:T(8,128)S(1)} %get-tuple-element.41), channel_id=1, source_target_pairs={{0,8},{8,0},{16,24},{24,16},{1,9},{9,1},{17,25},{25,17},{2,10},{10... | collective-permute-start | bytes 98312 | tf_op jit(solution)/shard_map/ppermute | solution.py:430
  19.7 1.9 %collective-permute-done.5.odd_x = f32[64,128]{1,0:T(8,128)S(1)} collective-permute-done((f32[64,128]{1,0:T(8,128)S(1)}, f32[64,128]{1,0:T(8,128)S(1)}, u32[]{:S(2)}, u32[]{:S(2)}) %collective-permute-start.5) | collective-permute-done | bytes 32800 | tf_op jit(solution)/shard_map/ppermute | solution.py:430
  21.6 0.0 collective-permute-done.4.even_x
  21.6 0.1 edges.5
  21.7 0.0 collective-permute-start.6
  21.7 3.6 %collective-permute-start.7 = (f32[64,128]{1,0:T(8,128)S(1)}, f32[64,128]{1,0:T(8,128)S(1)}, u32[]{:S(2)}, u32[]{:S(2)}) collective-permute-start(f32[64,128]{1,0:T(8,128)S(1)} %get-tuple-element.44), channel_id=1, source_target_pairs={{0,7},{1,2},{2,1},{3,4},{4,3},{5,6},{6,5},{7,0},{8,15},{9,10},{10,... | collective-permute-start | bytes 98312 | tf_op jit(solution)/shard_map/ppermute | solution.py:430
  25.3 0.3 collective-permute-done.6.even_y
  25.6 2.8 %collective-permute-done.7.odd_y = f32[64,128]{1,0:T(8,128)S(1)} collective-permute-done((f32[64,128]{1,0:T(8,128)S(1)}, f32[64,128]{1,0:T(8,128)S(1)}, u32[]{:S(2)}, u32[]{:S(2)}) %collective-permute-start.7) | collective-permute-done | bytes 32800 | tf_op jit(solution)/shard_map/ppermute | solution.py:430
  28.4 0.8 %second.1 = (f32[512,128]{1,0:T(8,128)S(1)}, f32[512,128]{1,0:T(8,128)S(1)}, f32[64,128]{1,0:T(8,128)S(1)}, f32[128,128]{1,0:T(8,128)S(1)}, f32[16,128]{1,0:T(8,128)S(1)}) custom-call(f32[512,128]{1,0:T(8,128)S(1)} %get-tuple-element.40.before_image, f32[64,128]{1,0:T(8,128)S(1)} %collective-permute-done.4.even_x, ...), custom_call_target="tpu_custom_call" | custom-call | tf_op jit(solution)/shard_map/second/pallas_call | solution.py:415
  29.2 0.1 collective-permute-start.9
  29.2 1.5 %collective-permute-start.8 = (f32[64,128]{1,0:T(8,128)S(1)}, f32[64,128]{1,0:T(8,128)S(1)}, u32[]{:S(2)}, u32[]{:S(2)}) collective-permute-start(f32[64,128]{1,0:T(8,128)S(1)} %get-tuple-element.48), channel_id=1, source_target_pairs={{0,8},{8,0},{16,24},{24,16},{1,9},{9,1},{17,25},{25,17},{2,10},{10... | collective-permute-start | bytes 98312 | tf_op jit(solution)/shard_map/ppermute | solution.py:430
  30.7 2.1 %collective-permute-done.9.odd_x = f32[64,128]{1,0:T(8,128)S(1)} collective-permute-done((f32[64,128]{1,0:T(8,128)S(1)}, f32[64,128]{1,0:T(8,128)S(1)}, u32[]{:S(2)}, u32[]{:S(2)}) %collective-permute-start.9) | collective-permute-done | bytes 32800 | tf_op jit(solution)/shard_map/ppermute | solution.py:430
  32.8 0.0 collective-permute-done.8.even_x
  32.8 0.1 edges.6
  32.9 0.2 collective-permute-start.10
  33.1 3.6 %collective-permute-start.11 = (f32[64,128]{1,0:T(8,128)S(1)}, f32[64,128]{1,0:T(8,128)S(1)}, u32[]{:S(2)}, u32[]{:S(2)}) collective-permute-start(f32[64,128]{1,0:T(8,128)S(1)} %get-tuple-element.51), channel_id=1, source_target_pairs={{0,7},{1,2},{2,1},{3,4},{4,3},{5,6},{6,5},{7,0},{8,15},{9,10},{10,... | collective-permute-start | bytes 98312 | tf_op jit(solution)/shard_map/ppermute | solution.py:430
  36.7 0.2 collective-permute-done.10.even_y
  36.8 2.8 %collective-permute-done.11.odd_y = f32[64,128]{1,0:T(8,128)S(1)} collective-permute-done((f32[64,128]{1,0:T(8,128)S(1)}, f32[64,128]{1,0:T(8,128)S(1)}, u32[]{:S(2)}, u32[]{:S(2)}) %collective-permute-start.11) | collective-permute-done | bytes 32800 | tf_op jit(solution)/shard_map/ppermute | solution.py:430
  39.7 0.9 %third.1 = (f32[512,128]{1,0:T(8,128)S(1)}, f32[512,128]{1,0:T(8,128)S(1)}, f32[64,128]{1,0:T(8,128)S(1)}, f32[128,128]{1,0:T(8,128)S(1)}, f32[32,1,128]{2,1,0:T(1,128)S(1)}) custom-call(f32[512,128]{1,0:T(8,128)S(1)} %get-tuple-element.47.before_image, f32[64,128]{1,0:T(8,128)S(1)} %collective-permute-done.8.even_x, ...), custom_call_target="tpu_custom_call" | custom-call | tf_op jit(solution)/shard_map/third/pallas_call | solution.py:415
  40.6 0.1 collective-permute-start.13
  40.6 1.2 %collective-permute-start.12 = (f32[64,128]{1,0:T(8,128)S(1)}, f32[64,128]{1,0:T(8,128)S(1)}, u32[]{:S(2)}, u32[]{:S(2)}) collective-permute-start(f32[64,128]{1,0:T(8,128)S(1)} %get-tuple-element.56), channel_id=1, source_target_pairs={{0,8},{8,0},{16,24},{24,16},{1,9},{9,1},{17,25},{25,17},{2,10},{10... | collective-permute-start | bytes 98312 | tf_op jit(solution)/shard_map/ppermute | solution.py:430
  41.8 2.1 %collective-permute-done.13.odd_x = f32[64,128]{1,0:T(8,128)S(1)} collective-permute-done((f32[64,128]{1,0:T(8,128)S(1)}, f32[64,128]{1,0:T(8,128)S(1)}, u32[]{:S(2)}, u32[]{:S(2)}) %collective-permute-start.13) | collective-permute-done | bytes 32800 | tf_op jit(solution)/shard_map/ppermute | solution.py:430
  44.0 0.0 collective-permute-done.12.even_x
  44.0 0.1 edges.7
  44.1 0.1 collective-permute-start.14
  44.2 3.6 %collective-permute-start.15 = (f32[64,128]{1,0:T(8,128)S(1)}, f32[64,128]{1,0:T(8,128)S(1)}, u32[]{:S(2)}, u32[]{:S(2)}) collective-permute-start(f32[64,128]{1,0:T(8,128)S(1)} %get-tuple-element.59), channel_id=1, source_target_pairs={{0,7},{1,2},{2,1},{3,4},{4,3},{5,6},{6,5},{7,0},{8,15},{9,10},{10,... | collective-permute-start | bytes 98312 | tf_op jit(solution)/shard_map/ppermute | solution.py:430
  47.7 9.8 %all_to_all.5.sums = f32[32,1,128]{2,1,0:T(1,128)S(1)} all-to-all(f32[32,1,128]{2,1,0:T(1,128)S(1)} %get-tuple-element.61), channel_id=1, replica_groups=mesh['gx'=4,'yz'=8] {'gx','yz'}, dimensions={0} | all-to-all | bytes 32768 | tf_op jit(solution)/shard_map/all_to_all | solution.py:471
  57.5 0.0 collective-permute-done.14.even_y
  57.5 0.0 collective-permute-done.15.odd_y
  57.5 0.0 copy-start
  57.5 0.7 %copy-done = s32[1,1,128]{2,1,0:T(1,128)S(1)} copy-done((s32[1,1,128]{2,1,0:T(1,128)S(1)}, s32[1,1,128]{2,1,0:T(1,128)}, u32[]{:S(2)}) %copy-start) | copy-done | bytes 536
  58.1 1.3 %last.1 = (f32[1,1,128,512]{3,2,1,0:T(8,128)}, f32[1,1,128,512]{3,2,1,0:T(8,128)}) custom-call(f32[512,128]{1,0:T(8,128)S(1)} %get-tuple-element.55.before_image, f32[64,128]{1,0:T(8,128)S(1)} %collective-permute-done.12.even_x, f32[64,128]{1,0:T(8,128)S(1)} %collective-permute-done.13.odd_x, f32[64,128]{1,0:T(8,128)S(1)} %collective-permute-done.14.even_y, ...), custom_call_target="tpu_custom_call" | custom-call | tf_op jit(solution)/shard_map/last/pallas_call | solution.py:415
Async XLA Ops:
  2.8 5.0 %collective-permute-start.1 = (f32[128,128]{1,0:T(8,128)S(1)}, f32[128,128]{1,0:T(8,128)S(1)}, u32[]{:S(2)}, u32[]{:S(2)}) collective-permute-start(f32[128,128]{1,0:T(8,128)S(1)} %get-tuple-element.34), channel_id=1, source_target_pairs={{0,24},{8,16},{16,8},{24,0},{1,25},{9,17},{17,9},{25,1},{2,26},{10... | collective-permute-start | bytes 196616 | tf_op jit(solution)/shard_map/ppermute | solution.py:430
  5.3 2.5 %collective-permute-start = (f32[128,128]{1,0:T(8,128)S(1)}, f32[128,128]{1,0:T(8,128)S(1)}, u32[]{:S(2)}, u32[]{:S(2)}) collective-permute-start(f32[128,128]{1,0:T(8,128)S(1)} %get-tuple-element.34), channel_id=1, source_target_pairs={{0,8},{8,0},{16,24},{24,16},{1,9},{9,1},{17,25},{25,17},{2,10},{10... | collective-permute-start | bytes 196616 | tf_op jit(solution)/shard_map/ppermute | solution.py:430
  7.8 6.0 %collective-permute-start.2 = (f32[128,128]{1,0:T(8,128)S(1)}, f32[128,128]{1,0:T(8,128)S(1)}, u32[]{:S(2)}, u32[]{:S(2)}) collective-permute-start(f32[128,128]{1,0:T(8,128)S(1)} %get-tuple-element.36), channel_id=1, source_target_pairs={{0,1},{1,0},{2,3},{3,2},{4,5},{5,4},{6,7},{7,6},{8,9},{9,8},{10,11... | collective-permute-start | bytes 196616 | tf_op jit(solution)/shard_map/ppermute | solution.py:430
  10.2 7.0 %collective-permute-start.3 = (f32[128,128]{1,0:T(8,128)S(1)}, f32[128,128]{1,0:T(8,128)S(1)}, u32[]{:S(2)}, u32[]{:S(2)}) collective-permute-start(f32[128,128]{1,0:T(8,128)S(1)} %get-tuple-element.37), channel_id=1, source_target_pairs={{0,7},{1,2},{2,1},{3,4},{4,3},{5,6},{6,5},{7,0},{8,15},{9,10},{10,... | collective-permute-start | bytes 196616 | tf_op jit(solution)/shard_map/ppermute | solution.py:430
  18.0 3.6 %collective-permute-start.5 = (f32[64,128]{1,0:T(8,128)S(1)}, f32[64,128]{1,0:T(8,128)S(1)}, u32[]{:S(2)}, u32[]{:S(2)}) collective-permute-start(f32[64,128]{1,0:T(8,128)S(1)} %get-tuple-element.41), channel_id=1, source_target_pairs={{0,24},{8,16},{16,8},{24,0},{1,25},{9,17},{17,9},{25,1},{2,26},{10... | collective-permute-start | bytes 98312 | tf_op jit(solution)/shard_map/ppermute | solution.py:430
  18.0 3.5 %collective-permute-start.4 = (f32[64,128]{1,0:T(8,128)S(1)}, f32[64,128]{1,0:T(8,128)S(1)}, u32[]{:S(2)}, u32[]{:S(2)}) collective-permute-start(f32[64,128]{1,0:T(8,128)S(1)} %get-tuple-element.41), channel_id=1, source_target_pairs={{0,8},{8,0},{16,24},{24,16},{1,9},{9,1},{17,25},{25,17},{2,10},{10... | collective-permute-start | bytes 98312 | tf_op jit(solution)/shard_map/ppermute | solution.py:430
  21.7 3.9 %collective-permute-start.6 = (f32[64,128]{1,0:T(8,128)S(1)}, f32[64,128]{1,0:T(8,128)S(1)}, u32[]{:S(2)}, u32[]{:S(2)}) collective-permute-start(f32[64,128]{1,0:T(8,128)S(1)} %get-tuple-element.43), channel_id=1, source_target_pairs={{0,1},{1,0},{2,3},{3,2},{4,5},{5,4},{6,7},{7,6},{8,9},{9,8},{10,11... | collective-permute-start | bytes 98312 | tf_op jit(solution)/shard_map/ppermute | solution.py:430
  21.7 6.7 %collective-permute-start.7 = (f32[64,128]{1,0:T(8,128)S(1)}, f32[64,128]{1,0:T(8,128)S(1)}, u32[]{:S(2)}, u32[]{:S(2)}) collective-permute-start(f32[64,128]{1,0:T(8,128)S(1)} %get-tuple-element.44), channel_id=1, source_target_pairs={{0,7},{1,2},{2,1},{3,4},{4,3},{5,6},{6,5},{7,0},{8,15},{9,10},{10,... | collective-permute-start | bytes 98312 | tf_op jit(solution)/shard_map/ppermute | solution.py:430
  29.2 3.7 %collective-permute-start.9 = (f32[64,128]{1,0:T(8,128)S(1)}, f32[64,128]{1,0:T(8,128)S(1)}, u32[]{:S(2)}, u32[]{:S(2)}) collective-permute-start(f32[64,128]{1,0:T(8,128)S(1)} %get-tuple-element.48), channel_id=1, source_target_pairs={{0,24},{8,16},{16,8},{24,0},{1,25},{9,17},{17,9},{25,1},{2,26},{10... | collective-permute-start | bytes 98312 | tf_op jit(solution)/shard_map/ppermute | solution.py:430
  29.2 3.6 %collective-permute-start.8 = (f32[64,128]{1,0:T(8,128)S(1)}, f32[64,128]{1,0:T(8,128)S(1)}, u32[]{:S(2)}, u32[]{:S(2)}) collective-permute-start(f32[64,128]{1,0:T(8,128)S(1)} %get-tuple-element.48), channel_id=1, source_target_pairs={{0,8},{8,0},{16,24},{24,16},{1,9},{9,1},{17,25},{25,17},{2,10},{10... | collective-permute-start | bytes 98312 | tf_op jit(solution)/shard_map/ppermute | solution.py:430
  32.9 3.9 %collective-permute-start.10 = (f32[64,128]{1,0:T(8,128)S(1)}, f32[64,128]{1,0:T(8,128)S(1)}, u32[]{:S(2)}, u32[]{:S(2)}) collective-permute-start(f32[64,128]{1,0:T(8,128)S(1)} %get-tuple-element.50), channel_id=1, source_target_pairs={{0,1},{1,0},{2,3},{3,2},{4,5},{5,4},{6,7},{7,6},{8,9},{9,8},{10,11... | collective-permute-start | bytes 98312 | tf_op jit(solution)/shard_map/ppermute | solution.py:430
  33.1 6.6 %collective-permute-start.11 = (f32[64,128]{1,0:T(8,128)S(1)}, f32[64,128]{1,0:T(8,128)S(1)}, u32[]{:S(2)}, u32[]{:S(2)}) collective-permute-start(f32[64,128]{1,0:T(8,128)S(1)} %get-tuple-element.51), channel_id=1, source_target_pairs={{0,7},{1,2},{2,1},{3,4},{4,3},{5,6},{6,5},{7,0},{8,15},{9,10},{10,... | collective-permute-start | bytes 98312 | tf_op jit(solution)/shard_map/ppermute | solution.py:430
  40.6 3.4 %collective-permute-start.13 = (f32[64,128]{1,0:T(8,128)S(1)}, f32[64,128]{1,0:T(8,128)S(1)}, u32[]{:S(2)}, u32[]{:S(2)}) collective-permute-start(f32[64,128]{1,0:T(8,128)S(1)} %get-tuple-element.56), channel_id=1, source_target_pairs={{0,24},{8,16},{16,8},{24,0},{1,25},{9,17},{17,9},{25,1},{2,26},{10... | collective-permute-start | bytes 98312 | tf_op jit(solution)/shard_map/ppermute | solution.py:430
  40.6 3.3 %collective-permute-start.12 = (f32[64,128]{1,0:T(8,128)S(1)}, f32[64,128]{1,0:T(8,128)S(1)}, u32[]{:S(2)}, u32[]{:S(2)}) collective-permute-start(f32[64,128]{1,0:T(8,128)S(1)} %get-tuple-element.56), channel_id=1, source_target_pairs={{0,8},{8,0},{16,24},{24,16},{1,9},{9,1},{17,25},{25,17},{2,10},{10... | collective-permute-start | bytes 98312 | tf_op jit(solution)/shard_map/ppermute | solution.py:430
  44.1 13.4 %collective-permute-start.14 = (f32[64,128]{1,0:T(8,128)S(1)}, f32[64,128]{1,0:T(8,128)S(1)}, u32[]{:S(2)}, u32[]{:S(2)}) collective-permute-start(f32[64,128]{1,0:T(8,128)S(1)} %get-tuple-element.58), channel_id=1, source_target_pairs={{0,1},{1,0},{2,3},{3,2},{4,5},{5,4},{6,7},{7,6},{8,9},{9,8},{10,11... | collective-permute-start | bytes 98312 | tf_op jit(solution)/shard_map/ppermute | solution.py:430
  44.2 13.3 %collective-permute-start.15 = (f32[64,128]{1,0:T(8,128)S(1)}, f32[64,128]{1,0:T(8,128)S(1)}, u32[]{:S(2)}, u32[]{:S(2)}) collective-permute-start(f32[64,128]{1,0:T(8,128)S(1)} %get-tuple-element.59), channel_id=1, source_target_pairs={{0,7},{1,2},{2,1},{3,4},{4,3},{5,6},{6,5},{7,0},{8,15},{9,10},{10,... | collective-permute-start | bytes 98312 | tf_op jit(solution)/shard_map/ppermute | solution.py:430
  57.5 0.7 %copy-start = (s32[1,1,128]{2,1,0:T(1,128)S(1)}, s32[1,1,128]{2,1,0:T(1,128)}, u32[]{:S(2)}) copy-start(s32[1,1,128]{2,1,0:T(1,128)} %param.7) | copy-start | bytes 1540

commit v4 on v3

--- a/solution.py
+++ b/solution.py
@@ -1,5 +1,3 @@
-import functools
-
 import jax
 import jax.numpy as jnp
 import numpy as np
@@ -87,15 +85,25 @@
     return new_low, new_high
 
 
+def packed_x(grid, b):
+    return jnp.where(lane_index() < HALF, grid[row(0, b), :], grid[row(7, b), :])
+
+
 def pack_faces(grid, face_x, face_y, field):
-    first = lane_index() < HALF
     for b in range(8):
-        face_x[pl.ds(64 * field + 8 * b, 8), :] = jnp.where(
-            first, grid[row(0, b), :], grid[row(7, b), :]
-        )
+        face_x[pl.ds(64 * field + 8 * b, 8), :] = packed_x(grid, b)
     for a in range(8):
         face_y[pl.ds(128 * field + 8 * a, 8), :] = grid[row(a, 0), :]
         face_y[pl.ds(128 * field + 64 + 8 * a, 8), :] = grid[row(a, 7), :]
+
+
+def lowest_to_highest(low_side, to_even, to_odd, rows, low, high):
+    to_even[rows, :] = jnp.where(low_side, low, high)
+    to_odd[rows, :] = jnp.where(low_side, high, low)
+
+
+def is_odd(axis):
+    return lax.axis_index(axis) % 2 == 1
 
 
 def ghost_x(from_even, from_odd, field, b):
@@ -110,6 +118,12 @@
     if a == 0:
         return low + pltpu.roll(jnp.where(first, high, ghost), HALF, 1)
     return high + pltpu.roll(jnp.where(first, ghost, low), HALF, 1)
+
+
+def from_y(even_y, odd_y, b, rows):
+    odd = is_odd("yz")
+    pick = odd if b == 0 else jnp.logical_not(odd)
+    return jnp.where(pick, even_y[rows, :], odd_y[rows, :])
 
 
 def assembled(a, b, grid, received, field):
@@ -121,15 +135,13 @@
         )
     if b in (0, 7):
         rows = pl.ds(64 * field + 8 * a, 8)
-        odd = lax.axis_index("yz") % 2 == 1
-        pick = odd if b == 0 else jnp.logical_not(odd)
-        value = value + jnp.where(pick, even_y[rows, :], odd_y[rows, :])
+        value = value + from_y(even_y, odd_y, b, rows)
     return value
 
 
-def edges_kernel(fields, face_y, even_x, odd_x, to_even, to_odd):
-    odd = lax.axis_index("yz") % 2 == 1
-    for field in range(fields):
+def edges_kernel(face_y, fixed_y, even_x, odd_x, to_even, to_odd):
+    odd = is_odd("yz")
+    for field in range(2):
         faces = []
         for side in range(2):
             part = [face_y[pl.ds(128 * field + 64 * side + 8 * a, 8), :] for a in range(8)]
@@ -140,8 +152,11 @@
             faces.append(part)
         for a in range(8):
             rows = pl.ds(64 * field + 8 * a, 8)
-            to_even[rows, :] = jnp.where(odd, faces[0][a], faces[1][a])
-            to_odd[rows, :] = jnp.where(odd, faces[1][a], faces[0][a])
+            lowest_to_highest(odd, to_even, to_odd, rows, faces[0][a], faces[1][a])
+    for k in range(9):
+        rows = pl.ds(128 + 8 * k, 8)
+        low, high = fixed_y[pl.ds(8 * k, 8), :], fixed_y[pl.ds(72 + 8 * k, 8), :]
+        lowest_to_highest(odd, to_even, to_odd, rows, low, high)
 
 
 def selection(slots):
@@ -168,8 +183,8 @@
 
 
 def setup_kernel(
-    slots, forcing, viscosity, mass_rate, right, diagonal, spread, mass, face_x, face_y,
-    order, held, arrived,
+    slots, forcing, viscosity, mass_rate,
+    right, diagonal, spread, mass, face_x, face_y, fixed_y, shifts, order, held, arrived,
 ):
     ordered = pltpu.make_async_copy(slots, order, arrived.at[3])
     copies = [
@@ -215,9 +230,91 @@
         right[across(a, 7), :] = high
     pack_faces(right, face_x, face_y, 0)
     pack_faces(diagonal, face_x, face_y, 1)
-
-
-def operate(values, spread, mass, image, face_x, face_y):
+    for b in range(8):
+        face_x[pl.ds(128 + 8 * b, 8), :] = packed_x(spread, b)
+    for side in range(2):
+        for a in range(8):
+            fixed_y[pl.ds(72 * side + 8 * a, 8), :] = spread[row(a, 7 * side), :]
+        fixed_y[pl.ds(72 * side + 64, 8), :] = packed_x(mass, 7 * side)
+    for k in range(8):
+        along_shift = back_shift = jnp.zeros((8, LANES), jnp.float32)
+        for c in range(8):
+            other = (c + k) % 8
+            along_shift = jnp.where(point == c, float(DERIVATIVE[c, other]), along_shift)
+            back_shift = jnp.where(
+                point == c, float(VERTICAL * DERIVATIVE[other, c]), back_shift
+            )
+        shifts[pl.ds(8 * k, 8), :] = along_shift
+        shifts[pl.ds(64 + 8 * k, 8), :] = back_shift
+
+
+def join_vertical_packed(value):
+    layer, point = lane_index() % EZ, sublane_index()
+    from_below = pltpu.roll(pltpu.roll(value, 1, 0), 1, 1)
+    from_above = pltpu.roll(pltpu.roll(value, 7, 0), LANES - 1, 1)
+    below = jnp.logical_and(point == 0, layer > 0)
+    above = jnp.logical_and(point == 7, layer < EZ - 1)
+    return value + jnp.where(below, from_below, jnp.where(above, from_above, 0.0))
+
+
+def shifted_sum(shifts, start, value):
+    total = shifts[pl.ds(start, 8), :] * value
+    for k in range(1, 8):
+        total = total + shifts[pl.ds(start + 8 * k, 8), :] * pltpu.roll(value, 8 - k, 0)
+    return total
+
+
+def end_row(lines, end):
+    total = None
+    for q in range(8):
+        term = lines[q] * float(DERIVATIVE[q, end])
+        total = term if total is None else total + term
+    return total
+
+
+def corner_shares(values, outer, shifts):
+    first = lane_index() < HALF
+    lines = [packed_x(values, b) for b in range(8)]
+    slopes = along(DERIVATIVE, lines, -1)
+    slopes = [slopes[q] * outer[pl.ds(8 * q, 8), :] for q in range(8)]
+    for_y = [end_row(slopes, 0), end_row(slopes, 7)]
+    for_x = []
+    for side in range(2):
+        base = 64 + 72 * side
+        spread = [outer[pl.ds(base + 8 * a, 8), :] for a in range(8)]
+        slopes = along(DERIVATIVE, [values[row(a, 7 * side), :] for a in range(8)], -1)
+        slopes = [slopes[q] * spread[q] for q in range(8)]
+        share = jnp.where(first, end_row(slopes, 0), end_row(slopes, 7))
+        corner = lines[7 * side]
+        slope = shifted_sum(shifts, 0, corner) * jnp.where(first, spread[0], spread[7])
+        share = share + shifted_sum(shifts, 64, slope) + outer[pl.ds(base + 64, 8), :] * corner
+        for_x.append(share)
+    return [join_vertical_packed(share) for share in for_x], [
+        join_vertical_packed(share) for share in for_y
+    ]
+
+
+def send_faces(image, values, outer, shifts, face_x, to_even, to_odd):
+    for_x, for_y = corner_shares(values, outer, shifts)
+    first = lane_index() < HALF
+    odd = is_odd("yz")
+    for b in range(8):
+        face = packed_x(image, b)
+        if b in (0, 7):
+            face = face + for_x[b // 7]
+        face_x[pl.ds(8 * b, 8), :] = face
+    faces = []
+    for side in range(2):
+        part = [image[row(a, 7 * side), :] for a in range(8)]
+        low, high = part[0], part[7]
+        part[0] = low + jnp.where(first, for_y[side], pltpu.roll(high, HALF, 1))
+        part[7] = high + jnp.where(first, pltpu.roll(low, HALF, 1), for_y[side])
+        faces.append(part)
+    for a in range(8):
+        lowest_to_highest(odd, to_even, to_odd, pl.ds(8 * a, 8), faces[0][a], faces[1][a])
+
+
+def operate(values, spread, mass, image):
     forward, backward = DERIVATIVE, DERIVATIVE.T
     for b in range(8):
         lines = [values[row(a, b), :] for a in range(8)]
@@ -243,7 +340,6 @@
         back[0], back[7] = join_vertical(back[0], back[7])
         for c in range(8):
             image[across(a, c), :] = back[c]
-    pack_faces(image, face_x, face_y, 0)
     return energy
 
 
@@ -260,8 +356,8 @@
 
 
 def first_kernel(
-    right, diagonal, even_x, odd_x, even_y, odd_y, spread, mass,
-    whole_diagonal, values, image, face_x, face_y, moments,
+    right, diagonal, even_x, odd_x, even_y, odd_y, spread, mass, shifts,
+    whole_diagonal, values, image, outer, face_x, to_even, to_odd, moments,
 ):
     received = (even_x, odd_x, even_y, odd_y)
     sums = [jnp.zeros((8, LANES), jnp.float32)] * 3
@@ -274,7 +370,15 @@
             values[row(a, b), :] = value
             sums[ends(a, b)] = sums[ends(a, b)] + source * value
     moments[...] = weighted(sums)
-    operate(values, spread, mass, image, face_x, face_y)
+    for b in range(8):
+        outer[pl.ds(8 * b, 8), :] = pltpu.roll(ghost_x(even_x, odd_x, 2, b), HALF, 1)
+    for side in range(2):
+        for k in range(9):
+            outer[pl.ds(64 + 72 * side + 8 * k, 8), :] = from_y(
+                even_y, odd_y, 7 * side, pl.ds(128 + 8 * k, 8)
+            )
+    operate(values, spread, mass, image)
+    send_faces(image, values, outer, shifts, face_x, to_even, to_odd)
 
 
 def next_values(before_image, received, diagonal, before, values):
@@ -294,23 +398,25 @@
 
 
 def second_kernel(
-    before_image, even_x, odd_x, even_y, odd_y, diagonal, before, spread, mass,
-    values, image, face_x, face_y, moments,
+    before_image, even_x, odd_x, even_y, odd_y, diagonal, before, spread, mass, shifts, outer,
+    values, image, face_x, to_even, to_odd, moments,
 ):
     received = (even_x, odd_x, even_y, odd_y)
     cross, square = next_values(before_image, received, diagonal, before, values)
     moments[pl.ds(0, 8), :] = cross
     moments[pl.ds(8, 8), :] = square
-    operate(values, spread, mass, image, face_x, face_y)
+    operate(values, spread, mass, image)
+    send_faces(image, values, outer, shifts, face_x, to_even, to_odd)
 
 
 def third_kernel(
-    before_image, even_x, odd_x, even_y, odd_y, diagonal, before, spread, mass, moments0, moments1,
-    values, image, face_x, face_y, sums,
+    before_image, even_x, odd_x, even_y, odd_y, diagonal, before, spread, mass, shifts, outer,
+    moments0, moments1, values, image, face_x, to_even, to_odd, sums,
 ):
     received = (even_x, odd_x, even_y, odd_y)
     cross, square = next_values(before_image, received, diagonal, before, values)
-    energy = operate(values, spread, mass, image, face_x, face_y)
+    energy = operate(values, spread, mass, image)
+    send_faces(image, values, outer, shifts, face_x, to_even, to_odd)
     parts = [
         moments0[...], moments1[pl.ds(0, 8), :], moments1[pl.ds(8, 8), :], cross, square, energy
     ]
@@ -430,22 +536,13 @@
     return lax.ppermute(block[0], axis, even), lax.ppermute(block[1], axis, odd)
 
 
-def exchange(fields, face_x, face_y):
-    received_x = swapped((face_x, face_x), "gx")
-    shape = (64 * fields, LANES)
-    sent_y = call(
-        functools.partial(edges_kernel, fields), "edges", [shape, shape], [], face_y, *received_x
-    )
-    return (*received_x, *swapped(sent_y, "yz"))
-
-
 def body(forcing, viscosity, mass_rate, slot_element):
     devices = lax.axis_size("gx") * lax.axis_size("yz")
     slots = slot_element[0]
-    grid = (POINTS, LANES)
-    face_x, face_y, moment = (64, LANES), (128, LANES), (8, LANES)
-    right, diagonal, spread, mass, out_x, out_y = call(
-        setup_kernel, "setup", [grid] * 4 + [(128, LANES), (256, LANES)],
+    grid, face, tile = (POINTS, LANES), (64, LANES), (8, LANES)
+    right, diagonal, spread, mass, out_x, out_y, fixed_y, shifts = call(
+        setup_kernel, "setup",
+        [grid] * 4 + [(192, LANES), (256, LANES), (144, LANES), (128, LANES)],
         [
             pltpu.VMEM((1, LANES), jnp.int32),
             pltpu.VMEM((3, LANES, POINTS), jnp.float32),
@@ -453,23 +550,27 @@
         ],
         slots, forcing, viscosity, mass_rate, outside=4,
     )
-    received = exchange(2, out_x, out_y)
-    diagonal, values0, image, out_x, out_y, moments0 = call(
-        first_kernel, "first", [grid] * 3 + [face_x, face_y, moment], [],
-        right, diagonal, *received, spread, mass,
-    )
-    received = exchange(1, out_x, out_y)
-    values1, image, out_x, out_y, moments1 = call(
-        second_kernel, "second", [grid] * 2 + [face_x, face_y, (16, LANES)], [],
-        image, *received, diagonal, values0, spread, mass,
-    )
-    received = exchange(1, out_x, out_y)
-    values2, image, out_x, out_y, sums = call(
-        third_kernel, "third", [grid] * 2 + [face_x, face_y, (devices, 1, LANES)], [],
-        image, *received, diagonal, values1, spread, mass, moments0, moments1,
+    received_x = swapped((out_x, out_x), "gx")
+    sent_y = call(
+        edges_kernel, "edges", [(200, LANES)] * 2, [], out_y, fixed_y, *received_x
+    )
+    received_y = swapped(sent_y, "yz")
+    diagonal, values0, image, outer, out_x, *sent_y, moments0 = call(
+        first_kernel, "first", [grid] * 3 + [(208, LANES)] + [face] * 3 + [tile], [],
+        right, diagonal, *received_x, *received_y, spread, mass, shifts,
+    )
+    received = (*swapped((out_x, out_x), "gx"), *swapped(sent_y, "yz"))
+    values1, image, out_x, *sent_y, moments1 = call(
+        second_kernel, "second", [grid] * 2 + [face] * 3 + [(16, LANES)], [],
+        image, *received, diagonal, values0, spread, mass, shifts, outer,
+    )
+    received = (*swapped((out_x, out_x), "gx"), *swapped(sent_y, "yz"))
+    values2, image, out_x, *sent_y, sums = call(
+        third_kernel, "third", [grid] * 2 + [face] * 3 + [(devices, 1, LANES)], [],
+        image, *received, diagonal, values1, spread, mass, shifts, outer, moments0, moments1,
     )
     sums = lax.all_to_all(sums, ("gx", "yz"), 0, 0)
-    received = exchange(1, out_x, out_y)
+    received = (*swapped((out_x, out_x), "gx"), *swapped(sent_y, "yz"))
     return call(
         last_kernel, "last", [forcing.shape] * 2, [pltpu.VMEM(grid, jnp.float32)] * 2,
         image, *received, diagonal, values0, values1, values2, sums, slots,

time: 59.6 us -> 51.4 us (0.86)
  waiting for transfers between devices: 17.4 us -> 10 us
    ppermute x8, waiting for transfers between devices: 16.9 us -> 8.97 us  [swapped(): lax.ppermute(block[1], axis, odd)]
    ppermute x8, starting transfers between devices: 17 us -> 15.9 us  [swapped(): lax.ppermute(block[1], axis, odd)]
    ppermute x8, starting transfers between devices: 7.66 us -> 8.42 us  [swapped(): lax.ppermute(block[0], axis, even)]
    pallas_call x9 -> x6, Pallas kernels: 6.26 us -> 6.24 us  [call(): pl.pallas_call(kernel, out_shape=[jax.ShapeDtypeStruct(shape, jnp.float32...]
  transfers between devices with their start and end apart: 16 -> 16, of which waited for: 9 -> 7; matrix products, arithmetic and copies ran while one was open for 0% -> 0% of each run, Pallas kernels for 0% -> 0%
where the time goes in v4:
time: 51.4 us; the launch traced here: 51.2 us
  starting transfers between devices  24.4 us (47%)
  waiting for transfers between devices  10 us (19%)
  blocking collectives  9.23 us (18%)
  Pallas kernels  6.24 us (12%)
  between operations  0.7 us (1%)
  local copies, waits for them, and re-layouts  0.65 us (1%)
    ppermute x8, starting transfers between devices, swapped(): lax.ppermute(block[1], axis, odd)  15.9 us
    all_to_all x1, blocking collectives, body(): sums = lax.all_to_all(sums, ('gx', 'yz'), 0, 0)  9.23 us
    ppermute x8, waiting for transfers between devices, swapped(): lax.ppermute(block[1], axis, odd)  8.97 us
    ppermute x8, starting transfers between devices, swapped(): lax.ppermute(block[0], axis, even)  8.42 us
    pallas_call x6, Pallas kernels, call(): pl.pallas_call(kernel, out_shape=[jax.ShapeDtypeStruct(shape, jnp.float32...  6.24 us
    ppermute x8, waiting for transfers between devices, swapped(): lax.ppermute(block[0], axis, even)  1.06 us
  transfers between devices with their start and end apart: 16, of which 7 were waited for; matrix products, arithmetic and copies ran while one was open for 0% of the time, Pallas kernels for 0%

profile of v4, /device:TPU:0, one launch (start us, length us, event | category | flops | bytes accessed | tf_op | source)
XLA Modules:
  0.0 51.2 jit_solution(18115993916283856961)
XLA Ops:
  0.6 2.2 %setup.1 = (f32[512,128]{1,0:T(8,128)S(1)}, f32[512,128]{1,0:T(8,128)S(1)}, f32[512,128]{1,0:T(8,128)S(1)}, f32[512,128]{1,0:T(8,128)S(1)}, f32[192,128]{1,0:T(8...) custom-call(s32[1,128]{1,0:T(1,128)} %bitcast.1, f32[1,1,128,512]{3,2,1,0:T(8,128)} %forcing.1, ...), custom_call_target="tpu_custom_call" | custom-call | tf_op jit(solution)/shard_map/setup/pallas_call | solution.py:521
  2.8 2.5 %collective-permute-start.1 = (f32[192,128]{1,0:T(8,128)S(1)}, f32[192,128]{1,0:T(8,128)S(1)}, u32[]{:S(2)}, u32[]{:S(2)}) collective-permute-start(f32[192,128]{1,0:T(8,128)S(1)} %get-tuple-element.34), channel_id=1, source_target_pairs={{0,24},{8,16},{16,8},{24,0},{1,25},{9,17},{17,9},{25,1},{2,26},{10... | collective-permute-start | bytes 294920 | tf_op jit(solution)/shard_map/ppermute | solution.py:536
  5.3 0.7 %collective-permute-start = (f32[192,128]{1,0:T(8,128)S(1)}, f32[192,128]{1,0:T(8,128)S(1)}, u32[]{:S(2)}, u32[]{:S(2)}) collective-permute-start(f32[192,128]{1,0:T(8,128)S(1)} %get-tuple-element.34), channel_id=1, source_target_pairs={{0,8},{8,0},{16,24},{24,16},{1,9},{9,1},{17,25},{25,17},{2,10},{10... | collective-permute-start | bytes 294920 | tf_op jit(solution)/shard_map/ppermute | solution.py:536
  6.0 2.5 %collective-permute-done.1.odd_x = f32[192,128]{1,0:T(8,128)S(1)} collective-permute-done((f32[192,128]{1,0:T(8,128)S(1)}, f32[192,128]{1,0:T(8,128)S(1)}, u32[]{:S(2)}, u32[]{:S(2)}) %collective-permute-start.1) | collective-permute-done | bytes 98336 | tf_op jit(solution)/shard_map/ppermute | solution.py:536
  8.5 0.0 collective-permute-done.even_x
  8.5 0.1 edges.1
  8.6 2.4 %collective-permute-start.2 = (f32[200,128]{1,0:T(8,128)S(1)}, f32[200,128]{1,0:T(8,128)S(1)}, u32[]{:S(2)}, u32[]{:S(2)}) collective-permute-start(f32[200,128]{1,0:T(8,128)S(1)} %get-tuple-element.37), channel_id=1, source_target_pairs={{0,1},{1,0},{2,3},{3,2},{4,5},{5,4},{6,7},{7,6},{8,9},{9,8},{10,11... | collective-permute-start | bytes 307208 | tf_op jit(solution)/shard_map/ppermute | solution.py:536
  11.0 3.6 %collective-permute-start.3 = (f32[200,128]{1,0:T(8,128)S(1)}, f32[200,128]{1,0:T(8,128)S(1)}, u32[]{:S(2)}, u32[]{:S(2)}) collective-permute-start(f32[200,128]{1,0:T(8,128)S(1)} %get-tuple-element.38), channel_id=1, source_target_pairs={{0,7},{1,2},{2,1},{3,4},{4,3},{5,6},{6,5},{7,0},{8,15},{9,10},{10,... | collective-permute-start | bytes 307208 | tf_op jit(solution)/shard_map/ppermute | solution.py:536
  14.5 1.0 %collective-permute-done.2.even_y = f32[200,128]{1,0:T(8,128)S(1)} collective-permute-done((f32[200,128]{1,0:T(8,128)S(1)}, f32[200,128]{1,0:T(8,128)S(1)}, u32[]{:S(2)}, u32[]{:S(2)}) %collective-permute-start.2) | collective-permute-done | bytes 102432 | tf_op jit(solution)/shard_map/ppermute | solution.py:536
  15.6 2.7 %collective-permute-done.3.odd_y = f32[200,128]{1,0:T(8,128)S(1)} collective-permute-done((f32[200,128]{1,0:T(8,128)S(1)}, f32[200,128]{1,0:T(8,128)S(1)}, u32[]{:S(2)}, u32[]{:S(2)}) %collective-permute-start.3) | collective-permute-done | bytes 102432 | tf_op jit(solution)/shard_map/ppermute | solution.py:536
  18.3 0.9 %first.1 = (f32[512,128]{1,0:T(8,128)S(1)}, f32[512,128]{1,0:T(8,128)S(1)}, f32[512,128]{1,0:T(8,128)S(1)}, f32[208,128]{1,0:T(8,128)S(1)}, f32[64,128]{1,0:T(8,...) custom-call(f32[512,128]{1,0:T(8,128)S(1)} %get-tuple-element.32.right, ...), custom_call_target="tpu_custom_call" | custom-call | tf_op jit(solution)/shard_map/first/pallas_call | solution.py:521
  19.2 0.1 collective-permute-start.6
  19.3 3.6 %collective-permute-start.7 = (f32[64,128]{1,0:T(8,128)S(1)}, f32[64,128]{1,0:T(8,128)S(1)}, u32[]{:S(2)}, u32[]{:S(2)}) collective-permute-start(f32[64,128]{1,0:T(8,128)S(1)} %get-tuple-element.45), channel_id=1, source_target_pairs={{0,7},{1,2},{2,1},{3,4},{4,3},{5,6},{6,5},{7,0},{8,15},{9,10},{10,... | collective-permute-start | bytes 98312 | tf_op jit(solution)/shard_map/ppermute | solution.py:536
  22.9 0.0 collective-permute-start.5
  22.9 1.7 %collective-permute-start.4 = (f32[64,128]{1,0:T(8,128)S(1)}, f32[64,128]{1,0:T(8,128)S(1)}, u32[]{:S(2)}, u32[]{:S(2)}) collective-permute-start(f32[64,128]{1,0:T(8,128)S(1)} %get-tuple-element.43), channel_id=1, source_target_pairs={{0,8},{8,0},{16,24},{24,16},{1,9},{9,1},{17,25},{25,17},{2,10},{10... | collective-permute-start | bytes 98312 | tf_op jit(solution)/shard_map/ppermute | solution.py:536
  24.6 0.0 collective-permute-done.6.even_y
  24.6 1.3 %collective-permute-done.7.odd_y = f32[64,128]{1,0:T(8,128)S(1)} collective-permute-done((f32[64,128]{1,0:T(8,128)S(1)}, f32[64,128]{1,0:T(8,128)S(1)}, u32[]{:S(2)}, u32[]{:S(2)}) %collective-permute-start.7) | collective-permute-done | bytes 32800 | tf_op jit(solution)/shard_map/ppermute | solution.py:536
  25.9 0.5 %collective-permute-done.5.odd_x = f32[64,128]{1,0:T(8,128)S(1)} collective-permute-done((f32[64,128]{1,0:T(8,128)S(1)}, f32[64,128]{1,0:T(8,128)S(1)}, u32[]{:S(2)}, u32[]{:S(2)}) %collective-permute-start.5) | collective-permute-done | bytes 32800 | tf_op jit(solution)/shard_map/ppermute | solution.py:536
  26.5 0.0 collective-permute-done.4.even_x
  26.5 0.8 %second.1 = (f32[512,128]{1,0:T(8,128)S(1)}, f32[512,128]{1,0:T(8,128)S(1)}, f32[64,128]{1,0:T(8,128)S(1)}, f32[64,128]{1,0:T(8,128)S(1)}, f32[64,128]{1,0:T(8,128)S(1)}, /*index=5*/f32[16,128]{1,0:T(8,128)S(1)}) custom-call(f32[512,128]{1,0:T(8,128)S(1)} %get-tuple-element.42.before_image, f32[64,128]{1,0:T(8,128)S(1)} %collective-permute-done.4.even_x, ...), custom_call_target="tpu_custom_call" | custom-call | tf_op jit(solution)/shard_map/second/pallas_call | solution.py:521
  27.3 0.1 collective-permute-start.10
  27.4 3.2 %collective-permute-start.11 = (f32[64,128]{1,0:T(8,128)S(1)}, f32[64,128]{1,0:T(8,128)S(1)}, u32[]{:S(2)}, u32[]{:S(2)}) collective-permute-start(f32[64,128]{1,0:T(8,128)S(1)} %get-tuple-element.52), channel_id=1, source_target_pairs={{0,7},{1,2},{2,1},{3,4},{4,3},{5,6},{6,5},{7,0},{8,15},{9,10},{10,... | collective-permute-start | bytes 98312 | tf_op jit(solution)/shard_map/ppermute | solution.py:536
  30.6 0.0 collective-permute-start.9
  30.6 1.7 %collective-permute-start.8 = (f32[64,128]{1,0:T(8,128)S(1)}, f32[64,128]{1,0:T(8,128)S(1)}, u32[]{:S(2)}, u32[]{:S(2)}) collective-permute-start(f32[64,128]{1,0:T(8,128)S(1)} %get-tuple-element.50), channel_id=1, source_target_pairs={{0,8},{8,0},{16,24},{24,16},{1,9},{9,1},{17,25},{25,17},{2,10},{10... | collective-permute-start | bytes 98312 | tf_op jit(solution)/shard_map/ppermute | solution.py:536
  32.3 0.0 collective-permute-done.10.even_y
  32.3 1.8 %collective-permute-done.11.odd_y = f32[64,128]{1,0:T(8,128)S(1)} collective-permute-done((f32[64,128]{1,0:T(8,128)S(1)}, f32[64,128]{1,0:T(8,128)S(1)}, u32[]{:S(2)}, u32[]{:S(2)}) %collective-permute-start.11) | collective-permute-done | bytes 32800 | tf_op jit(solution)/shard_map/ppermute | solution.py:536
  34.1 0.1 collective-permute-done.9.odd_x
  34.1 0.0 collective-permute-done.8.even_x
  34.1 0.9 %third.1 = (f32[512,128]{1,0:T(8,128)S(1)}, f32[512,128]{1,0:T(8,128)S(1)}, f32[64,128]{1,0:T(8,128)S(1)}, f32[64,128]{1,0:T(8,128)S(1)}, f32[64,128]{1,0:T(8,128)S(1)}, /*index=5*/f32[32,1,128]{2,1,0:T(1,128)S(1)}) custom-call(f32[512,128]{1,0:T(8,128)S(1)} %get-tuple-element.49.before_image, f32[64,128]{1,0:T(8,128)S(1)} %collective-permute-done.8.even_x, ...), custom_call_target="tpu_custom_call" | custom-call | tf_op jit(solution)/shard_map/third/pallas_call | solution.py:521
  35.1 0.1 collective-permute-start.14
  35.2 3.1 %collective-permute-start.15 = (f32[64,128]{1,0:T(8,128)S(1)}, f32[64,128]{1,0:T(8,128)S(1)}, u32[]{:S(2)}, u32[]{:S(2)}) collective-permute-start(f32[64,128]{1,0:T(8,128)S(1)} %get-tuple-element.59), channel_id=1, source_target_pairs={{0,7},{1,2},{2,1},{3,4},{4,3},{5,6},{6,5},{7,0},{8,15},{9,10},{10,... | collective-permute-start | bytes 98312 | tf_op jit(solution)/shard_map/ppermute | solution.py:536
  38.3 0.0 collective-permute-start.13
  38.3 1.7 %collective-permute-start.12 = (f32[64,128]{1,0:T(8,128)S(1)}, f32[64,128]{1,0:T(8,128)S(1)}, u32[]{:S(2)}, u32[]{:S(2)}) collective-permute-start(f32[64,128]{1,0:T(8,128)S(1)} %get-tuple-element.57), channel_id=1, source_target_pairs={{0,8},{8,0},{16,24},{24,16},{1,9},{9,1},{17,25},{25,17},{2,10},{10... | collective-permute-start | bytes 98312 | tf_op jit(solution)/shard_map/ppermute | solution.py:536
  40.0 9.2 %all_to_all.5.sums = f32[32,1,128]{2,1,0:T(1,128)S(1)} all-to-all(f32[32,1,128]{2,1,0:T(1,128)S(1)} %get-tuple-element.61), channel_id=1, replica_groups=mesh['gx'=4,'yz'=8] {'gx','yz'}, dimensions={0} | all-to-all | bytes 32768 | tf_op jit(solution)/shard_map/all_to_all | solution.py:572
  49.2 0.0 collective-permute-done.14.even_y
  49.2 0.0 collective-permute-done.15.odd_y
  49.2 0.0 collective-permute-done.13.odd_x
  49.2 0.0 collective-permute-done.12.even_x
  49.2 0.0 copy-start
  49.2 0.6 %copy-done = s32[1,1,128]{2,1,0:T(1,128)S(1)} copy-done((s32[1,1,128]{2,1,0:T(1,128)S(1)}, s32[1,1,128]{2,1,0:T(1,128)}, u32[]{:S(2)}) %copy-start) | copy-done | bytes 536
  49.9 1.3 %last.1 = (f32[1,1,128,512]{3,2,1,0:T(8,128)}, f32[1,1,128,512]{3,2,1,0:T(8,128)}) custom-call(f32[512,128]{1,0:T(8,128)S(1)} %get-tuple-element.56.before_image, f32[64,128]{1,0:T(8,128)S(1)} %collective-permute-done.12.even_x, f32[64,128]{1,0:T(8,128)S(1)} %collective-permute-done.13.odd_x, f32[64,128]{1,0:T(8,128)S(1)} %collective-permute-done.14.even_y, ...), custom_call_target="tpu_custom_call" | custom-call | tf_op jit(solution)/shard_map/last/pallas_call | solution.py:521
Async XLA Ops:
  2.8 5.7 %collective-permute-start.1 = (f32[192,128]{1,0:T(8,128)S(1)}, f32[192,128]{1,0:T(8,128)S(1)}, u32[]{:S(2)}, u32[]{:S(2)}) collective-permute-start(f32[192,128]{1,0:T(8,128)S(1)} %get-tuple-element.34), channel_id=1, source_target_pairs={{0,24},{8,16},{16,8},{24,0},{1,25},{9,17},{17,9},{25,1},{2,26},{10... | collective-permute-start | bytes 294920 | tf_op jit(solution)/shard_map/ppermute | solution.py:536
  5.3 3.2 %collective-permute-start = (f32[192,128]{1,0:T(8,128)S(1)}, f32[192,128]{1,0:T(8,128)S(1)}, u32[]{:S(2)}, u32[]{:S(2)}) collective-permute-start(f32[192,128]{1,0:T(8,128)S(1)} %get-tuple-element.34), channel_id=1, source_target_pairs={{0,8},{8,0},{16,24},{24,16},{1,9},{9,1},{17,25},{25,17},{2,10},{10... | collective-permute-start | bytes 294920 | tf_op jit(solution)/shard_map/ppermute | solution.py:536
  8.6 7.0 %collective-permute-start.2 = (f32[200,128]{1,0:T(8,128)S(1)}, f32[200,128]{1,0:T(8,128)S(1)}, u32[]{:S(2)}, u32[]{:S(2)}) collective-permute-start(f32[200,128]{1,0:T(8,128)S(1)} %get-tuple-element.37), channel_id=1, source_target_pairs={{0,1},{1,0},{2,3},{3,2},{4,5},{5,4},{6,7},{7,6},{8,9},{9,8},{10,11... | collective-permute-start | bytes 307208 | tf_op jit(solution)/shard_map/ppermute | solution.py:536
  11.0 7.4 %collective-permute-start.3 = (f32[200,128]{1,0:T(8,128)S(1)}, f32[200,128]{1,0:T(8,128)S(1)}, u32[]{:S(2)}, u32[]{:S(2)}) collective-permute-start(f32[200,128]{1,0:T(8,128)S(1)} %get-tuple-element.38), channel_id=1, source_target_pairs={{0,7},{1,2},{2,1},{3,4},{4,3},{5,6},{6,5},{7,0},{8,15},{9,10},{10,... | collective-permute-start | bytes 307208 | tf_op jit(solution)/shard_map/ppermute | solution.py:536
  19.2 5.4 %collective-permute-start.6 = (f32[64,128]{1,0:T(8,128)S(1)}, f32[64,128]{1,0:T(8,128)S(1)}, u32[]{:S(2)}, u32[]{:S(2)}) collective-permute-start(f32[64,128]{1,0:T(8,128)S(1)} %get-tuple-element.44), channel_id=1, source_target_pairs={{0,1},{1,0},{2,3},{3,2},{4,5},{5,4},{6,7},{7,6},{8,9},{9,8},{10,11... | collective-permute-start | bytes 98312 | tf_op jit(solution)/shard_map/ppermute | solution.py:536
  19.3 6.7 %collective-permute-start.7 = (f32[64,128]{1,0:T(8,128)S(1)}, f32[64,128]{1,0:T(8,128)S(1)}, u32[]{:S(2)}, u32[]{:S(2)}) collective-permute-start(f32[64,128]{1,0:T(8,128)S(1)} %get-tuple-element.45), channel_id=1, source_target_pairs={{0,7},{1,2},{2,1},{3,4},{4,3},{5,6},{6,5},{7,0},{8,15},{9,10},{10,... | collective-permute-start | bytes 98312 | tf_op jit(solution)/shard_map/ppermute | solution.py:536
  22.9 3.6 %collective-permute-start.5 = (f32[64,128]{1,0:T(8,128)S(1)}, f32[64,128]{1,0:T(8,128)S(1)}, u32[]{:S(2)}, u32[]{:S(2)}) collective-permute-start(f32[64,128]{1,0:T(8,128)S(1)} %get-tuple-element.43), channel_id=1, source_target_pairs={{0,24},{8,16},{16,8},{24,0},{1,25},{9,17},{17,9},{25,1},{2,26},{10... | collective-permute-start | bytes 98312 | tf_op jit(solution)/shard_map/ppermute | solution.py:536
  22.9 3.6 %collective-permute-start.4 = (f32[64,128]{1,0:T(8,128)S(1)}, f32[64,128]{1,0:T(8,128)S(1)}, u32[]{:S(2)}, u32[]{:S(2)}) collective-permute-start(f32[64,128]{1,0:T(8,128)S(1)} %get-tuple-element.43), channel_id=1, source_target_pairs={{0,8},{8,0},{16,24},{24,16},{1,9},{9,1},{17,25},{25,17},{2,10},{10... | collective-permute-start | bytes 98312 | tf_op jit(solution)/shard_map/ppermute | solution.py:536
  27.3 5.0 %collective-permute-start.10 = (f32[64,128]{1,0:T(8,128)S(1)}, f32[64,128]{1,0:T(8,128)S(1)}, u32[]{:S(2)}, u32[]{:S(2)}) collective-permute-start(f32[64,128]{1,0:T(8,128)S(1)} %get-tuple-element.51), channel_id=1, source_target_pairs={{0,1},{1,0},{2,3},{3,2},{4,5},{5,4},{6,7},{7,6},{8,9},{9,8},{10,11... | collective-permute-start | bytes 98312 | tf_op jit(solution)/shard_map/ppermute | solution.py:536
  27.4 6.7 %collective-permute-start.11 = (f32[64,128]{1,0:T(8,128)S(1)}, f32[64,128]{1,0:T(8,128)S(1)}, u32[]{:S(2)}, u32[]{:S(2)}) collective-permute-start(f32[64,128]{1,0:T(8,128)S(1)} %get-tuple-element.52), channel_id=1, source_target_pairs={{0,7},{1,2},{2,1},{3,4},{4,3},{5,6},{6,5},{7,0},{8,15},{9,10},{10,... | collective-permute-start | bytes 98312 | tf_op jit(solution)/shard_map/ppermute | solution.py:536
  30.6 3.6 %collective-permute-start.9 = (f32[64,128]{1,0:T(8,128)S(1)}, f32[64,128]{1,0:T(8,128)S(1)}, u32[]{:S(2)}, u32[]{:S(2)}) collective-permute-start(f32[64,128]{1,0:T(8,128)S(1)} %get-tuple-element.50), channel_id=1, source_target_pairs={{0,24},{8,16},{16,8},{24,0},{1,25},{9,17},{17,9},{25,1},{2,26},{10... | collective-permute-start | bytes 98312 | tf_op jit(solution)/shard_map/ppermute | solution.py:536
  30.6 3.6 %collective-permute-start.8 = (f32[64,128]{1,0:T(8,128)S(1)}, f32[64,128]{1,0:T(8,128)S(1)}, u32[]{:S(2)}, u32[]{:S(2)}) collective-permute-start(f32[64,128]{1,0:T(8,128)S(1)} %get-tuple-element.50), channel_id=1, source_target_pairs={{0,8},{8,0},{16,24},{24,16},{1,9},{9,1},{17,25},{25,17},{2,10},{10... | collective-permute-start | bytes 98312 | tf_op jit(solution)/shard_map/ppermute | solution.py:536
  35.1 14.1 %collective-permute-start.14 = (f32[64,128]{1,0:T(8,128)S(1)}, f32[64,128]{1,0:T(8,128)S(1)}, u32[]{:S(2)}, u32[]{:S(2)}) collective-permute-start(f32[64,128]{1,0:T(8,128)S(1)} %get-tuple-element.58), channel_id=1, source_target_pairs={{0,1},{1,0},{2,3},{3,2},{4,5},{5,4},{6,7},{7,6},{8,9},{9,8},{10,11... | collective-permute-start | bytes 98312 | tf_op jit(solution)/shard_map/ppermute | solution.py:536
  35.2 14.0 %collective-permute-start.15 = (f32[64,128]{1,0:T(8,128)S(1)}, f32[64,128]{1,0:T(8,128)S(1)}, u32[]{:S(2)}, u32[]{:S(2)}) collective-permute-start(f32[64,128]{1,0:T(8,128)S(1)} %get-tuple-element.59), channel_id=1, source_target_pairs={{0,7},{1,2},{2,1},{3,4},{4,3},{5,6},{6,5},{7,0},{8,15},{9,10},{10,... | collective-permute-start | bytes 98312 | tf_op jit(solution)/shard_map/ppermute | solution.py:536
  38.3 10.9 %collective-permute-start.13 = (f32[64,128]{1,0:T(8,128)S(1)}, f32[64,128]{1,0:T(8,128)S(1)}, u32[]{:S(2)}, u32[]{:S(2)}) collective-permute-start(f32[64,128]{1,0:T(8,128)S(1)} %get-tuple-element.57), channel_id=1, source_target_pairs={{0,24},{8,16},{16,8},{24,0},{1,25},{9,17},{17,9},{25,1},{2,26},{10... | collective-permute-start | bytes 98312 | tf_op jit(solution)/shard_map/ppermute | solution.py:536
  38.3 10.9 %collective-permute-start.12 = (f32[64,128]{1,0:T(8,128)S(1)}, f32[64,128]{1,0:T(8,128)S(1)}, u32[]{:S(2)}, u32[]{:S(2)}) collective-permute-start(f32[64,128]{1,0:T(8,128)S(1)} %get-tuple-element.57), channel_id=1, source_target_pairs={{0,8},{8,0},{16,24},{24,16},{1,9},{9,1},{17,25},{25,17},{2,10},{10... | collective-permute-start | bytes 98312 | tf_op jit(solution)/shard_map/ppermute | solution.py:536
  49.2 0.7 %copy-start = (s32[1,1,128]{2,1,0:T(1,128)S(1)}, s32[1,1,128]{2,1,0:T(1,128)}, u32[]{:S(2)}) copy-start(s32[1,1,128]{2,1,0:T(1,128)} %param.7) | copy-start | bytes 1540

commit v5 on v4

--- a/solution.py
+++ b/solution.py
@@ -89,14 +89,6 @@
     return jnp.where(lane_index() < HALF, grid[row(0, b), :], grid[row(7, b), :])
 
 
-def pack_faces(grid, face_x, face_y, field):
-    for b in range(8):
-        face_x[pl.ds(64 * field + 8 * b, 8), :] = packed_x(grid, b)
-    for a in range(8):
-        face_y[pl.ds(128 * field + 8 * a, 8), :] = grid[row(a, 0), :]
-        face_y[pl.ds(128 * field + 64 + 8 * a, 8), :] = grid[row(a, 7), :]
-
-
 def lowest_to_highest(low_side, to_even, to_odd, rows, low, high):
     to_even[rows, :] = jnp.where(low_side, low, high)
     to_odd[rows, :] = jnp.where(low_side, high, low)
@@ -106,8 +98,7 @@
     return lax.axis_index(axis) % 2 == 1
 
 
-def ghost_x(from_even, from_odd, field, b):
-    rows = pl.ds(64 * field + 8 * b, 8)
+def ghost_x(from_even, from_odd, rows):
     odd = lax.axis_index("gx") % 2
     first = (lane_index() < HALF).astype(jnp.int32)
     return jnp.where(first != odd, from_even[rows, :], from_odd[rows, :])
@@ -127,41 +118,33 @@
 
 
 def assembled(a, b, grid, received, field):
-    even_x, odd_x, even_y, odd_y = received
+    even_x, odd_x, even_y, odd_y, *shared = received
     value = grid[row(a, b), :]
     if a in (0, 7):
-        value = joined_x(
-            a, grid[row(0, b), :], grid[row(7, b), :], ghost_x(even_x, odd_x, field, b)
-        )
+        if shared and b in (0, 7):
+            ghost = ghost_x(*shared, pl.ds(16 * field + 8 * (b // 7), 8))
+        else:
+            ghost = ghost_x(even_x, odd_x, pl.ds(64 * field + 8 * b, 8))
+        value = joined_x(a, grid[row(0, b), :], grid[row(7, b), :], ghost)
     if b in (0, 7):
         rows = pl.ds(64 * field + 8 * a, 8)
         value = value + from_y(even_y, odd_y, b, rows)
     return value
 
 
-def edges_kernel(face_y, fixed_y, even_x, odd_x, to_even, to_odd):
-    odd = is_odd("yz")
+def corners_kernel(corners, even_y, odd_y, shared):
+    first = lane_index() < HALF
     for field in range(2):
-        faces = []
         for side in range(2):
-            part = [face_y[pl.ds(128 * field + 64 * side + 8 * a, 8), :] for a in range(8)]
-            ghost = ghost_x(even_x, odd_x, field, 7 * side)
-            low, high = part[0], part[7]
-            part[0] = joined_x(0, low, high, ghost)
-            part[7] = joined_x(7, low, high, ghost)
-            faces.append(part)
-        for a in range(8):
-            rows = pl.ds(64 * field + 8 * a, 8)
-            lowest_to_highest(odd, to_even, to_odd, rows, faces[0][a], faces[1][a])
-    for k in range(9):
-        rows = pl.ds(128 + 8 * k, 8)
-        low, high = fixed_y[pl.ds(8 * k, 8), :], fixed_y[pl.ds(72 + 8 * k, 8), :]
-        lowest_to_highest(odd, to_even, to_odd, rows, low, high)
+            rows = pl.ds(16 * field + 8 * side, 8)
+            low = from_y(even_y, odd_y, 7 * side, pl.ds(64 * field, 8))
+            high = from_y(even_y, odd_y, 7 * side, pl.ds(64 * field + 56, 8))
+            shared[rows, :] = corners[rows, :] + jnp.where(first, low, high)
 
 
 def selection(slots):
     elements = lax.broadcasted_iota(jnp.int32, (LANES, LANES), 0)
-    return jnp.where(elements == slots[...], 1.0, 0.0)
+    return jnp.where(elements.astype(jnp.float32) == slots[pl.ds(0, 1), :], 1.0, 0.0)
 
 
 def parts_of(values):
@@ -184,7 +167,8 @@
 
 def setup_kernel(
     slots, forcing, viscosity, mass_rate,
-    right, diagonal, spread, mass, face_x, face_y, fixed_y, shifts, order, held, arrived,
+    right, diagonal, spread, mass, face_x, to_even, to_odd, corners, shifts, slot_rows,
+    order, held, arrived,
 ):
     ordered = pltpu.make_async_copy(slots, order, arrived.at[3])
     copies = [
@@ -198,7 +182,8 @@
     for c in range(8):
         last_weight = jnp.where(point == c, float(WEIGHTS[c]), last_weight)
     ordered.wait()
-    chosen = selection(order)
+    slot_rows[...] = jnp.broadcast_to(order[...].astype(jnp.float32), slot_rows.shape)
+    chosen = selection(slot_rows)
     copies[0].wait()
     spread[...] = to_grid(chosen, held[0])
     copies[1].wait()
@@ -228,14 +213,22 @@
         low, high = join_vertical(right[across(a, 0), :], right[across(a, 7), :])
         right[across(a, 0), :] = low
         right[across(a, 7), :] = high
-    pack_faces(right, face_x, face_y, 0)
-    pack_faces(diagonal, face_x, face_y, 1)
-    for b in range(8):
-        face_x[pl.ds(128 + 8 * b, 8), :] = packed_x(spread, b)
-    for side in range(2):
+    odd = is_odd("yz")
+    for field, source in enumerate((right, diagonal, spread)):
+        for b in range(8):
+            face_x[pl.ds(64 * field + 8 * b, 8), :] = packed_x(source, b)
+        faces = []
+        for side in range(2):
+            part = [source[row(a, 7 * side), :] for a in range(8)]
+            if field < 2:
+                corners[pl.ds(16 * field + 8 * side, 8), :] = packed_x(source, 7 * side)
+                part = joined_inside(part, 0.0)
+            faces.append(part)
         for a in range(8):
-            fixed_y[pl.ds(72 * side + 8 * a, 8), :] = spread[row(a, 7 * side), :]
-        fixed_y[pl.ds(72 * side + 64, 8), :] = packed_x(mass, 7 * side)
+            rows = pl.ds(64 * field + 8 * a, 8)
+            lowest_to_highest(odd, to_even, to_odd, rows, faces[0][a], faces[1][a])
+    rows = pl.ds(192, 8)
+    lowest_to_highest(odd, to_even, to_odd, rows, packed_x(mass, 0), packed_x(mass, 7))
     for k in range(8):
         along_shift = back_shift = jnp.zeros((8, LANES), jnp.float32)
         for c in range(8):
@@ -294,9 +287,16 @@
     ]
 
 
+def joined_inside(lines, share):
+    first = lane_index() < HALF
+    low, high = lines[0], lines[7]
+    new_low = low + jnp.where(first, share, pltpu.roll(high, HALF, 1))
+    new_high = high + jnp.where(first, pltpu.roll(low, HALF, 1), share)
+    return [new_low] + lines[1:7] + [new_high]
+
+
 def send_faces(image, values, outer, shifts, face_x, to_even, to_odd):
     for_x, for_y = corner_shares(values, outer, shifts)
-    first = lane_index() < HALF
     odd = is_odd("yz")
     for b in range(8):
         face = packed_x(image, b)
@@ -306,9 +306,7 @@
     faces = []
     for side in range(2):
         part = [image[row(a, 7 * side), :] for a in range(8)]
-        low, high = part[0], part[7]
-        part[0] = low + jnp.where(first, for_y[side], pltpu.roll(high, HALF, 1))
-        part[7] = high + jnp.where(first, pltpu.roll(low, HALF, 1), for_y[side])
+        part = joined_inside(part, for_y[side])
         faces.append(part)
     for a in range(8):
         lowest_to_highest(odd, to_even, to_odd, pl.ds(8 * a, 8), faces[0][a], faces[1][a])
@@ -356,10 +354,10 @@
 
 
 def first_kernel(
-    right, diagonal, even_x, odd_x, even_y, odd_y, spread, mass, shifts,
+    right, diagonal, even_x, odd_x, even_y, odd_y, even_shared, odd_shared, spread, mass, shifts,
     whole_diagonal, values, image, outer, face_x, to_even, to_odd, moments,
 ):
-    received = (even_x, odd_x, even_y, odd_y)
+    received = (even_x, odd_x, even_y, odd_y, even_shared, odd_shared)
     sums = [jnp.zeros((8, LANES), jnp.float32)] * 3
     for a in range(8):
         for b in range(8):
@@ -371,7 +369,9 @@
             sums[ends(a, b)] = sums[ends(a, b)] + source * value
     moments[...] = weighted(sums)
     for b in range(8):
-        outer[pl.ds(8 * b, 8), :] = pltpu.roll(ghost_x(even_x, odd_x, 2, b), HALF, 1)
+        outer[pl.ds(8 * b, 8), :] = pltpu.roll(
+            ghost_x(even_x, odd_x, pl.ds(128 + 8 * b, 8)), HALF, 1
+        )
     for side in range(2):
         for k in range(9):
             outer[pl.ds(64 + 72 * side + 8 * k, 8), :] = from_y(
@@ -398,7 +398,7 @@
 
 
 def second_kernel(
-    before_image, even_x, odd_x, even_y, odd_y, diagonal, before, spread, mass, shifts, outer,
+    before_image, even_x, odd_x, odd_y, even_y, diagonal, before, spread, mass, shifts, outer,
     values, image, face_x, to_even, to_odd, moments,
 ):
     received = (even_x, odd_x, even_y, odd_y)
@@ -410,7 +410,7 @@
 
 
 def third_kernel(
-    before_image, even_x, odd_x, even_y, odd_y, diagonal, before, spread, mass, shifts, outer,
+    before_image, even_x, odd_x, odd_y, even_y, diagonal, before, spread, mass, shifts, outer,
     moments0, moments1, values, image, face_x, to_even, to_odd, sums,
 ):
     received = (even_x, odd_x, even_y, odd_y)
@@ -478,11 +478,11 @@
 
 
 def last_kernel(
-    before_image, even_x, odd_x, even_y, odd_y, diagonal, values0, values1, values2, sums, slots,
-    solution, residual, solution_grid, residual_grid,
+    before_image, even_x, odd_x, odd_y, even_y, diagonal, values0, values1, values2, sums,
+    slot_rows, solution, residual, solution_grid, residual_grid,
 ):
     received = (even_x, odd_x, even_y, odd_y)
-    line = jnp.sum(sums[...], 0)
+    line = jnp.sum(sums[...], 0)[0:1]
     lane = lax.broadcasted_iota(jnp.int32, (1, LANES), 1)
     moments = [
         jnp.sum(jnp.where(lane == k, line, 0.0), 1, keepdims=True) for k in range(6)
@@ -501,7 +501,7 @@
             far = precond[0] * basis[0] + precond[1] * basis[1] + precond[2] * basis[2]
             solution_grid[rows, :] = near
             residual_grid[rows, :] = scale * far + precond[3] * image
-    chosen = selection(slots).T.astype(jnp.bfloat16)
+    chosen = selection(slot_rows).T.astype(jnp.bfloat16)
     for grid, out in ((solution_grid, solution), (residual_grid, residual)):
         total = None
         for part in parts_of(grid[...]):
@@ -540,9 +540,10 @@
     devices = lax.axis_size("gx") * lax.axis_size("yz")
     slots = slot_element[0]
     grid, face, tile = (POINTS, LANES), (64, LANES), (8, LANES)
-    right, diagonal, spread, mass, out_x, out_y, fixed_y, shifts = call(
+    right, diagonal, spread, mass, out_x, *sent_y, corners, shifts, slot_rows = call(
         setup_kernel, "setup",
-        [grid] * 4 + [(192, LANES), (256, LANES), (144, LANES), (128, LANES)],
+        [grid] * 4 + [(192, LANES), (200, LANES), (200, LANES), (32, LANES), (128, LANES)]
+        + [tile],
         [
             pltpu.VMEM((1, LANES), jnp.int32),
             pltpu.VMEM((3, LANES, POINTS), jnp.float32),
@@ -550,30 +551,28 @@
         ],
         slots, forcing, viscosity, mass_rate, outside=4,
     )
-    received_x = swapped((out_x, out_x), "gx")
-    sent_y = call(
-        edges_kernel, "edges", [(200, LANES)] * 2, [], out_y, fixed_y, *received_x
-    )
-    received_y = swapped(sent_y, "yz")
+    received_x, received_y = swapped((out_x, out_x), "gx"), swapped(sent_y, "yz")
+    [shared] = call(corners_kernel, "corners", [(32, LANES)], [], corners, *received_y)
+    received = (*received_x, *received_y, *swapped((shared, shared), "gx"))
     diagonal, values0, image, outer, out_x, *sent_y, moments0 = call(
         first_kernel, "first", [grid] * 3 + [(208, LANES)] + [face] * 3 + [tile], [],
-        right, diagonal, *received_x, *received_y, spread, mass, shifts,
-    )
-    received = (*swapped((out_x, out_x), "gx"), *swapped(sent_y, "yz"))
+        right, diagonal, *received, spread, mass, shifts,
+    )
+    received = (*swapped((out_x, out_x), "gx"), *swapped(sent_y, "yz")[::-1])
     values1, image, out_x, *sent_y, moments1 = call(
         second_kernel, "second", [grid] * 2 + [face] * 3 + [(16, LANES)], [],
         image, *received, diagonal, values0, spread, mass, shifts, outer,
     )
-    received = (*swapped((out_x, out_x), "gx"), *swapped(sent_y, "yz"))
+    received = (*swapped((out_x, out_x), "gx"), *swapped(sent_y, "yz")[::-1])
     values2, image, out_x, *sent_y, sums = call(
-        third_kernel, "third", [grid] * 2 + [face] * 3 + [(devices, 1, LANES)], [],
+        third_kernel, "third", [grid] * 2 + [face] * 3 + [(devices, 2, LANES)], [],
         image, *received, diagonal, values1, spread, mass, shifts, outer, moments0, moments1,
     )
     sums = lax.all_to_all(sums, ("gx", "yz"), 0, 0)
-    received = (*swapped((out_x, out_x), "gx"), *swapped(sent_y, "yz"))
+    received = (*swapped((out_x, out_x), "gx"), *swapped(sent_y, "yz")[::-1])
     return call(
         last_kernel, "last", [forcing.shape] * 2, [pltpu.VMEM(grid, jnp.float32)] * 2,
-        image, *received, diagonal, values0, values1, values2, sums, slots,
+        image, *received, diagonal, values0, values1, values2, sums, slot_rows,
     )
 
 

time: 51.4 us -> 48 us (0.934)
  blocking collectives: 9.23 us -> 0 us
  starting transfers between devices: 24.4 us -> 29.2 us
  waiting for transfers between devices: 10 us -> 11.2 us
  local copies, waits for them, and re-layouts: 0.65 us -> 0 us
  Pallas kernels: 6.24 us -> 6.76 us
    all_to_all x1 -> x0, blocking collectives: 9.23 us -> none  [body(): sums = lax.all_to_all(sums, ('gx', 'yz'), 0, 0)]
    all_to_all x0 -> x1, starting transfers between devices: none -> 3.6 us  [body(): sums = lax.all_to_all(sums, ('gx', 'yz'), 0, 0)]
    ppermute x8 -> x9, waiting for transfers between devices: 1.06 us -> 2.78 us  [swapped(): lax.ppermute(block[0], axis, even)]
    ppermute x8 -> x9, starting transfers between devices: 8.42 us -> 9.58 us  [swapped(): lax.ppermute(block[0], axis, even)]
    unnamed x2 -> x0, local copies, waits for them, and re-layouts: 0.65 us -> none
    ppermute x8 -> x9, waiting for transfers between devices: 8.97 us -> 8.41 us  [swapped(): lax.ppermute(block[1], axis, odd)]
    pallas_call x6, Pallas kernels: 6.24 us -> 6.76 us  [call(): pl.pallas_call(kernel, out_shape=[jax.ShapeDtypeStruct(shape, jnp.float32...]
    ppermute x8 -> x9, starting transfers between devices: 15.9 us -> 16 us  [swapped(): lax.ppermute(block[1], axis, odd)]
  transfers between devices with their start and end apart: 16 -> 19, of which waited for: 7 -> 8; matrix products, arithmetic and copies ran while one was open for 0% -> 0% of each run, Pallas kernels for 0% -> 0%
where the time goes in v5:
time: 48 us; the launch traced here: 47.8 us
  starting transfers between devices  29.2 us (61%)
  waiting for transfers between devices  11.2 us (23%)
  Pallas kernels  6.76 us (14%)
  between operations  0.69 us (1%)
    ppermute x9, starting transfers between devices, swapped(): lax.ppermute(block[1], axis, odd)  16 us
    ppermute x9, starting transfers between devices, swapped(): lax.ppermute(block[0], axis, even)  9.58 us
    ppermute x9, waiting for transfers between devices, swapped(): lax.ppermute(block[1], axis, odd)  8.41 us
    pallas_call x6, Pallas kernels, call(): pl.pallas_call(kernel, out_shape=[jax.ShapeDtypeStruct(shape, jnp.float32...  6.76 us
    all_to_all x1, starting transfers between devices, body(): sums = lax.all_to_all(sums, ('gx', 'yz'), 0, 0)  3.6 us
    ppermute x9, waiting for transfers between devices, swapped(): lax.ppermute(block[0], axis, even)  2.78 us
  transfers between devices with their start and end apart: 19, of which 8 were waited for; matrix products, arithmetic and copies ran while one was open for 0% of the time, Pallas kernels for 0%

profile of v5, /device:TPU:0, one launch (start us, length us, event | category | flops | bytes accessed | tf_op | source)
XLA Modules:
  0.0 47.8 jit_solution(7067414710442080619)
XLA Ops:
  0.6 2.2 %setup.1 = (f32[512,128]{1,0:T(8,128)S(1)}, f32[512,128]{1,0:T(8,128)S(1)}, f32[512,128]{1,0:T(8,128)S(1)}, f32[512,128]{1,0:T(8,128)S(1)}, f32[192,128]{1,0:T(8...) custom-call(s32[1,128]{1,0:T(1,128)} %bitcast.1, ...), custom_call_target="tpu_custom_call" | custom-call | tf_op jit(solution)/shard_map/setup/pallas_call | solution.py:521
  2.8 3.0 %collective-permute-start.2 = (f32[200,128]{1,0:T(8,128)S(1)}, f32[200,128]{1,0:T(8,128)S(1)}, u32[]{:S(2)}, u32[]{:S(2)}) collective-permute-start(f32[200,128]{1,0:T(8,128)S(1)} %get-tuple-element.35), channel_id=1, source_target_pairs={{0,1},{1,0},{2,3},{3,2},{4,5},{5,4},{6,7},{7,6},{8,9},{9,8},{10,11... | collective-permute-start | bytes 307208 | tf_op jit(solution)/shard_map/ppermute | solution.py:536
  5.8 3.6 %collective-permute-start.3 = (f32[200,128]{1,0:T(8,128)S(1)}, f32[200,128]{1,0:T(8,128)S(1)}, u32[]{:S(2)}, u32[]{:S(2)}) collective-permute-start(f32[200,128]{1,0:T(8,128)S(1)} %get-tuple-element.36), channel_id=1, source_target_pairs={{0,7},{1,2},{2,1},{3,4},{4,3},{5,6},{6,5},{7,0},{8,15},{9,10},{10,... | collective-permute-start | bytes 307208 | tf_op jit(solution)/shard_map/ppermute | solution.py:536
  9.4 0.4 collective-permute-start.1
  9.8 1.2 %collective-permute-start = (f32[192,128]{1,0:T(8,128)S(1)}, f32[192,128]{1,0:T(8,128)S(1)}, u32[]{:S(2)}, u32[]{:S(2)}) collective-permute-start(f32[192,128]{1,0:T(8,128)S(1)} %get-tuple-element.34), channel_id=1, source_target_pairs={{0,8},{8,0},{16,24},{24,16},{1,9},{9,1},{17,25},{25,17},{2,10},{10... | collective-permute-start | bytes 294920 | tf_op jit(solution)/shard_map/ppermute | solution.py:536
  11.0 0.0 collective-permute-done.2.even_y
  11.0 2.1 %collective-permute-done.3.odd_y = f32[200,128]{1,0:T(8,128)S(1)} collective-permute-done((f32[200,128]{1,0:T(8,128)S(1)}, f32[200,128]{1,0:T(8,128)S(1)}, u32[]{:S(2)}, u32[]{:S(2)}) %collective-permute-start.3) | collective-permute-done | bytes 102432 | tf_op jit(solution)/shard_map/ppermute | solution.py:536
  13.2 0.1 collective-permute-start.5
  13.3 1.6 %collective-permute-start.4 = (f32[32,128]{1,0:T(8,128)S(1)}, f32[32,128]{1,0:T(8,128)S(1)}, u32[]{:S(2)}, u32[]{:S(2)}) collective-permute-start(f32[32,128]{1,0:T(8,128)S(1)} %corners.1), channel_id=1, source_target_pairs={{0,8},{8,0},{16,24},{24,16},{1,9},{9,1},{17,25},{25,17},{2,10},{10... | collective-permute-start | bytes 49160 | tf_op jit(solution)/shard_map/ppermute | solution.py:536
  14.9 0.0 collective-permute-done.1.odd_x
  14.9 0.0 collective-permute-done.even_x
  14.9 1.6 %collective-permute-done.5.odd_shared = f32[32,128]{1,0:T(8,128)S(1)} collective-permute-done((f32[32,128]{1,0:T(8,128)S(1)}, f32[32,128]{1,0:T(8,128)S(1)}, u32[]{:S(2)}, u32[]{:S(2)}) %collective-permute-start.5) | collective-permute-done | bytes 16416 | tf_op jit(solution)/shard_map/ppermute | solution.py:536
  16.5 0.0 collective-permute-done.4.even_shared
  16.5 0.9 %first.1 = (f32[512,128]{1,0:T(8,128)S(1)}, f32[512,128]{1,0:T(8,128)S(1)}, f32[512,128]{1,0:T(8,128)S(1)}, f32[208,128]{1,0:T(8,128)S(1)}, f32[64,128]{1,0:T(8,...) custom-call(f32[512,128]{1,0:T(8,128)S(1)} %get-tuple-element.32.right, ...), custom_call_target="tpu_custom_call" | custom-call | tf_op jit(solution)/shard_map/first/pallas_call | solution.py:521
  17.4 3.6 %collective-permute-start.8 = (f32[64,128]{1,0:T(8,128)S(1)}, f32[64,128]{1,0:T(8,128)S(1)}, u32[]{:S(2)}, u32[]{:S(2)}) collective-permute-start(f32[64,128]{1,0:T(8,128)S(1)} %get-tuple-element.43), channel_id=1, source_target_pairs={{0,7},{1,2},{2,1},{3,4},{4,3},{5,6},{6,5},{7,0},{8,15},{9,10},{10,... | collective-permute-start | bytes 98312 | tf_op jit(solution)/shard_map/ppermute | solution.py:536
  21.0 0.0 collective-permute-start.9
  21.0 0.0 collective-permute-start.7
  21.0 1.5 %collective-permute-start.6 = (f32[64,128]{1,0:T(8,128)S(1)}, f32[64,128]{1,0:T(8,128)S(1)}, u32[]{:S(2)}, u32[]{:S(2)}) collective-permute-start(f32[64,128]{1,0:T(8,128)S(1)} %get-tuple-element.42), channel_id=1, source_target_pairs={{0,8},{8,0},{16,24},{24,16},{1,9},{9,1},{17,25},{25,17},{2,10},{10... | collective-permute-start | bytes 98312 | tf_op jit(solution)/shard_map/ppermute | solution.py:536
  22.6 1.6 %collective-permute-done.8.odd_y = f32[64,128]{1,0:T(8,128)S(1)} collective-permute-done((f32[64,128]{1,0:T(8,128)S(1)}, f32[64,128]{1,0:T(8,128)S(1)}, u32[]{:S(2)}, u32[]{:S(2)}) %collective-permute-start.8) | collective-permute-done | bytes 32800 | tf_op jit(solution)/shard_map/ppermute | solution.py:536
  24.2 0.8 %collective-permute-done.9.even_y = f32[64,128]{1,0:T(8,128)S(1)} collective-permute-done((f32[64,128]{1,0:T(8,128)S(1)}, f32[64,128]{1,0:T(8,128)S(1)}, u32[]{:S(2)}, u32[]{:S(2)}) %collective-permute-start.9) | collective-permute-done | bytes 32800 | tf_op jit(solution)/shard_map/ppermute | solution.py:536
  24.9 0.0 collective-permute-done.7.odd_x
  24.9 0.0 collective-permute-done.6.even_x
  24.9 0.8 %second.1 = (f32[512,128]{1,0:T(8,128)S(1)}, f32[512,128]{1,0:T(8,128)S(1)}, f32[64,128]{1,0:T(8,128)S(1)}, f32[64,128]{1,0:T(8,128)S(1)}, f32[64,128]{1,0:T(8,128)S(1)}, /*index=5*/f32[16,128]{1,0:T(8,128)S(1)}) custom-call(f32[512,128]{1,0:T(8,128)S(1)} %get-tuple-element.41.before_image, f32[64,128]{1,0:T(8,128)S(1)} %collective-permute-done.6.even_x, ...), custom_call_target="tpu_custom_call" | custom-call | tf_op jit(solution)/shard_map/second/pallas_call | solution.py:521
  25.8 2.8 %collective-permute-start.12 = (f32[64,128]{1,0:T(8,128)S(1)}, f32[64,128]{1,0:T(8,128)S(1)}, u32[]{:S(2)}, u32[]{:S(2)}) collective-permute-start(f32[64,128]{1,0:T(8,128)S(1)} %get-tuple-element.50), channel_id=1, source_target_pairs={{0,7},{1,2},{2,1},{3,4},{4,3},{5,6},{6,5},{7,0},{8,15},{9,10},{10,... | collective-permute-start | bytes 98312 | tf_op jit(solution)/shard_map/ppermute | solution.py:536
  28.6 0.0 collective-permute-start.13
  28.6 0.0 collective-permute-start.11
  28.6 1.5 %collective-permute-start.10 = (f32[64,128]{1,0:T(8,128)S(1)}, f32[64,128]{1,0:T(8,128)S(1)}, u32[]{:S(2)}, u32[]{:S(2)}) collective-permute-start(f32[64,128]{1,0:T(8,128)S(1)} %get-tuple-element.49), channel_id=1, source_target_pairs={{0,8},{8,0},{16,24},{24,16},{1,9},{9,1},{17,25},{25,17},{2,10},{10... | collective-permute-start | bytes 98312 | tf_op jit(solution)/shard_map/ppermute | solution.py:536
  30.1 2.4 %collective-permute-done.12.odd_y = f32[64,128]{1,0:T(8,128)S(1)} collective-permute-done((f32[64,128]{1,0:T(8,128)S(1)}, f32[64,128]{1,0:T(8,128)S(1)}, u32[]{:S(2)}, u32[]{:S(2)}) %collective-permute-start.12) | collective-permute-done | bytes 32800 | tf_op jit(solution)/shard_map/ppermute | solution.py:536
  32.5 0.3 collective-permute-done.13.even_y
  32.8 0.0 collective-permute-done.11.odd_x
  32.8 0.0 collective-permute-done.10.even_x
  32.8 1.6 %third.1 = (f32[512,128]{1,0:T(8,128)S(1)}, f32[512,128]{1,0:T(8,128)S(1)}, f32[64,128]{1,0:T(8,128)S(1)}, f32[64,128]{1,0:T(8,128)S(1)}, f32[64,128]{1,0:T(8,128)S(1)}, /*index=5*/f32[32,2,128]{2,1,0:T(2,128)}) custom-call(f32[512,128]{1,0:T(8,128)S(1)} %get-tuple-element.48.before_image, f32[64,128]{1,0:T(8,128)S(1)} %collective-permute-done.10.even_x, ...), custom_call_target="tpu_custom_call" | custom-call | tf_op jit(solution)/shard_map/third/pallas_call | solution.py:521
  34.4 3.6 %all-to-all-start = ((f32[32,2,128]{2,1,0:T(2,128)}), f32[32,2,128]{2,1,0:T(2,128)S(1)}, u32[]{:S(2)}, u32[]{:S(2)}) async-start(f32[32,2,128]{2,1,0:T(2,128)} %get-tuple-element.60), calls=%async_computation | async-start | bytes 65536 | tf_op jit(solution)/shard_map/all_to_all | solution.py:571
  38.0 4.6 %collective-permute-start.16 = (f32[64,128]{1,0:T(8,128)S(1)}, f32[64,128]{1,0:T(8,128)S(1)}, u32[]{:S(2)}, u32[]{:S(2)}) collective-permute-start(f32[64,128]{1,0:T(8,128)S(1)} %get-tuple-element.57), channel_id=1, source_target_pairs={{0,7},{1,2},{2,1},{3,4},{4,3},{5,6},{6,5},{7,0},{8,15},{9,10},{10,... | collective-permute-start | bytes 98312 | tf_op jit(solution)/shard_map/ppermute | solution.py:536
  42.6 0.0 collective-permute-start.17
  42.6 1.0 %collective-permute-start.15 = (f32[64,128]{1,0:T(8,128)S(1)}, f32[64,128]{1,0:T(8,128)S(1)}, u32[]{:S(2)}, u32[]{:S(2)}) collective-permute-start(f32[64,128]{1,0:T(8,128)S(1)} %get-tuple-element.56), channel_id=1, source_target_pairs={{0,24},{8,16},{16,8},{24,0},{1,25},{9,17},{17,9},{25,1},{2,26},{10... | collective-permute-start | bytes 98312 | tf_op jit(solution)/shard_map/ppermute | solution.py:536
  43.6 0.6 %collective-permute-start.14 = (f32[64,128]{1,0:T(8,128)S(1)}, f32[64,128]{1,0:T(8,128)S(1)}, u32[]{:S(2)}, u32[]{:S(2)}) collective-permute-start(f32[64,128]{1,0:T(8,128)S(1)} %get-tuple-element.56), channel_id=1, source_target_pairs={{0,8},{8,0},{16,24},{24,16},{1,9},{9,1},{17,25},{25,17},{2,10},{10... | collective-permute-start | bytes 98312 | tf_op jit(solution)/shard_map/ppermute | solution.py:536
  44.2 0.6 %collective-permute-done.16.odd_y = f32[64,128]{1,0:T(8,128)S(1)} collective-permute-done((f32[64,128]{1,0:T(8,128)S(1)}, f32[64,128]{1,0:T(8,128)S(1)}, u32[]{:S(2)}, u32[]{:S(2)}) %collective-permute-start.16) | collective-permute-done | bytes 32800 | tf_op jit(solution)/shard_map/ppermute | solution.py:536
  44.8 1.7 %collective-permute-done.17.even_y = f32[64,128]{1,0:T(8,128)S(1)} collective-permute-done((f32[64,128]{1,0:T(8,128)S(1)}, f32[64,128]{1,0:T(8,128)S(1)}, u32[]{:S(2)}, u32[]{:S(2)}) %collective-permute-start.17) | collective-permute-done | bytes 32800 | tf_op jit(solution)/shard_map/ppermute | solution.py:536
  46.5 0.0 collective-permute-done.15.odd_x
  46.5 0.0 collective-permute-done.14.even_x
  46.5 0.0 all-to-all-done.sums
  46.5 1.3 %last.1 = (f32[1,1,128,512]{3,2,1,0:T(8,128)}, f32[1,1,128,512]{3,2,1,0:T(8,128)}) custom-call(f32[512,128]{1,0:T(8,128)S(1)} %get-tuple-element.55.before_image, f32[64,128]{1,0:T(8,128)S(1)} %collective-permute-done.14.even_x, f32[64,128]{1,0:T(8,128)S(1)} %collective-permute-done.15.odd_x, f32[64,128]{1,0:T(8,128)S(1)} %collective-permute-done.16.odd_y, ...), custom_call_target="tpu_custom_call" | custom-call | tf_op jit(solution)/shard_map/last/pallas_call | solution.py:521
  (1 shorter events, 0.0 us)
Async XLA Ops:
  2.8 8.2 %collective-permute-start.2 = (f32[200,128]{1,0:T(8,128)S(1)}, f32[200,128]{1,0:T(8,128)S(1)}, u32[]{:S(2)}, u32[]{:S(2)}) collective-permute-start(f32[200,128]{1,0:T(8,128)S(1)} %get-tuple-element.35), channel_id=1, source_target_pairs={{0,1},{1,0},{2,3},{3,2},{4,5},{5,4},{6,7},{7,6},{8,9},{9,8},{10,11... | collective-permute-start | bytes 307208 | tf_op jit(solution)/shard_map/ppermute | solution.py:536
  5.8 7.4 %collective-permute-start.3 = (f32[200,128]{1,0:T(8,128)S(1)}, f32[200,128]{1,0:T(8,128)S(1)}, u32[]{:S(2)}, u32[]{:S(2)}) collective-permute-start(f32[200,128]{1,0:T(8,128)S(1)} %get-tuple-element.36), channel_id=1, source_target_pairs={{0,7},{1,2},{2,1},{3,4},{4,3},{5,6},{6,5},{7,0},{8,15},{9,10},{10,... | collective-permute-start | bytes 307208 | tf_op jit(solution)/shard_map/ppermute | solution.py:536
  9.4 5.5 %collective-permute-start.1 = (f32[192,128]{1,0:T(8,128)S(1)}, f32[192,128]{1,0:T(8,128)S(1)}, u32[]{:S(2)}, u32[]{:S(2)}) collective-permute-start(f32[192,128]{1,0:T(8,128)S(1)} %get-tuple-element.34), channel_id=1, source_target_pairs={{0,24},{8,16},{16,8},{24,0},{1,25},{9,17},{17,9},{25,1},{2,26},{10... | collective-permute-start | bytes 294920 | tf_op jit(solution)/shard_map/ppermute | solution.py:536
  9.8 5.1 %collective-permute-start = (f32[192,128]{1,0:T(8,128)S(1)}, f32[192,128]{1,0:T(8,128)S(1)}, u32[]{:S(2)}, u32[]{:S(2)}) collective-permute-start(f32[192,128]{1,0:T(8,128)S(1)} %get-tuple-element.34), channel_id=1, source_target_pairs={{0,8},{8,0},{16,24},{24,16},{1,9},{9,1},{17,25},{25,17},{2,10},{10... | collective-permute-start | bytes 294920 | tf_op jit(solution)/shard_map/ppermute | solution.py:536
  13.2 3.3 %collective-permute-start.5 = (f32[32,128]{1,0:T(8,128)S(1)}, f32[32,128]{1,0:T(8,128)S(1)}, u32[]{:S(2)}, u32[]{:S(2)}) collective-permute-start(f32[32,128]{1,0:T(8,128)S(1)} %corners.1), channel_id=1, source_target_pairs={{0,24},{8,16},{16,8},{24,0},{1,25},{9,17},{17,9},{25,1},{2,26},{10... | collective-permute-start | bytes 49160 | tf_op jit(solution)/shard_map/ppermute | solution.py:536
  13.3 3.3 %collective-permute-start.4 = (f32[32,128]{1,0:T(8,128)S(1)}, f32[32,128]{1,0:T(8,128)S(1)}, u32[]{:S(2)}, u32[]{:S(2)}) collective-permute-start(f32[32,128]{1,0:T(8,128)S(1)} %corners.1), channel_id=1, source_target_pairs={{0,8},{8,0},{16,24},{24,16},{1,9},{9,1},{17,25},{25,17},{2,10},{10... | collective-permute-start | bytes 49160 | tf_op jit(solution)/shard_map/ppermute | solution.py:536
  17.4 6.8 %collective-permute-start.8 = (f32[64,128]{1,0:T(8,128)S(1)}, f32[64,128]{1,0:T(8,128)S(1)}, u32[]{:S(2)}, u32[]{:S(2)}) collective-permute-start(f32[64,128]{1,0:T(8,128)S(1)} %get-tuple-element.43), channel_id=1, source_target_pairs={{0,7},{1,2},{2,1},{3,4},{4,3},{5,6},{6,5},{7,0},{8,15},{9,10},{10,... | collective-permute-start | bytes 98312 | tf_op jit(solution)/shard_map/ppermute | solution.py:536
  21.0 3.9 %collective-permute-start.9 = (f32[64,128]{1,0:T(8,128)S(1)}, f32[64,128]{1,0:T(8,128)S(1)}, u32[]{:S(2)}, u32[]{:S(2)}) collective-permute-start(f32[64,128]{1,0:T(8,128)S(1)} %get-tuple-element.44), channel_id=1, source_target_pairs={{0,1},{1,0},{2,3},{3,2},{4,5},{5,4},{6,7},{7,6},{8,9},{9,8},{10,11... | collective-permute-start | bytes 98312 | tf_op jit(solution)/shard_map/ppermute | solution.py:536
  21.0 3.9 %collective-permute-start.7 = (f32[64,128]{1,0:T(8,128)S(1)}, f32[64,128]{1,0:T(8,128)S(1)}, u32[]{:S(2)}, u32[]{:S(2)}) collective-permute-start(f32[64,128]{1,0:T(8,128)S(1)} %get-tuple-element.42), channel_id=1, source_target_pairs={{0,24},{8,16},{16,8},{24,0},{1,25},{9,17},{17,9},{25,1},{2,26},{10... | collective-permute-start | bytes 98312 | tf_op jit(solution)/shard_map/ppermute | solution.py:536
  21.0 3.9 %collective-permute-start.6 = (f32[64,128]{1,0:T(8,128)S(1)}, f32[64,128]{1,0:T(8,128)S(1)}, u32[]{:S(2)}, u32[]{:S(2)}) collective-permute-start(f32[64,128]{1,0:T(8,128)S(1)} %get-tuple-element.42), channel_id=1, source_target_pairs={{0,8},{8,0},{16,24},{24,16},{1,9},{9,1},{17,25},{25,17},{2,10},{10... | collective-permute-start | bytes 98312 | tf_op jit(solution)/shard_map/ppermute | solution.py:536
  25.8 6.7 %collective-permute-start.12 = (f32[64,128]{1,0:T(8,128)S(1)}, f32[64,128]{1,0:T(8,128)S(1)}, u32[]{:S(2)}, u32[]{:S(2)}) collective-permute-start(f32[64,128]{1,0:T(8,128)S(1)} %get-tuple-element.50), channel_id=1, source_target_pairs={{0,7},{1,2},{2,1},{3,4},{4,3},{5,6},{6,5},{7,0},{8,15},{9,10},{10,... | collective-permute-start | bytes 98312 | tf_op jit(solution)/shard_map/ppermute | solution.py:536
  28.6 4.3 %collective-permute-start.13 = (f32[64,128]{1,0:T(8,128)S(1)}, f32[64,128]{1,0:T(8,128)S(1)}, u32[]{:S(2)}, u32[]{:S(2)}) collective-permute-start(f32[64,128]{1,0:T(8,128)S(1)} %get-tuple-element.51), channel_id=1, source_target_pairs={{0,1},{1,0},{2,3},{3,2},{4,5},{5,4},{6,7},{7,6},{8,9},{9,8},{10,11... | collective-permute-start | bytes 98312 | tf_op jit(solution)/shard_map/ppermute | solution.py:536
  28.6 4.3 %collective-permute-start.11 = (f32[64,128]{1,0:T(8,128)S(1)}, f32[64,128]{1,0:T(8,128)S(1)}, u32[]{:S(2)}, u32[]{:S(2)}) collective-permute-start(f32[64,128]{1,0:T(8,128)S(1)} %get-tuple-element.49), channel_id=1, source_target_pairs={{0,24},{8,16},{16,8},{24,0},{1,25},{9,17},{17,9},{25,1},{2,26},{10... | collective-permute-start | bytes 98312 | tf_op jit(solution)/shard_map/ppermute | solution.py:536
  28.6 4.3 %collective-permute-start.10 = (f32[64,128]{1,0:T(8,128)S(1)}, f32[64,128]{1,0:T(8,128)S(1)}, u32[]{:S(2)}, u32[]{:S(2)}) collective-permute-start(f32[64,128]{1,0:T(8,128)S(1)} %get-tuple-element.49), channel_id=1, source_target_pairs={{0,8},{8,0},{16,24},{24,16},{1,9},{9,1},{17,25},{25,17},{2,10},{10... | collective-permute-start | bytes 98312 | tf_op jit(solution)/shard_map/ppermute | solution.py:536
  34.4 12.1 %all-to-all-start = ((f32[32,2,128]{2,1,0:T(2,128)}), f32[32,2,128]{2,1,0:T(2,128)S(1)}, u32[]{:S(2)}, u32[]{:S(2)}) async-start(f32[32,2,128]{2,1,0:T(2,128)} %get-tuple-element.60), calls=%async_computation | async-start | bytes 65536 | tf_op jit(solution)/shard_map/all_to_all | solution.py:571
  38.0 6.9 %collective-permute-start.16 = (f32[64,128]{1,0:T(8,128)S(1)}, f32[64,128]{1,0:T(8,128)S(1)}, u32[]{:S(2)}, u32[]{:S(2)}) collective-permute-start(f32[64,128]{1,0:T(8,128)S(1)} %get-tuple-element.57), channel_id=1, source_target_pairs={{0,7},{1,2},{2,1},{3,4},{4,3},{5,6},{6,5},{7,0},{8,15},{9,10},{10,... | collective-permute-start | bytes 98312 | tf_op jit(solution)/shard_map/ppermute | solution.py:536
  42.6 3.9 %collective-permute-start.17 = (f32[64,128]{1,0:T(8,128)S(1)}, f32[64,128]{1,0:T(8,128)S(1)}, u32[]{:S(2)}, u32[]{:S(2)}) collective-permute-start(f32[64,128]{1,0:T(8,128)S(1)} %get-tuple-element.58), channel_id=1, source_target_pairs={{0,1},{1,0},{2,3},{3,2},{4,5},{5,4},{6,7},{7,6},{8,9},{9,8},{10,11... | collective-permute-start | bytes 98312 | tf_op jit(solution)/shard_map/ppermute | solution.py:536
  42.6 3.9 %collective-permute-start.15 = (f32[64,128]{1,0:T(8,128)S(1)}, f32[64,128]{1,0:T(8,128)S(1)}, u32[]{:S(2)}, u32[]{:S(2)}) collective-permute-start(f32[64,128]{1,0:T(8,128)S(1)} %get-tuple-element.56), channel_id=1, source_target_pairs={{0,24},{8,16},{16,8},{24,0},{1,25},{9,17},{17,9},{25,1},{2,26},{10... | collective-permute-start | bytes 98312 | tf_op jit(solution)/shard_map/ppermute | solution.py:536
  43.6 2.9 %collective-permute-start.14 = (f32[64,128]{1,0:T(8,128)S(1)}, f32[64,128]{1,0:T(8,128)S(1)}, u32[]{:S(2)}, u32[]{:S(2)}) collective-permute-start(f32[64,128]{1,0:T(8,128)S(1)} %get-tuple-element.56), channel_id=1, source_target_pairs={{0,8},{8,0},{16,24},{24,16},{1,9},{9,1},{17,25},{25,17},{2,10},{10... | collective-permute-start | bytes 98312 | tf_op jit(solution)/shard_map/ppermute | solution.py:536

commit v6 on v5

--- a/solution.py
+++ b/solution.py
@@ -132,7 +132,7 @@
     return value
 
 
-def corners_kernel(corners, even_y, odd_y, shared):
+def corners_kernel(corners, odd_y, even_y, shared):
     first = lane_index() < HALF
     for field in range(2):
         for side in range(2):
@@ -354,7 +354,7 @@
 
 
 def first_kernel(
-    right, diagonal, even_x, odd_x, even_y, odd_y, even_shared, odd_shared, spread, mass, shifts,
+    right, diagonal, even_x, odd_x, odd_y, even_y, even_shared, odd_shared, spread, mass, shifts,
     whole_diagonal, values, image, outer, face_x, to_even, to_odd, moments,
 ):
     received = (even_x, odd_x, even_y, odd_y, even_shared, odd_shared)
@@ -411,14 +411,19 @@
 
 def third_kernel(
     before_image, even_x, odd_x, odd_y, even_y, diagonal, before, spread, mass, shifts, outer,
-    moments0, moments1, values, image, face_x, to_even, to_odd, sums,
+    values, image, face_x, to_even, to_odd, moments,
 ):
     received = (even_x, odd_x, even_y, odd_y)
     cross, square = next_values(before_image, received, diagonal, before, values)
     energy = operate(values, spread, mass, image)
     send_faces(image, values, outer, shifts, face_x, to_even, to_odd)
+    for k, part in enumerate((cross, square, energy)):
+        moments[pl.ds(8 * k, 8), :] = part
+
+
+def sums_kernel(moments0, moments1, moments2, sums):
     parts = [
-        moments0[...], moments1[pl.ds(0, 8), :], moments1[pl.ds(8, 8), :], cross, square, energy
+        moments0[...], moments1[pl.ds(0, 8), :], moments1[pl.ds(8, 8), :], *(moments2[pl.ds(8 * k, 8), :] for k in range(3))
     ]
     lane = lax.broadcasted_iota(jnp.int32, (1, LANES), 1)
     line = jnp.zeros((1, LANES), jnp.float32)
@@ -551,7 +556,7 @@
         ],
         slots, forcing, viscosity, mass_rate, outside=4,
     )
-    received_x, received_y = swapped((out_x, out_x), "gx"), swapped(sent_y, "yz")
+    received_x, received_y = swapped((out_x, out_x), "gx"), swapped(sent_y, "yz")[::-1]
     [shared] = call(corners_kernel, "corners", [(32, LANES)], [], corners, *received_y)
     received = (*received_x, *received_y, *swapped((shared, shared), "gx"))
     diagonal, values0, image, outer, out_x, *sent_y, moments0 = call(
@@ -564,10 +569,11 @@
         image, *received, diagonal, values0, spread, mass, shifts, outer,
     )
     received = (*swapped((out_x, out_x), "gx"), *swapped(sent_y, "yz")[::-1])
-    values2, image, out_x, *sent_y, sums = call(
-        third_kernel, "third", [grid] * 2 + [face] * 3 + [(devices, 2, LANES)], [],
-        image, *received, diagonal, values1, spread, mass, shifts, outer, moments0, moments1,
-    )
+    values2, image, out_x, *sent_y, moments2 = call(
+        third_kernel, "third", [grid] * 2 + [face] * 3 + [(24, LANES)], [],
+        image, *received, diagonal, values1, spread, mass, shifts, outer,
+    )
+    [sums] = call(sums_kernel, "sums", [(devices, 2, LANES)], [], moments0, moments1, moments2)
     sums = lax.all_to_all(sums, ("gx", "yz"), 0, 0)
     received = (*swapped((out_x, out_x), "gx"), *swapped(sent_y, "yz")[::-1])
     return call(

time: 48 us -> 47.5 us (0.990)
  starting transfers between devices: 29.2 us -> 27 us
  waiting for transfers between devices: 11.2 us -> 12.9 us
    ppermute x9, starting transfers between devices: 9.58 us -> 5.81 us  [swapped(): lax.ppermute(block[0], axis, even)]
    ppermute x9, starting transfers between devices: 16 us -> 17.7 us  [swapped(): lax.ppermute(block[1], axis, odd)]
    ppermute x9, waiting for transfers between devices: 2.78 us -> 3.79 us  [swapped(): lax.ppermute(block[0], axis, even)]
    ppermute x9, waiting for transfers between devices: 8.41 us -> 9.1 us  [swapped(): lax.ppermute(block[1], axis, odd)]
    pallas_call x6 -> x7, Pallas kernels: 6.76 us -> 6.74 us  [call(): pl.pallas_call(kernel, out_shape=[jax.ShapeDtypeStruct(shape, jnp.float32...]
  transfers between devices with their start and end apart: 19 -> 19, of which waited for: 8 -> 7; matrix products, arithmetic and copies ran while one was open for 0% -> 0% of each run, Pallas kernels for 0% -> 0%
where the time goes in v6:
time: 47.5 us; the launch traced here: 47.4 us
  starting transfers between devices  27 us (57%)
  waiting for transfers between devices  12.9 us (27%)
  Pallas kernels  6.74 us (14%)
  between operations  0.68 us (1%)
    ppermute x9, starting transfers between devices, swapped(): lax.ppermute(block[1], axis, odd)  17.7 us
    ppermute x9, waiting for transfers between devices, swapped(): lax.ppermute(block[1], axis, odd)  9.1 us
    pallas_call x7, Pallas kernels, call(): pl.pallas_call(kernel, out_shape=[jax.ShapeDtypeStruct(shape, jnp.float32...  6.74 us
    ppermute x9, starting transfers between devices, swapped(): lax.ppermute(block[0], axis, even)  5.81 us
    ppermute x9, waiting for transfers between devices, swapped(): lax.ppermute(block[0], axis, even)  3.79 us
    all_to_all x1, starting transfers between devices, body(): sums = lax.all_to_all(sums, ('gx', 'yz'), 0, 0)  3.57 us
  transfers between devices with their start and end apart: 19, of which 7 were waited for; matrix products, arithmetic and copies ran while one was open for 0% of the time, Pallas kernels for 0%

profile of v6, /device:TPU:0, one launch (start us, length us, event | category | flops | bytes accessed | tf_op | source)
XLA Modules:
  0.0 47.4 jit_solution(17286169648175705012)
XLA Ops:
  0.6 2.2 %setup.1 = (f32[512,128]{1,0:T(8,128)S(1)}, f32[512,128]{1,0:T(8,128)S(1)}, f32[512,128]{1,0:T(8,128)S(1)}, f32[512,128]{1,0:T(8,128)S(1)}, f32[192,128]{1,0:T(8...) custom-call(s32[1,128]{1,0:T(1,128)} %bitcast.1, ...), custom_call_target="tpu_custom_call" | custom-call | tf_op jit(solution)/shard_map/setup/pallas_call | solution.py:526
  2.8 6.0 %collective-permute-start.2 = (f32[200,128]{1,0:T(8,128)S(1)}, f32[200,128]{1,0:T(8,128)S(1)}, u32[]{:S(2)}, u32[]{:S(2)}) collective-permute-start(f32[200,128]{1,0:T(8,128)S(1)} %get-tuple-element.35), channel_id=1, source_target_pairs={{0,7},{1,2},{2,1},{3,4},{4,3},{5,6},{6,5},{7,0},{8,15},{9,10},{10,... | collective-permute-start | bytes 307208 | tf_op jit(solution)/shard_map/ppermute | solution.py:541
  8.9 0.0 collective-permute-start.3
  8.9 0.7 %collective-permute-start.1 = (f32[192,128]{1,0:T(8,128)S(1)}, f32[192,128]{1,0:T(8,128)S(1)}, u32[]{:S(2)}, u32[]{:S(2)}) collective-permute-start(f32[192,128]{1,0:T(8,128)S(1)} %get-tuple-element.34), channel_id=1, source_target_pairs={{0,24},{8,16},{16,8},{24,0},{1,25},{9,17},{17,9},{25,1},{2,26},{10... | collective-permute-start | bytes 294920 | tf_op jit(solution)/shard_map/ppermute | solution.py:541
  9.5 1.0 %collective-permute-start = (f32[192,128]{1,0:T(8,128)S(1)}, f32[192,128]{1,0:T(8,128)S(1)}, u32[]{:S(2)}, u32[]{:S(2)}) collective-permute-start(f32[192,128]{1,0:T(8,128)S(1)} %get-tuple-element.34), channel_id=1, source_target_pairs={{0,8},{8,0},{16,24},{24,16},{1,9},{9,1},{17,25},{25,17},{2,10},{10... | collective-permute-start | bytes 294920 | tf_op jit(solution)/shard_map/ppermute | solution.py:541
  10.5 1.3 %collective-permute-done.2.odd_y = f32[200,128]{1,0:T(8,128)S(1)} collective-permute-done((f32[200,128]{1,0:T(8,128)S(1)}, f32[200,128]{1,0:T(8,128)S(1)}, u32[]{:S(2)}, u32[]{:S(2)}) %collective-permute-start.2) | collective-permute-done | bytes 102432 | tf_op jit(solution)/shard_map/ppermute | solution.py:541
  11.8 2.1 %collective-permute-done.3.even_y = f32[200,128]{1,0:T(8,128)S(1)} collective-permute-done((f32[200,128]{1,0:T(8,128)S(1)}, f32[200,128]{1,0:T(8,128)S(1)}, u32[]{:S(2)}, u32[]{:S(2)}) %collective-permute-start.3) | collective-permute-done | bytes 102432 | tf_op jit(solution)/shard_map/ppermute | solution.py:541
  13.9 0.6 %collective-permute-start.5 = (f32[32,128]{1,0:T(8,128)S(1)}, f32[32,128]{1,0:T(8,128)S(1)}, u32[]{:S(2)}, u32[]{:S(2)}) collective-permute-start(f32[32,128]{1,0:T(8,128)S(1)} %corners.1), channel_id=1, source_target_pairs={{0,24},{8,16},{16,8},{24,0},{1,25},{9,17},{17,9},{25,1},{2,26},{10... | collective-permute-start | bytes 49160 | tf_op jit(solution)/shard_map/ppermute | solution.py:541
  14.5 1.1 %collective-permute-start.4 = (f32[32,128]{1,0:T(8,128)S(1)}, f32[32,128]{1,0:T(8,128)S(1)}, u32[]{:S(2)}, u32[]{:S(2)}) collective-permute-start(f32[32,128]{1,0:T(8,128)S(1)} %corners.1), channel_id=1, source_target_pairs={{0,8},{8,0},{16,24},{24,16},{1,9},{9,1},{17,25},{25,17},{2,10},{10... | collective-permute-start | bytes 49160 | tf_op jit(solution)/shard_map/ppermute | solution.py:541
  15.7 0.0 collective-permute-done.1.odd_x
  15.7 0.0 collective-permute-done.even_x
  15.7 1.6 %collective-permute-done.5.odd_shared = f32[32,128]{1,0:T(8,128)S(1)} collective-permute-done((f32[32,128]{1,0:T(8,128)S(1)}, f32[32,128]{1,0:T(8,128)S(1)}, u32[]{:S(2)}, u32[]{:S(2)}) %collective-permute-start.5) | collective-permute-done | bytes 16416 | tf_op jit(solution)/shard_map/ppermute | solution.py:541
  17.3 0.0 collective-permute-done.4.even_shared
  17.3 0.9 %first.1 = (f32[512,128]{1,0:T(8,128)S(1)}, f32[512,128]{1,0:T(8,128)S(1)}, f32[512,128]{1,0:T(8,128)S(1)}, f32[208,128]{1,0:T(8,128)S(1)}, f32[64,128]{1,0:T(8,...) custom-call(f32[512,128]{1,0:T(8,128)S(1)} %get-tuple-element.32.right, ...), custom_call_target="tpu_custom_call" | custom-call | tf_op jit(solution)/shard_map/first/pallas_call | solution.py:526
  18.1 2.3 %collective-permute-start.8 = (f32[64,128]{1,0:T(8,128)S(1)}, f32[64,128]{1,0:T(8,128)S(1)}, u32[]{:S(2)}, u32[]{:S(2)}) collective-permute-start(f32[64,128]{1,0:T(8,128)S(1)} %get-tuple-element.43), channel_id=1, source_target_pairs={{0,7},{1,2},{2,1},{3,4},{4,3},{5,6},{6,5},{7,0},{8,15},{9,10},{10,... | collective-permute-start | bytes 98312 | tf_op jit(solution)/shard_map/ppermute | solution.py:541
  20.5 0.0 collective-permute-start.9
  20.5 0.0 collective-permute-start.7
  20.5 1.5 %collective-permute-start.6 = (f32[64,128]{1,0:T(8,128)S(1)}, f32[64,128]{1,0:T(8,128)S(1)}, u32[]{:S(2)}, u32[]{:S(2)}) collective-permute-start(f32[64,128]{1,0:T(8,128)S(1)} %get-tuple-element.42), channel_id=1, source_target_pairs={{0,8},{8,0},{16,24},{24,16},{1,9},{9,1},{17,25},{25,17},{2,10},{10... | collective-permute-start | bytes 98312 | tf_op jit(solution)/shard_map/ppermute | solution.py:541
  22.0 2.8 %collective-permute-done.8.odd_y = f32[64,128]{1,0:T(8,128)S(1)} collective-permute-done((f32[64,128]{1,0:T(8,128)S(1)}, f32[64,128]{1,0:T(8,128)S(1)}, u32[]{:S(2)}, u32[]{:S(2)}) %collective-permute-start.8) | collective-permute-done | bytes 32800 | tf_op jit(solution)/shard_map/ppermute | solution.py:541
  24.8 0.0 collective-permute-done.9.even_y
  24.8 0.0 collective-permute-done.7.odd_x
  24.8 0.0 collective-permute-done.6.even_x
  24.8 0.8 %second.1 = (f32[512,128]{1,0:T(8,128)S(1)}, f32[512,128]{1,0:T(8,128)S(1)}, f32[64,128]{1,0:T(8,128)S(1)}, f32[64,128]{1,0:T(8,128)S(1)}, f32[64,128]{1,0:T(8,128)S(1)}, /*index=5*/f32[16,128]{1,0:T(8,128)S(1)}) custom-call(f32[512,128]{1,0:T(8,128)S(1)} %get-tuple-element.41.before_image, f32[64,128]{1,0:T(8,128)S(1)} %collective-permute-done.6.even_x, ...), custom_call_target="tpu_custom_call" | custom-call | tf_op jit(solution)/shard_map/second/pallas_call | solution.py:526
  25.6 2.4 %collective-permute-start.12 = (f32[64,128]{1,0:T(8,128)S(1)}, f32[64,128]{1,0:T(8,128)S(1)}, u32[]{:S(2)}, u32[]{:S(2)}) collective-permute-start(f32[64,128]{1,0:T(8,128)S(1)} %get-tuple-element.50), channel_id=1, source_target_pairs={{0,7},{1,2},{2,1},{3,4},{4,3},{5,6},{6,5},{7,0},{8,15},{9,10},{10,... | collective-permute-start | bytes 98312 | tf_op jit(solution)/shard_map/ppermute | solution.py:541
  28.1 0.0 collective-permute-start.13
  28.1 0.0 collective-permute-start.11
  28.1 1.5 %collective-permute-start.10 = (f32[64,128]{1,0:T(8,128)S(1)}, f32[64,128]{1,0:T(8,128)S(1)}, u32[]{:S(2)}, u32[]{:S(2)}) collective-permute-start(f32[64,128]{1,0:T(8,128)S(1)} %get-tuple-element.49), channel_id=1, source_target_pairs={{0,8},{8,0},{16,24},{24,16},{1,9},{9,1},{17,25},{25,17},{2,10},{10... | collective-permute-start | bytes 98312 | tf_op jit(solution)/shard_map/ppermute | solution.py:541
  29.6 2.7 %collective-permute-done.12.odd_y = f32[64,128]{1,0:T(8,128)S(1)} collective-permute-done((f32[64,128]{1,0:T(8,128)S(1)}, f32[64,128]{1,0:T(8,128)S(1)}, u32[]{:S(2)}, u32[]{:S(2)}) %collective-permute-start.12) | collective-permute-done | bytes 32800 | tf_op jit(solution)/shard_map/ppermute | solution.py:541
  32.4 0.0 collective-permute-done.13.even_y
  32.4 0.0 collective-permute-done.11.odd_x
  32.4 0.0 collective-permute-done.10.even_x
  32.4 0.8 %third.1 = (f32[512,128]{1,0:T(8,128)S(1)}, f32[512,128]{1,0:T(8,128)S(1)}, f32[64,128]{1,0:T(8,128)S(1)}, f32[64,128]{1,0:T(8,128)S(1)}, f32[64,128]{1,0:T(8,128)S(1)}, /*index=5*/f32[24,128]{1,0:T(8,128)S(1)}) custom-call(f32[512,128]{1,0:T(8,128)S(1)} %get-tuple-element.48.before_image, f32[64,128]{1,0:T(8,128)S(1)} %collective-permute-done.10.even_x, ...), custom_call_target="tpu_custom_call" | custom-call | tf_op jit(solution)/shard_map/third/pallas_call | solution.py:526
  33.2 0.7 %sums.1 = f32[32,2,128]{2,1,0:T(2,128)} custom-call(f32[8,128]{1,0:T(8,128)S(1)} %get-tuple-element.58.moments0, f32[16,128]{1,0:T(8,128)S(1)} %get-tuple-element.59.moments1, f32[24,128]{1,0:T(8,128)S(1)} %get-tuple-element.60.moments2), custom_call_target="tpu_custom_call" | custom-call | tf_op jit(solution)/shard_map/sums/pallas_call | solution.py:526
  33.9 3.6 %all-to-all-start = ((f32[32,2,128]{2,1,0:T(2,128)}), f32[32,2,128]{2,1,0:T(2,128)S(1)}, u32[]{:S(2)}, u32[]{:S(2)}) async-start(f32[32,2,128]{2,1,0:T(2,128)} %sums.1), calls=%async_computation | async-start | bytes 65536 | tf_op jit(solution)/shard_map/all_to_all | solution.py:577
  37.5 4.6 %collective-permute-start.16 = (f32[64,128]{1,0:T(8,128)S(1)}, f32[64,128]{1,0:T(8,128)S(1)}, u32[]{:S(2)}, u32[]{:S(2)}) collective-permute-start(f32[64,128]{1,0:T(8,128)S(1)} %get-tuple-element.55), channel_id=1, source_target_pairs={{0,7},{1,2},{2,1},{3,4},{4,3},{5,6},{6,5},{7,0},{8,15},{9,10},{10,... | collective-permute-start | bytes 98312 | tf_op jit(solution)/shard_map/ppermute | solution.py:541
  42.1 0.0 collective-permute-start.17
  42.1 1.0 %collective-permute-start.15 = (f32[64,128]{1,0:T(8,128)S(1)}, f32[64,128]{1,0:T(8,128)S(1)}, u32[]{:S(2)}, u32[]{:S(2)}) collective-permute-start(f32[64,128]{1,0:T(8,128)S(1)} %get-tuple-element.54), channel_id=1, source_target_pairs={{0,24},{8,16},{16,8},{24,0},{1,25},{9,17},{17,9},{25,1},{2,26},{10... | collective-permute-start | bytes 98312 | tf_op jit(solution)/shard_map/ppermute | solution.py:541
  43.1 0.6 %collective-permute-start.14 = (f32[64,128]{1,0:T(8,128)S(1)}, f32[64,128]{1,0:T(8,128)S(1)}, u32[]{:S(2)}, u32[]{:S(2)}) collective-permute-start(f32[64,128]{1,0:T(8,128)S(1)} %get-tuple-element.54), channel_id=1, source_target_pairs={{0,8},{8,0},{16,24},{24,16},{1,9},{9,1},{17,25},{25,17},{2,10},{10... | collective-permute-start | bytes 98312 | tf_op jit(solution)/shard_map/ppermute | solution.py:541
  43.7 0.6 %collective-permute-done.16.odd_y = f32[64,128]{1,0:T(8,128)S(1)} collective-permute-done((f32[64,128]{1,0:T(8,128)S(1)}, f32[64,128]{1,0:T(8,128)S(1)}, u32[]{:S(2)}, u32[]{:S(2)}) %collective-permute-start.16) | collective-permute-done | bytes 32800 | tf_op jit(solution)/shard_map/ppermute | solution.py:541
  44.4 1.7 %collective-permute-done.17.even_y = f32[64,128]{1,0:T(8,128)S(1)} collective-permute-done((f32[64,128]{1,0:T(8,128)S(1)}, f32[64,128]{1,0:T(8,128)S(1)}, u32[]{:S(2)}, u32[]{:S(2)}) %collective-permute-start.17) | collective-permute-done | bytes 32800 | tf_op jit(solution)/shard_map/ppermute | solution.py:541
  46.0 0.0 collective-permute-done.15.odd_x
  46.0 0.0 collective-permute-done.14.even_x
  46.0 0.0 all-to-all-done.sums
  46.0 1.3 %last.1 = (f32[1,1,128,512]{3,2,1,0:T(8,128)}, f32[1,1,128,512]{3,2,1,0:T(8,128)}) custom-call(f32[512,128]{1,0:T(8,128)S(1)} %get-tuple-element.53.before_image, f32[64,128]{1,0:T(8,128)S(1)} %collective-permute-done.14.even_x, f32[64,128]{1,0:T(8,128)S(1)} %collective-permute-done.15.odd_x, f32[64,128]{1,0:T(8,128)S(1)} %collective-permute-done.16.odd_y, ...), custom_call_target="tpu_custom_call" | custom-call | tf_op jit(solution)/shard_map/last/pallas_call | solution.py:526
  (1 shorter events, 0.0 us)
Async XLA Ops:
  2.8 9.0 %collective-permute-start.2 = (f32[200,128]{1,0:T(8,128)S(1)}, f32[200,128]{1,0:T(8,128)S(1)}, u32[]{:S(2)}, u32[]{:S(2)}) collective-permute-start(f32[200,128]{1,0:T(8,128)S(1)} %get-tuple-element.35), channel_id=1, source_target_pairs={{0,7},{1,2},{2,1},{3,4},{4,3},{5,6},{6,5},{7,0},{8,15},{9,10},{10,... | collective-permute-start | bytes 307208 | tf_op jit(solution)/shard_map/ppermute | solution.py:541
  8.9 5.1 %collective-permute-start.3 = (f32[200,128]{1,0:T(8,128)S(1)}, f32[200,128]{1,0:T(8,128)S(1)}, u32[]{:S(2)}, u32[]{:S(2)}) collective-permute-start(f32[200,128]{1,0:T(8,128)S(1)} %get-tuple-element.36), channel_id=1, source_target_pairs={{0,1},{1,0},{2,3},{3,2},{4,5},{5,4},{6,7},{7,6},{8,9},{9,8},{10,11... | collective-permute-start | bytes 307208 | tf_op jit(solution)/shard_map/ppermute | solution.py:541
  8.9 6.8 %collective-permute-start.1 = (f32[192,128]{1,0:T(8,128)S(1)}, f32[192,128]{1,0:T(8,128)S(1)}, u32[]{:S(2)}, u32[]{:S(2)}) collective-permute-start(f32[192,128]{1,0:T(8,128)S(1)} %get-tuple-element.34), channel_id=1, source_target_pairs={{0,24},{8,16},{16,8},{24,0},{1,25},{9,17},{17,9},{25,1},{2,26},{10... | collective-permute-start | bytes 294920 | tf_op jit(solution)/shard_map/ppermute | solution.py:541
  9.5 6.1 %collective-permute-start = (f32[192,128]{1,0:T(8,128)S(1)}, f32[192,128]{1,0:T(8,128)S(1)}, u32[]{:S(2)}, u32[]{:S(2)}) collective-permute-start(f32[192,128]{1,0:T(8,128)S(1)} %get-tuple-element.34), channel_id=1, source_target_pairs={{0,8},{8,0},{16,24},{24,16},{1,9},{9,1},{17,25},{25,17},{2,10},{10... | collective-permute-start | bytes 294920 | tf_op jit(solution)/shard_map/ppermute | solution.py:541
  13.9 3.3 %collective-permute-start.5 = (f32[32,128]{1,0:T(8,128)S(1)}, f32[32,128]{1,0:T(8,128)S(1)}, u32[]{:S(2)}, u32[]{:S(2)}) collective-permute-start(f32[32,128]{1,0:T(8,128)S(1)} %corners.1), channel_id=1, source_target_pairs={{0,24},{8,16},{16,8},{24,0},{1,25},{9,17},{17,9},{25,1},{2,26},{10... | collective-permute-start | bytes 49160 | tf_op jit(solution)/shard_map/ppermute | solution.py:541
  14.5 2.8 %collective-permute-start.4 = (f32[32,128]{1,0:T(8,128)S(1)}, f32[32,128]{1,0:T(8,128)S(1)}, u32[]{:S(2)}, u32[]{:S(2)}) collective-permute-start(f32[32,128]{1,0:T(8,128)S(1)} %corners.1), channel_id=1, source_target_pairs={{0,8},{8,0},{16,24},{24,16},{1,9},{9,1},{17,25},{25,17},{2,10},{10... | collective-permute-start | bytes 49160 | tf_op jit(solution)/shard_map/ppermute | solution.py:541
  18.1 6.7 %collective-permute-start.8 = (f32[64,128]{1,0:T(8,128)S(1)}, f32[64,128]{1,0:T(8,128)S(1)}, u32[]{:S(2)}, u32[]{:S(2)}) collective-permute-start(f32[64,128]{1,0:T(8,128)S(1)} %get-tuple-element.43), channel_id=1, source_target_pairs={{0,7},{1,2},{2,1},{3,4},{4,3},{5,6},{6,5},{7,0},{8,15},{9,10},{10,... | collective-permute-start | bytes 98312 | tf_op jit(solution)/shard_map/ppermute | solution.py:541
  20.5 4.3 %collective-permute-start.9 = (f32[64,128]{1,0:T(8,128)S(1)}, f32[64,128]{1,0:T(8,128)S(1)}, u32[]{:S(2)}, u32[]{:S(2)}) collective-permute-start(f32[64,128]{1,0:T(8,128)S(1)} %get-tuple-element.44), channel_id=1, source_target_pairs={{0,1},{1,0},{2,3},{3,2},{4,5},{5,4},{6,7},{7,6},{8,9},{9,8},{10,11... | collective-permute-start | bytes 98312 | tf_op jit(solution)/shard_map/ppermute | solution.py:541
  20.5 4.3 %collective-permute-start.7 = (f32[64,128]{1,0:T(8,128)S(1)}, f32[64,128]{1,0:T(8,128)S(1)}, u32[]{:S(2)}, u32[]{:S(2)}) collective-permute-start(f32[64,128]{1,0:T(8,128)S(1)} %get-tuple-element.42), channel_id=1, source_target_pairs={{0,24},{8,16},{16,8},{24,0},{1,25},{9,17},{17,9},{25,1},{2,26},{10... | collective-permute-start | bytes 98312 | tf_op jit(solution)/shard_map/ppermute | solution.py:541
  20.5 4.3 %collective-permute-start.6 = (f32[64,128]{1,0:T(8,128)S(1)}, f32[64,128]{1,0:T(8,128)S(1)}, u32[]{:S(2)}, u32[]{:S(2)}) collective-permute-start(f32[64,128]{1,0:T(8,128)S(1)} %get-tuple-element.42), channel_id=1, source_target_pairs={{0,8},{8,0},{16,24},{24,16},{1,9},{9,1},{17,25},{25,17},{2,10},{10... | collective-permute-start | bytes 98312 | tf_op jit(solution)/shard_map/ppermute | solution.py:541
  25.6 6.7 %collective-permute-start.12 = (f32[64,128]{1,0:T(8,128)S(1)}, f32[64,128]{1,0:T(8,128)S(1)}, u32[]{:S(2)}, u32[]{:S(2)}) collective-permute-start(f32[64,128]{1,0:T(8,128)S(1)} %get-tuple-element.50), channel_id=1, source_target_pairs={{0,7},{1,2},{2,1},{3,4},{4,3},{5,6},{6,5},{7,0},{8,15},{9,10},{10,... | collective-permute-start | bytes 98312 | tf_op jit(solution)/shard_map/ppermute | solution.py:541
  28.1 4.3 %collective-permute-start.13 = (f32[64,128]{1,0:T(8,128)S(1)}, f32[64,128]{1,0:T(8,128)S(1)}, u32[]{:S(2)}, u32[]{:S(2)}) collective-permute-start(f32[64,128]{1,0:T(8,128)S(1)} %get-tuple-element.51), channel_id=1, source_target_pairs={{0,1},{1,0},{2,3},{3,2},{4,5},{5,4},{6,7},{7,6},{8,9},{9,8},{10,11... | collective-permute-start | bytes 98312 | tf_op jit(solution)/shard_map/ppermute | solution.py:541
  28.1 4.3 %collective-permute-start.11 = (f32[64,128]{1,0:T(8,128)S(1)}, f32[64,128]{1,0:T(8,128)S(1)}, u32[]{:S(2)}, u32[]{:S(2)}) collective-permute-start(f32[64,128]{1,0:T(8,128)S(1)} %get-tuple-element.49), channel_id=1, source_target_pairs={{0,24},{8,16},{16,8},{24,0},{1,25},{9,17},{17,9},{25,1},{2,26},{10... | collective-permute-start | bytes 98312 | tf_op jit(solution)/shard_map/ppermute | solution.py:541
  28.1 4.3 %collective-permute-start.10 = (f32[64,128]{1,0:T(8,128)S(1)}, f32[64,128]{1,0:T(8,128)S(1)}, u32[]{:S(2)}, u32[]{:S(2)}) collective-permute-start(f32[64,128]{1,0:T(8,128)S(1)} %get-tuple-element.49), channel_id=1, source_target_pairs={{0,8},{8,0},{16,24},{24,16},{1,9},{9,1},{17,25},{25,17},{2,10},{10... | collective-permute-start | bytes 98312 | tf_op jit(solution)/shard_map/ppermute | solution.py:541
  33.9 12.1 %all-to-all-start = ((f32[32,2,128]{2,1,0:T(2,128)}), f32[32,2,128]{2,1,0:T(2,128)S(1)}, u32[]{:S(2)}, u32[]{:S(2)}) async-start(f32[32,2,128]{2,1,0:T(2,128)} %sums.1), calls=%async_computation | async-start | bytes 65536 | tf_op jit(solution)/shard_map/all_to_all | solution.py:577
  37.5 6.9 %collective-permute-start.16 = (f32[64,128]{1,0:T(8,128)S(1)}, f32[64,128]{1,0:T(8,128)S(1)}, u32[]{:S(2)}, u32[]{:S(2)}) collective-permute-start(f32[64,128]{1,0:T(8,128)S(1)} %get-tuple-element.55), channel_id=1, source_target_pairs={{0,7},{1,2},{2,1},{3,4},{4,3},{5,6},{6,5},{7,0},{8,15},{9,10},{10,... | collective-permute-start | bytes 98312 | tf_op jit(solution)/shard_map/ppermute | solution.py:541
  42.1 3.9 %collective-permute-start.17 = (f32[64,128]{1,0:T(8,128)S(1)}, f32[64,128]{1,0:T(8,128)S(1)}, u32[]{:S(2)}, u32[]{:S(2)}) collective-permute-start(f32[64,128]{1,0:T(8,128)S(1)} %get-tuple-element.56), channel_id=1, source_target_pairs={{0,1},{1,0},{2,3},{3,2},{4,5},{5,4},{6,7},{7,6},{8,9},{9,8},{10,11... | collective-permute-start | bytes 98312 | tf_op jit(solution)/shard_map/ppermute | solution.py:541
  42.1 3.9 %collective-permute-start.15 = (f32[64,128]{1,0:T(8,128)S(1)}, f32[64,128]{1,0:T(8,128)S(1)}, u32[]{:S(2)}, u32[]{:S(2)}) collective-permute-start(f32[64,128]{1,0:T(8,128)S(1)} %get-tuple-element.54), channel_id=1, source_target_pairs={{0,24},{8,16},{16,8},{24,0},{1,25},{9,17},{17,9},{25,1},{2,26},{10... | collective-permute-start | bytes 98312 | tf_op jit(solution)/shard_map/ppermute | solution.py:541
  43.1 2.9 %collective-permute-start.14 = (f32[64,128]{1,0:T(8,128)S(1)}, f32[64,128]{1,0:T(8,128)S(1)}, u32[]{:S(2)}, u32[]{:S(2)}) collective-permute-start(f32[64,128]{1,0:T(8,128)S(1)} %get-tuple-element.54), channel_id=1, source_target_pairs={{0,8},{8,0},{16,24},{24,16},{1,9},{9,1},{17,25},{25,17},{2,10},{10... | collective-permute-start | bytes 98312 | tf_op jit(solution)/shard_map/ppermute | solution.py:541

commit v7 on v6

--- a/solution.py
+++ b/solution.py
@@ -184,16 +184,15 @@
     ordered.wait()
     slot_rows[...] = jnp.broadcast_to(order[...].astype(jnp.float32), slot_rows.shape)
     chosen = selection(slot_rows)
-    copies[0].wait()
+    for copy in copies:
+        copy.wait()
     spread[...] = to_grid(chosen, held[0])
-    copies[1].wait()
     mass[...] = to_grid(chosen, held[1])
     for a in range(8):
         for b in range(8):
             weight = last_weight * float(WEIGHTS[a] * WEIGHTS[b])
             spread[row(a, b), :] *= weight
             mass[row(a, b), :] *= weight
-    copies[2].wait()
     right[...] = to_grid(chosen, held[2])
     squares = (DERIVATIVE * DERIVATIVE).T
     for b in range(8):
@@ -312,14 +311,15 @@
         lowest_to_highest(odd, to_even, to_odd, pl.ds(8 * a, 8), faces[0][a], faces[1][a])
 
 
-def operate(values, spread, mass, image):
+def streamwise(lines, b, spread, mass, image):
+    slopes = along(DERIVATIVE, lines, -1)
+    back = along(DERIVATIVE.T, [slopes[a] * spread[row(a, b), :] for a in range(8)], -1)
+    for a in range(8):
+        image[row(a, b), :] = back[a] + mass[row(a, b), :] * lines[a]
+
+
+def operate(values, spread, image):
     forward, backward = DERIVATIVE, DERIVATIVE.T
-    for b in range(8):
-        lines = [values[row(a, b), :] for a in range(8)]
-        slopes = along(forward, lines, -1)
-        back = along(backward, [slopes[a] * spread[row(a, b), :] for a in range(8)], -1)
-        for a in range(8):
-            image[row(a, b), :] = back[a] + mass[row(a, b), :] * lines[a]
     for a in range(8):
         slopes = along(forward, [values[row(a, b), :] for b in range(8)], -1)
         back = along(backward, [slopes[b] * spread[row(a, b), :] for b in range(8)], -1)
@@ -353,20 +353,28 @@
     return int(a in (0, 7)) + int(b in (0, 7))
 
 
-def first_kernel(
-    right, diagonal, even_x, odd_x, odd_y, even_y, even_shared, odd_shared, spread, mass, shifts,
-    whole_diagonal, values, image, outer, face_x, to_even, to_odd, moments,
+def early_kernel(
+    right, diagonal, even_x, odd_x, odd_y, even_y, spread, mass,
+    whole_diagonal, jacobi, values, image, outer, moments,
 ):
-    received = (even_x, odd_x, even_y, odd_y, even_shared, odd_shared)
+    received = (even_x, odd_x, even_y, odd_y)
+    first = lane_index() < HALF
     sums = [jnp.zeros((8, LANES), jnp.float32)] * 3
-    for a in range(8):
-        for b in range(8):
+    for b in range(8):
+        lines = []
+        for a in range(8):
             source = assembled(a, b, right, received, 0)
             scale = assembled(a, b, diagonal, received, 1)
-            value = source / scale
+            inverse = 1.0 / scale
+            value = source * inverse
+            if ends(a, b) == 2:
+                value = jnp.where(first, 0.0, value) if a == 0 else jnp.where(first, value, 0.0)
             whole_diagonal[row(a, b), :] = scale
+            jacobi[row(a, b), :] = inverse
             values[row(a, b), :] = value
             sums[ends(a, b)] = sums[ends(a, b)] + source * value
+            lines.append(value)
+        streamwise(lines, b, spread, mass, image)
     moments[...] = weighted(sums)
     for b in range(8):
         outer[pl.ds(8 * b, 8), :] = pltpu.roll(
@@ -377,45 +385,105 @@
             outer[pl.ds(64 + 72 * side + 8 * k, 8), :] = from_y(
                 even_y, odd_y, 7 * side, pl.ds(128 + 8 * k, 8)
             )
-    operate(values, spread, mass, image)
+    operate(values, spread, image)
+
+
+def add_packed(grid, b, value):
+    first = lane_index() < HALF
+    grid[row(0, b), :] += jnp.where(first, value, 0.0)
+    grid[row(7, b), :] += jnp.where(first, 0.0, value)
+
+
+def first_kernel(
+    right, diagonal, even_x, odd_x, odd_y, even_y, even_shared, odd_shared, spread, mass, shifts,
+    outer, early_diagonal, early_jacobi, early_values, early_image, early_moments,
+    whole_diagonal, jacobi, values, image, face_x, to_even, to_odd, moments,
+):
+    received = (even_x, odd_x, even_y, odd_y, even_shared, odd_shared)
+    first = lane_index() < HALF
+    corners = []
+    total = jnp.zeros((8, LANES), jnp.float32)
+    for b in (0, 7):
+        packed = []
+        for a in (0, 7):
+            source = assembled(a, b, right, received, 0)
+            scale = assembled(a, b, diagonal, received, 1)
+            inverse = 1.0 / scale
+            value = source * inverse
+            whole_diagonal[row(a, b), :] = scale
+            jacobi[row(a, b), :] = inverse
+            values[row(a, b), :] = value
+            packed.append((value, source * value))
+        corners.append(jnp.where(first, packed[0][0], packed[1][0]))
+        total = total + jnp.where(first, packed[0][1], packed[1][1])
+    zero = jnp.zeros((8, LANES), jnp.float32)
+    moments[...] = early_moments[...] + weighted([zero, zero, total])
+    for side, corner in enumerate(corners):
+        b = 7 * side
+        slopes = []
+        for q in range(8):
+            slope = jnp.where(first, float(DERIVATIVE[q, 0]), float(DERIVATIVE[q, 7]))
+            slopes.append(spread[row(q, b), :] * (slope * corner))
+        back = along(DERIVATIVE.T, slopes, -1)
+        for a in range(8):
+            image[row(a, b), :] += join_vertical_packed(back[a])
+    slopes = []
+    for q in range(8):
+        slope = corners[0] * float(DERIVATIVE[q, 0]) + corners[1] * float(DERIVATIVE[q, 7])
+        slopes.append(packed_x(spread, q) * slope)
+    back = along(DERIVATIVE.T, slopes, -1)
+    for side, corner in enumerate(corners):
+        b = 7 * side
+        slope = shifted_sum(shifts, 0, corner) * packed_x(spread, b)
+        back[b] = back[b] + shifted_sum(shifts, 64, slope) + packed_x(mass, b) * corner
+    for b in range(8):
+        add_packed(image, b, join_vertical_packed(back[b]))
     send_faces(image, values, outer, shifts, face_x, to_even, to_odd)
 
 
-def next_values(before_image, received, diagonal, before, values):
+def next_values(before_image, received, diagonal, jacobi, before, spread, mass, values, image):
     cross = [jnp.zeros((8, LANES), jnp.float32)] * 3
     square = [jnp.zeros((8, LANES), jnp.float32)] * 3
-    for a in range(8):
-        for b in range(8):
-            scale = diagonal[row(a, b), :]
+    for b in range(8):
+        lines = []
+        for a in range(8):
             old = before[row(a, b), :]
-            value = assembled(a, b, before_image, received, 0) / scale - old
+            scaled = assembled(a, b, before_image, received, 0) - diagonal[row(a, b), :] * old
+            value = scaled * jacobi[row(a, b), :]
             values[row(a, b), :] = value
-            scaled = scale * value
             kind = ends(a, b)
             cross[kind] = cross[kind] + scaled * old
             square[kind] = square[kind] + scaled * value
+            lines.append(value)
+        streamwise(lines, b, spread, mass, image)
     return weighted(cross), weighted(square)
 
 
 def second_kernel(
-    before_image, even_x, odd_x, odd_y, even_y, diagonal, before, spread, mass, shifts, outer,
+    before_image, even_x, odd_x, odd_y, even_y, diagonal, jacobi, before, spread, mass,
+    shifts, outer,
     values, image, face_x, to_even, to_odd, moments,
 ):
     received = (even_x, odd_x, even_y, odd_y)
-    cross, square = next_values(before_image, received, diagonal, before, values)
+    cross, square = next_values(
+        before_image, received, diagonal, jacobi, before, spread, mass, values, image
+    )
     moments[pl.ds(0, 8), :] = cross
     moments[pl.ds(8, 8), :] = square
-    operate(values, spread, mass, image)
+    operate(values, spread, image)
     send_faces(image, values, outer, shifts, face_x, to_even, to_odd)
 
 
 def third_kernel(
-    before_image, even_x, odd_x, odd_y, even_y, diagonal, before, spread, mass, shifts, outer,
+    before_image, even_x, odd_x, odd_y, even_y, diagonal, jacobi, before, spread, mass,
+    shifts, outer,
     values, image, face_x, to_even, to_odd, moments,
 ):
     received = (even_x, odd_x, even_y, odd_y)
-    cross, square = next_values(before_image, received, diagonal, before, values)
-    energy = operate(values, spread, mass, image)
+    cross, square = next_values(
+        before_image, received, diagonal, jacobi, before, spread, mass, values, image
+    )
+    energy = operate(values, spread, image)
     send_faces(image, values, outer, shifts, face_x, to_even, to_odd)
     for k, part in enumerate((cross, square, energy)):
         moments[pl.ds(8 * k, 8), :] = part
@@ -482,42 +550,61 @@
     return result[:3], precond
 
 
-def last_kernel(
-    before_image, even_x, odd_x, odd_y, even_y, diagonal, values0, values1, values2, sums,
-    slot_rows, solution, residual, solution_grid, residual_grid,
+def to_slots(chosen, grid):
+    total = None
+    for part in parts_of(grid):
+        term = lax.dot_general(
+            chosen, part, (((1,), (1,)), ((), ())), preferred_element_type=jnp.float32
+        )
+        total = term if total is None else total + term
+    return total
+
+
+def solution_kernel(
+    values0, values1, values2, sums, slot_rows, solution, precond_rows, solution_grid
 ):
-    received = (even_x, odd_x, even_y, odd_y)
     line = jnp.sum(sums[...], 0)[0:1]
     lane = lax.broadcasted_iota(jnp.int32, (1, LANES), 1)
     moments = [
         jnp.sum(jnp.where(lane == k, line, 0.0), 1, keepdims=True) for k in range(6)
     ]
     result, precond = recurrence(moments)
-    spread_out = lambda scalar: jnp.broadcast_to(scalar, (8, LANES))
-    result = [spread_out(entry) for entry in result]
-    precond = [spread_out(entry) for entry in precond]
+    result = [jnp.broadcast_to(entry, (8, LANES)) for entry in result]
+    for k in range(4):
+        precond_rows[pl.ds(8 * k, 8), :] = jnp.broadcast_to(precond[k], (8, LANES))
     for a in range(8):
         for b in range(8):
             rows = row(a, b)
-            basis = [values0[rows, :], values1[rows, :], values2[rows, :]]
-            scale = diagonal[rows, :]
-            image = assembled(a, b, before_image, received, 0) - scale * basis[2]
-            near = result[0] * basis[0] + result[1] * basis[1] + result[2] * basis[2]
-            far = precond[0] * basis[0] + precond[1] * basis[1] + precond[2] * basis[2]
-            solution_grid[rows, :] = near
-            residual_grid[rows, :] = scale * far + precond[3] * image
+            solution_grid[rows, :] = (
+                result[0] * values0[rows, :]
+                + result[1] * values1[rows, :]
+                + result[2] * values2[rows, :]
+            )
     chosen = selection(slot_rows).T.astype(jnp.bfloat16)
-    for grid, out in ((solution_grid, solution), (residual_grid, residual)):
-        total = None
-        for part in parts_of(grid[...]):
-            term = lax.dot_general(
-                chosen, part, (((1,), (1,)), ((), ())), preferred_element_type=jnp.float32
+    solution[0, 0] = to_slots(chosen, solution_grid[...])
+
+
+def last_kernel(
+    before_image, even_x, odd_x, odd_y, even_y, diagonal, values0, values1, values2, precond_rows,
+    slot_rows, residual, residual_grid,
+):
+    received = (even_x, odd_x, even_y, odd_y)
+    precond = [precond_rows[pl.ds(8 * k, 8), :] for k in range(4)]
+    for a in range(8):
+        for b in range(8):
+            rows = row(a, b)
+            far = (
+                precond[0] * values0[rows, :]
+                + precond[1] * values1[rows, :]
+                + (precond[2] - precond[3]) * values2[rows, :]
             )
-            total = term if total is None else total + term
-        out[0, 0] = total
-
-
-def call(kernel, name, shapes, scratch, *operands, outside=0):
+            image = assembled(a, b, before_image, received, 0)
+            residual_grid[rows, :] = diagonal[rows, :] * far + precond[3] * image
+    chosen = selection(slot_rows).T.astype(jnp.bfloat16)
+    residual[0, 0] = to_slots(chosen, residual_grid[...])
+
+
+def call(kernel, name, shapes, scratch, *operands, outside=0, aliases=None):
     places = [pltpu.HBM] * outside + [pltpu.VMEM] * (len(operands) - outside)
     operands = [
         pltpu.with_memory_space_constraint(operand, place) if place == pltpu.HBM else operand
@@ -529,6 +616,7 @@
         in_specs=[pl.BlockSpec(memory_space=place) for place in places],
         out_specs=[pl.BlockSpec(memory_space=pltpu.VMEM)] * len(shapes),
         scratch_shapes=scratch,
+        input_output_aliases=aliases or {},
         compiler_params=pltpu.CompilerParams(vmem_limit_bytes=VMEM_BYTES),
         name=name,
     )(*operands)
@@ -559,27 +647,38 @@
     received_x, received_y = swapped((out_x, out_x), "gx"), swapped(sent_y, "yz")[::-1]
     [shared] = call(corners_kernel, "corners", [(32, LANES)], [], corners, *received_y)
     received = (*received_x, *received_y, *swapped((shared, shared), "gx"))
-    diagonal, values0, image, outer, out_x, *sent_y, moments0 = call(
-        first_kernel, "first", [grid] * 3 + [(208, LANES)] + [face] * 3 + [tile], [],
-        right, diagonal, *received, spread, mass, shifts,
+    *early, outer, moments0 = call(
+        early_kernel, "early", [grid] * 4 + [(208, LANES), tile], [],
+        right, diagonal, *received_x, *received_y, spread, mass,
+    )
+    diagonal, jacobi, values0, image, out_x, *sent_y, moments0 = call(
+        first_kernel, "first", [grid] * 4 + [face] * 3 + [tile], [],
+        right, diagonal, *received, spread, mass, shifts, outer, *early, moments0,
+        aliases={12: 0, 13: 1, 14: 2, 15: 3},
     )
     received = (*swapped((out_x, out_x), "gx"), *swapped(sent_y, "yz")[::-1])
     values1, image, out_x, *sent_y, moments1 = call(
         second_kernel, "second", [grid] * 2 + [face] * 3 + [(16, LANES)], [],
-        image, *received, diagonal, values0, spread, mass, shifts, outer,
+        image, *received, diagonal, jacobi, values0, spread, mass, shifts, outer,
     )
     received = (*swapped((out_x, out_x), "gx"), *swapped(sent_y, "yz")[::-1])
     values2, image, out_x, *sent_y, moments2 = call(
         third_kernel, "third", [grid] * 2 + [face] * 3 + [(24, LANES)], [],
-        image, *received, diagonal, values1, spread, mass, shifts, outer,
+        image, *received, diagonal, jacobi, values1, spread, mass, shifts, outer,
     )
     [sums] = call(sums_kernel, "sums", [(devices, 2, LANES)], [], moments0, moments1, moments2)
     sums = lax.all_to_all(sums, ("gx", "yz"), 0, 0)
     received = (*swapped((out_x, out_x), "gx"), *swapped(sent_y, "yz")[::-1])
-    return call(
-        last_kernel, "last", [forcing.shape] * 2, [pltpu.VMEM(grid, jnp.float32)] * 2,
-        image, *received, diagonal, values0, values1, values2, sums, slot_rows,
-    )
+    result, precond = call(
+        solution_kernel, "solution", [forcing.shape, (32, LANES)],
+        [pltpu.VMEM(grid, jnp.float32)],
+        values0, values1, values2, sums, slot_rows,
+    )
+    [residual] = call(
+        last_kernel, "last", [forcing.shape], [pltpu.VMEM(grid, jnp.float32)],
+        image, *received, diagonal, values0, values1, values2, precond, slot_rows,
+    )
+    return result, residual
 
 
 def solution(mesh):

time: 47.5 us -> 46.5 us (0.979)
  waiting for transfers between devices: 12.9 us -> 10.9 us
  Pallas kernels: 6.74 us -> 7.68 us
    ppermute x9, waiting for transfers between devices: 3.79 us -> 2.27 us  [swapped(): lax.ppermute(block[0], axis, even)]
    ppermute x9, waiting for transfers between devices: 9.1 us -> 7.65 us  [swapped(): lax.ppermute(block[1], axis, odd)]
    all_to_all x1, waiting for transfers between devices: 0.01 us -> 0.99 us  [body(): sums = lax.all_to_all(sums, ('gx', 'yz'), 0, 0)]
    pallas_call x7 -> x9, Pallas kernels: 6.74 us -> 7.68 us  [call(): pl.pallas_call(kernel, out_shape=[jax.ShapeDtypeStruct(shape, jnp.float32...]
  transfers between devices with their start and end apart: 19 -> 19, of which waited for: 7 -> 7; matrix products, arithmetic and copies ran while one was open for 0% -> 0% of each run, Pallas kernels for 0% -> 4%
where the time goes in v7:
time: 46.5 us; the launch traced here: 46.3 us
  starting transfers between devices  27 us (58%)
  waiting for transfers between devices  10.9 us (23%)
  Pallas kernels  7.68 us (17%)
  between operations  0.68 us (1%)
    ppermute x9, starting transfers between devices, swapped(): lax.ppermute(block[1], axis, odd)  17.7 us
    pallas_call x9, Pallas kernels, call(): pl.pallas_call(kernel, out_shape=[jax.ShapeDtypeStruct(shape, jnp.float32...  7.68 us
    ppermute x9, waiting for transfers between devices, swapped(): lax.ppermute(block[1], axis, odd)  7.65 us
    ppermute x9, starting transfers between devices, swapped(): lax.ppermute(block[0], axis, even)  5.81 us
    all_to_all x1, starting transfers between devices, body(): sums = lax.all_to_all(sums, ('gx', 'yz'), 0, 0)  3.57 us
    ppermute x9, waiting for transfers between devices, swapped(): lax.ppermute(block[0], axis, even)  2.27 us
    all_to_all x1, waiting for transfers between devices, body(): sums = lax.all_to_all(sums, ('gx', 'yz'), 0, 0)  0.99 us
  transfers between devices with their start and end apart: 19, of which 7 were waited for; matrix products, arithmetic and copies ran while one was open for 0% of the time, Pallas kernels for 4%

profile of v7, /device:TPU:0, one launch (start us, length us, event | category | flops | bytes accessed | tf_op | source)
XLA Modules:
  0.0 46.3 jit_solution(2574196017116441819)
XLA Ops:
  0.6 1.9 %setup.1 = (f32[512,128]{1,0:T(8,128)S(1)}, f32[512,128]{1,0:T(8,128)S(1)}, f32[512,128]{1,0:T(8,128)S(1)}, f32[512,128]{1,0:T(8,128)S(1)}, f32[192,128]{1,0:T(8...) custom-call(s32[1,128]{1,0:T(1,128)} %bitcast.1, ...), custom_call_target="tpu_custom_call" | custom-call | tf_op jit(solution)/shard_map/setup/pallas_call | solution.py:613
  2.6 6.0 %collective-permute-start.2 = (f32[200,128]{1,0:T(8,128)S(1)}, f32[200,128]{1,0:T(8,128)S(1)}, u32[]{:S(2)}, u32[]{:S(2)}) collective-permute-start(f32[200,128]{1,0:T(8,128)S(1)} %get-tuple-element.43), channel_id=1, source_target_pairs={{0,7},{1,2},{2,1},{3,4},{4,3},{5,6},{6,5},{7,0},{8,15},{9,10},{10,... | collective-permute-start | bytes 307208 | tf_op jit(solution)/shard_map/ppermute | solution.py:629
  8.6 0.0 collective-permute-start.3
  8.6 0.7 %collective-permute-start.1 = (f32[192,128]{1,0:T(8,128)S(1)}, f32[192,128]{1,0:T(8,128)S(1)}, u32[]{:S(2)}, u32[]{:S(2)}) collective-permute-start(f32[192,128]{1,0:T(8,128)S(1)} %get-tuple-element.42), channel_id=1, source_target_pairs={{0,24},{8,16},{16,8},{24,0},{1,25},{9,17},{17,9},{25,1},{2,26},{10... | collective-permute-start | bytes 294920 | tf_op jit(solution)/shard_map/ppermute | solution.py:629
  9.3 1.0 %collective-permute-start = (f32[192,128]{1,0:T(8,128)S(1)}, f32[192,128]{1,0:T(8,128)S(1)}, u32[]{:S(2)}, u32[]{:S(2)}) collective-permute-start(f32[192,128]{1,0:T(8,128)S(1)} %get-tuple-element.42), channel_id=1, source_target_pairs={{0,8},{8,0},{16,24},{24,16},{1,9},{9,1},{17,25},{25,17},{2,10},{10... | collective-permute-start | bytes 294920 | tf_op jit(solution)/shard_map/ppermute | solution.py:629
  10.3 1.3 %collective-permute-done.2.odd_y = f32[200,128]{1,0:T(8,128)S(1)} collective-permute-done((f32[200,128]{1,0:T(8,128)S(1)}, f32[200,128]{1,0:T(8,128)S(1)}, u32[]{:S(2)}, u32[]{:S(2)}) %collective-permute-start.2) | collective-permute-done | bytes 102432 | tf_op jit(solution)/shard_map/ppermute | solution.py:629
  11.6 2.1 %collective-permute-done.3.even_y = f32[200,128]{1,0:T(8,128)S(1)} collective-permute-done((f32[200,128]{1,0:T(8,128)S(1)}, f32[200,128]{1,0:T(8,128)S(1)}, u32[]{:S(2)}, u32[]{:S(2)}) %collective-permute-start.3) | collective-permute-done | bytes 102432 | tf_op jit(solution)/shard_map/ppermute | solution.py:629
  13.7 0.6 %collective-permute-start.5 = (f32[32,128]{1,0:T(8,128)S(1)}, f32[32,128]{1,0:T(8,128)S(1)}, u32[]{:S(2)}, u32[]{:S(2)}) collective-permute-start(f32[32,128]{1,0:T(8,128)S(1)} %corners.1), channel_id=1, source_target_pairs={{0,24},{8,16},{16,8},{24,0},{1,25},{9,17},{17,9},{25,1},{2,26},{10... | collective-permute-start | bytes 49160 | tf_op jit(solution)/shard_map/ppermute | solution.py:629
  14.3 1.1 %collective-permute-start.4 = (f32[32,128]{1,0:T(8,128)S(1)}, f32[32,128]{1,0:T(8,128)S(1)}, u32[]{:S(2)}, u32[]{:S(2)}) collective-permute-start(f32[32,128]{1,0:T(8,128)S(1)} %corners.1), channel_id=1, source_target_pairs={{0,8},{8,0},{16,24},{24,16},{1,9},{9,1},{17,25},{25,17},{2,10},{10... | collective-permute-start | bytes 49160 | tf_op jit(solution)/shard_map/ppermute | solution.py:629
  15.4 0.0 collective-permute-done.1.odd_x
  15.4 0.0 collective-permute-done.even_x
  15.4 0.8 %early.1 = (f32[512,128]{1,0:T(8,128)S(1)}, f32[512,128]{1,0:T(8,128)S(1)}, f32[512,128]{1,0:T(8,128)S(1)}, f32[512,128]{1,0:T(8,128)S(1)}, f32[208,128]{1,0:T(8,128)S(1)}, /*index=5*/f32[8,128]{1,0:T(8,128)S(1)}) custom-call(f32[512,128]{1,0:T(8,128)S(1)} %get-tuple-element.40.right, f32[512,128]{1,0:T(8,128)S(1)} %get-tuple-element.41.diagonal, ...), custom_call_target="tpu_custom_call" | custom-call | tf_op jit(solution)/shard_map/early/pallas_call | solution.py:613
  16.2 0.8 %collective-permute-done.5.odd_shared = f32[32,128]{1,0:T(8,128)S(1)} collective-permute-done((f32[32,128]{1,0:T(8,128)S(1)}, f32[32,128]{1,0:T(8,128)S(1)}, u32[]{:S(2)}, u32[]{:S(2)}) %collective-permute-start.5) | collective-permute-done | bytes 16416 | tf_op jit(solution)/shard_map/ppermute | solution.py:629
  17.0 0.0 collective-permute-done.4.even_shared
  17.0 0.3 first.1
  17.3 2.4 %collective-permute-start.8 = (f32[64,128]{1,0:T(8,128)S(1)}, f32[64,128]{1,0:T(8,128)S(1)}, u32[]{:S(2)}, u32[]{:S(2)}) collective-permute-start(f32[64,128]{1,0:T(8,128)S(1)} %get-tuple-element.58), channel_id=1, source_target_pairs={{0,7},{1,2},{2,1},{3,4},{4,3},{5,6},{6,5},{7,0},{8,15},{9,10},{10,... | collective-permute-start | bytes 98312 | tf_op jit(solution)/shard_map/ppermute | solution.py:629
  19.7 0.0 collective-permute-start.9
  19.7 0.0 collective-permute-start.7
  19.7 1.5 %collective-permute-start.6 = (f32[64,128]{1,0:T(8,128)S(1)}, f32[64,128]{1,0:T(8,128)S(1)}, u32[]{:S(2)}, u32[]{:S(2)}) collective-permute-start(f32[64,128]{1,0:T(8,128)S(1)} %get-tuple-element.57), channel_id=1, source_target_pairs={{0,8},{8,0},{16,24},{24,16},{1,9},{9,1},{17,25},{25,17},{2,10},{10... | collective-permute-start | bytes 98312 | tf_op jit(solution)/shard_map/ppermute | solution.py:629
  21.2 2.8 %collective-permute-done.8.odd_y = f32[64,128]{1,0:T(8,128)S(1)} collective-permute-done((f32[64,128]{1,0:T(8,128)S(1)}, f32[64,128]{1,0:T(8,128)S(1)}, u32[]{:S(2)}, u32[]{:S(2)}) %collective-permute-start.8) | collective-permute-done | bytes 32800 | tf_op jit(solution)/shard_map/ppermute | solution.py:629
  24.0 0.0 collective-permute-done.9.even_y
  24.0 0.0 collective-permute-done.7.odd_x
  24.0 0.0 collective-permute-done.6.even_x
  24.0 0.9 %second.1 = (f32[512,128]{1,0:T(8,128)S(1)}, f32[512,128]{1,0:T(8,128)S(1)}, f32[64,128]{1,0:T(8,128)S(1)}, f32[64,128]{1,0:T(8,128)S(1)}, f32[64,128]{1,0:T(8,128)S(1)}, /*index=5*/f32[16,128]{1,0:T(8,128)S(1)}) custom-call(f32[512,128]{1,0:T(8,128)S(1)} %get-tuple-element.56.before_image, f32[64,128]{1,0:T(8,128)S(1)} %collective-permute-done.6.even_x, ...), custom_call_target="tpu_custom_call" | custom-call | tf_op jit(solution)/shard_map/second/pallas_call | solution.py:613
  24.9 2.4 %collective-permute-start.12 = (f32[64,128]{1,0:T(8,128)S(1)}, f32[64,128]{1,0:T(8,128)S(1)}, u32[]{:S(2)}, u32[]{:S(2)}) collective-permute-start(f32[64,128]{1,0:T(8,128)S(1)} %get-tuple-element.65), channel_id=1, source_target_pairs={{0,7},{1,2},{2,1},{3,4},{4,3},{5,6},{6,5},{7,0},{8,15},{9,10},{10,... | collective-permute-start | bytes 98312 | tf_op jit(solution)/shard_map/ppermute | solution.py:629
  27.3 0.0 collective-permute-start.13
  27.3 0.0 collective-permute-start.11
  27.3 1.5 %collective-permute-start.10 = (f32[64,128]{1,0:T(8,128)S(1)}, f32[64,128]{1,0:T(8,128)S(1)}, u32[]{:S(2)}, u32[]{:S(2)}) collective-permute-start(f32[64,128]{1,0:T(8,128)S(1)} %get-tuple-element.64), channel_id=1, source_target_pairs={{0,8},{8,0},{16,24},{24,16},{1,9},{9,1},{17,25},{25,17},{2,10},{10... | collective-permute-start | bytes 98312 | tf_op jit(solution)/shard_map/ppermute | solution.py:629
  28.8 2.7 %collective-permute-done.12.odd_y = f32[64,128]{1,0:T(8,128)S(1)} collective-permute-done((f32[64,128]{1,0:T(8,128)S(1)}, f32[64,128]{1,0:T(8,128)S(1)}, u32[]{:S(2)}, u32[]{:S(2)}) %collective-permute-start.12) | collective-permute-done | bytes 32800 | tf_op jit(solution)/shard_map/ppermute | solution.py:629
  31.6 0.0 collective-permute-done.13.even_y
  31.6 0.0 collective-permute-done.11.odd_x
  31.6 0.0 collective-permute-done.10.even_x
  31.6 0.9 %third.1 = (f32[512,128]{1,0:T(8,128)S(1)}, f32[512,128]{1,0:T(8,128)S(1)}, f32[64,128]{1,0:T(8,128)S(1)}, f32[64,128]{1,0:T(8,128)S(1)}, f32[64,128]{1,0:T(8,128)S(1)}, /*index=5*/f32[24,128]{1,0:T(8,128)S(1)}) custom-call(f32[512,128]{1,0:T(8,128)S(1)} %get-tuple-element.63.before_image, f32[64,128]{1,0:T(8,128)S(1)} %collective-permute-done.10.even_x, ...), custom_call_target="tpu_custom_call" | custom-call | tf_op jit(solution)/shard_map/third/pallas_call | solution.py:613
  32.5 0.7 %sums.1 = f32[32,2,128]{2,1,0:T(2,128)} custom-call(f32[8,128]{1,0:T(8,128)S(1)} %get-tuple-element.68.moments0, f32[16,128]{1,0:T(8,128)S(1)} %get-tuple-element.69.moments1, f32[24,128]{1,0:T(8,128)S(1)} %get-tuple-element.70.moments2), custom_call_target="tpu_custom_call" | custom-call | tf_op jit(solution)/shard_map/sums/pallas_call | solution.py:613
  33.2 3.6 %all-to-all-start = ((f32[32,2,128]{2,1,0:T(2,128)}), f32[32,2,128]{2,1,0:T(2,128)S(1)}, u32[]{:S(2)}, u32[]{:S(2)}) async-start(f32[32,2,128]{2,1,0:T(2,128)} %sums.1), calls=%async_computation | async-start | bytes 65536 | tf_op jit(solution)/shard_map/all_to_all | solution.py:670
  36.8 4.6 %collective-permute-start.16 = (f32[64,128]{1,0:T(8,128)S(1)}, f32[64,128]{1,0:T(8,128)S(1)}, u32[]{:S(2)}, u32[]{:S(2)}) collective-permute-start(f32[64,128]{1,0:T(8,128)S(1)} %get-tuple-element.75), channel_id=1, source_target_pairs={{0,7},{1,2},{2,1},{3,4},{4,3},{5,6},{6,5},{7,0},{8,15},{9,10},{10,... | collective-permute-start | bytes 98312 | tf_op jit(solution)/shard_map/ppermute | solution.py:629
  41.4 0.0 collective-permute-start.17
  41.4 1.0 %collective-permute-start.15 = (f32[64,128]{1,0:T(8,128)S(1)}, f32[64,128]{1,0:T(8,128)S(1)}, u32[]{:S(2)}, u32[]{:S(2)}) collective-permute-start(f32[64,128]{1,0:T(8,128)S(1)} %get-tuple-element.74), channel_id=1, source_target_pairs={{0,24},{8,16},{16,8},{24,0},{1,25},{9,17},{17,9},{25,1},{2,26},{10... | collective-permute-start | bytes 98312 | tf_op jit(solution)/shard_map/ppermute | solution.py:629
  42.3 0.6 %collective-permute-start.14 = (f32[64,128]{1,0:T(8,128)S(1)}, f32[64,128]{1,0:T(8,128)S(1)}, u32[]{:S(2)}, u32[]{:S(2)}) collective-permute-start(f32[64,128]{1,0:T(8,128)S(1)} %get-tuple-element.74), channel_id=1, source_target_pairs={{0,8},{8,0},{16,24},{24,16},{1,9},{9,1},{17,25},{25,17},{2,10},{10... | collective-permute-start | bytes 98312 | tf_op jit(solution)/shard_map/ppermute | solution.py:629
  43.0 1.0 %all-to-all-done.sums = f32[32,2,128]{2,1,0:T(2,128)S(1)} async-done(((f32[32,2,128]{2,1,0:T(2,128)}), f32[32,2,128]{2,1,0:T(2,128)S(1)}, u32[]{:S(2)}, u32[]{:S(2)}) %all-to-all-start) | async-done | bytes 32800 | tf_op jit(solution)/shard_map/all_to_all | solution.py:670
  44.0 1.2 %solution.1 = (f32[1,1,128,512]{3,2,1,0:T(8,128)}, f32[32,128]{1,0:T(8,128)S(1)}) custom-call(f32[512,128]{1,0:T(8,128)S(1)} %get-tuple-element.55.before.values0, f32[512,128]{1,0:T(8,128)S(1)} %get-tuple-element.62.before.values1, f32[512,128]{1,0:T(8,128)S(1)} %get-tuple-element.67.values2, f32[32,2,128]{2,1,0:T(2,128)S(1)} %all-to-all-done.sums, ...), custom_call_target="tpu_custom_call" | custom-call | tf_op jit(solution)/shard_map/solution/pallas_call | solution.py:613
  45.1 0.0 collective-permute-done.16.odd_y
  45.1 0.1 collective-permute-done.17.even_y
  45.3 0.0 collective-permute-done.15.odd_x
  45.3 0.0 collective-permute-done.14.even_x
  45.3 1.0 %last.1 = f32[1,1,128,512]{3,2,1,0:T(8,128)} custom-call(f32[512,128]{1,0:T(8,128)S(1)} %get-tuple-element.73.before_image, f32[64,128]{1,0:T(8,128)S(1)} %collective-permute-done.14.even_x, f32[64,128]{1,0:T(8,128)S(1)} %collective-permute-done.15.odd_x, f32[64,128]{1,0:T(8,128)S(1)} %collective-permute-done.16.odd_y, ...), custom_call_target="tpu_custom_call" | custom-call | tf_op jit(solution)/shard_map/last/pallas_call | solution.py:613
  (1 shorter events, 0.0 us)
Async XLA Ops:
  2.6 9.0 %collective-permute-start.2 = (f32[200,128]{1,0:T(8,128)S(1)}, f32[200,128]{1,0:T(8,128)S(1)}, u32[]{:S(2)}, u32[]{:S(2)}) collective-permute-start(f32[200,128]{1,0:T(8,128)S(1)} %get-tuple-element.43), channel_id=1, source_target_pairs={{0,7},{1,2},{2,1},{3,4},{4,3},{5,6},{6,5},{7,0},{8,15},{9,10},{10,... | collective-permute-start | bytes 307208 | tf_op jit(solution)/shard_map/ppermute | solution.py:629
  8.6 5.1 %collective-permute-start.3 = (f32[200,128]{1,0:T(8,128)S(1)}, f32[200,128]{1,0:T(8,128)S(1)}, u32[]{:S(2)}, u32[]{:S(2)}) collective-permute-start(f32[200,128]{1,0:T(8,128)S(1)} %get-tuple-element.44), channel_id=1, source_target_pairs={{0,1},{1,0},{2,3},{3,2},{4,5},{5,4},{6,7},{7,6},{8,9},{9,8},{10,11... | collective-permute-start | bytes 307208 | tf_op jit(solution)/shard_map/ppermute | solution.py:629
  8.6 6.8 %collective-permute-start.1 = (f32[192,128]{1,0:T(8,128)S(1)}, f32[192,128]{1,0:T(8,128)S(1)}, u32[]{:S(2)}, u32[]{:S(2)}) collective-permute-start(f32[192,128]{1,0:T(8,128)S(1)} %get-tuple-element.42), channel_id=1, source_target_pairs={{0,24},{8,16},{16,8},{24,0},{1,25},{9,17},{17,9},{25,1},{2,26},{10... | collective-permute-start | bytes 294920 | tf_op jit(solution)/shard_map/ppermute | solution.py:629
  9.3 6.1 %collective-permute-start = (f32[192,128]{1,0:T(8,128)S(1)}, f32[192,128]{1,0:T(8,128)S(1)}, u32[]{:S(2)}, u32[]{:S(2)}) collective-permute-start(f32[192,128]{1,0:T(8,128)S(1)} %get-tuple-element.42), channel_id=1, source_target_pairs={{0,8},{8,0},{16,24},{24,16},{1,9},{9,1},{17,25},{25,17},{2,10},{10... | collective-permute-start | bytes 294920 | tf_op jit(solution)/shard_map/ppermute | solution.py:629
  13.7 3.3 %collective-permute-start.5 = (f32[32,128]{1,0:T(8,128)S(1)}, f32[32,128]{1,0:T(8,128)S(1)}, u32[]{:S(2)}, u32[]{:S(2)}) collective-permute-start(f32[32,128]{1,0:T(8,128)S(1)} %corners.1), channel_id=1, source_target_pairs={{0,24},{8,16},{16,8},{24,0},{1,25},{9,17},{17,9},{25,1},{2,26},{10... | collective-permute-start | bytes 49160 | tf_op jit(solution)/shard_map/ppermute | solution.py:629
  14.3 2.8 %collective-permute-start.4 = (f32[32,128]{1,0:T(8,128)S(1)}, f32[32,128]{1,0:T(8,128)S(1)}, u32[]{:S(2)}, u32[]{:S(2)}) collective-permute-start(f32[32,128]{1,0:T(8,128)S(1)} %corners.1), channel_id=1, source_target_pairs={{0,8},{8,0},{16,24},{24,16},{1,9},{9,1},{17,25},{25,17},{2,10},{10... | collective-permute-start | bytes 49160 | tf_op jit(solution)/shard_map/ppermute | solution.py:629
  17.3 6.7 %collective-permute-start.8 = (f32[64,128]{1,0:T(8,128)S(1)}, f32[64,128]{1,0:T(8,128)S(1)}, u32[]{:S(2)}, u32[]{:S(2)}) collective-permute-start(f32[64,128]{1,0:T(8,128)S(1)} %get-tuple-element.58), channel_id=1, source_target_pairs={{0,7},{1,2},{2,1},{3,4},{4,3},{5,6},{6,5},{7,0},{8,15},{9,10},{10,... | collective-permute-start | bytes 98312 | tf_op jit(solution)/shard_map/ppermute | solution.py:629
  19.7 4.3 %collective-permute-start.9 = (f32[64,128]{1,0:T(8,128)S(1)}, f32[64,128]{1,0:T(8,128)S(1)}, u32[]{:S(2)}, u32[]{:S(2)}) collective-permute-start(f32[64,128]{1,0:T(8,128)S(1)} %get-tuple-element.59), channel_id=1, source_target_pairs={{0,1},{1,0},{2,3},{3,2},{4,5},{5,4},{6,7},{7,6},{8,9},{9,8},{10,11... | collective-permute-start | bytes 98312 | tf_op jit(solution)/shard_map/ppermute | solution.py:629
  19.7 4.3 %collective-permute-start.7 = (f32[64,128]{1,0:T(8,128)S(1)}, f32[64,128]{1,0:T(8,128)S(1)}, u32[]{:S(2)}, u32[]{:S(2)}) collective-permute-start(f32[64,128]{1,0:T(8,128)S(1)} %get-tuple-element.57), channel_id=1, source_target_pairs={{0,24},{8,16},{16,8},{24,0},{1,25},{9,17},{17,9},{25,1},{2,26},{10... | collective-permute-start | bytes 98312 | tf_op jit(solution)/shard_map/ppermute | solution.py:629
  19.7 4.3 %collective-permute-start.6 = (f32[64,128]{1,0:T(8,128)S(1)}, f32[64,128]{1,0:T(8,128)S(1)}, u32[]{:S(2)}, u32[]{:S(2)}) collective-permute-start(f32[64,128]{1,0:T(8,128)S(1)} %get-tuple-element.57), channel_id=1, source_target_pairs={{0,8},{8,0},{16,24},{24,16},{1,9},{9,1},{17,25},{25,17},{2,10},{10... | collective-permute-start | bytes 98312 | tf_op jit(solution)/shard_map/ppermute | solution.py:629
  24.9 6.7 %collective-permute-start.12 = (f32[64,128]{1,0:T(8,128)S(1)}, f32[64,128]{1,0:T(8,128)S(1)}, u32[]{:S(2)}, u32[]{:S(2)}) collective-permute-start(f32[64,128]{1,0:T(8,128)S(1)} %get-tuple-element.65), channel_id=1, source_target_pairs={{0,7},{1,2},{2,1},{3,4},{4,3},{5,6},{6,5},{7,0},{8,15},{9,10},{10,... | collective-permute-start | bytes 98312 | tf_op jit(solution)/shard_map/ppermute | solution.py:629
  27.3 4.3 %collective-permute-start.13 = (f32[64,128]{1,0:T(8,128)S(1)}, f32[64,128]{1,0:T(8,128)S(1)}, u32[]{:S(2)}, u32[]{:S(2)}) collective-permute-start(f32[64,128]{1,0:T(8,128)S(1)} %get-tuple-element.66), channel_id=1, source_target_pairs={{0,1},{1,0},{2,3},{3,2},{4,5},{5,4},{6,7},{7,6},{8,9},{9,8},{10,11... | collective-permute-start | bytes 98312 | tf_op jit(solution)/shard_map/ppermute | solution.py:629
  27.3 4.3 %collective-permute-start.11 = (f32[64,128]{1,0:T(8,128)S(1)}, f32[64,128]{1,0:T(8,128)S(1)}, u32[]{:S(2)}, u32[]{:S(2)}) collective-permute-start(f32[64,128]{1,0:T(8,128)S(1)} %get-tuple-element.64), channel_id=1, source_target_pairs={{0,24},{8,16},{16,8},{24,0},{1,25},{9,17},{17,9},{25,1},{2,26},{10... | collective-permute-start | bytes 98312 | tf_op jit(solution)/shard_map/ppermute | solution.py:629
  27.3 4.3 %collective-permute-start.10 = (f32[64,128]{1,0:T(8,128)S(1)}, f32[64,128]{1,0:T(8,128)S(1)}, u32[]{:S(2)}, u32[]{:S(2)}) collective-permute-start(f32[64,128]{1,0:T(8,128)S(1)} %get-tuple-element.64), channel_id=1, source_target_pairs={{0,8},{8,0},{16,24},{24,16},{1,9},{9,1},{17,25},{25,17},{2,10},{10... | collective-permute-start | bytes 98312 | tf_op jit(solution)/shard_map/ppermute | solution.py:629
  33.2 10.8 %all-to-all-start = ((f32[32,2,128]{2,1,0:T(2,128)}), f32[32,2,128]{2,1,0:T(2,128)S(1)}, u32[]{:S(2)}, u32[]{:S(2)}) async-start(f32[32,2,128]{2,1,0:T(2,128)} %sums.1), calls=%async_computation | async-start | bytes 65536 | tf_op jit(solution)/shard_map/all_to_all | solution.py:670
  36.8 8.4 %collective-permute-start.16 = (f32[64,128]{1,0:T(8,128)S(1)}, f32[64,128]{1,0:T(8,128)S(1)}, u32[]{:S(2)}, u32[]{:S(2)}) collective-permute-start(f32[64,128]{1,0:T(8,128)S(1)} %get-tuple-element.75), channel_id=1, source_target_pairs={{0,7},{1,2},{2,1},{3,4},{4,3},{5,6},{6,5},{7,0},{8,15},{9,10},{10,... | collective-permute-start | bytes 98312 | tf_op jit(solution)/shard_map/ppermute | solution.py:629
  41.4 3.9 %collective-permute-start.17 = (f32[64,128]{1,0:T(8,128)S(1)}, f32[64,128]{1,0:T(8,128)S(1)}, u32[]{:S(2)}, u32[]{:S(2)}) collective-permute-start(f32[64,128]{1,0:T(8,128)S(1)} %get-tuple-element.76), channel_id=1, source_target_pairs={{0,1},{1,0},{2,3},{3,2},{4,5},{5,4},{6,7},{7,6},{8,9},{9,8},{10,11... | collective-permute-start | bytes 98312 | tf_op jit(solution)/shard_map/ppermute | solution.py:629
  41.4 3.9 %collective-permute-start.15 = (f32[64,128]{1,0:T(8,128)S(1)}, f32[64,128]{1,0:T(8,128)S(1)}, u32[]{:S(2)}, u32[]{:S(2)}) collective-permute-start(f32[64,128]{1,0:T(8,128)S(1)} %get-tuple-element.74), channel_id=1, source_target_pairs={{0,24},{8,16},{16,8},{24,0},{1,25},{9,17},{17,9},{25,1},{2,26},{10... | collective-permute-start | bytes 98312 | tf_op jit(solution)/shard_map/ppermute | solution.py:629
  42.3 2.9 %collective-permute-start.14 = (f32[64,128]{1,0:T(8,128)S(1)}, f32[64,128]{1,0:T(8,128)S(1)}, u32[]{:S(2)}, u32[]{:S(2)}) collective-permute-start(f32[64,128]{1,0:T(8,128)S(1)} %get-tuple-element.74), channel_id=1, source_target_pairs={{0,8},{8,0},{16,24},{24,16},{1,9},{9,1},{17,25},{25,17},{2,10},{10... | collective-permute-start | bytes 98312 | tf_op jit(solution)/shard_map/ppermute | solution.py:629

commit v8 on v7

--- a/solution.py
+++ b/solution.py
@@ -311,34 +311,37 @@
         lowest_to_highest(odd, to_even, to_odd, pl.ds(8 * a, 8), faces[0][a], faces[1][a])
 
 
-def streamwise(lines, b, spread, mass, image):
+def streamwise(lines, b, spread, mass):
     slopes = along(DERIVATIVE, lines, -1)
     back = along(DERIVATIVE.T, [slopes[a] * spread[row(a, b), :] for a in range(8)], -1)
-    for a in range(8):
-        image[row(a, b), :] = back[a] + mass[row(a, b), :] * lines[a]
+    return [back[a] + mass[row(a, b), :] * lines[a] for a in range(8)]
+
+
+def join_layers(image):
+    for a in range(8):
+        low, high = join_vertical(image[across(a, 0), :], image[across(a, 7), :])
+        image[across(a, 0), :] = low
+        image[across(a, 7), :] = high
+
+
+def vertical_part(lines, spread):
+    slopes = along(DERIVATIVE, lines, -1)
+    return along(VERTICAL * DERIVATIVE.T, [slopes[c] * spread[c] for c in range(8)], -1)
 
 
 def operate(values, spread, image):
-    forward, backward = DERIVATIVE, DERIVATIVE.T
-    for a in range(8):
-        slopes = along(forward, [values[row(a, b), :] for b in range(8)], -1)
-        back = along(backward, [slopes[b] * spread[row(a, b), :] for b in range(8)], -1)
+    for a in range(8):
+        slopes = along(DERIVATIVE, [values[row(a, b), :] for b in range(8)], -1)
+        back = along(DERIVATIVE.T, [slopes[b] * spread[row(a, b), :] for b in range(8)], -1)
         for b in range(8):
             image[row(a, b), :] += back[b]
-    energy = jnp.zeros((8, LANES), jnp.float32)
-    for a in range(8):
-        lines = [values[across(a, c), :] for c in range(8)]
-        slopes = along(forward, lines, -1)
-        back = along(
-            VERTICAL * backward, [slopes[c] * spread[across(a, c), :] for c in range(8)], -1
+    for a in range(8):
+        back = vertical_part(
+            [values[across(a, c), :] for c in range(8)],
+            [spread[across(a, c), :] for c in range(8)],
         )
-        back = [back[c] + image[across(a, c), :] for c in range(8)]
         for c in range(8):
-            energy = energy + back[c] * lines[c]
-        back[0], back[7] = join_vertical(back[0], back[7])
-        for c in range(8):
-            image[across(a, c), :] = back[c]
-    return energy
+            image[across(a, c), :] += back[c]
 
 
 def weighted(sums):
@@ -355,7 +358,7 @@
 
 def early_kernel(
     right, diagonal, even_x, odd_x, odd_y, even_y, spread, mass,
-    whole_diagonal, jacobi, values, image, outer, moments,
+    whole_diagonal, jacobi, values, image, outer, moments, from_low, from_high, from_side, packed,
 ):
     received = (even_x, odd_x, even_y, odd_y)
     first = lane_index() < HALF
@@ -374,7 +377,9 @@
             values[row(a, b), :] = value
             sums[ends(a, b)] = sums[ends(a, b)] + source * value
             lines.append(value)
-        streamwise(lines, b, spread, mass, image)
+        back = streamwise(lines, b, spread, mass)
+        for a in range(8):
+            image[row(a, b), :] = back[a]
     moments[...] = weighted(sums)
     for b in range(8):
         outer[pl.ds(8 * b, 8), :] = pltpu.roll(
@@ -386,6 +391,25 @@
                 even_y, odd_y, 7 * side, pl.ds(128 + 8 * k, 8)
             )
     operate(values, spread, image)
+    join_layers(image)
+    for a in range(8):
+        for end, out in ((0, from_low), (7, from_high)):
+            slopes = [spread[row(a, q), :] * float(DERIVATIVE[q, end]) for q in range(8)]
+            back = along(DERIVATIVE.T, slopes, -1)
+            for b in range(8):
+                out[row(a, b), :] = back[b]
+    for b in range(8):
+        packed[pl.ds(8 * b, 8), :] = packed_x(spread, b)
+        back = along(
+            DERIVATIVE.T, [spread[row(q, b), :] * outer_slope(q) for q in range(8)], -1
+        )
+        for a in range(8):
+            from_side[row(a, b), :] = back[a]
+
+
+def outer_slope(q):
+    first = lane_index() < HALF
+    return jnp.where(first, float(DERIVATIVE[q, 0]), float(DERIVATIVE[q, 7]))
 
 
 def add_packed(grid, b, value):
@@ -422,8 +446,7 @@
         b = 7 * side
         slopes = []
         for q in range(8):
-            slope = jnp.where(first, float(DERIVATIVE[q, 0]), float(DERIVATIVE[q, 7]))
-            slopes.append(spread[row(q, b), :] * (slope * corner))
+            slopes.append(spread[row(q, b), :] * (outer_slope(q) * corner))
         back = along(DERIVATIVE.T, slopes, -1)
         for a in range(8):
             image[row(a, b), :] += join_vertical_packed(back[a])
@@ -441,10 +464,51 @@
     send_faces(image, values, outer, shifts, face_x, to_even, to_odd)
 
 
-def next_values(before_image, received, diagonal, jacobi, before, spread, mass, values, image):
-    cross = [jnp.zeros((8, LANES), jnp.float32)] * 3
-    square = [jnp.zeros((8, LANES), jnp.float32)] * 3
-    for b in range(8):
+def inner_kernel(
+    before_image, diagonal, jacobi, before, spread, mass, values, image, moments
+):
+    first = lane_index() < HALF
+    zero = jnp.zeros((8, LANES), jnp.float32)
+    cross, square = [zero] * 3, [zero] * 3
+    for b in range(8):
+        lines = []
+        for a in range(8):
+            if b in (0, 7):
+                values[row(a, b), :] = zero
+                image[row(a, b), :] = zero
+                continue
+            joined = before_image[row(a, b), :]
+            if a in (0, 7):
+                joined = joined_x(a, before_image[row(0, b), :], before_image[row(7, b), :], 0.0)
+            old = before[row(a, b), :]
+            scaled = joined - diagonal[row(a, b), :] * old
+            if a in (0, 7):
+                scaled = jnp.where(first, 0.0, scaled) if a == 0 else jnp.where(first, scaled, 0.0)
+            value = scaled * jacobi[row(a, b), :]
+            values[row(a, b), :] = value
+            kind = ends(a, b)
+            cross[kind] = cross[kind] + scaled * old
+            square[kind] = square[kind] + scaled * value
+            lines.append(value)
+        if lines:
+            back = streamwise(lines, b, spread, mass)
+            for a in range(8):
+                image[row(a, b), :] = back[a]
+    moments[pl.ds(0, 8), :] = weighted(cross)
+    moments[pl.ds(8, 8), :] = weighted(square)
+    operate(values, spread, image)
+
+
+def outer_kernel(
+    before_image, even_x, odd_x, odd_y, even_y, diagonal, jacobi, before, spread, mass, shifts,
+    outer, from_low, from_high, from_side, packed, inner_moments, inner_values, inner_image,
+    values, image, face_x, to_even, to_odd, moments, face, face_back,
+):
+    received = (even_x, odd_x, even_y, odd_y)
+    zero = jnp.zeros((8, LANES), jnp.float32)
+    cross, square = [zero] * 3, [zero] * 3
+    sides = []
+    for b in (0, 7):
         lines = []
         for a in range(8):
             old = before[row(a, b), :]
@@ -455,38 +519,58 @@
             cross[kind] = cross[kind] + scaled * old
             square[kind] = square[kind] + scaled * value
             lines.append(value)
-        streamwise(lines, b, spread, mass, image)
-    return weighted(cross), weighted(square)
-
-
-def second_kernel(
-    before_image, even_x, odd_x, odd_y, even_y, diagonal, jacobi, before, spread, mass,
-    shifts, outer,
-    values, image, face_x, to_even, to_odd, moments,
-):
-    received = (even_x, odd_x, even_y, odd_y)
-    cross, square = next_values(
-        before_image, received, diagonal, jacobi, before, spread, mass, values, image
-    )
-    moments[pl.ds(0, 8), :] = cross
-    moments[pl.ds(8, 8), :] = square
-    operate(values, spread, image)
+        sides.append(lines)
+    lines = [zero] * 8
+    for b in range(1, 7):
+        old = packed_x(before, b)
+        ghost = pltpu.roll(ghost_x(even_x, odd_x, pl.ds(8 * b, 8)), HALF, 1)
+        scaled = packed_x(before_image, b) + ghost - packed_x(diagonal, b) * old
+        lines[b] = scaled * packed_x(jacobi, b)
+        add_packed(values, b, lines[b])
+        cross[1] = cross[1] + scaled * old
+        square[1] = square[1] + scaled * lines[b]
+    for b in range(8):
+        face[pl.ds(8 * b, 8), :] = lines[b]
+    back = vertical_part(
+        [face[pl.ds(c, 8, stride=8), :] for c in range(8)],
+        [packed[pl.ds(c, 8, stride=8), :] for c in range(8)],
+    )
+    for c in range(8):
+        face_back[pl.ds(c, 8, stride=8), :] = back[c]
+    slopes = along(DERIVATIVE, lines, -1)
+    back = along(DERIVATIVE.T, [slopes[q] * packed[pl.ds(8 * q, 8), :] for q in range(8)], -1)
+    for b in range(8):
+        share = back[b] + face_back[pl.ds(8 * b, 8), :]
+        if b not in (0, 7):
+            share = share + packed_x(mass, b) * lines[b]
+        add_packed(image, b, share)
+    ends_back = [streamwise(sides[k], 7 * k, spread, mass) for k in range(2)]
+    for a in range(8):
+        for b in range(8):
+            rows = row(a, b)
+            share = from_low[rows, :] * sides[0][a] + from_high[rows, :] * sides[1][a]
+            if b in (0, 7):
+                share = share + ends_back[b // 7][a]
+            else:
+                share = share + from_side[rows, :] * lines[b]
+            image[rows, :] += share
+    for b in (0, 7):
+        at = [pl.ds(8 * b + c, 8, stride=64) for c in range(8)]
+        back = vertical_part(
+            [values[at[c], :] for c in range(8)], [spread[at[c], :] for c in range(8)]
+        )
+        for c in range(8):
+            image[at[c], :] += back[c]
+    moments[pl.ds(0, 8), :] = inner_moments[pl.ds(0, 8), :] + weighted(cross)
+    moments[pl.ds(8, 8), :] = inner_moments[pl.ds(8, 8), :] + weighted(square)
+    if moments.shape[0] > 16:
+        energy = [zero] * 4
+        for a in range(8):
+            for b in range(8):
+                energy[b % 4] = energy[b % 4] + values[row(a, b), :] * image[row(a, b), :]
+        moments[pl.ds(16, 8), :] = (energy[0] + energy[1]) + (energy[2] + energy[3])
+    join_layers(image)
     send_faces(image, values, outer, shifts, face_x, to_even, to_odd)
-
-
-def third_kernel(
-    before_image, even_x, odd_x, odd_y, even_y, diagonal, jacobi, before, spread, mass,
-    shifts, outer,
-    values, image, face_x, to_even, to_odd, moments,
-):
-    received = (even_x, odd_x, even_y, odd_y)
-    cross, square = next_values(
-        before_image, received, diagonal, jacobi, before, spread, mass, values, image
-    )
-    energy = operate(values, spread, image)
-    send_faces(image, values, outer, shifts, face_x, to_even, to_odd)
-    for k, part in enumerate((cross, square, energy)):
-        moments[pl.ds(8 * k, 8), :] = part
 
 
 def sums_kernel(moments0, moments1, moments2, sums):
@@ -647,8 +731,8 @@
     received_x, received_y = swapped((out_x, out_x), "gx"), swapped(sent_y, "yz")[::-1]
     [shared] = call(corners_kernel, "corners", [(32, LANES)], [], corners, *received_y)
     received = (*received_x, *received_y, *swapped((shared, shared), "gx"))
-    *early, outer, moments0 = call(
-        early_kernel, "early", [grid] * 4 + [(208, LANES), tile], [],
+    *early, outer, moments0, from_low, from_high, from_side, packed = call(
+        early_kernel, "early", [grid] * 4 + [(208, LANES), tile] + [grid] * 3 + [face], [],
         right, diagonal, *received_x, *received_y, spread, mass,
     )
     diagonal, jacobi, values0, image, out_x, *sent_y, moments0 = call(
@@ -656,15 +740,26 @@
         right, diagonal, *received, spread, mass, shifts, outer, *early, moments0,
         aliases={12: 0, 13: 1, 14: 2, 15: 3},
     )
-    received = (*swapped((out_x, out_x), "gx"), *swapped(sent_y, "yz")[::-1])
-    values1, image, out_x, *sent_y, moments1 = call(
-        second_kernel, "second", [grid] * 2 + [face] * 3 + [(16, LANES)], [],
-        image, *received, diagonal, jacobi, values0, spread, mass, shifts, outer,
-    )
-    received = (*swapped((out_x, out_x), "gx"), *swapped(sent_y, "yz")[::-1])
-    values2, image, out_x, *sent_y, moments2 = call(
-        third_kernel, "third", [grid] * 2 + [face] * 3 + [(24, LANES)], [],
-        image, *received, diagonal, jacobi, values1, spread, mass, shifts, outer,
+    fixed = (spread, mass, shifts, outer, from_low, from_high, from_side, packed)
+
+    def advance(name, rows, image, before, out_x, sent_y):
+        received = (*swapped((out_x, out_x), "gx"), *swapped(sent_y, "yz")[::-1])
+        values, inner_image, moments = call(
+            inner_kernel, "inner", [grid] * 2 + [(16, LANES)], [],
+            image, diagonal, jacobi, before, spread, mass,
+        )
+        return call(
+            outer_kernel, name, [grid] * 2 + [face] * 3 + [(rows, LANES)],
+            [pltpu.VMEM(face, jnp.float32)] * 2,
+            image, *received, diagonal, jacobi, before, *fixed, moments, values, inner_image,
+            aliases={17: 0, 18: 1},
+        )
+
+    values1, image, out_x, *sent_y, moments1 = advance(
+        "second", 16, image, values0, out_x, sent_y
+    )
+    values2, image, out_x, *sent_y, moments2 = advance(
+        "third", 24, image, values1, out_x, sent_y
     )
     [sums] = call(sums_kernel, "sums", [(devices, 2, LANES)], [], moments0, moments1, moments2)
     sums = lax.all_to_all(sums, ("gx", "yz"), 0, 0)

time: 46.5 us -> 45.9 us (0.987)
  waiting for transfers between devices: 10.9 us -> 9.3 us
  Pallas kernels: 7.68 us -> 8.77 us
    ppermute x9, waiting for transfers between devices: 7.65 us -> 6.04 us  [swapped(): lax.ppermute(block[1], axis, odd)]
    pallas_call x9 -> x11, Pallas kernels: 7.68 us -> 8.77 us  [call(): pl.pallas_call(kernel, out_shape=[jax.ShapeDtypeStruct(shape, jnp.float32...]
  transfers between devices with their start and end apart: 19 -> 19, of which waited for: 7 -> 7; matrix products, arithmetic and copies ran while one was open for 0% -> 0% of each run, Pallas kernels for 4% -> 8%
where the time goes in v8:
time: 45.9 us; the launch traced here: 45.8 us
  starting transfers between devices  27 us (59%)
  waiting for transfers between devices  9.3 us (20%)
  Pallas kernels  8.77 us (19%)
  between operations  0.69 us (2%)
    ppermute x9, starting transfers between devices, swapped(): lax.ppermute(block[1], axis, odd)  17.6 us
    pallas_call x11, Pallas kernels, call(): pl.pallas_call(kernel, out_shape=[jax.ShapeDtypeStruct(shape, jnp.float32...  8.77 us
    ppermute x9, waiting for transfers between devices, swapped(): lax.ppermute(block[1], axis, odd)  6.04 us
    ppermute x9, starting transfers between devices, swapped(): lax.ppermute(block[0], axis, even)  5.81 us
    all_to_all x1, starting transfers between devices, body(): sums = lax.all_to_all(sums, ('gx', 'yz'), 0, 0)  3.57 us
    ppermute x9, waiting for transfers between devices, swapped(): lax.ppermute(block[0], axis, even)  2.27 us
    all_to_all x1, waiting for transfers between devices, body(): sums = lax.all_to_all(sums, ('gx', 'yz'), 0, 0)  0.99 us
  transfers between devices with their start and end apart: 19, of which 7 were waited for; matrix products, arithmetic and copies ran while one was open for 0% of the time, Pallas kernels for 8%

profile of v8, /device:TPU:0, one launch (start us, length us, event | category | flops | bytes accessed | tf_op | source)
XLA Modules:
  0.0 45.8 jit_solution(16666734765061676867)
XLA Ops:
  0.6 1.9 %setup.1 = (f32[512,128]{1,0:T(8,128)S(1)}, f32[512,128]{1,0:T(8,128)S(1)}, f32[512,128]{1,0:T(8,128)S(1)}, f32[512,128]{1,0:T(8,128)S(1)}, f32[192,128]{1,0:T(8...) custom-call(s32[1,128]{1,0:T(1,128)} %bitcast.1, ...), custom_call_target="tpu_custom_call" | custom-call | tf_op jit(solution)/shard_map/setup/pallas_call | solution.py:697
  2.6 6.0 %collective-permute-start.2 = (f32[200,128]{1,0:T(8,128)S(1)}, f32[200,128]{1,0:T(8,128)S(1)}, u32[]{:S(2)}, u32[]{:S(2)}) collective-permute-start(f32[200,128]{1,0:T(8,128)S(1)} %get-tuple-element.53), channel_id=1, source_target_pairs={{0,7},{1,2},{2,1},{3,4},{4,3},{5,6},{6,5},{7,0},{8,15},{9,10},{10,... | collective-permute-start | bytes 307208 | tf_op jit(solution)/shard_map/ppermute | solution.py:713
  8.6 0.0 collective-permute-start.3
  8.6 0.7 %collective-permute-start.1 = (f32[192,128]{1,0:T(8,128)S(1)}, f32[192,128]{1,0:T(8,128)S(1)}, u32[]{:S(2)}, u32[]{:S(2)}) collective-permute-start(f32[192,128]{1,0:T(8,128)S(1)} %get-tuple-element.52), channel_id=1, source_target_pairs={{0,24},{8,16},{16,8},{24,0},{1,25},{9,17},{17,9},{25,1},{2,26},{10... | collective-permute-start | bytes 294920 | tf_op jit(solution)/shard_map/ppermute | solution.py:713
  9.3 1.0 %collective-permute-start = (f32[192,128]{1,0:T(8,128)S(1)}, f32[192,128]{1,0:T(8,128)S(1)}, u32[]{:S(2)}, u32[]{:S(2)}) collective-permute-start(f32[192,128]{1,0:T(8,128)S(1)} %get-tuple-element.52), channel_id=1, source_target_pairs={{0,8},{8,0},{16,24},{24,16},{1,9},{9,1},{17,25},{25,17},{2,10},{10... | collective-permute-start | bytes 294920 | tf_op jit(solution)/shard_map/ppermute | solution.py:713
  10.3 1.3 %collective-permute-done.2.odd_y = f32[200,128]{1,0:T(8,128)S(1)} collective-permute-done((f32[200,128]{1,0:T(8,128)S(1)}, f32[200,128]{1,0:T(8,128)S(1)}, u32[]{:S(2)}, u32[]{:S(2)}) %collective-permute-start.2) | collective-permute-done | bytes 102432 | tf_op jit(solution)/shard_map/ppermute | solution.py:713
  11.6 2.1 %collective-permute-done.3.even_y = f32[200,128]{1,0:T(8,128)S(1)} collective-permute-done((f32[200,128]{1,0:T(8,128)S(1)}, f32[200,128]{1,0:T(8,128)S(1)}, u32[]{:S(2)}, u32[]{:S(2)}) %collective-permute-start.3) | collective-permute-done | bytes 102432 | tf_op jit(solution)/shard_map/ppermute | solution.py:713
  13.7 0.6 %collective-permute-start.5 = (f32[32,128]{1,0:T(8,128)S(1)}, f32[32,128]{1,0:T(8,128)S(1)}, u32[]{:S(2)}, u32[]{:S(2)}) collective-permute-start(f32[32,128]{1,0:T(8,128)S(1)} %corners.1), channel_id=1, source_target_pairs={{0,24},{8,16},{16,8},{24,0},{1,25},{9,17},{17,9},{25,1},{2,26},{10... | collective-permute-start | bytes 49160 | tf_op jit(solution)/shard_map/ppermute | solution.py:713
  14.3 1.1 %collective-permute-start.4 = (f32[32,128]{1,0:T(8,128)S(1)}, f32[32,128]{1,0:T(8,128)S(1)}, u32[]{:S(2)}, u32[]{:S(2)}) collective-permute-start(f32[32,128]{1,0:T(8,128)S(1)} %corners.1), channel_id=1, source_target_pairs={{0,8},{8,0},{16,24},{24,16},{1,9},{9,1},{17,25},{25,17},{2,10},{10... | collective-permute-start | bytes 49160 | tf_op jit(solution)/shard_map/ppermute | solution.py:713
  15.4 0.0 collective-permute-done.1.odd_x
  15.4 0.0 collective-permute-done.even_x
  15.4 1.1 %early.1 = (f32[512,128]{1,0:T(8,128)S(1)}, f32[512,128]{1,0:T(8,128)S(1)}, f32[512,128]{1,0:T(8,128)S(1)}, f32[512,128]{1,0:T(8,128)S(1)}, f32[208,128]{1,0:T(8...) custom-call(f32[512,128]{1,0:T(8,128)S(1)} %get-tuple-element.50.rig, ...), custom_call_target="tpu_custom_call" | custom-call | tf_op jit(solution)/shard_map/early/pallas_call | solution.py:697
  16.5 0.5 %collective-permute-done.5.odd_shared = f32[32,128]{1,0:T(8,128)S(1)} collective-permute-done((f32[32,128]{1,0:T(8,128)S(1)}, f32[32,128]{1,0:T(8,128)S(1)}, u32[]{:S(2)}, u32[]{:S(2)}) %collective-permute-start.5) | collective-permute-done | bytes 16416 | tf_op jit(solution)/shard_map/ppermute | solution.py:713
  17.0 0.0 collective-permute-done.4.even_shared
  17.0 0.3 first.1
  17.3 2.3 %collective-permute-start.8 = (f32[64,128]{1,0:T(8,128)S(1)}, f32[64,128]{1,0:T(8,128)S(1)}, u32[]{:S(2)}, u32[]{:S(2)}) collective-permute-start(f32[64,128]{1,0:T(8,128)S(1)} %get-tuple-element.68), channel_id=1, source_target_pairs={{0,7},{1,2},{2,1},{3,4},{4,3},{5,6},{6,5},{7,0},{8,15},{9,10},{10,... | collective-permute-start | bytes 98312 | tf_op jit(solution)/shard_map/ppermute | solution.py:713
  19.7 0.0 collective-permute-start.9
  19.7 0.0 collective-permute-start.7
  19.7 1.5 %collective-permute-start.6 = (f32[64,128]{1,0:T(8,128)S(1)}, f32[64,128]{1,0:T(8,128)S(1)}, u32[]{:S(2)}, u32[]{:S(2)}) collective-permute-start(f32[64,128]{1,0:T(8,128)S(1)} %get-tuple-element.67), channel_id=1, source_target_pairs={{0,8},{8,0},{16,24},{24,16},{1,9},{9,1},{17,25},{25,17},{2,10},{10... | collective-permute-start | bytes 98312 | tf_op jit(solution)/shard_map/ppermute | solution.py:713
  21.2 0.7 %inner.2 = (f32[512,128]{1,0:T(8,128)S(1)}, f32[512,128]{1,0:T(8,128)S(1)}, f32[16,128]{1,0:T(8,128)S(1)}) custom-call(f32[512,128]{1,0:T(8,128)S(1)} %get-tuple-element.66.before_image, f32[512,128]{1,0:T(8,128)S(1)} %get-tuple-element.70.diagonal, f32[512,128]{1,0:T(8,128)S(1)} %get-tuple-element.71.jacobi, ...), custom_call_target="tpu_custom_call" | custom-call | tf_op jit(solution)/shard_map/inner/pallas_call | solution.py:697
  21.9 2.1 %collective-permute-done.8.odd_y = f32[64,128]{1,0:T(8,128)S(1)} collective-permute-done((f32[64,128]{1,0:T(8,128)S(1)}, f32[64,128]{1,0:T(8,128)S(1)}, u32[]{:S(2)}, u32[]{:S(2)}) %collective-permute-start.8) | collective-permute-done | bytes 32800 | tf_op jit(solution)/shard_map/ppermute | solution.py:713
  24.0 0.0 collective-permute-done.9.even_y
  24.0 0.0 collective-permute-done.7.odd_x
  24.0 0.0 collective-permute-done.6.even_x
  24.0 0.6 %second.1 = (f32[512,128]{1,0:T(8,128)S(1)}, f32[512,128]{1,0:T(8,128)S(1)}, f32[64,128]{1,0:T(8,128)S(1)}, f32[64,128]{1,0:T(8,128)S(1)}, f32[64,128]{1,0:T(8,128)S(1)}, /*index=5*/f32[16,128]{1,0:T(8,128)S(1)}) custom-call(f32[512,128]{1,0:T(8,128)S(1)} %get-tuple-element.66.before_image, ...), custom_call_target="tpu_custom_call", output_to_operand_aliasing={{0}: (17, {}), {1}: (18, {})} | custom-call | tf_op jit(solution)/shard_map/second/pallas_call | solution.py:697
  24.6 2.4 %collective-permute-start.12 = (f32[64,128]{1,0:T(8,128)S(1)}, f32[64,128]{1,0:T(8,128)S(1)}, u32[]{:S(2)}, u32[]{:S(2)}) collective-permute-start(f32[64,128]{1,0:T(8,128)S(1)} %get-tuple-element.82), channel_id=1, source_target_pairs={{0,7},{1,2},{2,1},{3,4},{4,3},{5,6},{6,5},{7,0},{8,15},{9,10},{10,... | collective-permute-start | bytes 98312 | tf_op jit(solution)/shard_map/ppermute | solution.py:713
  27.0 0.0 collective-permute-start.13
  27.0 0.0 collective-permute-start.11
  27.0 1.5 %collective-permute-start.10 = (f32[64,128]{1,0:T(8,128)S(1)}, f32[64,128]{1,0:T(8,128)S(1)}, u32[]{:S(2)}, u32[]{:S(2)}) collective-permute-start(f32[64,128]{1,0:T(8,128)S(1)} %get-tuple-element.81), channel_id=1, source_target_pairs={{0,8},{8,0},{16,24},{24,16},{1,9},{9,1},{17,25},{25,17},{2,10},{10... | collective-permute-start | bytes 98312 | tf_op jit(solution)/shard_map/ppermute | solution.py:713
  28.6 0.7 %inner.3 = (f32[512,128]{1,0:T(8,128)S(1)}, f32[512,128]{1,0:T(8,128)S(1)}, f32[16,128]{1,0:T(8,128)S(1)}) custom-call(f32[512,128]{1,0:T(8,128)S(1)} %get-tuple-element.80.before_image, f32[512,128]{1,0:T(8,128)S(1)} %get-tuple-element.70.diagonal, f32[512,128]{1,0:T(8,128)S(1)} %get-tuple-element.71.jacobi, ...), custom_call_target="tpu_custom_call" | custom-call | tf_op jit(solution)/shard_map/inner/pallas_call | solution.py:697
  29.2 2.1 %collective-permute-done.12.odd_y = f32[64,128]{1,0:T(8,128)S(1)} collective-permute-done((f32[64,128]{1,0:T(8,128)S(1)}, f32[64,128]{1,0:T(8,128)S(1)}, u32[]{:S(2)}, u32[]{:S(2)}) %collective-permute-start.12) | collective-permute-done | bytes 32800 | tf_op jit(solution)/shard_map/ppermute | solution.py:713
  31.3 0.0 collective-permute-done.13.even_y
  31.3 0.0 collective-permute-done.11.odd_x
  31.3 0.0 collective-permute-done.10.even_x
  31.3 0.6 %third.1 = (f32[512,128]{1,0:T(8,128)S(1)}, f32[512,128]{1,0:T(8,128)S(1)}, f32[64,128]{1,0:T(8,128)S(1)}, f32[64,128]{1,0:T(8,128)S(1)}, f32[64,128]{1,0:T(8,128)S(1)}, /*index=5*/f32[24,128]{1,0:T(8,128)S(1)}) custom-call(f32[512,128]{1,0:T(8,128)S(1)} %get-tuple-element.80.before_image, ...), custom_call_target="tpu_custom_call", output_to_operand_aliasing={{0}: (17, {}), {1}: (18, {})} | custom-call | tf_op jit(solution)/shard_map/third/pallas_call | solution.py:697
  31.9 0.7 %sums.1 = f32[32,2,128]{2,1,0:T(2,128)} custom-call(f32[8,128]{1,0:T(8,128)S(1)} %get-tuple-element.88.moments0, f32[16,128]{1,0:T(8,128)S(1)} %get-tuple-element.89.moments1, f32[24,128]{1,0:T(8,128)S(1)} %get-tuple-element.90.moments2), custom_call_target="tpu_custom_call" | custom-call | tf_op jit(solution)/shard_map/sums/pallas_call | solution.py:697
  32.6 3.6 %all-to-all-start = ((f32[32,2,128]{2,1,0:T(2,128)}), f32[32,2,128]{2,1,0:T(2,128)S(1)}, u32[]{:S(2)}, u32[]{:S(2)}) async-start(f32[32,2,128]{2,1,0:T(2,128)} %sums.1), calls=%async_computation | async-start | bytes 65536 | tf_op jit(solution)/shard_map/all_to_all | solution.py:765
  36.2 4.6 %collective-permute-start.16 = (f32[64,128]{1,0:T(8,128)S(1)}, f32[64,128]{1,0:T(8,128)S(1)}, u32[]{:S(2)}, u32[]{:S(2)}) collective-permute-start(f32[64,128]{1,0:T(8,128)S(1)} %get-tuple-element.95), channel_id=1, source_target_pairs={{0,7},{1,2},{2,1},{3,4},{4,3},{5,6},{6,5},{7,0},{8,15},{9,10},{10,... | collective-permute-start | bytes 98312 | tf_op jit(solution)/shard_map/ppermute | solution.py:713
  40.8 0.0 collective-permute-start.17
  40.8 1.0 %collective-permute-start.15 = (f32[64,128]{1,0:T(8,128)S(1)}, f32[64,128]{1,0:T(8,128)S(1)}, u32[]{:S(2)}, u32[]{:S(2)}) collective-permute-start(f32[64,128]{1,0:T(8,128)S(1)} %get-tuple-element.94), channel_id=1, source_target_pairs={{0,24},{8,16},{16,8},{24,0},{1,25},{9,17},{17,9},{25,1},{2,26},{10... | collective-permute-start | bytes 98312 | tf_op jit(solution)/shard_map/ppermute | solution.py:713
  41.8 0.6 %collective-permute-start.14 = (f32[64,128]{1,0:T(8,128)S(1)}, f32[64,128]{1,0:T(8,128)S(1)}, u32[]{:S(2)}, u32[]{:S(2)}) collective-permute-start(f32[64,128]{1,0:T(8,128)S(1)} %get-tuple-element.94), channel_id=1, source_target_pairs={{0,8},{8,0},{16,24},{24,16},{1,9},{9,1},{17,25},{25,17},{2,10},{10... | collective-permute-start | bytes 98312 | tf_op jit(solution)/shard_map/ppermute | solution.py:713
  42.4 1.0 %all-to-all-done.sums = f32[32,2,128]{2,1,0:T(2,128)S(1)} async-done(((f32[32,2,128]{2,1,0:T(2,128)}), f32[32,2,128]{2,1,0:T(2,128)S(1)}, u32[]{:S(2)}, u32[]{:S(2)}) %all-to-all-start) | async-done | bytes 32800 | tf_op jit(solution)/shard_map/all_to_all | solution.py:765
  43.4 1.2 %solution.1 = (f32[1,1,128,512]{3,2,1,0:T(8,128)}, f32[32,128]{1,0:T(8,128)S(1)}) custom-call(f32[512,128]{1,0:T(8,128)S(1)} %get-tuple-element.65.before.values0, f32[512,128]{1,0:T(8,128)S(1)} %get-tuple-element.79.before.values1, f32[512,128]{1,0:T(8,128)S(1)} %get-tuple-element.87.values2, f32[32,2,128]{2,1,0:T(2,128)S(1)} %all-to-all-done.sums, ...), custom_call_target="tpu_custom_call" | custom-call | tf_op jit(solution)/shard_map/solution/pallas_call | solution.py:697
  44.6 0.0 collective-permute-done.16.odd_y
  44.6 0.1 collective-permute-done.17.even_y
  44.7 0.0 collective-permute-done.15.odd_x
  44.7 0.0 collective-permute-done.14.even_x
  44.7 1.0 %last.1 = f32[1,1,128,512]{3,2,1,0:T(8,128)} custom-call(f32[512,128]{1,0:T(8,128)S(1)} %get-tuple-element.93.before_image, f32[64,128]{1,0:T(8,128)S(1)} %collective-permute-done.14.even_x, f32[64,128]{1,0:T(8,128)S(1)} %collective-permute-done.15.odd_x, f32[64,128]{1,0:T(8,128)S(1)} %collective-permute-done.16.odd_y, ...), custom_call_target="tpu_custom_call" | custom-call | tf_op jit(solution)/shard_map/last/pallas_call | solution.py:697
  (1 shorter events, 0.0 us)
Async XLA Ops:
  2.6 9.0 %collective-permute-start.2 = (f32[200,128]{1,0:T(8,128)S(1)}, f32[200,128]{1,0:T(8,128)S(1)}, u32[]{:S(2)}, u32[]{:S(2)}) collective-permute-start(f32[200,128]{1,0:T(8,128)S(1)} %get-tuple-element.53), channel_id=1, source_target_pairs={{0,7},{1,2},{2,1},{3,4},{4,3},{5,6},{6,5},{7,0},{8,15},{9,10},{10,... | collective-permute-start | bytes 307208 | tf_op jit(solution)/shard_map/ppermute | solution.py:713
  8.6 5.1 %collective-permute-start.3 = (f32[200,128]{1,0:T(8,128)S(1)}, f32[200,128]{1,0:T(8,128)S(1)}, u32[]{:S(2)}, u32[]{:S(2)}) collective-permute-start(f32[200,128]{1,0:T(8,128)S(1)} %get-tuple-element.54), channel_id=1, source_target_pairs={{0,1},{1,0},{2,3},{3,2},{4,5},{5,4},{6,7},{7,6},{8,9},{9,8},{10,11... | collective-permute-start | bytes 307208 | tf_op jit(solution)/shard_map/ppermute | solution.py:713
  8.6 6.8 %collective-permute-start.1 = (f32[192,128]{1,0:T(8,128)S(1)}, f32[192,128]{1,0:T(8,128)S(1)}, u32[]{:S(2)}, u32[]{:S(2)}) collective-permute-start(f32[192,128]{1,0:T(8,128)S(1)} %get-tuple-element.52), channel_id=1, source_target_pairs={{0,24},{8,16},{16,8},{24,0},{1,25},{9,17},{17,9},{25,1},{2,26},{10... | collective-permute-start | bytes 294920 | tf_op jit(solution)/shard_map/ppermute | solution.py:713
  9.3 6.1 %collective-permute-start = (f32[192,128]{1,0:T(8,128)S(1)}, f32[192,128]{1,0:T(8,128)S(1)}, u32[]{:S(2)}, u32[]{:S(2)}) collective-permute-start(f32[192,128]{1,0:T(8,128)S(1)} %get-tuple-element.52), channel_id=1, source_target_pairs={{0,8},{8,0},{16,24},{24,16},{1,9},{9,1},{17,25},{25,17},{2,10},{10... | collective-permute-start | bytes 294920 | tf_op jit(solution)/shard_map/ppermute | solution.py:713
  13.7 3.3 %collective-permute-start.5 = (f32[32,128]{1,0:T(8,128)S(1)}, f32[32,128]{1,0:T(8,128)S(1)}, u32[]{:S(2)}, u32[]{:S(2)}) collective-permute-start(f32[32,128]{1,0:T(8,128)S(1)} %corners.1), channel_id=1, source_target_pairs={{0,24},{8,16},{16,8},{24,0},{1,25},{9,17},{17,9},{25,1},{2,26},{10... | collective-permute-start | bytes 49160 | tf_op jit(solution)/shard_map/ppermute | solution.py:713
  14.3 2.8 %collective-permute-start.4 = (f32[32,128]{1,0:T(8,128)S(1)}, f32[32,128]{1,0:T(8,128)S(1)}, u32[]{:S(2)}, u32[]{:S(2)}) collective-permute-start(f32[32,128]{1,0:T(8,128)S(1)} %corners.1), channel_id=1, source_target_pairs={{0,8},{8,0},{16,24},{24,16},{1,9},{9,1},{17,25},{25,17},{2,10},{10... | collective-permute-start | bytes 49160 | tf_op jit(solution)/shard_map/ppermute | solution.py:713
  17.3 6.7 %collective-permute-start.8 = (f32[64,128]{1,0:T(8,128)S(1)}, f32[64,128]{1,0:T(8,128)S(1)}, u32[]{:S(2)}, u32[]{:S(2)}) collective-permute-start(f32[64,128]{1,0:T(8,128)S(1)} %get-tuple-element.68), channel_id=1, source_target_pairs={{0,7},{1,2},{2,1},{3,4},{4,3},{5,6},{6,5},{7,0},{8,15},{9,10},{10,... | collective-permute-start | bytes 98312 | tf_op jit(solution)/shard_map/ppermute | solution.py:713
  19.7 4.3 %collective-permute-start.9 = (f32[64,128]{1,0:T(8,128)S(1)}, f32[64,128]{1,0:T(8,128)S(1)}, u32[]{:S(2)}, u32[]{:S(2)}) collective-permute-start(f32[64,128]{1,0:T(8,128)S(1)} %get-tuple-element.69), channel_id=1, source_target_pairs={{0,1},{1,0},{2,3},{3,2},{4,5},{5,4},{6,7},{7,6},{8,9},{9,8},{10,11... | collective-permute-start | bytes 98312 | tf_op jit(solution)/shard_map/ppermute | solution.py:713
  19.7 4.3 %collective-permute-start.7 = (f32[64,128]{1,0:T(8,128)S(1)}, f32[64,128]{1,0:T(8,128)S(1)}, u32[]{:S(2)}, u32[]{:S(2)}) collective-permute-start(f32[64,128]{1,0:T(8,128)S(1)} %get-tuple-element.67), channel_id=1, source_target_pairs={{0,24},{8,16},{16,8},{24,0},{1,25},{9,17},{17,9},{25,1},{2,26},{10... | collective-permute-start | bytes 98312 | tf_op jit(solution)/shard_map/ppermute | solution.py:713
  19.7 4.3 %collective-permute-start.6 = (f32[64,128]{1,0:T(8,128)S(1)}, f32[64,128]{1,0:T(8,128)S(1)}, u32[]{:S(2)}, u32[]{:S(2)}) collective-permute-start(f32[64,128]{1,0:T(8,128)S(1)} %get-tuple-element.67), channel_id=1, source_target_pairs={{0,8},{8,0},{16,24},{24,16},{1,9},{9,1},{17,25},{25,17},{2,10},{10... | collective-permute-start | bytes 98312 | tf_op jit(solution)/shard_map/ppermute | solution.py:713
  24.6 6.7 %collective-permute-start.12 = (f32[64,128]{1,0:T(8,128)S(1)}, f32[64,128]{1,0:T(8,128)S(1)}, u32[]{:S(2)}, u32[]{:S(2)}) collective-permute-start(f32[64,128]{1,0:T(8,128)S(1)} %get-tuple-element.82), channel_id=1, source_target_pairs={{0,7},{1,2},{2,1},{3,4},{4,3},{5,6},{6,5},{7,0},{8,15},{9,10},{10,... | collective-permute-start | bytes 98312 | tf_op jit(solution)/shard_map/ppermute | solution.py:713
  27.0 4.3 %collective-permute-start.13 = (f32[64,128]{1,0:T(8,128)S(1)}, f32[64,128]{1,0:T(8,128)S(1)}, u32[]{:S(2)}, u32[]{:S(2)}) collective-permute-start(f32[64,128]{1,0:T(8,128)S(1)} %get-tuple-element.83), channel_id=1, source_target_pairs={{0,1},{1,0},{2,3},{3,2},{4,5},{5,4},{6,7},{7,6},{8,9},{9,8},{10,11... | collective-permute-start | bytes 98312 | tf_op jit(solution)/shard_map/ppermute | solution.py:713
  27.0 4.3 %collective-permute-start.11 = (f32[64,128]{1,0:T(8,128)S(1)}, f32[64,128]{1,0:T(8,128)S(1)}, u32[]{:S(2)}, u32[]{:S(2)}) collective-permute-start(f32[64,128]{1,0:T(8,128)S(1)} %get-tuple-element.81), channel_id=1, source_target_pairs={{0,24},{8,16},{16,8},{24,0},{1,25},{9,17},{17,9},{25,1},{2,26},{10... | collective-permute-start | bytes 98312 | tf_op jit(solution)/shard_map/ppermute | solution.py:713
  27.0 4.3 %collective-permute-start.10 = (f32[64,128]{1,0:T(8,128)S(1)}, f32[64,128]{1,0:T(8,128)S(1)}, u32[]{:S(2)}, u32[]{:S(2)}) collective-permute-start(f32[64,128]{1,0:T(8,128)S(1)} %get-tuple-element.81), channel_id=1, source_target_pairs={{0,8},{8,0},{16,24},{24,16},{1,9},{9,1},{17,25},{25,17},{2,10},{10... | collective-permute-start | bytes 98312 | tf_op jit(solution)/shard_map/ppermute | solution.py:713
  32.6 10.8 %all-to-all-start = ((f32[32,2,128]{2,1,0:T(2,128)}), f32[32,2,128]{2,1,0:T(2,128)S(1)}, u32[]{:S(2)}, u32[]{:S(2)}) async-start(f32[32,2,128]{2,1,0:T(2,128)} %sums.1), calls=%async_computation | async-start | bytes 65536 | tf_op jit(solution)/shard_map/all_to_all | solution.py:765
  36.2 8.4 %collective-permute-start.16 = (f32[64,128]{1,0:T(8,128)S(1)}, f32[64,128]{1,0:T(8,128)S(1)}, u32[]{:S(2)}, u32[]{:S(2)}) collective-permute-start(f32[64,128]{1,0:T(8,128)S(1)} %get-tuple-element.95), channel_id=1, source_target_pairs={{0,7},{1,2},{2,1},{3,4},{4,3},{5,6},{6,5},{7,0},{8,15},{9,10},{10,... | collective-permute-start | bytes 98312 | tf_op jit(solution)/shard_map/ppermute | solution.py:713
  40.8 3.9 %collective-permute-start.17 = (f32[64,128]{1,0:T(8,128)S(1)}, f32[64,128]{1,0:T(8,128)S(1)}, u32[]{:S(2)}, u32[]{:S(2)}) collective-permute-start(f32[64,128]{1,0:T(8,128)S(1)} %get-tuple-element.96), channel_id=1, source_target_pairs={{0,1},{1,0},{2,3},{3,2},{4,5},{5,4},{6,7},{7,6},{8,9},{9,8},{10,11... | collective-permute-start | bytes 98312 | tf_op jit(solution)/shard_map/ppermute | solution.py:713
  40.8 3.9 %collective-permute-start.15 = (f32[64,128]{1,0:T(8,128)S(1)}, f32[64,128]{1,0:T(8,128)S(1)}, u32[]{:S(2)}, u32[]{:S(2)}) collective-permute-start(f32[64,128]{1,0:T(8,128)S(1)} %get-tuple-element.94), channel_id=1, source_target_pairs={{0,24},{8,16},{16,8},{24,0},{1,25},{9,17},{17,9},{25,1},{2,26},{10... | collective-permute-start | bytes 98312 | tf_op jit(solution)/shard_map/ppermute | solution.py:713
  41.8 2.9 %collective-permute-start.14 = (f32[64,128]{1,0:T(8,128)S(1)}, f32[64,128]{1,0:T(8,128)S(1)}, u32[]{:S(2)}, u32[]{:S(2)}) collective-permute-start(f32[64,128]{1,0:T(8,128)S(1)} %get-tuple-element.94), channel_id=1, source_target_pairs={{0,8},{8,0},{16,24},{24,16},{1,9},{9,1},{17,25},{25,17},{2,10},{10... | collective-permute-start | bytes 98312 | tf_op jit(solution)/shard_map/ppermute | solution.py:713

commit v9 on v8

--- a/solution.py
+++ b/solution.py
@@ -400,6 +400,8 @@
                 out[row(a, b), :] = back[b]
     for b in range(8):
         packed[pl.ds(8 * b, 8), :] = packed_x(spread, b)
+        packed[pl.ds(64 + 8 * b, 8), :] = spread[row(b, 0), :]
+        packed[pl.ds(128 + 8 * b, 8), :] = spread[row(b, 7), :]
         back = along(
             DERIVATIVE.T, [spread[row(q, b), :] * outer_slope(q) for q in range(8)], -1
         )
@@ -505,6 +507,7 @@
     values, image, face_x, to_even, to_odd, moments, face, face_back,
 ):
     received = (even_x, odd_x, even_y, odd_y)
+    first = lane_index() < HALF
     zero = jnp.zeros((8, LANES), jnp.float32)
     cross, square = [zero] * 3, [zero] * 3
     sides = []
@@ -529,45 +532,44 @@
         add_packed(values, b, lines[b])
         cross[1] = cross[1] + scaled * old
         square[1] = square[1] + scaled * lines[b]
-    for b in range(8):
-        face[pl.ds(8 * b, 8), :] = lines[b]
-    back = vertical_part(
-        [face[pl.ds(c, 8, stride=8), :] for c in range(8)],
-        [packed[pl.ds(c, 8, stride=8), :] for c in range(8)],
-    )
-    for c in range(8):
-        face_back[pl.ds(c, 8, stride=8), :] = back[c]
+    for group, part in enumerate((lines, *sides)):
+        base = 64 * group
+        for k in range(8):
+            face[pl.ds(base + 8 * k, 8), :] = part[k]
+        back = vertical_part(
+            [face[pl.ds(base + c, 8, stride=8), :] for c in range(8)],
+            [packed[pl.ds(base + c, 8, stride=8), :] for c in range(8)],
+        )
+        for c in range(8):
+            face_back[pl.ds(base + c, 8, stride=8), :] = back[c]
     slopes = along(DERIVATIVE, lines, -1)
     back = along(DERIVATIVE.T, [slopes[q] * packed[pl.ds(8 * q, 8), :] for q in range(8)], -1)
-    for b in range(8):
-        share = back[b] + face_back[pl.ds(8 * b, 8), :]
-        if b not in (0, 7):
-            share = share + packed_x(mass, b) * lines[b]
-        add_packed(image, b, share)
+    shares = [back[b] + face_back[pl.ds(8 * b, 8), :] for b in range(8)]
+    for b in range(1, 7):
+        shares[b] = shares[b] + packed_x(mass, b) * lines[b]
     ends_back = [streamwise(sides[k], 7 * k, spread, mass) for k in range(2)]
+    energy = [zero] * 4
     for a in range(8):
         for b in range(8):
             rows = row(a, b)
             share = from_low[rows, :] * sides[0][a] + from_high[rows, :] * sides[1][a]
             if b in (0, 7):
-                share = share + ends_back[b // 7][a]
+                side = b // 7
+                share = share + ends_back[side][a]
+                share = share + face_back[pl.ds(64 + 64 * side + 8 * a, 8), :]
             else:
                 share = share + from_side[rows, :] * lines[b]
-            image[rows, :] += share
-    for b in (0, 7):
-        at = [pl.ds(8 * b + c, 8, stride=64) for c in range(8)]
-        back = vertical_part(
-            [values[at[c], :] for c in range(8)], [spread[at[c], :] for c in range(8)]
-        )
-        for c in range(8):
-            image[at[c], :] += back[c]
+            if a == 0:
+                share = share + jnp.where(first, shares[b], 0.0)
+            if a == 7:
+                share = share + jnp.where(first, 0.0, shares[b])
+            share = image[rows, :] + share
+            image[rows, :] = share
+            if moments.shape[0] > 16:
+                energy[b % 4] = energy[b % 4] + values[rows, :] * share
     moments[pl.ds(0, 8), :] = inner_moments[pl.ds(0, 8), :] + weighted(cross)
     moments[pl.ds(8, 8), :] = inner_moments[pl.ds(8, 8), :] + weighted(square)
     if moments.shape[0] > 16:
-        energy = [zero] * 4
-        for a in range(8):
-            for b in range(8):
-                energy[b % 4] = energy[b % 4] + values[row(a, b), :] * image[row(a, b), :]
         moments[pl.ds(16, 8), :] = (energy[0] + energy[1]) + (energy[2] + energy[3])
     join_layers(image)
     send_faces(image, values, outer, shifts, face_x, to_even, to_odd)
@@ -732,7 +734,7 @@
     [shared] = call(corners_kernel, "corners", [(32, LANES)], [], corners, *received_y)
     received = (*received_x, *received_y, *swapped((shared, shared), "gx"))
     *early, outer, moments0, from_low, from_high, from_side, packed = call(
-        early_kernel, "early", [grid] * 4 + [(208, LANES), tile] + [grid] * 3 + [face], [],
+        early_kernel, "early", [grid] * 4 + [(208, LANES), tile] + [grid] * 3 + [(192, LANES)], [],
         right, diagonal, *received_x, *received_y, spread, mass,
     )
     diagonal, jacobi, values0, image, out_x, *sent_y, moments0 = call(
@@ -750,7 +752,7 @@
         )
         return call(
             outer_kernel, name, [grid] * 2 + [face] * 3 + [(rows, LANES)],
-            [pltpu.VMEM(face, jnp.float32)] * 2,
+            [pltpu.VMEM((192, LANES), jnp.float32)] * 2,
             image, *received, diagonal, jacobi, before, *fixed, moments, values, inner_image,
             aliases={17: 0, 18: 1},
         )

time: 45.9 us -> 45.8 us (level)
  no operation moved by 1% of the time
where the time goes in v9:
time: 45.8 us; the launch traced here: 45.6 us
  starting transfers between devices  27 us (59%)
  waiting for transfers between devices  9.3 us (20%)
  Pallas kernels  8.59 us (19%)
  between operations  0.69 us (2%)
    ppermute x9, starting transfers between devices, swapped(): lax.ppermute(block[1], axis, odd)  17.6 us
    pallas_call x11, Pallas kernels, call(): pl.pallas_call(kernel, out_shape=[jax.ShapeDtypeStruct(shape, jnp.float32...  8.59 us
    ppermute x9, waiting for transfers between devices, swapped(): lax.ppermute(block[1], axis, odd)  6.04 us
    ppermute x9, starting transfers between devices, swapped(): lax.ppermute(block[0], axis, even)  5.81 us
    all_to_all x1, starting transfers between devices, body(): sums = lax.all_to_all(sums, ('gx', 'yz'), 0, 0)  3.57 us
    ppermute x9, waiting for transfers between devices, swapped(): lax.ppermute(block[0], axis, even)  2.27 us
    all_to_all x1, waiting for transfers between devices, body(): sums = lax.all_to_all(sums, ('gx', 'yz'), 0, 0)  0.99 us
  transfers between devices with their start and end apart: 19, of which 7 were waited for; matrix products, arithmetic and copies ran while one was open for 0% of the time, Pallas kernels for 8%

profile of v9, /device:TPU:0, one launch (start us, length us, event | category | flops | bytes accessed | tf_op | source)
XLA Modules:
  0.0 45.6 jit_solution(10584935155066020194)
XLA Ops:
  0.6 1.9 %setup.1 = (f32[512,128]{1,0:T(8,128)S(1)}, f32[512,128]{1,0:T(8,128)S(1)}, f32[512,128]{1,0:T(8,128)S(1)}, f32[512,128]{1,0:T(8,128)S(1)}, f32[192,128]{1,0:T(8...) custom-call(s32[1,128]{1,0:T(1,128)} %bitcast.1, ...), custom_call_target="tpu_custom_call" | custom-call | tf_op jit(solution)/shard_map/setup/pallas_call | solution.py:699
  2.6 6.0 %collective-permute-start.2 = (f32[200,128]{1,0:T(8,128)S(1)}, f32[200,128]{1,0:T(8,128)S(1)}, u32[]{:S(2)}, u32[]{:S(2)}) collective-permute-start(f32[200,128]{1,0:T(8,128)S(1)} %get-tuple-element.53), channel_id=1, source_target_pairs={{0,7},{1,2},{2,1},{3,4},{4,3},{5,6},{6,5},{7,0},{8,15},{9,10},{10,... | collective-permute-start | bytes 307208 | tf_op jit(solution)/shard_map/ppermute | solution.py:715
  8.6 0.0 collective-permute-start.3
  8.6 0.7 %collective-permute-start.1 = (f32[192,128]{1,0:T(8,128)S(1)}, f32[192,128]{1,0:T(8,128)S(1)}, u32[]{:S(2)}, u32[]{:S(2)}) collective-permute-start(f32[192,128]{1,0:T(8,128)S(1)} %get-tuple-element.52), channel_id=1, source_target_pairs={{0,24},{8,16},{16,8},{24,0},{1,25},{9,17},{17,9},{25,1},{2,26},{10... | collective-permute-start | bytes 294920 | tf_op jit(solution)/shard_map/ppermute | solution.py:715
  9.3 1.0 %collective-permute-start = (f32[192,128]{1,0:T(8,128)S(1)}, f32[192,128]{1,0:T(8,128)S(1)}, u32[]{:S(2)}, u32[]{:S(2)}) collective-permute-start(f32[192,128]{1,0:T(8,128)S(1)} %get-tuple-element.52), channel_id=1, source_target_pairs={{0,8},{8,0},{16,24},{24,16},{1,9},{9,1},{17,25},{25,17},{2,10},{10... | collective-permute-start | bytes 294920 | tf_op jit(solution)/shard_map/ppermute | solution.py:715
  10.3 1.3 %collective-permute-done.2.odd_y = f32[200,128]{1,0:T(8,128)S(1)} collective-permute-done((f32[200,128]{1,0:T(8,128)S(1)}, f32[200,128]{1,0:T(8,128)S(1)}, u32[]{:S(2)}, u32[]{:S(2)}) %collective-permute-start.2) | collective-permute-done | bytes 102432 | tf_op jit(solution)/shard_map/ppermute | solution.py:715
  11.6 2.1 %collective-permute-done.3.even_y = f32[200,128]{1,0:T(8,128)S(1)} collective-permute-done((f32[200,128]{1,0:T(8,128)S(1)}, f32[200,128]{1,0:T(8,128)S(1)}, u32[]{:S(2)}, u32[]{:S(2)}) %collective-permute-start.3) | collective-permute-done | bytes 102432 | tf_op jit(solution)/shard_map/ppermute | solution.py:715
  13.7 0.6 %collective-permute-start.5 = (f32[32,128]{1,0:T(8,128)S(1)}, f32[32,128]{1,0:T(8,128)S(1)}, u32[]{:S(2)}, u32[]{:S(2)}) collective-permute-start(f32[32,128]{1,0:T(8,128)S(1)} %corners.1), channel_id=1, source_target_pairs={{0,24},{8,16},{16,8},{24,0},{1,25},{9,17},{17,9},{25,1},{2,26},{10... | collective-permute-start | bytes 49160 | tf_op jit(solution)/shard_map/ppermute | solution.py:715
  14.3 1.1 %collective-permute-start.4 = (f32[32,128]{1,0:T(8,128)S(1)}, f32[32,128]{1,0:T(8,128)S(1)}, u32[]{:S(2)}, u32[]{:S(2)}) collective-permute-start(f32[32,128]{1,0:T(8,128)S(1)} %corners.1), channel_id=1, source_target_pairs={{0,8},{8,0},{16,24},{24,16},{1,9},{9,1},{17,25},{25,17},{2,10},{10... | collective-permute-start | bytes 49160 | tf_op jit(solution)/shard_map/ppermute | solution.py:715
  15.4 0.0 collective-permute-done.1.odd_x
  15.4 0.0 collective-permute-done.even_x
  15.4 1.1 %early.1 = (f32[512,128]{1,0:T(8,128)S(1)}, f32[512,128]{1,0:T(8,128)S(1)}, f32[512,128]{1,0:T(8,128)S(1)}, f32[512,128]{1,0:T(8,128)S(1)}, f32[208,128]{1,0:T(8...) custom-call(f32[512,128]{1,0:T(8,128)S(1)} %get-tuple-element.50.rig, ...), custom_call_target="tpu_custom_call" | custom-call | tf_op jit(solution)/shard_map/early/pallas_call | solution.py:699
  16.5 0.5 %collective-permute-done.5.odd_shared = f32[32,128]{1,0:T(8,128)S(1)} collective-permute-done((f32[32,128]{1,0:T(8,128)S(1)}, f32[32,128]{1,0:T(8,128)S(1)}, u32[]{:S(2)}, u32[]{:S(2)}) %collective-permute-start.5) | collective-permute-done | bytes 16416 | tf_op jit(solution)/shard_map/ppermute | solution.py:715
  17.0 0.0 collective-permute-done.4.even_shared
  17.0 0.3 first.1
  17.3 2.3 %collective-permute-start.8 = (f32[64,128]{1,0:T(8,128)S(1)}, f32[64,128]{1,0:T(8,128)S(1)}, u32[]{:S(2)}, u32[]{:S(2)}) collective-permute-start(f32[64,128]{1,0:T(8,128)S(1)} %get-tuple-element.68), channel_id=1, source_target_pairs={{0,7},{1,2},{2,1},{3,4},{4,3},{5,6},{6,5},{7,0},{8,15},{9,10},{10,... | collective-permute-start | bytes 98312 | tf_op jit(solution)/shard_map/ppermute | solution.py:715
  19.7 0.0 collective-permute-start.9
  19.7 0.0 collective-permute-start.7
  19.7 1.5 %collective-permute-start.6 = (f32[64,128]{1,0:T(8,128)S(1)}, f32[64,128]{1,0:T(8,128)S(1)}, u32[]{:S(2)}, u32[]{:S(2)}) collective-permute-start(f32[64,128]{1,0:T(8,128)S(1)} %get-tuple-element.67), channel_id=1, source_target_pairs={{0,8},{8,0},{16,24},{24,16},{1,9},{9,1},{17,25},{25,17},{2,10},{10... | collective-permute-start | bytes 98312 | tf_op jit(solution)/shard_map/ppermute | solution.py:715
  21.2 0.7 %inner.2 = (f32[512,128]{1,0:T(8,128)S(1)}, f32[512,128]{1,0:T(8,128)S(1)}, f32[16,128]{1,0:T(8,128)S(1)}) custom-call(f32[512,128]{1,0:T(8,128)S(1)} %get-tuple-element.66.before_image, f32[512,128]{1,0:T(8,128)S(1)} %get-tuple-element.70.diagonal, f32[512,128]{1,0:T(8,128)S(1)} %get-tuple-element.71.jacobi, ...), custom_call_target="tpu_custom_call" | custom-call | tf_op jit(solution)/shard_map/inner/pallas_call | solution.py:699
  21.9 2.1 %collective-permute-done.8.odd_y = f32[64,128]{1,0:T(8,128)S(1)} collective-permute-done((f32[64,128]{1,0:T(8,128)S(1)}, f32[64,128]{1,0:T(8,128)S(1)}, u32[]{:S(2)}, u32[]{:S(2)}) %collective-permute-start.8) | collective-permute-done | bytes 32800 | tf_op jit(solution)/shard_map/ppermute | solution.py:715
  24.0 0.0 collective-permute-done.9.even_y
  24.0 0.0 collective-permute-done.7.odd_x
  24.0 0.0 collective-permute-done.6.even_x
  24.0 0.5 %second.1 = (f32[512,128]{1,0:T(8,128)S(1)}, f32[512,128]{1,0:T(8,128)S(1)}, f32[64,128]{1,0:T(8,128)S(1)}, f32[64,128]{1,0:T(8,128)S(1)}, f32[64,128]{1,0:T(8,128)S(1)}, /*index=5*/f32[16,128]{1,0:T(8,128)S(1)}) custom-call(f32[512,128]{1,0:T(8,128)S(1)} %get-tuple-element.66.before_image, ...), custom_call_target="tpu_custom_call", output_to_operand_aliasing={{0}: (17, {}), {1}: (18, {})} | custom-call | tf_op jit(solution)/shard_map/second/pallas_call | solution.py:699
  24.5 2.4 %collective-permute-start.12 = (f32[64,128]{1,0:T(8,128)S(1)}, f32[64,128]{1,0:T(8,128)S(1)}, u32[]{:S(2)}, u32[]{:S(2)}) collective-permute-start(f32[64,128]{1,0:T(8,128)S(1)} %get-tuple-element.82), channel_id=1, source_target_pairs={{0,7},{1,2},{2,1},{3,4},{4,3},{5,6},{6,5},{7,0},{8,15},{9,10},{10,... | collective-permute-start | bytes 98312 | tf_op jit(solution)/shard_map/ppermute | solution.py:715
  27.0 0.0 collective-permute-start.13
  27.0 0.0 collective-permute-start.11
  27.0 1.5 %collective-permute-start.10 = (f32[64,128]{1,0:T(8,128)S(1)}, f32[64,128]{1,0:T(8,128)S(1)}, u32[]{:S(2)}, u32[]{:S(2)}) collective-permute-start(f32[64,128]{1,0:T(8,128)S(1)} %get-tuple-element.81), channel_id=1, source_target_pairs={{0,8},{8,0},{16,24},{24,16},{1,9},{9,1},{17,25},{25,17},{2,10},{10... | collective-permute-start | bytes 98312 | tf_op jit(solution)/shard_map/ppermute | solution.py:715
  28.5 0.7 %inner.3 = (f32[512,128]{1,0:T(8,128)S(1)}, f32[512,128]{1,0:T(8,128)S(1)}, f32[16,128]{1,0:T(8,128)S(1)}) custom-call(f32[512,128]{1,0:T(8,128)S(1)} %get-tuple-element.80.before_image, f32[512,128]{1,0:T(8,128)S(1)} %get-tuple-element.70.diagonal, f32[512,128]{1,0:T(8,128)S(1)} %get-tuple-element.71.jacobi, ...), custom_call_target="tpu_custom_call" | custom-call | tf_op jit(solution)/shard_map/inner/pallas_call | solution.py:699
  29.2 2.1 %collective-permute-done.12.odd_y = f32[64,128]{1,0:T(8,128)S(1)} collective-permute-done((f32[64,128]{1,0:T(8,128)S(1)}, f32[64,128]{1,0:T(8,128)S(1)}, u32[]{:S(2)}, u32[]{:S(2)}) %collective-permute-start.12) | collective-permute-done | bytes 32800 | tf_op jit(solution)/shard_map/ppermute | solution.py:715
  31.2 0.0 collective-permute-done.13.even_y
  31.2 0.0 collective-permute-done.11.odd_x
  31.2 0.0 collective-permute-done.10.even_x
  31.2 0.5 %third.1 = (f32[512,128]{1,0:T(8,128)S(1)}, f32[512,128]{1,0:T(8,128)S(1)}, f32[64,128]{1,0:T(8,128)S(1)}, f32[64,128]{1,0:T(8,128)S(1)}, f32[64,128]{1,0:T(8,128)S(1)}, /*index=5*/f32[24,128]{1,0:T(8,128)S(1)}) custom-call(f32[512,128]{1,0:T(8,128)S(1)} %get-tuple-element.80.before_image, ...), custom_call_target="tpu_custom_call", output_to_operand_aliasing={{0}: (17, {}), {1}: (18, {})} | custom-call | tf_op jit(solution)/shard_map/third/pallas_call | solution.py:699
  31.8 0.7 %sums.1 = f32[32,2,128]{2,1,0:T(2,128)} custom-call(f32[8,128]{1,0:T(8,128)S(1)} %get-tuple-element.88.moments0, f32[16,128]{1,0:T(8,128)S(1)} %get-tuple-element.89.moments1, f32[24,128]{1,0:T(8,128)S(1)} %get-tuple-element.90.moments2), custom_call_target="tpu_custom_call" | custom-call | tf_op jit(solution)/shard_map/sums/pallas_call | solution.py:699
  32.5 3.6 %all-to-all-start = ((f32[32,2,128]{2,1,0:T(2,128)}), f32[32,2,128]{2,1,0:T(2,128)S(1)}, u32[]{:S(2)}, u32[]{:S(2)}) async-start(f32[32,2,128]{2,1,0:T(2,128)} %sums.1), calls=%async_computation | async-start | bytes 65536 | tf_op jit(solution)/shard_map/all_to_all | solution.py:767
  36.0 4.6 %collective-permute-start.16 = (f32[64,128]{1,0:T(8,128)S(1)}, f32[64,128]{1,0:T(8,128)S(1)}, u32[]{:S(2)}, u32[]{:S(2)}) collective-permute-start(f32[64,128]{1,0:T(8,128)S(1)} %get-tuple-element.95), channel_id=1, source_target_pairs={{0,7},{1,2},{2,1},{3,4},{4,3},{5,6},{6,5},{7,0},{8,15},{9,10},{10,... | collective-permute-start | bytes 98312 | tf_op jit(solution)/shard_map/ppermute | solution.py:715
  40.6 0.0 collective-permute-start.17
  40.6 1.0 %collective-permute-start.15 = (f32[64,128]{1,0:T(8,128)S(1)}, f32[64,128]{1,0:T(8,128)S(1)}, u32[]{:S(2)}, u32[]{:S(2)}) collective-permute-start(f32[64,128]{1,0:T(8,128)S(1)} %get-tuple-element.94), channel_id=1, source_target_pairs={{0,24},{8,16},{16,8},{24,0},{1,25},{9,17},{17,9},{25,1},{2,26},{10... | collective-permute-start | bytes 98312 | tf_op jit(solution)/shard_map/ppermute | solution.py:715
  41.6 0.6 %collective-permute-start.14 = (f32[64,128]{1,0:T(8,128)S(1)}, f32[64,128]{1,0:T(8,128)S(1)}, u32[]{:S(2)}, u32[]{:S(2)}) collective-permute-start(f32[64,128]{1,0:T(8,128)S(1)} %get-tuple-element.94), channel_id=1, source_target_pairs={{0,8},{8,0},{16,24},{24,16},{1,9},{9,1},{17,25},{25,17},{2,10},{10... | collective-permute-start | bytes 98312 | tf_op jit(solution)/shard_map/ppermute | solution.py:715
  42.3 1.0 %all-to-all-done.sums = f32[32,2,128]{2,1,0:T(2,128)S(1)} async-done(((f32[32,2,128]{2,1,0:T(2,128)}), f32[32,2,128]{2,1,0:T(2,128)S(1)}, u32[]{:S(2)}, u32[]{:S(2)}) %all-to-all-start) | async-done | bytes 32800 | tf_op jit(solution)/shard_map/all_to_all | solution.py:767
  43.2 1.2 %solution.1 = (f32[1,1,128,512]{3,2,1,0:T(8,128)}, f32[32,128]{1,0:T(8,128)S(1)}) custom-call(f32[512,128]{1,0:T(8,128)S(1)} %get-tuple-element.65.before.values0, f32[512,128]{1,0:T(8,128)S(1)} %get-tuple-element.79.before.values1, f32[512,128]{1,0:T(8,128)S(1)} %get-tuple-element.87.values2, f32[32,2,128]{2,1,0:T(2,128)S(1)} %all-to-all-done.sums, ...), custom_call_target="tpu_custom_call" | custom-call | tf_op jit(solution)/shard_map/solution/pallas_call | solution.py:699
  44.4 0.0 collective-permute-done.16.odd_y
  44.4 0.1 collective-permute-done.17.even_y
  44.6 0.0 collective-permute-done.15.odd_x
  44.6 0.0 collective-permute-done.14.even_x
  44.6 1.0 %last.1 = f32[1,1,128,512]{3,2,1,0:T(8,128)} custom-call(f32[512,128]{1,0:T(8,128)S(1)} %get-tuple-element.93.before_image, f32[64,128]{1,0:T(8,128)S(1)} %collective-permute-done.14.even_x, f32[64,128]{1,0:T(8,128)S(1)} %collective-permute-done.15.odd_x, f32[64,128]{1,0:T(8,128)S(1)} %collective-permute-done.16.odd_y, ...), custom_call_target="tpu_custom_call" | custom-call | tf_op jit(solution)/shard_map/last/pallas_call | solution.py:699
  (1 shorter events, 0.0 us)
Async XLA Ops:
  2.6 9.0 %collective-permute-start.2 = (f32[200,128]{1,0:T(8,128)S(1)}, f32[200,128]{1,0:T(8,128)S(1)}, u32[]{:S(2)}, u32[]{:S(2)}) collective-permute-start(f32[200,128]{1,0:T(8,128)S(1)} %get-tuple-element.53), channel_id=1, source_target_pairs={{0,7},{1,2},{2,1},{3,4},{4,3},{5,6},{6,5},{7,0},{8,15},{9,10},{10,... | collective-permute-start | bytes 307208 | tf_op jit(solution)/shard_map/ppermute | solution.py:715
  8.6 5.1 %collective-permute-start.3 = (f32[200,128]{1,0:T(8,128)S(1)}, f32[200,128]{1,0:T(8,128)S(1)}, u32[]{:S(2)}, u32[]{:S(2)}) collective-permute-start(f32[200,128]{1,0:T(8,128)S(1)} %get-tuple-element.54), channel_id=1, source_target_pairs={{0,1},{1,0},{2,3},{3,2},{4,5},{5,4},{6,7},{7,6},{8,9},{9,8},{10,11... | collective-permute-start | bytes 307208 | tf_op jit(solution)/shard_map/ppermute | solution.py:715
  8.6 6.8 %collective-permute-start.1 = (f32[192,128]{1,0:T(8,128)S(1)}, f32[192,128]{1,0:T(8,128)S(1)}, u32[]{:S(2)}, u32[]{:S(2)}) collective-permute-start(f32[192,128]{1,0:T(8,128)S(1)} %get-tuple-element.52), channel_id=1, source_target_pairs={{0,24},{8,16},{16,8},{24,0},{1,25},{9,17},{17,9},{25,1},{2,26},{10... | collective-permute-start | bytes 294920 | tf_op jit(solution)/shard_map/ppermute | solution.py:715
  9.3 6.1 %collective-permute-start = (f32[192,128]{1,0:T(8,128)S(1)}, f32[192,128]{1,0:T(8,128)S(1)}, u32[]{:S(2)}, u32[]{:S(2)}) collective-permute-start(f32[192,128]{1,0:T(8,128)S(1)} %get-tuple-element.52), channel_id=1, source_target_pairs={{0,8},{8,0},{16,24},{24,16},{1,9},{9,1},{17,25},{25,17},{2,10},{10... | collective-permute-start | bytes 294920 | tf_op jit(solution)/shard_map/ppermute | solution.py:715
  13.7 3.3 %collective-permute-start.5 = (f32[32,128]{1,0:T(8,128)S(1)}, f32[32,128]{1,0:T(8,128)S(1)}, u32[]{:S(2)}, u32[]{:S(2)}) collective-permute-start(f32[32,128]{1,0:T(8,128)S(1)} %corners.1), channel_id=1, source_target_pairs={{0,24},{8,16},{16,8},{24,0},{1,25},{9,17},{17,9},{25,1},{2,26},{10... | collective-permute-start | bytes 49160 | tf_op jit(solution)/shard_map/ppermute | solution.py:715
  14.3 2.8 %collective-permute-start.4 = (f32[32,128]{1,0:T(8,128)S(1)}, f32[32,128]{1,0:T(8,128)S(1)}, u32[]{:S(2)}, u32[]{:S(2)}) collective-permute-start(f32[32,128]{1,0:T(8,128)S(1)} %corners.1), channel_id=1, source_target_pairs={{0,8},{8,0},{16,24},{24,16},{1,9},{9,1},{17,25},{25,17},{2,10},{10... | collective-permute-start | bytes 49160 | tf_op jit(solution)/shard_map/ppermute | solution.py:715
  17.3 6.7 %collective-permute-start.8 = (f32[64,128]{1,0:T(8,128)S(1)}, f32[64,128]{1,0:T(8,128)S(1)}, u32[]{:S(2)}, u32[]{:S(2)}) collective-permute-start(f32[64,128]{1,0:T(8,128)S(1)} %get-tuple-element.68), channel_id=1, source_target_pairs={{0,7},{1,2},{2,1},{3,4},{4,3},{5,6},{6,5},{7,0},{8,15},{9,10},{10,... | collective-permute-start | bytes 98312 | tf_op jit(solution)/shard_map/ppermute | solution.py:715
  19.7 4.3 %collective-permute-start.9 = (f32[64,128]{1,0:T(8,128)S(1)}, f32[64,128]{1,0:T(8,128)S(1)}, u32[]{:S(2)}, u32[]{:S(2)}) collective-permute-start(f32[64,128]{1,0:T(8,128)S(1)} %get-tuple-element.69), channel_id=1, source_target_pairs={{0,1},{1,0},{2,3},{3,2},{4,5},{5,4},{6,7},{7,6},{8,9},{9,8},{10,11... | collective-permute-start | bytes 98312 | tf_op jit(solution)/shard_map/ppermute | solution.py:715
  19.7 4.3 %collective-permute-start.7 = (f32[64,128]{1,0:T(8,128)S(1)}, f32[64,128]{1,0:T(8,128)S(1)}, u32[]{:S(2)}, u32[]{:S(2)}) collective-permute-start(f32[64,128]{1,0:T(8,128)S(1)} %get-tuple-element.67), channel_id=1, source_target_pairs={{0,24},{8,16},{16,8},{24,0},{1,25},{9,17},{17,9},{25,1},{2,26},{10... | collective-permute-start | bytes 98312 | tf_op jit(solution)/shard_map/ppermute | solution.py:715
  19.7 4.3 %collective-permute-start.6 = (f32[64,128]{1,0:T(8,128)S(1)}, f32[64,128]{1,0:T(8,128)S(1)}, u32[]{:S(2)}, u32[]{:S(2)}) collective-permute-start(f32[64,128]{1,0:T(8,128)S(1)} %get-tuple-element.67), channel_id=1, source_target_pairs={{0,8},{8,0},{16,24},{24,16},{1,9},{9,1},{17,25},{25,17},{2,10},{10... | collective-permute-start | bytes 98312 | tf_op jit(solution)/shard_map/ppermute | solution.py:715
  24.5 6.7 %collective-permute-start.12 = (f32[64,128]{1,0:T(8,128)S(1)}, f32[64,128]{1,0:T(8,128)S(1)}, u32[]{:S(2)}, u32[]{:S(2)}) collective-permute-start(f32[64,128]{1,0:T(8,128)S(1)} %get-tuple-element.82), channel_id=1, source_target_pairs={{0,7},{1,2},{2,1},{3,4},{4,3},{5,6},{6,5},{7,0},{8,15},{9,10},{10,... | collective-permute-start | bytes 98312 | tf_op jit(solution)/shard_map/ppermute | solution.py:715
  27.0 4.3 %collective-permute-start.13 = (f32[64,128]{1,0:T(8,128)S(1)}, f32[64,128]{1,0:T(8,128)S(1)}, u32[]{:S(2)}, u32[]{:S(2)}) collective-permute-start(f32[64,128]{1,0:T(8,128)S(1)} %get-tuple-element.83), channel_id=1, source_target_pairs={{0,1},{1,0},{2,3},{3,2},{4,5},{5,4},{6,7},{7,6},{8,9},{9,8},{10,11... | collective-permute-start | bytes 98312 | tf_op jit(solution)/shard_map/ppermute | solution.py:715
  27.0 4.3 %collective-permute-start.11 = (f32[64,128]{1,0:T(8,128)S(1)}, f32[64,128]{1,0:T(8,128)S(1)}, u32[]{:S(2)}, u32[]{:S(2)}) collective-permute-start(f32[64,128]{1,0:T(8,128)S(1)} %get-tuple-element.81), channel_id=1, source_target_pairs={{0,24},{8,16},{16,8},{24,0},{1,25},{9,17},{17,9},{25,1},{2,26},{10... | collective-permute-start | bytes 98312 | tf_op jit(solution)/shard_map/ppermute | solution.py:715
  27.0 4.3 %collective-permute-start.10 = (f32[64,128]{1,0:T(8,128)S(1)}, f32[64,128]{1,0:T(8,128)S(1)}, u32[]{:S(2)}, u32[]{:S(2)}) collective-permute-start(f32[64,128]{1,0:T(8,128)S(1)} %get-tuple-element.81), channel_id=1, source_target_pairs={{0,8},{8,0},{16,24},{24,16},{1,9},{9,1},{17,25},{25,17},{2,10},{10... | collective-permute-start | bytes 98312 | tf_op jit(solution)/shard_map/ppermute | solution.py:715
  32.5 10.8 %all-to-all-start = ((f32[32,2,128]{2,1,0:T(2,128)}), f32[32,2,128]{2,1,0:T(2,128)S(1)}, u32[]{:S(2)}, u32[]{:S(2)}) async-start(f32[32,2,128]{2,1,0:T(2,128)} %sums.1), calls=%async_computation | async-start | bytes 65536 | tf_op jit(solution)/shard_map/all_to_all | solution.py:767
  36.0 8.4 %collective-permute-start.16 = (f32[64,128]{1,0:T(8,128)S(1)}, f32[64,128]{1,0:T(8,128)S(1)}, u32[]{:S(2)}, u32[]{:S(2)}) collective-permute-start(f32[64,128]{1,0:T(8,128)S(1)} %get-tuple-element.95), channel_id=1, source_target_pairs={{0,7},{1,2},{2,1},{3,4},{4,3},{5,6},{6,5},{7,0},{8,15},{9,10},{10,... | collective-permute-start | bytes 98312 | tf_op jit(solution)/shard_map/ppermute | solution.py:715
  40.6 3.9 %collective-permute-start.17 = (f32[64,128]{1,0:T(8,128)S(1)}, f32[64,128]{1,0:T(8,128)S(1)}, u32[]{:S(2)}, u32[]{:S(2)}) collective-permute-start(f32[64,128]{1,0:T(8,128)S(1)} %get-tuple-element.96), channel_id=1, source_target_pairs={{0,1},{1,0},{2,3},{3,2},{4,5},{5,4},{6,7},{7,6},{8,9},{9,8},{10,11... | collective-permute-start | bytes 98312 | tf_op jit(solution)/shard_map/ppermute | solution.py:715
  40.6 3.9 %collective-permute-start.15 = (f32[64,128]{1,0:T(8,128)S(1)}, f32[64,128]{1,0:T(8,128)S(1)}, u32[]{:S(2)}, u32[]{:S(2)}) collective-permute-start(f32[64,128]{1,0:T(8,128)S(1)} %get-tuple-element.94), channel_id=1, source_target_pairs={{0,24},{8,16},{16,8},{24,0},{1,25},{9,17},{17,9},{25,1},{2,26},{10... | collective-permute-start | bytes 98312 | tf_op jit(solution)/shard_map/ppermute | solution.py:715
  41.6 2.9 %collective-permute-start.14 = (f32[64,128]{1,0:T(8,128)S(1)}, f32[64,128]{1,0:T(8,128)S(1)}, u32[]{:S(2)}, u32[]{:S(2)}) collective-permute-start(f32[64,128]{1,0:T(8,128)S(1)} %get-tuple-element.94), channel_id=1, source_target_pairs={{0,8},{8,0},{16,24},{24,16},{1,9},{9,1},{17,25},{25,17},{2,10},{10... | collective-permute-start | bytes 98312 | tf_op jit(solution)/shard_map/ppermute | solution.py:715

commit v10 on v9

--- a/solution.py
+++ b/solution.py
@@ -503,8 +503,8 @@
 
 def outer_kernel(
     before_image, even_x, odd_x, odd_y, even_y, diagonal, jacobi, before, spread, mass, shifts,
-    outer, from_low, from_high, from_side, packed, inner_moments, inner_values, inner_image,
-    values, image, face_x, to_even, to_odd, moments, face, face_back,
+    outer, from_low, from_high, from_side, packed, inner_moments, earlier, inner_values,
+    inner_image, values, image, face_x, to_even, to_odd, moments, face, face_back, *summed,
 ):
     received = (even_x, odd_x, even_y, odd_y)
     first = lane_index() < HALF
@@ -565,26 +565,34 @@
                 share = share + jnp.where(first, 0.0, shares[b])
             share = image[rows, :] + share
             image[rows, :] = share
-            if moments.shape[0] > 16:
+            if summed:
                 energy[b % 4] = energy[b % 4] + values[rows, :] * share
-    moments[pl.ds(0, 8), :] = inner_moments[pl.ds(0, 8), :] + weighted(cross)
-    moments[pl.ds(8, 8), :] = inner_moments[pl.ds(8, 8), :] + weighted(square)
-    if moments.shape[0] > 16:
-        moments[pl.ds(16, 8), :] = (energy[0] + energy[1]) + (energy[2] + energy[3])
+    cross = inner_moments[pl.ds(0, 8), :] + weighted(cross)
+    square = inner_moments[pl.ds(8, 8), :] + weighted(square)
+    if summed:
+        held, copied = summed
+        energy = (energy[0] + energy[1]) + (energy[2] + energy[3])
+        parts = [earlier[pl.ds(8 * k, 8), :] for k in range(3)] + [cross, square, energy]
+        held[...] = jnp.broadcast_to(sums_line(parts)[None], held.shape)
+        copy = pltpu.make_async_copy(held, moments, copied)
+        copy.start()
+    else:
+        moments[pl.ds(0, 8), :] = earlier[...]
+        moments[pl.ds(8, 8), :] = cross
+        moments[pl.ds(16, 8), :] = square
     join_layers(image)
     send_faces(image, values, outer, shifts, face_x, to_even, to_odd)
-
-
-def sums_kernel(moments0, moments1, moments2, sums):
-    parts = [
-        moments0[...], moments1[pl.ds(0, 8), :], moments1[pl.ds(8, 8), :], *(moments2[pl.ds(8 * k, 8), :] for k in range(3))
-    ]
+    if summed:
+        copy.wait()
+
+
+def sums_line(parts):
     lane = lax.broadcasted_iota(jnp.int32, (1, LANES), 1)
     line = jnp.zeros((1, LANES), jnp.float32)
     for k, part in enumerate(parts):
         total = jnp.sum(jnp.sum(part, 0, keepdims=True), 1, keepdims=True)
         line = jnp.where(lane == k, total, line)
-    sums[...] = jnp.broadcast_to(line[None], sums.shape)
+    return line
 
 
 def recurrence(moments):
@@ -690,7 +698,7 @@
     residual[0, 0] = to_slots(chosen, residual_grid[...])
 
 
-def call(kernel, name, shapes, scratch, *operands, outside=0, aliases=None):
+def call(kernel, name, shapes, scratch, *operands, outside=0, aliases=None, copied=0):
     places = [pltpu.HBM] * outside + [pltpu.VMEM] * (len(operands) - outside)
     operands = [
         pltpu.with_memory_space_constraint(operand, place) if place == pltpu.HBM else operand
@@ -700,7 +708,8 @@
         kernel,
         out_shape=[jax.ShapeDtypeStruct(shape, jnp.float32) for shape in shapes],
         in_specs=[pl.BlockSpec(memory_space=place) for place in places],
-        out_specs=[pl.BlockSpec(memory_space=pltpu.VMEM)] * len(shapes),
+        out_specs=[pl.BlockSpec(memory_space=pltpu.VMEM)] * (len(shapes) - copied)
+        + [pl.BlockSpec(memory_space=pltpu.HBM)] * copied,
         scratch_shapes=scratch,
         input_output_aliases=aliases or {},
         compiler_params=pltpu.CompilerParams(vmem_limit_bytes=VMEM_BYTES),
@@ -744,26 +753,29 @@
     )
     fixed = (spread, mass, shifts, outer, from_low, from_high, from_side, packed)
 
-    def advance(name, rows, image, before, out_x, sent_y):
+    def advance(name, earlier, image, before, out_x, sent_y, last=False):
         received = (*swapped((out_x, out_x), "gx"), *swapped(sent_y, "yz")[::-1])
         values, inner_image, moments = call(
             inner_kernel, "inner", [grid] * 2 + [(16, LANES)], [],
             image, diagonal, jacobi, before, spread, mass,
         )
+        out = (devices, 2, LANES) if last else (24, LANES)
+        scratch = [pltpu.VMEM((192, LANES), jnp.float32)] * 2
+        if last:
+            scratch = scratch + [pltpu.VMEM(out, jnp.float32), pltpu.SemaphoreType.DMA]
         return call(
-            outer_kernel, name, [grid] * 2 + [face] * 3 + [(rows, LANES)],
-            [pltpu.VMEM((192, LANES), jnp.float32)] * 2,
-            image, *received, diagonal, jacobi, before, *fixed, moments, values, inner_image,
-            aliases={17: 0, 18: 1},
+            outer_kernel, name, [grid] * 2 + [face] * 3 + [out], scratch,
+            image, *received, diagonal, jacobi, before, *fixed, moments, earlier, values,
+            inner_image,
+            aliases={18: 0, 19: 1}, copied=int(last),
         )
 
     values1, image, out_x, *sent_y, moments1 = advance(
-        "second", 16, image, values0, out_x, sent_y
-    )
-    values2, image, out_x, *sent_y, moments2 = advance(
-        "third", 24, image, values1, out_x, sent_y
-    )
-    [sums] = call(sums_kernel, "sums", [(devices, 2, LANES)], [], moments0, moments1, moments2)
+        "second", moments0, image, values0, out_x, sent_y
+    )
+    values2, image, out_x, *sent_y, sums = advance(
+        "third", moments1, image, values1, out_x, sent_y, last=True
+    )
     sums = lax.all_to_all(sums, ("gx", "yz"), 0, 0)
     received = (*swapped((out_x, out_x), "gx"), *swapped(sent_y, "yz")[::-1])
     result, precond = call(

time: 45.8 us -> 45.7 us (level)
    pallas_call x11 -> x10, Pallas kernels: 8.59 us -> 8.51 us  [call(): pl.pallas_call(kernel, out_shape=[jax.ShapeDtypeStruct(shape, jnp.float32...]
where the time goes in v10:
time: 45.7 us; the launch traced here: 45.5 us
  starting transfers between devices  27 us (59%)
  waiting for transfers between devices  9.3 us (20%)
  Pallas kernels  8.51 us (19%)
  between operations  0.7 us (2%)
    ppermute x9, starting transfers between devices, swapped(): lax.ppermute(block[1], axis, odd)  17.6 us
    pallas_call x10, Pallas kernels, call(): pl.pallas_call(kernel, out_shape=[jax.ShapeDtypeStruct(shape, jnp.float32...  8.51 us
    ppermute x9, waiting for transfers between devices, swapped(): lax.ppermute(block[1], axis, odd)  6.04 us
    ppermute x9, starting transfers between devices, swapped(): lax.ppermute(block[0], axis, even)  5.81 us
    all_to_all x1, starting transfers between devices, body(): sums = lax.all_to_all(sums, ('gx', 'yz'), 0, 0)  3.58 us
    ppermute x9, waiting for transfers between devices, swapped(): lax.ppermute(block[0], axis, even)  2.27 us
    all_to_all x1, waiting for transfers between devices, body(): sums = lax.all_to_all(sums, ('gx', 'yz'), 0, 0)  0.99 us
  transfers between devices with their start and end apart: 19, of which 7 were waited for; matrix products, arithmetic and copies ran while one was open for 0% of the time, Pallas kernels for 8%

profile of v10, /device:TPU:0, one launch (start us, length us, event | category | flops | bytes accessed | tf_op | source)
XLA Modules:
  0.0 45.5 jit_solution(12177362997413279215)
XLA Ops:
  0.6 1.9 %setup.1 = (f32[512,128]{1,0:T(8,128)S(1)}, f32[512,128]{1,0:T(8,128)S(1)}, f32[512,128]{1,0:T(8,128)S(1)}, f32[512,128]{1,0:T(8,128)S(1)}, f32[192,128]{1,0:T(8...) custom-call(s32[1,128]{1,0:T(1,128)} %bitcast.1, ...), custom_call_target="tpu_custom_call" | custom-call | tf_op jit(solution)/shard_map/setup/pallas_call | solution.py:707
  2.6 6.0 %collective-permute-start.2 = (f32[200,128]{1,0:T(8,128)S(1)}, f32[200,128]{1,0:T(8,128)S(1)}, u32[]{:S(2)}, u32[]{:S(2)}) collective-permute-start(f32[200,128]{1,0:T(8,128)S(1)} %get-tuple-element.53), channel_id=1, source_target_pairs={{0,7},{1,2},{2,1},{3,4},{4,3},{5,6},{6,5},{7,0},{8,15},{9,10},{10,... | collective-permute-start | bytes 307208 | tf_op jit(solution)/shard_map/ppermute | solution.py:724
  8.6 0.0 collective-permute-start.3
  8.6 0.7 %collective-permute-start.1 = (f32[192,128]{1,0:T(8,128)S(1)}, f32[192,128]{1,0:T(8,128)S(1)}, u32[]{:S(2)}, u32[]{:S(2)}) collective-permute-start(f32[192,128]{1,0:T(8,128)S(1)} %get-tuple-element.52), channel_id=1, source_target_pairs={{0,24},{8,16},{16,8},{24,0},{1,25},{9,17},{17,9},{25,1},{2,26},{10... | collective-permute-start | bytes 294920 | tf_op jit(solution)/shard_map/ppermute | solution.py:724
  9.3 1.0 %collective-permute-start = (f32[192,128]{1,0:T(8,128)S(1)}, f32[192,128]{1,0:T(8,128)S(1)}, u32[]{:S(2)}, u32[]{:S(2)}) collective-permute-start(f32[192,128]{1,0:T(8,128)S(1)} %get-tuple-element.52), channel_id=1, source_target_pairs={{0,8},{8,0},{16,24},{24,16},{1,9},{9,1},{17,25},{25,17},{2,10},{10... | collective-permute-start | bytes 294920 | tf_op jit(solution)/shard_map/ppermute | solution.py:724
  10.3 1.3 %collective-permute-done.2.odd_y = f32[200,128]{1,0:T(8,128)S(1)} collective-permute-done((f32[200,128]{1,0:T(8,128)S(1)}, f32[200,128]{1,0:T(8,128)S(1)}, u32[]{:S(2)}, u32[]{:S(2)}) %collective-permute-start.2) | collective-permute-done | bytes 102432 | tf_op jit(solution)/shard_map/ppermute | solution.py:724
  11.6 2.1 %collective-permute-done.3.even_y = f32[200,128]{1,0:T(8,128)S(1)} collective-permute-done((f32[200,128]{1,0:T(8,128)S(1)}, f32[200,128]{1,0:T(8,128)S(1)}, u32[]{:S(2)}, u32[]{:S(2)}) %collective-permute-start.3) | collective-permute-done | bytes 102432 | tf_op jit(solution)/shard_map/ppermute | solution.py:724
  13.7 0.6 %collective-permute-start.5 = (f32[32,128]{1,0:T(8,128)S(1)}, f32[32,128]{1,0:T(8,128)S(1)}, u32[]{:S(2)}, u32[]{:S(2)}) collective-permute-start(f32[32,128]{1,0:T(8,128)S(1)} %corners.1), channel_id=1, source_target_pairs={{0,24},{8,16},{16,8},{24,0},{1,25},{9,17},{17,9},{25,1},{2,26},{10... | collective-permute-start | bytes 49160 | tf_op jit(solution)/shard_map/ppermute | solution.py:724
  14.3 1.1 %collective-permute-start.4 = (f32[32,128]{1,0:T(8,128)S(1)}, f32[32,128]{1,0:T(8,128)S(1)}, u32[]{:S(2)}, u32[]{:S(2)}) collective-permute-start(f32[32,128]{1,0:T(8,128)S(1)} %corners.1), channel_id=1, source_target_pairs={{0,8},{8,0},{16,24},{24,16},{1,9},{9,1},{17,25},{25,17},{2,10},{10... | collective-permute-start | bytes 49160 | tf_op jit(solution)/shard_map/ppermute | solution.py:724
  15.4 0.0 collective-permute-done.1.odd_x
  15.4 0.0 collective-permute-done.even_x
  15.4 1.1 %early.1 = (f32[512,128]{1,0:T(8,128)S(1)}, f32[512,128]{1,0:T(8,128)S(1)}, f32[512,128]{1,0:T(8,128)S(1)}, f32[512,128]{1,0:T(8,128)S(1)}, f32[208,128]{1,0:T(8...) custom-call(f32[512,128]{1,0:T(8,128)S(1)} %get-tuple-element.50.rig, ...), custom_call_target="tpu_custom_call" | custom-call | tf_op jit(solution)/shard_map/early/pallas_call | solution.py:707
  16.5 0.5 %collective-permute-done.5.odd_shared = f32[32,128]{1,0:T(8,128)S(1)} collective-permute-done((f32[32,128]{1,0:T(8,128)S(1)}, f32[32,128]{1,0:T(8,128)S(1)}, u32[]{:S(2)}, u32[]{:S(2)}) %collective-permute-start.5) | collective-permute-done | bytes 16416 | tf_op jit(solution)/shard_map/ppermute | solution.py:724
  17.0 0.0 collective-permute-done.4.even_shared
  17.0 0.3 first.1
  17.3 2.3 %collective-permute-start.8 = (f32[64,128]{1,0:T(8,128)S(1)}, f32[64,128]{1,0:T(8,128)S(1)}, u32[]{:S(2)}, u32[]{:S(2)}) collective-permute-start(f32[64,128]{1,0:T(8,128)S(1)} %get-tuple-element.68), channel_id=1, source_target_pairs={{0,7},{1,2},{2,1},{3,4},{4,3},{5,6},{6,5},{7,0},{8,15},{9,10},{10,... | collective-permute-start | bytes 98312 | tf_op jit(solution)/shard_map/ppermute | solution.py:724
  19.7 0.0 collective-permute-start.9
  19.7 0.0 collective-permute-start.7
  19.7 1.5 %collective-permute-start.6 = (f32[64,128]{1,0:T(8,128)S(1)}, f32[64,128]{1,0:T(8,128)S(1)}, u32[]{:S(2)}, u32[]{:S(2)}) collective-permute-start(f32[64,128]{1,0:T(8,128)S(1)} %get-tuple-element.67), channel_id=1, source_target_pairs={{0,8},{8,0},{16,24},{24,16},{1,9},{9,1},{17,25},{25,17},{2,10},{10... | collective-permute-start | bytes 98312 | tf_op jit(solution)/shard_map/ppermute | solution.py:724
  21.2 0.7 %inner.2 = (f32[512,128]{1,0:T(8,128)S(1)}, f32[512,128]{1,0:T(8,128)S(1)}, f32[16,128]{1,0:T(8,128)S(1)}) custom-call(f32[512,128]{1,0:T(8,128)S(1)} %get-tuple-element.66.before_image, f32[512,128]{1,0:T(8,128)S(1)} %get-tuple-element.70.diagonal, f32[512,128]{1,0:T(8,128)S(1)} %get-tuple-element.71.jacobi, ...), custom_call_target="tpu_custom_call" | custom-call | tf_op jit(solution)/shard_map/inner/pallas_call | solution.py:707
  21.9 2.1 %collective-permute-done.8.odd_y = f32[64,128]{1,0:T(8,128)S(1)} collective-permute-done((f32[64,128]{1,0:T(8,128)S(1)}, f32[64,128]{1,0:T(8,128)S(1)}, u32[]{:S(2)}, u32[]{:S(2)}) %collective-permute-start.8) | collective-permute-done | bytes 32800 | tf_op jit(solution)/shard_map/ppermute | solution.py:724
  24.0 0.0 collective-permute-done.9.even_y
  24.0 0.0 collective-permute-done.7.odd_x
  24.0 0.0 collective-permute-done.6.even_x
  24.0 0.5 %second.1 = (f32[512,128]{1,0:T(8,128)S(1)}, f32[512,128]{1,0:T(8,128)S(1)}, f32[64,128]{1,0:T(8,128)S(1)}, f32[64,128]{1,0:T(8,128)S(1)}, f32[64,128]{1,0:T(8,128)S(1)}, /*index=5*/f32[24,128]{1,0:T(8,128)S(1)}) custom-call(f32[512,128]{1,0:T(8,128)S(1)} %get-tuple-element.66.before_image, ...), custom_call_target="tpu_custom_call", output_to_operand_aliasing={{0}: (18, {}), {1}: (19, {})} | custom-call | tf_op jit(solution)/shard_map/second/pallas_call | solution.py:707
  24.5 2.4 %collective-permute-start.12 = (f32[64,128]{1,0:T(8,128)S(1)}, f32[64,128]{1,0:T(8,128)S(1)}, u32[]{:S(2)}, u32[]{:S(2)}) collective-permute-start(f32[64,128]{1,0:T(8,128)S(1)} %get-tuple-element.83), channel_id=1, source_target_pairs={{0,7},{1,2},{2,1},{3,4},{4,3},{5,6},{6,5},{7,0},{8,15},{9,10},{10,... | collective-permute-start | bytes 98312 | tf_op jit(solution)/shard_map/ppermute | solution.py:724
  27.0 0.0 collective-permute-start.13
  27.0 0.0 collective-permute-start.11
  27.0 1.5 %collective-permute-start.10 = (f32[64,128]{1,0:T(8,128)S(1)}, f32[64,128]{1,0:T(8,128)S(1)}, u32[]{:S(2)}, u32[]{:S(2)}) collective-permute-start(f32[64,128]{1,0:T(8,128)S(1)} %get-tuple-element.82), channel_id=1, source_target_pairs={{0,8},{8,0},{16,24},{24,16},{1,9},{9,1},{17,25},{25,17},{2,10},{10... | collective-permute-start | bytes 98312 | tf_op jit(solution)/shard_map/ppermute | solution.py:724
  28.5 0.7 %inner.3 = (f32[512,128]{1,0:T(8,128)S(1)}, f32[512,128]{1,0:T(8,128)S(1)}, f32[16,128]{1,0:T(8,128)S(1)}) custom-call(f32[512,128]{1,0:T(8,128)S(1)} %get-tuple-element.81.before_image, f32[512,128]{1,0:T(8,128)S(1)} %get-tuple-element.70.diagonal, f32[512,128]{1,0:T(8,128)S(1)} %get-tuple-element.71.jacobi, ...), custom_call_target="tpu_custom_call" | custom-call | tf_op jit(solution)/shard_map/inner/pallas_call | solution.py:707
  29.2 2.1 %collective-permute-done.12.odd_y = f32[64,128]{1,0:T(8,128)S(1)} collective-permute-done((f32[64,128]{1,0:T(8,128)S(1)}, f32[64,128]{1,0:T(8,128)S(1)}, u32[]{:S(2)}, u32[]{:S(2)}) %collective-permute-start.12) | collective-permute-done | bytes 32800 | tf_op jit(solution)/shard_map/ppermute | solution.py:724
  31.2 0.0 collective-permute-done.13.even_y
  31.2 0.0 collective-permute-done.11.odd_x
  31.2 0.0 collective-permute-done.10.even_x
  31.2 1.2 %third.1 = (f32[512,128]{1,0:T(8,128)S(1)}, f32[512,128]{1,0:T(8,128)S(1)}, f32[64,128]{1,0:T(8,128)S(1)}, f32[64,128]{1,0:T(8,128)S(1)}, f32[64,128]{1,0:T(8,128)S(1)}, /*index=5*/f32[32,2,128]{2,1,0:T(2,128)}) custom-call(f32[512,128]{1,0:T(8,128)S(1)} %get-tuple-element.81.before_image, ...), custom_call_target="tpu_custom_call", output_to_operand_aliasing={{0}: (18, {}), {1}: (19, {})} | custom-call | tf_op jit(solution)/shard_map/third/pallas_call | solution.py:707
  32.4 3.6 %all-to-all-start = ((f32[32,2,128]{2,1,0:T(2,128)}), f32[32,2,128]{2,1,0:T(2,128)S(1)}, u32[]{:S(2)}, u32[]{:S(2)}) async-start(f32[32,2,128]{2,1,0:T(2,128)} %get-tuple-element.90), calls=%async_computation | async-start | bytes 65536 | tf_op jit(solution)/shard_map/all_to_all | solution.py:779
  36.0 4.6 %collective-permute-start.16 = (f32[64,128]{1,0:T(8,128)S(1)}, f32[64,128]{1,0:T(8,128)S(1)}, u32[]{:S(2)}, u32[]{:S(2)}) collective-permute-start(f32[64,128]{1,0:T(8,128)S(1)} %get-tuple-element.95), channel_id=1, source_target_pairs={{0,7},{1,2},{2,1},{3,4},{4,3},{5,6},{6,5},{7,0},{8,15},{9,10},{10,... | collective-permute-start | bytes 98312 | tf_op jit(solution)/shard_map/ppermute | solution.py:724
  40.6 0.0 collective-permute-start.17
  40.6 1.0 %collective-permute-start.15 = (f32[64,128]{1,0:T(8,128)S(1)}, f32[64,128]{1,0:T(8,128)S(1)}, u32[]{:S(2)}, u32[]{:S(2)}) collective-permute-start(f32[64,128]{1,0:T(8,128)S(1)} %get-tuple-element.94), channel_id=1, source_target_pairs={{0,24},{8,16},{16,8},{24,0},{1,25},{9,17},{17,9},{25,1},{2,26},{10... | collective-permute-start | bytes 98312 | tf_op jit(solution)/shard_map/ppermute | solution.py:724
  41.6 0.6 %collective-permute-start.14 = (f32[64,128]{1,0:T(8,128)S(1)}, f32[64,128]{1,0:T(8,128)S(1)}, u32[]{:S(2)}, u32[]{:S(2)}) collective-permute-start(f32[64,128]{1,0:T(8,128)S(1)} %get-tuple-element.94), channel_id=1, source_target_pairs={{0,8},{8,0},{16,24},{24,16},{1,9},{9,1},{17,25},{25,17},{2,10},{10... | collective-permute-start | bytes 98312 | tf_op jit(solution)/shard_map/ppermute | solution.py:724
  42.2 1.0 %all-to-all-done.sums = f32[32,2,128]{2,1,0:T(2,128)S(1)} async-done(((f32[32,2,128]{2,1,0:T(2,128)}), f32[32,2,128]{2,1,0:T(2,128)S(1)}, u32[]{:S(2)}, u32[]{:S(2)}) %all-to-all-start) | async-done | bytes 32800 | tf_op jit(solution)/shard_map/all_to_all | solution.py:779
  43.2 1.2 %solution.1 = (f32[1,1,128,512]{3,2,1,0:T(8,128)}, f32[32,128]{1,0:T(8,128)S(1)}) custom-call(f32[512,128]{1,0:T(8,128)S(1)} %get-tuple-element.65.before.values0, f32[512,128]{1,0:T(8,128)S(1)} %get-tuple-element.80.before.values1, f32[512,128]{1,0:T(8,128)S(1)} %get-tuple-element.89.values2, f32[32,2,128]{2,1,0:T(2,128)S(1)} %all-to-all-done.sums, ...), custom_call_target="tpu_custom_call" | custom-call | tf_op jit(solution)/shard_map/solution/pallas_call | solution.py:707
  44.4 0.0 collective-permute-done.16.odd_y
  44.4 0.1 collective-permute-done.17.even_y
  44.5 0.0 collective-permute-done.15.odd_x
  44.5 0.0 collective-permute-done.14.even_x
  44.5 1.0 %last.1 = f32[1,1,128,512]{3,2,1,0:T(8,128)} custom-call(f32[512,128]{1,0:T(8,128)S(1)} %get-tuple-element.93.before_image, f32[64,128]{1,0:T(8,128)S(1)} %collective-permute-done.14.even_x, f32[64,128]{1,0:T(8,128)S(1)} %collective-permute-done.15.odd_x, f32[64,128]{1,0:T(8,128)S(1)} %collective-permute-done.16.odd_y, ...), custom_call_target="tpu_custom_call" | custom-call | tf_op jit(solution)/shard_map/last/pallas_call | solution.py:707
  (1 shorter events, 0.0 us)
Async XLA Ops:
  2.6 9.0 %collective-permute-start.2 = (f32[200,128]{1,0:T(8,128)S(1)}, f32[200,128]{1,0:T(8,128)S(1)}, u32[]{:S(2)}, u32[]{:S(2)}) collective-permute-start(f32[200,128]{1,0:T(8,128)S(1)} %get-tuple-element.53), channel_id=1, source_target_pairs={{0,7},{1,2},{2,1},{3,4},{4,3},{5,6},{6,5},{7,0},{8,15},{9,10},{10,... | collective-permute-start | bytes 307208 | tf_op jit(solution)/shard_map/ppermute | solution.py:724
  8.6 5.1 %collective-permute-start.3 = (f32[200,128]{1,0:T(8,128)S(1)}, f32[200,128]{1,0:T(8,128)S(1)}, u32[]{:S(2)}, u32[]{:S(2)}) collective-permute-start(f32[200,128]{1,0:T(8,128)S(1)} %get-tuple-element.54), channel_id=1, source_target_pairs={{0,1},{1,0},{2,3},{3,2},{4,5},{5,4},{6,7},{7,6},{8,9},{9,8},{10,11... | collective-permute-start | bytes 307208 | tf_op jit(solution)/shard_map/ppermute | solution.py:724
  8.6 6.8 %collective-permute-start.1 = (f32[192,128]{1,0:T(8,128)S(1)}, f32[192,128]{1,0:T(8,128)S(1)}, u32[]{:S(2)}, u32[]{:S(2)}) collective-permute-start(f32[192,128]{1,0:T(8,128)S(1)} %get-tuple-element.52), channel_id=1, source_target_pairs={{0,24},{8,16},{16,8},{24,0},{1,25},{9,17},{17,9},{25,1},{2,26},{10... | collective-permute-start | bytes 294920 | tf_op jit(solution)/shard_map/ppermute | solution.py:724
  9.3 6.1 %collective-permute-start = (f32[192,128]{1,0:T(8,128)S(1)}, f32[192,128]{1,0:T(8,128)S(1)}, u32[]{:S(2)}, u32[]{:S(2)}) collective-permute-start(f32[192,128]{1,0:T(8,128)S(1)} %get-tuple-element.52), channel_id=1, source_target_pairs={{0,8},{8,0},{16,24},{24,16},{1,9},{9,1},{17,25},{25,17},{2,10},{10... | collective-permute-start | bytes 294920 | tf_op jit(solution)/shard_map/ppermute | solution.py:724
  13.7 3.3 %collective-permute-start.5 = (f32[32,128]{1,0:T(8,128)S(1)}, f32[32,128]{1,0:T(8,128)S(1)}, u32[]{:S(2)}, u32[]{:S(2)}) collective-permute-start(f32[32,128]{1,0:T(8,128)S(1)} %corners.1), channel_id=1, source_target_pairs={{0,24},{8,16},{16,8},{24,0},{1,25},{9,17},{17,9},{25,1},{2,26},{10... | collective-permute-start | bytes 49160 | tf_op jit(solution)/shard_map/ppermute | solution.py:724
  14.3 2.8 %collective-permute-start.4 = (f32[32,128]{1,0:T(8,128)S(1)}, f32[32,128]{1,0:T(8,128)S(1)}, u32[]{:S(2)}, u32[]{:S(2)}) collective-permute-start(f32[32,128]{1,0:T(8,128)S(1)} %corners.1), channel_id=1, source_target_pairs={{0,8},{8,0},{16,24},{24,16},{1,9},{9,1},{17,25},{25,17},{2,10},{10... | collective-permute-start | bytes 49160 | tf_op jit(solution)/shard_map/ppermute | solution.py:724
  17.3 6.7 %collective-permute-start.8 = (f32[64,128]{1,0:T(8,128)S(1)}, f32[64,128]{1,0:T(8,128)S(1)}, u32[]{:S(2)}, u32[]{:S(2)}) collective-permute-start(f32[64,128]{1,0:T(8,128)S(1)} %get-tuple-element.68), channel_id=1, source_target_pairs={{0,7},{1,2},{2,1},{3,4},{4,3},{5,6},{6,5},{7,0},{8,15},{9,10},{10,... | collective-permute-start | bytes 98312 | tf_op jit(solution)/shard_map/ppermute | solution.py:724
  19.7 4.3 %collective-permute-start.9 = (f32[64,128]{1,0:T(8,128)S(1)}, f32[64,128]{1,0:T(8,128)S(1)}, u32[]{:S(2)}, u32[]{:S(2)}) collective-permute-start(f32[64,128]{1,0:T(8,128)S(1)} %get-tuple-element.69), channel_id=1, source_target_pairs={{0,1},{1,0},{2,3},{3,2},{4,5},{5,4},{6,7},{7,6},{8,9},{9,8},{10,11... | collective-permute-start | bytes 98312 | tf_op jit(solution)/shard_map/ppermute | solution.py:724
  19.7 4.3 %collective-permute-start.7 = (f32[64,128]{1,0:T(8,128)S(1)}, f32[64,128]{1,0:T(8,128)S(1)}, u32[]{:S(2)}, u32[]{:S(2)}) collective-permute-start(f32[64,128]{1,0:T(8,128)S(1)} %get-tuple-element.67), channel_id=1, source_target_pairs={{0,24},{8,16},{16,8},{24,0},{1,25},{9,17},{17,9},{25,1},{2,26},{10... | collective-permute-start | bytes 98312 | tf_op jit(solution)/shard_map/ppermute | solution.py:724
  19.7 4.3 %collective-permute-start.6 = (f32[64,128]{1,0:T(8,128)S(1)}, f32[64,128]{1,0:T(8,128)S(1)}, u32[]{:S(2)}, u32[]{:S(2)}) collective-permute-start(f32[64,128]{1,0:T(8,128)S(1)} %get-tuple-element.67), channel_id=1, source_target_pairs={{0,8},{8,0},{16,24},{24,16},{1,9},{9,1},{17,25},{25,17},{2,10},{10... | collective-permute-start | bytes 98312 | tf_op jit(solution)/shard_map/ppermute | solution.py:724
  24.5 6.7 %collective-permute-start.12 = (f32[64,128]{1,0:T(8,128)S(1)}, f32[64,128]{1,0:T(8,128)S(1)}, u32[]{:S(2)}, u32[]{:S(2)}) collective-permute-start(f32[64,128]{1,0:T(8,128)S(1)} %get-tuple-element.83), channel_id=1, source_target_pairs={{0,7},{1,2},{2,1},{3,4},{4,3},{5,6},{6,5},{7,0},{8,15},{9,10},{10,... | collective-permute-start | bytes 98312 | tf_op jit(solution)/shard_map/ppermute | solution.py:724
  27.0 4.3 %collective-permute-start.13 = (f32[64,128]{1,0:T(8,128)S(1)}, f32[64,128]{1,0:T(8,128)S(1)}, u32[]{:S(2)}, u32[]{:S(2)}) collective-permute-start(f32[64,128]{1,0:T(8,128)S(1)} %get-tuple-element.84), channel_id=1, source_target_pairs={{0,1},{1,0},{2,3},{3,2},{4,5},{5,4},{6,7},{7,6},{8,9},{9,8},{10,11... | collective-permute-start | bytes 98312 | tf_op jit(solution)/shard_map/ppermute | solution.py:724
  27.0 4.3 %collective-permute-start.11 = (f32[64,128]{1,0:T(8,128)S(1)}, f32[64,128]{1,0:T(8,128)S(1)}, u32[]{:S(2)}, u32[]{:S(2)}) collective-permute-start(f32[64,128]{1,0:T(8,128)S(1)} %get-tuple-element.82), channel_id=1, source_target_pairs={{0,24},{8,16},{16,8},{24,0},{1,25},{9,17},{17,9},{25,1},{2,26},{10... | collective-permute-start | bytes 98312 | tf_op jit(solution)/shard_map/ppermute | solution.py:724
  27.0 4.3 %collective-permute-start.10 = (f32[64,128]{1,0:T(8,128)S(1)}, f32[64,128]{1,0:T(8,128)S(1)}, u32[]{:S(2)}, u32[]{:S(2)}) collective-permute-start(f32[64,128]{1,0:T(8,128)S(1)} %get-tuple-element.82), channel_id=1, source_target_pairs={{0,8},{8,0},{16,24},{24,16},{1,9},{9,1},{17,25},{25,17},{2,10},{10... | collective-permute-start | bytes 98312 | tf_op jit(solution)/shard_map/ppermute | solution.py:724
  32.4 10.8 %all-to-all-start = ((f32[32,2,128]{2,1,0:T(2,128)}), f32[32,2,128]{2,1,0:T(2,128)S(1)}, u32[]{:S(2)}, u32[]{:S(2)}) async-start(f32[32,2,128]{2,1,0:T(2,128)} %get-tuple-element.90), calls=%async_computation | async-start | bytes 65536 | tf_op jit(solution)/shard_map/all_to_all | solution.py:779
  36.0 8.4 %collective-permute-start.16 = (f32[64,128]{1,0:T(8,128)S(1)}, f32[64,128]{1,0:T(8,128)S(1)}, u32[]{:S(2)}, u32[]{:S(2)}) collective-permute-start(f32[64,128]{1,0:T(8,128)S(1)} %get-tuple-element.95), channel_id=1, source_target_pairs={{0,7},{1,2},{2,1},{3,4},{4,3},{5,6},{6,5},{7,0},{8,15},{9,10},{10,... | collective-permute-start | bytes 98312 | tf_op jit(solution)/shard_map/ppermute | solution.py:724
  40.6 3.9 %collective-permute-start.17 = (f32[64,128]{1,0:T(8,128)S(1)}, f32[64,128]{1,0:T(8,128)S(1)}, u32[]{:S(2)}, u32[]{:S(2)}) collective-permute-start(f32[64,128]{1,0:T(8,128)S(1)} %get-tuple-element.96), channel_id=1, source_target_pairs={{0,1},{1,0},{2,3},{3,2},{4,5},{5,4},{6,7},{7,6},{8,9},{9,8},{10,11... | collective-permute-start | bytes 98312 | tf_op jit(solution)/shard_map/ppermute | solution.py:724
  40.6 3.9 %collective-permute-start.15 = (f32[64,128]{1,0:T(8,128)S(1)}, f32[64,128]{1,0:T(8,128)S(1)}, u32[]{:S(2)}, u32[]{:S(2)}) collective-permute-start(f32[64,128]{1,0:T(8,128)S(1)} %get-tuple-element.94), channel_id=1, source_target_pairs={{0,24},{8,16},{16,8},{24,0},{1,25},{9,17},{17,9},{25,1},{2,26},{10... | collective-permute-start | bytes 98312 | tf_op jit(solution)/shard_map/ppermute | solution.py:724
  41.6 2.9 %collective-permute-start.14 = (f32[64,128]{1,0:T(8,128)S(1)}, f32[64,128]{1,0:T(8,128)S(1)}, u32[]{:S(2)}, u32[]{:S(2)}) collective-permute-start(f32[64,128]{1,0:T(8,128)S(1)} %get-tuple-element.94), channel_id=1, source_target_pairs={{0,8},{8,0},{16,24},{24,16},{1,9},{9,1},{17,25},{25,17},{2,10},{10... | collective-permute-start | bytes 98312 | tf_op jit(solution)/shard_map/ppermute | solution.py:724

commit v11 on v10

--- a/solution.py
+++ b/solution.py
@@ -357,8 +357,9 @@
 
 
 def early_kernel(
-    right, diagonal, even_x, odd_x, odd_y, even_y, spread, mass,
+    right, diagonal, even_x, odd_x, odd_y, even_y, spread, mass, slot_rows,
     whole_diagonal, jacobi, values, image, outer, moments, from_low, from_high, from_side, packed,
+    chosen,
 ):
     received = (even_x, odd_x, even_y, odd_y)
     first = lane_index() < HALF
@@ -392,6 +393,7 @@
             )
     operate(values, spread, image)
     join_layers(image)
+    chosen[...] = selection(slot_rows).T
     for a in range(8):
         for end, out in ((0, from_low), (7, from_high)):
             slopes = [spread[row(a, q), :] * float(DERIVATIVE[q, end]) for q in range(8)]
@@ -655,7 +657,7 @@
 
 
 def solution_kernel(
-    values0, values1, values2, sums, slot_rows, solution, precond_rows, solution_grid
+    values0, values1, values2, sums, chosen, solution, precond_rows, solution_grid
 ):
     line = jnp.sum(sums[...], 0)[0:1]
     lane = lax.broadcasted_iota(jnp.int32, (1, LANES), 1)
@@ -674,13 +676,12 @@
                 + result[1] * values1[rows, :]
                 + result[2] * values2[rows, :]
             )
-    chosen = selection(slot_rows).T.astype(jnp.bfloat16)
-    solution[0, 0] = to_slots(chosen, solution_grid[...])
+    solution[0, 0] = to_slots(chosen[...].astype(jnp.bfloat16), solution_grid[...])
 
 
 def last_kernel(
     before_image, even_x, odd_x, odd_y, even_y, diagonal, values0, values1, values2, precond_rows,
-    slot_rows, residual, residual_grid,
+    chosen, residual, residual_grid,
 ):
     received = (even_x, odd_x, even_y, odd_y)
     precond = [precond_rows[pl.ds(8 * k, 8), :] for k in range(4)]
@@ -694,8 +695,7 @@
             )
             image = assembled(a, b, before_image, received, 0)
             residual_grid[rows, :] = diagonal[rows, :] * far + precond[3] * image
-    chosen = selection(slot_rows).T.astype(jnp.bfloat16)
-    residual[0, 0] = to_slots(chosen, residual_grid[...])
+    residual[0, 0] = to_slots(chosen[...].astype(jnp.bfloat16), residual_grid[...])
 
 
 def call(kernel, name, shapes, scratch, *operands, outside=0, aliases=None, copied=0):
@@ -742,9 +742,10 @@
     received_x, received_y = swapped((out_x, out_x), "gx"), swapped(sent_y, "yz")[::-1]
     [shared] = call(corners_kernel, "corners", [(32, LANES)], [], corners, *received_y)
     received = (*received_x, *received_y, *swapped((shared, shared), "gx"))
-    *early, outer, moments0, from_low, from_high, from_side, packed = call(
-        early_kernel, "early", [grid] * 4 + [(208, LANES), tile] + [grid] * 3 + [(192, LANES)], [],
-        right, diagonal, *received_x, *received_y, spread, mass,
+    *early, outer, moments0, from_low, from_high, from_side, packed, chosen = call(
+        early_kernel, "early", [grid] * 4 + [(208, LANES), tile] + [grid] * 3 + [(192, LANES)]
+        + [(LANES, LANES)], [],
+        right, diagonal, *received_x, *received_y, spread, mass, slot_rows,
     )
     diagonal, jacobi, values0, image, out_x, *sent_y, moments0 = call(
         first_kernel, "first", [grid] * 4 + [face] * 3 + [tile], [],
@@ -781,11 +782,11 @@
     result, precond = call(
         solution_kernel, "solution", [forcing.shape, (32, LANES)],
         [pltpu.VMEM(grid, jnp.float32)],
-        values0, values1, values2, sums, slot_rows,
+        values0, values1, values2, sums, chosen,
     )
     [residual] = call(
         last_kernel, "last", [forcing.shape], [pltpu.VMEM(grid, jnp.float32)],
-        image, *received, diagonal, values0, values1, values2, precond, slot_rows,
+        image, *received, diagonal, values0, values1, values2, precond, chosen,
     )
     return result, residual
 

time: 45.7 us -> 45.7 us (level)
  no operation moved by 1% of the time
where the time goes in v11:
time: 45.7 us; the launch traced here: 45.5 us
  starting transfers between devices  27 us (59%)
  waiting for transfers between devices  9.29 us (20%)
  Pallas kernels  8.5 us (19%)
  between operations  0.7 us (2%)
    ppermute x9, starting transfers between devices, swapped(): lax.ppermute(block[1], axis, odd)  17.6 us
    pallas_call x10, Pallas kernels, call(): pl.pallas_call(kernel, out_shape=[jax.ShapeDtypeStruct(shape, jnp.float32...  8.5 us
    ppermute x9, waiting for transfers between devices, swapped(): lax.ppermute(block[1], axis, odd)  6.04 us
    ppermute x9, starting transfers between devices, swapped(): lax.ppermute(block[0], axis, even)  5.81 us
    all_to_all x1, starting transfers between devices, body(): sums = lax.all_to_all(sums, ('gx', 'yz'), 0, 0)  3.58 us
    ppermute x9, waiting for transfers between devices, swapped(): lax.ppermute(block[0], axis, even)  2.27 us
    all_to_all x1, waiting for transfers between devices, body(): sums = lax.all_to_all(sums, ('gx', 'yz'), 0, 0)  0.99 us
  transfers between devices with their start and end apart: 19, of which 7 were waited for; matrix products, arithmetic and copies ran while one was open for 0% of the time, Pallas kernels for 8%

profile of v11, /device:TPU:0, one launch (start us, length us, event | category | flops | bytes accessed | tf_op | source)
XLA Modules:
  0.0 45.5 jit_solution(9434238666373550344)
XLA Ops:
  0.6 1.9 %setup.1 = (f32[512,128]{1,0:T(8,128)S(1)}, f32[512,128]{1,0:T(8,128)S(1)}, f32[512,128]{1,0:T(8,128)S(1)}, f32[512,128]{1,0:T(8,128)S(1)}, f32[192,128]{1,0:T(8...) custom-call(s32[1,128]{1,0:T(1,128)} %bitcast.1, ...), custom_call_target="tpu_custom_call" | custom-call | tf_op jit(solution)/shard_map/setup/pallas_call | solution.py:707
  2.6 6.0 %collective-permute-start.2 = (f32[200,128]{1,0:T(8,128)S(1)}, f32[200,128]{1,0:T(8,128)S(1)}, u32[]{:S(2)}, u32[]{:S(2)}) collective-permute-start(f32[200,128]{1,0:T(8,128)S(1)} %get-tuple-element.54), channel_id=1, source_target_pairs={{0,7},{1,2},{2,1},{3,4},{4,3},{5,6},{6,5},{7,0},{8,15},{9,10},{10,... | collective-permute-start | bytes 307208 | tf_op jit(solution)/shard_map/ppermute | solution.py:724
  8.6 0.0 collective-permute-start.3
  8.6 0.7 %collective-permute-start.1 = (f32[192,128]{1,0:T(8,128)S(1)}, f32[192,128]{1,0:T(8,128)S(1)}, u32[]{:S(2)}, u32[]{:S(2)}) collective-permute-start(f32[192,128]{1,0:T(8,128)S(1)} %get-tuple-element.53), channel_id=1, source_target_pairs={{0,24},{8,16},{16,8},{24,0},{1,25},{9,17},{17,9},{25,1},{2,26},{10... | collective-permute-start | bytes 294920 | tf_op jit(solution)/shard_map/ppermute | solution.py:724
  9.3 1.0 %collective-permute-start = (f32[192,128]{1,0:T(8,128)S(1)}, f32[192,128]{1,0:T(8,128)S(1)}, u32[]{:S(2)}, u32[]{:S(2)}) collective-permute-start(f32[192,128]{1,0:T(8,128)S(1)} %get-tuple-element.53), channel_id=1, source_target_pairs={{0,8},{8,0},{16,24},{24,16},{1,9},{9,1},{17,25},{25,17},{2,10},{10... | collective-permute-start | bytes 294920 | tf_op jit(solution)/shard_map/ppermute | solution.py:724
  10.3 1.3 %collective-permute-done.2.odd_y = f32[200,128]{1,0:T(8,128)S(1)} collective-permute-done((f32[200,128]{1,0:T(8,128)S(1)}, f32[200,128]{1,0:T(8,128)S(1)}, u32[]{:S(2)}, u32[]{:S(2)}) %collective-permute-start.2) | collective-permute-done | bytes 102432 | tf_op jit(solution)/shard_map/ppermute | solution.py:724
  11.6 2.1 %collective-permute-done.3.even_y = f32[200,128]{1,0:T(8,128)S(1)} collective-permute-done((f32[200,128]{1,0:T(8,128)S(1)}, f32[200,128]{1,0:T(8,128)S(1)}, u32[]{:S(2)}, u32[]{:S(2)}) %collective-permute-start.3) | collective-permute-done | bytes 102432 | tf_op jit(solution)/shard_map/ppermute | solution.py:724
  13.7 0.6 %collective-permute-start.5 = (f32[32,128]{1,0:T(8,128)S(1)}, f32[32,128]{1,0:T(8,128)S(1)}, u32[]{:S(2)}, u32[]{:S(2)}) collective-permute-start(f32[32,128]{1,0:T(8,128)S(1)} %corners.1), channel_id=1, source_target_pairs={{0,24},{8,16},{16,8},{24,0},{1,25},{9,17},{17,9},{25,1},{2,26},{10... | collective-permute-start | bytes 49160 | tf_op jit(solution)/shard_map/ppermute | solution.py:724
  14.3 1.1 %collective-permute-start.4 = (f32[32,128]{1,0:T(8,128)S(1)}, f32[32,128]{1,0:T(8,128)S(1)}, u32[]{:S(2)}, u32[]{:S(2)}) collective-permute-start(f32[32,128]{1,0:T(8,128)S(1)} %corners.1), channel_id=1, source_target_pairs={{0,8},{8,0},{16,24},{24,16},{1,9},{9,1},{17,25},{25,17},{2,10},{10... | collective-permute-start | bytes 49160 | tf_op jit(solution)/shard_map/ppermute | solution.py:724
  15.4 0.0 collective-permute-done.1.odd_x
  15.4 0.0 collective-permute-done.even_x
  15.4 1.1 %early.1 = (f32[512,128]{1,0:T(8,128)S(1)}, f32[512,128]{1,0:T(8,128)S(1)}, f32[512,128]{1,0:T(8,128)S(1)}, f32[512,128]{1,0:T(8,128)S(1)}, f32[208,128]{1,0:T(8...) custom-call(f32[512,128]{1,0:T(8,128)S(1)} %get-tuple-element.51.rig, ...), custom_call_target="tpu_custom_call" | custom-call | tf_op jit(solution)/shard_map/early/pallas_call | solution.py:707
  16.5 0.5 %collective-permute-done.5.odd_shared = f32[32,128]{1,0:T(8,128)S(1)} collective-permute-done((f32[32,128]{1,0:T(8,128)S(1)}, f32[32,128]{1,0:T(8,128)S(1)}, u32[]{:S(2)}, u32[]{:S(2)}) %collective-permute-start.5) | collective-permute-done | bytes 16416 | tf_op jit(solution)/shard_map/ppermute | solution.py:724
  17.0 0.0 collective-permute-done.4.even_shared
  17.0 0.3 first.1
  17.3 2.3 %collective-permute-start.8 = (f32[64,128]{1,0:T(8,128)S(1)}, f32[64,128]{1,0:T(8,128)S(1)}, u32[]{:S(2)}, u32[]{:S(2)}) collective-permute-start(f32[64,128]{1,0:T(8,128)S(1)} %get-tuple-element.70), channel_id=1, source_target_pairs={{0,7},{1,2},{2,1},{3,4},{4,3},{5,6},{6,5},{7,0},{8,15},{9,10},{10,... | collective-permute-start | bytes 98312 | tf_op jit(solution)/shard_map/ppermute | solution.py:724
  19.7 0.0 collective-permute-start.9
  19.7 0.0 collective-permute-start.7
  19.7 1.5 %collective-permute-start.6 = (f32[64,128]{1,0:T(8,128)S(1)}, f32[64,128]{1,0:T(8,128)S(1)}, u32[]{:S(2)}, u32[]{:S(2)}) collective-permute-start(f32[64,128]{1,0:T(8,128)S(1)} %get-tuple-element.69), channel_id=1, source_target_pairs={{0,8},{8,0},{16,24},{24,16},{1,9},{9,1},{17,25},{25,17},{2,10},{10... | collective-permute-start | bytes 98312 | tf_op jit(solution)/shard_map/ppermute | solution.py:724
  21.2 0.7 %inner.2 = (f32[512,128]{1,0:T(8,128)S(1)}, f32[512,128]{1,0:T(8,128)S(1)}, f32[16,128]{1,0:T(8,128)S(1)}) custom-call(f32[512,128]{1,0:T(8,128)S(1)} %get-tuple-element.68.before_image, f32[512,128]{1,0:T(8,128)S(1)} %get-tuple-element.72.diagonal, f32[512,128]{1,0:T(8,128)S(1)} %get-tuple-element.73.jacobi, ...), custom_call_target="tpu_custom_call" | custom-call | tf_op jit(solution)/shard_map/inner/pallas_call | solution.py:707
  21.9 2.1 %collective-permute-done.8.odd_y = f32[64,128]{1,0:T(8,128)S(1)} collective-permute-done((f32[64,128]{1,0:T(8,128)S(1)}, f32[64,128]{1,0:T(8,128)S(1)}, u32[]{:S(2)}, u32[]{:S(2)}) %collective-permute-start.8) | collective-permute-done | bytes 32800 | tf_op jit(solution)/shard_map/ppermute | solution.py:724
  24.0 0.0 collective-permute-done.9.even_y
  24.0 0.0 collective-permute-done.7.odd_x
  24.0 0.0 collective-permute-done.6.even_x
  24.0 0.5 %second.1 = (f32[512,128]{1,0:T(8,128)S(1)}, f32[512,128]{1,0:T(8,128)S(1)}, f32[64,128]{1,0:T(8,128)S(1)}, f32[64,128]{1,0:T(8,128)S(1)}, f32[64,128]{1,0:T(8,128)S(1)}, /*index=5*/f32[24,128]{1,0:T(8,128)S(1)}) custom-call(f32[512,128]{1,0:T(8,128)S(1)} %get-tuple-element.68.before_image, ...), custom_call_target="tpu_custom_call", output_to_operand_aliasing={{0}: (18, {}), {1}: (19, {})} | custom-call | tf_op jit(solution)/shard_map/second/pallas_call | solution.py:707
  24.5 2.4 %collective-permute-start.12 = (f32[64,128]{1,0:T(8,128)S(1)}, f32[64,128]{1,0:T(8,128)S(1)}, u32[]{:S(2)}, u32[]{:S(2)}) collective-permute-start(f32[64,128]{1,0:T(8,128)S(1)} %get-tuple-element.85), channel_id=1, source_target_pairs={{0,7},{1,2},{2,1},{3,4},{4,3},{5,6},{6,5},{7,0},{8,15},{9,10},{10,... | collective-permute-start | bytes 98312 | tf_op jit(solution)/shard_map/ppermute | solution.py:724
  27.0 0.0 collective-permute-start.13
  27.0 0.0 collective-permute-start.11
  27.0 1.5 %collective-permute-start.10 = (f32[64,128]{1,0:T(8,128)S(1)}, f32[64,128]{1,0:T(8,128)S(1)}, u32[]{:S(2)}, u32[]{:S(2)}) collective-permute-start(f32[64,128]{1,0:T(8,128)S(1)} %get-tuple-element.84), channel_id=1, source_target_pairs={{0,8},{8,0},{16,24},{24,16},{1,9},{9,1},{17,25},{25,17},{2,10},{10... | collective-permute-start | bytes 98312 | tf_op jit(solution)/shard_map/ppermute | solution.py:724
  28.5 0.7 %inner.3 = (f32[512,128]{1,0:T(8,128)S(1)}, f32[512,128]{1,0:T(8,128)S(1)}, f32[16,128]{1,0:T(8,128)S(1)}) custom-call(f32[512,128]{1,0:T(8,128)S(1)} %get-tuple-element.83.before_image, f32[512,128]{1,0:T(8,128)S(1)} %get-tuple-element.72.diagonal, f32[512,128]{1,0:T(8,128)S(1)} %get-tuple-element.73.jacobi, ...), custom_call_target="tpu_custom_call" | custom-call | tf_op jit(solution)/shard_map/inner/pallas_call | solution.py:707
  29.2 2.1 %collective-permute-done.12.odd_y = f32[64,128]{1,0:T(8,128)S(1)} collective-permute-done((f32[64,128]{1,0:T(8,128)S(1)}, f32[64,128]{1,0:T(8,128)S(1)}, u32[]{:S(2)}, u32[]{:S(2)}) %collective-permute-start.12) | collective-permute-done | bytes 32800 | tf_op jit(solution)/shard_map/ppermute | solution.py:724
  31.2 0.0 collective-permute-done.13.even_y
  31.2 0.0 collective-permute-done.11.odd_x
  31.2 0.0 collective-permute-done.10.even_x
  31.2 1.2 %third.1 = (f32[512,128]{1,0:T(8,128)S(1)}, f32[512,128]{1,0:T(8,128)S(1)}, f32[64,128]{1,0:T(8,128)S(1)}, f32[64,128]{1,0:T(8,128)S(1)}, f32[64,128]{1,0:T(8,128)S(1)}, /*index=5*/f32[32,2,128]{2,1,0:T(2,128)}) custom-call(f32[512,128]{1,0:T(8,128)S(1)} %get-tuple-element.83.before_image, ...), custom_call_target="tpu_custom_call", output_to_operand_aliasing={{0}: (18, {}), {1}: (19, {})} | custom-call | tf_op jit(solution)/shard_map/third/pallas_call | solution.py:707
  32.4 3.6 %all-to-all-start = ((f32[32,2,128]{2,1,0:T(2,128)}), f32[32,2,128]{2,1,0:T(2,128)S(1)}, u32[]{:S(2)}, u32[]{:S(2)}) async-start(f32[32,2,128]{2,1,0:T(2,128)} %get-tuple-element.92), calls=%async_computation | async-start | bytes 65536 | tf_op jit(solution)/shard_map/all_to_all | solution.py:780
  36.0 4.6 %collective-permute-start.16 = (f32[64,128]{1,0:T(8,128)S(1)}, f32[64,128]{1,0:T(8,128)S(1)}, u32[]{:S(2)}, u32[]{:S(2)}) collective-permute-start(f32[64,128]{1,0:T(8,128)S(1)} %get-tuple-element.97), channel_id=1, source_target_pairs={{0,7},{1,2},{2,1},{3,4},{4,3},{5,6},{6,5},{7,0},{8,15},{9,10},{10,... | collective-permute-start | bytes 98312 | tf_op jit(solution)/shard_map/ppermute | solution.py:724
  40.6 0.0 collective-permute-start.17
  40.6 1.0 %collective-permute-start.15 = (f32[64,128]{1,0:T(8,128)S(1)}, f32[64,128]{1,0:T(8,128)S(1)}, u32[]{:S(2)}, u32[]{:S(2)}) collective-permute-start(f32[64,128]{1,0:T(8,128)S(1)} %get-tuple-element.96), channel_id=1, source_target_pairs={{0,24},{8,16},{16,8},{24,0},{1,25},{9,17},{17,9},{25,1},{2,26},{10... | collective-permute-start | bytes 98312 | tf_op jit(solution)/shard_map/ppermute | solution.py:724
  41.6 0.6 %collective-permute-start.14 = (f32[64,128]{1,0:T(8,128)S(1)}, f32[64,128]{1,0:T(8,128)S(1)}, u32[]{:S(2)}, u32[]{:S(2)}) collective-permute-start(f32[64,128]{1,0:T(8,128)S(1)} %get-tuple-element.96), channel_id=1, source_target_pairs={{0,8},{8,0},{16,24},{24,16},{1,9},{9,1},{17,25},{25,17},{2,10},{10... | collective-permute-start | bytes 98312 | tf_op jit(solution)/shard_map/ppermute | solution.py:724
  42.2 1.0 %all-to-all-done.sums = f32[32,2,128]{2,1,0:T(2,128)S(1)} async-done(((f32[32,2,128]{2,1,0:T(2,128)}), f32[32,2,128]{2,1,0:T(2,128)S(1)}, u32[]{:S(2)}, u32[]{:S(2)}) %all-to-all-start) | async-done | bytes 32800 | tf_op jit(solution)/shard_map/all_to_all | solution.py:780
  43.2 1.2 %solution.1 = (f32[1,1,128,512]{3,2,1,0:T(8,128)}, f32[32,128]{1,0:T(8,128)S(1)}) custom-call(f32[512,128]{1,0:T(8,128)S(1)} %get-tuple-element.67.before.values0, f32[512,128]{1,0:T(8,128)S(1)} %get-tuple-element.82.before.values1, f32[512,128]{1,0:T(8,128)S(1)} %get-tuple-element.91.values2, f32[32,2,128]{2,1,0:T(2,128)S(1)} %all-to-all-done.sums, ...), custom_call_target="tpu_custom_call" | custom-call | tf_op jit(solution)/shard_map/solution/pallas_call | solution.py:707
  44.4 0.0 collective-permute-done.16.odd_y
  44.4 0.1 collective-permute-done.17.even_y
  44.5 0.0 collective-permute-done.15.odd_x
  44.5 0.0 collective-permute-done.14.even_x
  44.5 1.0 %last.1 = f32[1,1,128,512]{3,2,1,0:T(8,128)} custom-call(f32[512,128]{1,0:T(8,128)S(1)} %get-tuple-element.95.before_image, f32[64,128]{1,0:T(8,128)S(1)} %collective-permute-done.14.even_x, f32[64,128]{1,0:T(8,128)S(1)} %collective-permute-done.15.odd_x, f32[64,128]{1,0:T(8,128)S(1)} %collective-permute-done.16.odd_y, ...), custom_call_target="tpu_custom_call" | custom-call | tf_op jit(solution)/shard_map/last/pallas_call | solution.py:707
  (1 shorter events, 0.0 us)
Async XLA Ops:
  2.6 9.0 %collective-permute-start.2 = (f32[200,128]{1,0:T(8,128)S(1)}, f32[200,128]{1,0:T(8,128)S(1)}, u32[]{:S(2)}, u32[]{:S(2)}) collective-permute-start(f32[200,128]{1,0:T(8,128)S(1)} %get-tuple-element.54), channel_id=1, source_target_pairs={{0,7},{1,2},{2,1},{3,4},{4,3},{5,6},{6,5},{7,0},{8,15},{9,10},{10,... | collective-permute-start | bytes 307208 | tf_op jit(solution)/shard_map/ppermute | solution.py:724
  8.6 5.1 %collective-permute-start.3 = (f32[200,128]{1,0:T(8,128)S(1)}, f32[200,128]{1,0:T(8,128)S(1)}, u32[]{:S(2)}, u32[]{:S(2)}) collective-permute-start(f32[200,128]{1,0:T(8,128)S(1)} %get-tuple-element.55), channel_id=1, source_target_pairs={{0,1},{1,0},{2,3},{3,2},{4,5},{5,4},{6,7},{7,6},{8,9},{9,8},{10,11... | collective-permute-start | bytes 307208 | tf_op jit(solution)/shard_map/ppermute | solution.py:724
  8.6 6.8 %collective-permute-start.1 = (f32[192,128]{1,0:T(8,128)S(1)}, f32[192,128]{1,0:T(8,128)S(1)}, u32[]{:S(2)}, u32[]{:S(2)}) collective-permute-start(f32[192,128]{1,0:T(8,128)S(1)} %get-tuple-element.53), channel_id=1, source_target_pairs={{0,24},{8,16},{16,8},{24,0},{1,25},{9,17},{17,9},{25,1},{2,26},{10... | collective-permute-start | bytes 294920 | tf_op jit(solution)/shard_map/ppermute | solution.py:724
  9.3 6.1 %collective-permute-start = (f32[192,128]{1,0:T(8,128)S(1)}, f32[192,128]{1,0:T(8,128)S(1)}, u32[]{:S(2)}, u32[]{:S(2)}) collective-permute-start(f32[192,128]{1,0:T(8,128)S(1)} %get-tuple-element.53), channel_id=1, source_target_pairs={{0,8},{8,0},{16,24},{24,16},{1,9},{9,1},{17,25},{25,17},{2,10},{10... | collective-permute-start | bytes 294920 | tf_op jit(solution)/shard_map/ppermute | solution.py:724
  13.7 3.3 %collective-permute-start.5 = (f32[32,128]{1,0:T(8,128)S(1)}, f32[32,128]{1,0:T(8,128)S(1)}, u32[]{:S(2)}, u32[]{:S(2)}) collective-permute-start(f32[32,128]{1,0:T(8,128)S(1)} %corners.1), channel_id=1, source_target_pairs={{0,24},{8,16},{16,8},{24,0},{1,25},{9,17},{17,9},{25,1},{2,26},{10... | collective-permute-start | bytes 49160 | tf_op jit(solution)/shard_map/ppermute | solution.py:724
  14.3 2.8 %collective-permute-start.4 = (f32[32,128]{1,0:T(8,128)S(1)}, f32[32,128]{1,0:T(8,128)S(1)}, u32[]{:S(2)}, u32[]{:S(2)}) collective-permute-start(f32[32,128]{1,0:T(8,128)S(1)} %corners.1), channel_id=1, source_target_pairs={{0,8},{8,0},{16,24},{24,16},{1,9},{9,1},{17,25},{25,17},{2,10},{10... | collective-permute-start | bytes 49160 | tf_op jit(solution)/shard_map/ppermute | solution.py:724
  17.3 6.7 %collective-permute-start.8 = (f32[64,128]{1,0:T(8,128)S(1)}, f32[64,128]{1,0:T(8,128)S(1)}, u32[]{:S(2)}, u32[]{:S(2)}) collective-permute-start(f32[64,128]{1,0:T(8,128)S(1)} %get-tuple-element.70), channel_id=1, source_target_pairs={{0,7},{1,2},{2,1},{3,4},{4,3},{5,6},{6,5},{7,0},{8,15},{9,10},{10,... | collective-permute-start | bytes 98312 | tf_op jit(solution)/shard_map/ppermute | solution.py:724
  19.7 4.3 %collective-permute-start.9 = (f32[64,128]{1,0:T(8,128)S(1)}, f32[64,128]{1,0:T(8,128)S(1)}, u32[]{:S(2)}, u32[]{:S(2)}) collective-permute-start(f32[64,128]{1,0:T(8,128)S(1)} %get-tuple-element.71), channel_id=1, source_target_pairs={{0,1},{1,0},{2,3},{3,2},{4,5},{5,4},{6,7},{7,6},{8,9},{9,8},{10,11... | collective-permute-start | bytes 98312 | tf_op jit(solution)/shard_map/ppermute | solution.py:724
  19.7 4.3 %collective-permute-start.7 = (f32[64,128]{1,0:T(8,128)S(1)}, f32[64,128]{1,0:T(8,128)S(1)}, u32[]{:S(2)}, u32[]{:S(2)}) collective-permute-start(f32[64,128]{1,0:T(8,128)S(1)} %get-tuple-element.69), channel_id=1, source_target_pairs={{0,24},{8,16},{16,8},{24,0},{1,25},{9,17},{17,9},{25,1},{2,26},{10... | collective-permute-start | bytes 98312 | tf_op jit(solution)/shard_map/ppermute | solution.py:724
  19.7 4.3 %collective-permute-start.6 = (f32[64,128]{1,0:T(8,128)S(1)}, f32[64,128]{1,0:T(8,128)S(1)}, u32[]{:S(2)}, u32[]{:S(2)}) collective-permute-start(f32[64,128]{1,0:T(8,128)S(1)} %get-tuple-element.69), channel_id=1, source_target_pairs={{0,8},{8,0},{16,24},{24,16},{1,9},{9,1},{17,25},{25,17},{2,10},{10... | collective-permute-start | bytes 98312 | tf_op jit(solution)/shard_map/ppermute | solution.py:724
  24.5 6.7 %collective-permute-start.12 = (f32[64,128]{1,0:T(8,128)S(1)}, f32[64,128]{1,0:T(8,128)S(1)}, u32[]{:S(2)}, u32[]{:S(2)}) collective-permute-start(f32[64,128]{1,0:T(8,128)S(1)} %get-tuple-element.85), channel_id=1, source_target_pairs={{0,7},{1,2},{2,1},{3,4},{4,3},{5,6},{6,5},{7,0},{8,15},{9,10},{10,... | collective-permute-start | bytes 98312 | tf_op jit(solution)/shard_map/ppermute | solution.py:724
  27.0 4.3 %collective-permute-start.13 = (f32[64,128]{1,0:T(8,128)S(1)}, f32[64,128]{1,0:T(8,128)S(1)}, u32[]{:S(2)}, u32[]{:S(2)}) collective-permute-start(f32[64,128]{1,0:T(8,128)S(1)} %get-tuple-element.86), channel_id=1, source_target_pairs={{0,1},{1,0},{2,3},{3,2},{4,5},{5,4},{6,7},{7,6},{8,9},{9,8},{10,11... | collective-permute-start | bytes 98312 | tf_op jit(solution)/shard_map/ppermute | solution.py:724
  27.0 4.3 %collective-permute-start.11 = (f32[64,128]{1,0:T(8,128)S(1)}, f32[64,128]{1,0:T(8,128)S(1)}, u32[]{:S(2)}, u32[]{:S(2)}) collective-permute-start(f32[64,128]{1,0:T(8,128)S(1)} %get-tuple-element.84), channel_id=1, source_target_pairs={{0,24},{8,16},{16,8},{24,0},{1,25},{9,17},{17,9},{25,1},{2,26},{10... | collective-permute-start | bytes 98312 | tf_op jit(solution)/shard_map/ppermute | solution.py:724
  27.0 4.3 %collective-permute-start.10 = (f32[64,128]{1,0:T(8,128)S(1)}, f32[64,128]{1,0:T(8,128)S(1)}, u32[]{:S(2)}, u32[]{:S(2)}) collective-permute-start(f32[64,128]{1,0:T(8,128)S(1)} %get-tuple-element.84), channel_id=1, source_target_pairs={{0,8},{8,0},{16,24},{24,16},{1,9},{9,1},{17,25},{25,17},{2,10},{10... | collective-permute-start | bytes 98312 | tf_op jit(solution)/shard_map/ppermute | solution.py:724
  32.4 10.8 %all-to-all-start = ((f32[32,2,128]{2,1,0:T(2,128)}), f32[32,2,128]{2,1,0:T(2,128)S(1)}, u32[]{:S(2)}, u32[]{:S(2)}) async-start(f32[32,2,128]{2,1,0:T(2,128)} %get-tuple-element.92), calls=%async_computation | async-start | bytes 65536 | tf_op jit(solution)/shard_map/all_to_all | solution.py:780
  36.0 8.4 %collective-permute-start.16 = (f32[64,128]{1,0:T(8,128)S(1)}, f32[64,128]{1,0:T(8,128)S(1)}, u32[]{:S(2)}, u32[]{:S(2)}) collective-permute-start(f32[64,128]{1,0:T(8,128)S(1)} %get-tuple-element.97), channel_id=1, source_target_pairs={{0,7},{1,2},{2,1},{3,4},{4,3},{5,6},{6,5},{7,0},{8,15},{9,10},{10,... | collective-permute-start | bytes 98312 | tf_op jit(solution)/shard_map/ppermute | solution.py:724
  40.6 3.9 %collective-permute-start.17 = (f32[64,128]{1,0:T(8,128)S(1)}, f32[64,128]{1,0:T(8,128)S(1)}, u32[]{:S(2)}, u32[]{:S(2)}) collective-permute-start(f32[64,128]{1,0:T(8,128)S(1)} %get-tuple-element.98), channel_id=1, source_target_pairs={{0,1},{1,0},{2,3},{3,2},{4,5},{5,4},{6,7},{7,6},{8,9},{9,8},{10,11... | collective-permute-start | bytes 98312 | tf_op jit(solution)/shard_map/ppermute | solution.py:724
  40.6 3.9 %collective-permute-start.15 = (f32[64,128]{1,0:T(8,128)S(1)}, f32[64,128]{1,0:T(8,128)S(1)}, u32[]{:S(2)}, u32[]{:S(2)}) collective-permute-start(f32[64,128]{1,0:T(8,128)S(1)} %get-tuple-element.96), channel_id=1, source_target_pairs={{0,24},{8,16},{16,8},{24,0},{1,25},{9,17},{17,9},{25,1},{2,26},{10... | collective-permute-start | bytes 98312 | tf_op jit(solution)/shard_map/ppermute | solution.py:724
  41.6 2.9 %collective-permute-start.14 = (f32[64,128]{1,0:T(8,128)S(1)}, f32[64,128]{1,0:T(8,128)S(1)}, u32[]{:S(2)}, u32[]{:S(2)}) collective-permute-start(f32[64,128]{1,0:T(8,128)S(1)} %get-tuple-element.96), channel_id=1, source_target_pairs={{0,8},{8,0},{16,24},{24,16},{1,9},{9,1},{17,25},{25,17},{2,10},{10... | collective-permute-start | bytes 98312 | tf_op jit(solution)/shard_map/ppermute | solution.py:724
